TPU v7x, 32 devices: a whole 2x2x4 slice. The times are simulated.
32 devices in a mesh: gx: 8 (over z, core), gy: 4 (over y, x).
Axes of the slice: x: 2, y: 2, z: 4, core: 2. Of those that a mesh axis runs over, the one named last changes fastest.
Arguments:
- right_side: float32 [32, 128, 512], P(None, 'gx', 'gy'), may hold values from -8 to 8
- kappa_sq: float32 [32, 128, 512], P(None, 'gx', 'gy'), may hold values from 0.0001 to 0.003
- cond_x: float32 [32, 128, 512], P(None, 'gx', 'gy'), may hold values from 0.3 to 3
- cond_y: float32 [32, 128, 512], P(None, 'gx', 'gy'), may hold values from 0.3 to 3
- cond_z: float32 [32, 128, 512], P(None, 'gx', 'gy'), may hold values from 0.05 to 2
Outputs:
- solution_field: float32 [32, 128, 512], P(None, 'gx', 'gy')
- residual: float32 [32, 128, 512], P(None, 'gx', 'gy')
All inputs are finite; a program needn't handle non-finite values.
Results may differ from a plain program's by a relative error of at most 0.00014.
Values sent between devices are 32-bit elements; how exact they have to be, the bound alone decides.
No kernel may reach another device: no remote copies, remote signals or barrier semaphores. Data moves between devices by JAX's collectives and lax.ppermute only.
A program may use at most 128 MiB of HBM per device.

v0:
```python
import jax
import jax.numpy as jnp
from jax import lax
from jax.sharding import PartitionSpec as P

LEVELS = 4
COARSE_SWEEPS = 16


OMEGA = 0.8


def with_halo(cells, sides, width):
    for axis, dim in sides:
        count = lax.axis_size(axis)
        ends = count - 1
        head = lax.slice_in_dim(cells, 0, width, axis=dim)
        tail = lax.slice_in_dim(cells, cells.shape[dim] - width, cells.shape[dim], axis=dim)
        cells = jnp.concatenate(
            [
                lax.ppermute(tail, axis, [(i, (i + 1) % count) for i in range(ends)]),
                cells,
                lax.ppermute(head, axis, [((i + 1) % count, i) for i in range(ends)]),
            ],
            axis=dim,
        )
    return cells


def apply_op(field, padded, coeffs):
    kappa, x_up, x_low, y_up, y_low, z_up, z_low = coeffs
    zpad = jnp.pad(field, ((1, 1), (0, 0), (0, 0)))
    out = (
        kappa * field
        + x_up * (field - padded[:, 2:, 1:-1])
        + x_low * (field - padded[:, :-2, 1:-1])
    )
    out = out + y_up * (field - padded[:, 1:-1, 2:]) + y_low * (field - padded[:, 1:-1, :-2])
    return out + z_up * (field - zpad[2:]) + z_low * (field - zpad[:-2])


def face_pad(field):
    return with_halo(field, (("gx", 1), ("gy", 2)), 1)


def line_factors(coeffs):
    kappa, x_up, x_low, y_up, y_low, z_up, z_low = coeffs
    diag = kappa + x_up + x_low + y_up + y_low + z_up + z_low
    upper_src = z_up.at[-1].set(jnp.zeros_like(z_up[-1]))

    def factor_step(upper_prev, planes):
        diag_k, low_k, up_k = planes
        inv = 1.0 / (diag_k + low_k * upper_prev)
        upper = -up_k * inv
        return (upper, (inv, upper))

    start = jnp.zeros_like(diag[0])
    unused, stacked = lax.scan(factor_step, start, (diag, z_low, upper_src), unroll=True)
    return stacked


def line_solve(rhs, factors, z_low):
    inverses, uppers = factors

    def forward_step(prev, planes):
        rhs_k, low_k, inv_k = planes
        value = (rhs_k + low_k * prev) * inv_k
        return (value, value)

    start = jnp.zeros_like(rhs[0])
    unused, forward = lax.scan(forward_step, start, (rhs, z_low, inverses), unroll=True)

    def back_step(after, planes):
        fwd_k, up_k = planes
        value = fwd_k - up_k * after
        return (value, value)

    unused, result = lax.scan(back_step, start, (forward, uppers), reverse=True, unroll=True)
    return result


def mean_four(field):
    depth, rows, cols = field.shape
    return field.reshape(depth, rows // 2, 2, cols // 2, 2).mean(axis=(2, 4))


def coarsen(coeffs):
    kappa, x_up, x_low, y_up, y_low, z_up, z_low = coeffs
    depth, rows, cols = kappa.shape
    shape = (depth, rows // 2, 2, cols // 2, 2)
    xu_c = x_up.reshape(shape)[:, :, 1].mean(axis=-1) * 0.25
    xl_c = x_low.reshape(shape)[:, :, 0].mean(axis=-1) * 0.25
    yu_c = y_up.reshape(shape)[:, :, :, :, 1].mean(axis=2) * 0.25
    yl_c = y_low.reshape(shape)[:, :, :, :, 0].mean(axis=2) * 0.25
    return (mean_four(kappa), xu_c, xl_c, yu_c, yl_c, mean_four(z_up), mean_four(z_low))


def prolong(padded):
    depth = padded.shape[0]
    rows = padded.shape[1] - 2
    cols = padded.shape[2] - 2
    centre = padded[:, 1:-1, :]
    even = 0.75 * centre + 0.25 * padded[:, :-2, :]
    odd = 0.75 * centre + 0.25 * padded[:, 2:, :]
    spread = jnp.stack([even, odd], axis=2).reshape(depth, 2 * rows, cols + 2)
    centre = spread[:, :, 1:-1]
    even = 0.75 * centre + 0.25 * spread[:, :, :-2]
    odd = 0.75 * centre + 0.25 * spread[:, :, 2:]
    return jnp.stack([even, odd], axis=3).reshape(depth, 2 * rows, 2 * cols)


def coarse_solve(rhs, coeffs):
    factors = line_factors(coeffs)
    field = OMEGA * line_solve(rhs, factors, coeffs[6])

    def spread_sweep(sweep, current):
        padded = with_halo(current, (("gx", 1), ("gy", 2)), 1)
        defect = rhs - apply_op(current, padded, coeffs)
        return current + OMEGA * line_solve(defect, factors, coeffs[6])

    field = lax.fori_loop(0, COARSE_SWEEPS - 1, spread_sweep, field)
    return field


def cycle(rhs, coeffs, level):
    if level == LEVELS:
        return coarse_solve(rhs, coeffs)
    factors = line_factors(coeffs)
    field = OMEGA * line_solve(rhs, factors, coeffs[6])
    padded = face_pad(field)
    defect = rhs - apply_op(field, padded, coeffs)
    correction = cycle(mean_four(defect), coarsen(coeffs), level + 1)
    rimmed = with_halo(correction, (("gx", 1), ("gy", 2)), 1)
    field = field + prolong(rimmed)
    padded = face_pad(field)
    defect = rhs - apply_op(field, padded, coeffs)
    return field + OMEGA * line_solve(defect, factors, coeffs[6])


def body(right_side, kappa_sq, cond_x, cond_y, cond_z):
    padded_x = with_halo(cond_x, (("gx", 1),), 1)
    padded_y = with_halo(cond_y, (("gy", 2),), 1)
    padded_z = jnp.pad(cond_z, ((1, 1), (0, 0), (0, 0)))
    x_up = 0.5 * (cond_x + padded_x[:, 2:, :])
    x_low = 0.5 * (cond_x + padded_x[:, :-2, :])
    y_up = 0.5 * (cond_y + padded_y[:, :, 2:])
    y_low = 0.5 * (cond_y + padded_y[:, :, :-2])
    z_up = 0.5 * (cond_z + padded_z[2:])
    z_low = 0.5 * (cond_z + padded_z[:-2])
    coeffs = (kappa_sq, x_up, x_low, y_up, y_low, z_up, z_low)
    solution_field = cycle(right_side, coeffs, 0)
    residual = right_side - apply_op(solution_field, face_pad(solution_field), coeffs)
    return (solution_field, residual)


def solution(mesh):
    in_specs = (
        P(None, "gx", "gy"),
        P(None, "gx", "gy"),
        P(None, "gx", "gy"),
        P(None, "gx", "gy"),
        P(None, "gx", "gy"),
    )
    out_specs = (P(None, "gx", "gy"), P(None, "gx", "gy"))
    return jax.shard_map(body, mesh=mesh, in_specs=in_specs, out_specs=out_specs, check_vma=False)
```

profile of v0, /device:TPU:14, one launch (start us, length us, event | category | flops | bytes accessed | tf_op | source)
XLA Modules:
  0.0 982.2 jit_solution(1706652629171190890)
XLA Ops:
  13.0 3.8 collective-permute-done.6
  16.8 7.5 collective-permute-done.7
  37.8 3.1 slice_reduce_fusion
  44.0 3.1 slice_reduce_fusion.1
  92.7 5.2 collective-permute-done.10
  97.8 6.5 collective-permute-done.11
  117.6 3.2 collective-permute-start.12
  130.9 6.1 collective-permute-done.15
  150.5 3.0 collective-permute-start.16
  201.7 3.6 collective-permute-start.20
  218.7 3.6 collective-permute-start.22
  236.1 528.4 %while.17 = (s32[]{:T(128)}, f32[32,1,8]{2,1,0:T(1,128)S(1)}, f32[32,1,8]{2,1,0:T(1,128)S(1)}, f32[32,1,8]{2,1,0:T(1,128)}, f32[32,1,8]{2,1,0:T(1,128)}, /*index...) while((s32[]{:T(128)}, f32[32,1,8]{2,1,0:T(1,128)S(1)}, ...), condition=%wide.region_37.38_spmd, body=%wide.region_36.37_spmd.sunk | while | flops 10010 | bytes 63973 | solution.py:121
  238.0 3.6 collective-permute-start.1
  243.9 3.2 collective-permute-start.2
  249.3 4.2 collective-permute-done.3
  279.4 3.9 collective-permute-start.2
  285.6 4.2 collective-permute-done.3
  307.9 2.9 collective-permute-start
  320.7 4.2 collective-permute-done.3
  343.0 2.9 collective-permute-start
  355.8 4.2 collective-permute-done.3
  378.1 2.9 collective-permute-start
  390.9 4.2 collective-permute-done.3
  413.3 2.9 collective-permute-start
  426.1 4.2 collective-permute-done.3
  448.4 2.9 collective-permute-start
  461.2 4.2 collective-permute-done.3
  483.5 2.9 collective-permute-start
  496.3 4.2 collective-permute-done.3
  518.6 2.9 collective-permute-start
  531.4 4.2 collective-permute-done.3
  553.8 2.9 collective-permute-start
  566.6 4.2 collective-permute-done.3
  588.9 2.9 collective-permute-start
  601.7 4.2 collective-permute-done.3
  624.0 2.9 collective-permute-start
  636.8 4.2 collective-permute-done.3
  659.1 2.9 collective-permute-start
  671.9 4.2 collective-permute-done.3
  694.3 2.9 collective-permute-start
  707.1 4.2 collective-permute-done.3
  742.2 4.2 collective-permute-done.3
  773.0 4.5 collective-permute-start.27
  781.7 3.6 collective-permute-start.28
  787.6 4.8 collective-permute-start.30
  796.5 2.9 collective-permute-done.31
  803.9 3.0 collective-permute-start.32
  812.4 5.2 collective-permute-start.35
  821.7 3.5 collective-permute-start.37
  828.9 5.0 collective-permute-start.38
  836.4 6.9 collective-permute-done.39
  856.1 4.6 collective-permute-start.43
  869.0 3.3 collective-permute-start.45
  876.2 4.6 collective-permute-start.46
  882.1 3.9 collective-permute-done.46
  886.0 9.5 collective-permute-done.47
  899.6 3.1 collective-permute-start.48
  908.4 4.6 collective-permute-start.51
  913.0 3.6 collective-permute-done.50
  931.5 5.6 collective-permute-start.54
  938.5 5.4 collective-permute-done.54
  943.9 9.9 %collective-permute-done.55 = f32[32,18,1]{2,0,1:T(8,128)S(1)} collective-permute-done((f32[32,18,1]{2,0,1:T(8,128)S(1)}, f32[32,18,1]{2,0,1:T(8,128)S(1)}, u32[]{:S(2)}, u32[]{:S(2)}) %collective-permute-start.55) | collective-permute-done | bytes 2336 | tf_op jit(solution)/shard_map/ppermute | solution.py:21
  969.5 3.9 collective-permute-done.58
  973.5 7.1 collective-permute-done.59
  (4710 shorter events, 699.4 us)
Async XLA Ops:
  2.2 22.1 %collective-permute-start.4 = (f32[32,1,128]{2,1,0:T(1,128)}, f32[32,1,128]{2,1,0:T(1,128)}, u32[]{:S(2)}, u32[]{:S(2)}) collective-permute-start(f32[32,1,128]{2,1,0:T(1,128)} %get-tuple-element.2890), channel_id=1, source_target_pairs={{4,0},{8,4},{12,8},{16,12},{20,16},{24,20},{28,24},{5,1},{9,5},{13... | collective-permute-start | bytes 49160 | tf_op jit(solution)/shard_map/ppermute | solution.py:23
  4.2 20.1 %collective-permute-start.5 = (f32[32,1,128]{2,1,0:T(1,128)}, f32[32,1,128]{2,1,0:T(1,128)}, u32[]{:S(2)}, u32[]{:S(2)}) collective-permute-start(f32[32,1,128]{2,1,0:T(1,128)} %get-tuple-element.2891), channel_id=1, source_target_pairs={{0,4},{4,8},{8,12},{12,16},{16,20},{20,24},{24,28},{1,5},{5,9},{9,... | collective-permute-start | bytes 49160 | tf_op jit(solution)/shard_map/ppermute | solution.py:21
  7.9 8.9 collective-permute-start.6
  10.3 13.9 %collective-permute-start.7 = (f32[32,16,1]{2,1,0:T(8,128)S(1)}, f32[32,16,1]{2,1,0:T(8,128)S(1)}, u32[]{:S(2)}, u32[]{:S(2)}) collective-permute-start(f32[32,16,1]{2,1,0:T(8,128)S(1)} %get-tuple-element.2893), channel_id=1, source_target_pairs={{0,1},{1,2},{2,3},{4,5},{5,6},{6,7},{8,9},{9,10},{10,11},{12,13},{... | collective-permute-start | bytes 6152 | tf_op jit(solution)/shard_map/ppermute | solution.py:21
  31.9 55.3 %collective-permute-start.8 = (f32[32,1,128]{2,1,0:T(1,128)}, f32[32,1,128]{2,1,0:T(1,128)}, u32[]{:S(2)}, u32[]{:S(2)}) collective-permute-start(f32[32,1,128]{2,1,0:T(1,128)} %get-tuple-element.2888), channel_id=1, source_target_pairs={{4,0},{8,4},{12,8},{16,12},{20,16},{24,20},{28,24},{5,1},{9,5},{13... | collective-permute-start | bytes 49160 | tf_op jit(solution)/shard_map/ppermute | solution.py:23
  34.2 53.0 %collective-permute-start.9 = (f32[32,1,128]{2,1,0:T(1,128)}, f32[32,1,128]{2,1,0:T(1,128)}, u32[]{:S(2)}, u32[]{:S(2)}) collective-permute-start(f32[32,1,128]{2,1,0:T(1,128)} %get-tuple-element.2889), channel_id=1, source_target_pairs={{0,4},{4,8},{8,12},{12,16},{16,20},{20,24},{24,28},{1,5},{5,9},{9,... | collective-permute-start | bytes 49160 | tf_op jit(solution)/shard_map/ppermute | solution.py:21
  88.1 9.7 collective-permute-start.10
  90.8 13.6 %collective-permute-start.11 = (f32[32,18,1]{2,0,1:T(8,128)S(1)}, f32[32,18,1]{2,0,1:T(8,128)S(1)}, u32[]{:S(2)}, u32[]{:S(2)}) collective-permute-start(f32[32,18,1]{2,0,1:T(8,128)S(1)} %get-tuple-element.2875), channel_id=1, source_target_pairs={{0,1},{1,2},{2,3},{4,5},{5,6},{6,7},{8,9},{9,10},{10,11},{12,13},{... | collective-permute-start | bytes 6920 | tf_op jit(solution)/shard_map/ppermute | solution.py:21
  115.3 6.2 collective-permute-start.13
  123.3 7.6 collective-permute-start.14
  125.4 11.6 %collective-permute-start.15 = (f32[32,10,1]{2,1,0:T(8,128)}, f32[32,10,1]{2,1,0:T(8,128)}, u32[]{:S(2)}, u32[]{:S(2)}) collective-permute-start(f32[32,10,1]{2,1,0:T(8,128)} %get-tuple-element.2887), channel_id=1, source_target_pairs={{0,1},{1,2},{2,3},{4,5},{5,6},{6,7},{8,9},{9,10},{10,11},{12,13},{... | collective-permute-start | bytes 3848 | tf_op jit(solution)/shard_map/ppermute | solution.py:21
  148.0 33.3 %collective-permute-start.17 = (f32[32,1,32]{2,1,0:T(1,128)S(1)}, f32[32,1,32]{2,1,0:T(1,128)S(1)}, u32[]{:S(2)}, u32[]{:S(2)}) collective-permute-start(f32[32,1,32]{2,1,0:T(1,128)S(1)} %get-tuple-element.2932), channel_id=1, source_target_pairs={{0,4},{4,8},{8,12},{12,16},{16,20},{20,24},{24,28},{1,5},{5,9},{9,... | collective-permute-start | bytes 12296 | tf_op jit(solution)/shard_map/ppermute | solution.py:21
  150.5 31.4 %collective-permute-start.16 = (f32[32,1,32]{2,1,0:T(1,128)S(1)}, f32[32,1,32]{2,1,0:T(1,128)}, u32[]{:S(2)}, u32[]{:S(2)}) collective-permute-start(f32[32,1,32]{2,1,0:T(1,128)S(1)} %get-tuple-element.2933), channel_id=1, source_target_pairs={{4,0},{8,4},{12,8},{16,12},{20,16},{24,20},{28,24},{5,1},{9,5},{13... | collective-permute-start | bytes 12296 | tf_op jit(solution)/shard_map/ppermute | solution.py:23
  183.5 7.4 collective-permute-start.18
  185.1 8.2 collective-permute-start.19
  199.7 18.2 %collective-permute-start.21 = (f32[32,1,16]{2,1,0:T(1,128)S(1)}, f32[32,1,16]{2,1,0:T(1,128)S(1)}, u32[]{:S(2)}, u32[]{:S(2)}) collective-permute-start(f32[32,1,16]{2,1,0:T(1,128)S(1)} %get-tuple-element.2948), channel_id=1, source_target_pairs={{0,4},{4,8},{8,12},{12,16},{16,20},{20,24},{24,28},{1,5},{5,9},{9,... | collective-permute-start | bytes 6152 | tf_op jit(solution)/shard_map/ppermute | solution.py:21
  201.7 16.2 %collective-permute-start.20 = (f32[32,1,16]{2,1,0:T(1,128)S(1)}, f32[32,1,16]{2,1,0:T(1,128)S(1)}, u32[]{:S(2)}, u32[]{:S(2)}) collective-permute-start(f32[32,1,16]{2,1,0:T(1,128)S(1)} %get-tuple-element.2949), channel_id=1, source_target_pairs={{4,0},{8,4},{12,8},{16,12},{20,16},{24,20},{28,24},{5,1},{9,5},{13... | collective-permute-start | bytes 6152 | tf_op jit(solution)/shard_map/ppermute | solution.py:23
  218.7 8.8 collective-permute-start.22
  222.3 6.5 collective-permute-start.23
  247.1 6.4 collective-permute-start.3
  271.6 5.6 collective-permute-start
  279.4 6.2 collective-permute-start.2
  283.4 6.4 collective-permute-start.3
  318.5 6.4 collective-permute-start.3
  353.6 6.4 collective-permute-start.3
  388.7 6.4 collective-permute-start.3
  423.9 6.4 collective-permute-start.3
  459.0 6.4 collective-permute-start.3
  483.5 5.6 collective-permute-start
  494.1 6.4 collective-permute-start.3
  529.2 6.4 collective-permute-start.3
  553.8 5.6 collective-permute-start
  564.4 6.4 collective-permute-start.3
  599.5 6.4 collective-permute-start.3
  624.0 5.6 collective-permute-start
  634.6 6.4 collective-permute-start.3
  669.7 6.4 collective-permute-start.3
  694.3 5.6 collective-permute-start
  704.9 6.4 collective-permute-start.3
  740.0 6.4 collective-permute-start.3
  771.7 5.9 collective-permute-start.26
  773.0 5.8 collective-permute-start.27
  779.8 5.7 collective-permute-start.29
  787.6 8.9 collective-permute-start.30
  792.4 7.0 collective-permute-start.31
  803.9 5.6 collective-permute-start.32
  811.1 6.9 collective-permute-start.34
  812.4 7.1 collective-permute-start.35
  821.7 5.6 collective-permute-start.37
  828.9 7.5 collective-permute-start.38
  833.9 9.4 collective-permute-start.39
  847.5 5.6 collective-permute-start.40
  854.8 6.9 collective-permute-start.42
  856.1 7.1 collective-permute-start.43
  869.0 5.6 collective-permute-start.45
  876.2 9.8 collective-permute-start.46
  880.8 14.7 %collective-permute-start.47 = (f32[32,10,1]{2,1,0:T(8,128)S(1)}, f32[32,10,1]{2,1,0:T(8,128)S(1)}, u32[]{:S(2)}, u32[]{:S(2)}) collective-permute-start(f32[32,10,1]{2,1,0:T(8,128)S(1)} %get-tuple-element.2885), channel_id=1, source_target_pairs={{0,1},{1,2},{2,3},{4,5},{5,6},{6,7},{8,9},{9,10},{10,11},{12,13},{... | collective-permute-start | bytes 3848 | tf_op jit(solution)/shard_map/ppermute | solution.py:21
  899.6 5.6 collective-permute-start.48
  906.9 9.7 collective-permute-start.50
  908.4 10.0 %collective-permute-start.51 = (f32[32,10,1]{2,1,0:T(8,128)S(1)}, f32[32,10,1]{2,1,0:T(8,128)S(1)}, u32[]{:S(2)}, u32[]{:S(2)}) collective-permute-start(f32[32,10,1]{2,1,0:T(8,128)S(1)} %get-tuple-element.2883), channel_id=1, source_target_pairs={{1,0},{2,1},{3,2},{5,4},{6,5},{7,6},{9,8},{10,9},{11,10},{13,12},{... | collective-permute-start | bytes 3848 | tf_op jit(solution)/shard_map/ppermute | solution.py:23
  931.5 12.4 %collective-permute-start.54 = (f32[32,18,1]{2,0,1:T(8,128)S(1)}, f32[32,18,1]{2,0,1:T(8,128)S(1)}, u32[]{:S(2)}, u32[]{:S(2)}) collective-permute-start(f32[32,18,1]{2,0,1:T(8,128)S(1)} %get-tuple-element.2870), channel_id=1, source_target_pairs={{1,0},{2,1},{3,2},{5,4},{6,5},{7,6},{9,8},{10,9},{11,10},{13,12},{... | collective-permute-start | bytes 6920 | tf_op jit(solution)/shard_map/ppermute | solution.py:23
  937.2 16.6 %collective-permute-start.55 = (f32[32,18,1]{2,0,1:T(8,128)S(1)}, f32[32,18,1]{2,0,1:T(8,128)S(1)}, u32[]{:S(2)}, u32[]{:S(2)}) collective-permute-start(f32[32,18,1]{2,0,1:T(8,128)S(1)} %get-tuple-element.2871), channel_id=1, source_target_pairs={{0,1},{1,2},{2,3},{4,5},{5,6},{6,7},{8,9},{9,10},{10,11},{12,13},{... | collective-permute-start | bytes 6920 | tf_op jit(solution)/shard_map/ppermute | solution.py:21
  965.8 7.7 collective-permute-start.58
  968.2 12.3 %collective-permute-start.59 = (f32[32,18,1]{2,0,1:T(8,128)S(1)}, f32[32,18,1]{2,0,1:T(8,128)S(1)}, u32[]{:S(2)}, u32[]{:S(2)}) collective-permute-start(f32[32,18,1]{2,0,1:T(8,128)S(1)} %get-tuple-element.2867), channel_id=1, source_target_pairs={{0,1},{1,2},{2,3},{4,5},{5,6},{6,7},{8,9},{9,10},{10,11},{12,13},{... | collective-permute-start | bytes 6920 | tf_op jit(solution)/shard_map/ppermute | solution.py:21
  (1736 other events, 2188.1 us)
where the time goes:
time: 997 us; the launch traced here: 982 us
  local copies, waits for them, and re-layouts  364 us (37%)
  starting transfers between devices  292 us (29%)
  waiting for transfers between devices  208 us (21%)
  other arithmetic  99.9 us (10%)
  loops' own time  10.2 us (1%)
    while x2460, local copies, waits for them, and re-layouts  190 us
    ppermute x58, starting transfers between devices, with_halo(): lax.ppermute(head, axis, [((i + 1) % count, i) for i in range(ends)])  175 us
    ppermute x58, waiting for transfers between devices, with_halo(): lax.ppermute(tail, axis, [(i, (i + 1) % count) for i in range(ends)])  134 us
    ppermute x58, starting transfers between devices, with_halo(): lax.ppermute(tail, axis, [(i, (i + 1) % count) for i in range(ends)])  117 us
    ppermute x58, waiting for transfers between devices, with_halo(): lax.ppermute(head, axis, [((i + 1) % count, i) for i in range(ends)])  74.2 us
    while x73, local copies, waits for them, and re-layouts, coarse_solve(): field = lax.fori_loop(0, COARSE_SWEEPS - 1, spread_sweep, field)  42.8 us
    sub x480, local copies, waits for them, and re-layouts, back_step(): value = fwd_k - up_k * after  38.7 us
    unnamed x1031, local copies, waits for them, and re-layouts  26 us

commit v1 on v0

--- a/solution.py
+++ b/solution.py
@@ -1,6 +1,10 @@
+import functools
+
 import jax
 import jax.numpy as jnp
 from jax import lax
+from jax.experimental import pallas as pl
+from jax.experimental.pallas import tpu as pltpu
 from jax.sharding import PartitionSpec as P
 
 LEVELS = 4
@@ -137,7 +141,7 @@
     return field + OMEGA * line_solve(defect, factors, coeffs[6])
 
 
-def body(right_side, kappa_sq, cond_x, cond_y, cond_z):
+def spread_body(right_side, kappa_sq, cond_x, cond_y, cond_z):
     padded_x = with_halo(cond_x, (("gx", 1),), 1)
     padded_y = with_halo(cond_y, (("gy", 2),), 1)
     padded_z = jnp.pad(cond_z, ((1, 1), (0, 0), (0, 0)))
@@ -153,13 +157,528 @@
     return (solution_field, residual)
 
 
+F32 = jnp.float32
+BF16 = jnp.bfloat16
+NZ = 32
+TX, TY = 16, 128
+HALO = 8
+VMEM = pl.BlockSpec(memory_space=pltpu.VMEM)
+ANY = pl.BlockSpec(memory_space=pl.ANY)
+
+
+def iota(shape, dim):
+    return lax.broadcasted_iota(jnp.int32, shape, dim)
+
+
+def shift(x, by, axis):
+    return pltpu.roll(x, by % x.shape[axis], axis)
+
+
+def mix(x, weights):
+    high = x.astype(BF16)
+    rest = x - high.astype(F32)
+    mid = rest.astype(BF16)
+    low = (rest - mid.astype(F32)).astype(BF16)
+    dot = functools.partial(jnp.dot, preferred_element_type=F32)
+    return dot(low, weights) + dot(mid, weights) + dot(high, weights)
+
+
+def plane(k, rows):
+    return pl.ds(pl.multiple_of(k * rows, rows), rows)
+
+
+def matrix(mask):
+    return mask.astype(F32).astype(BF16)
+
+
+def pair_matrix(fine, coarse, offsets=(0, 1)):
+    y, j = iota((fine, coarse), 0), iota((fine, coarse), 1)
+    keep = y // 2 == j
+    if len(offsets) == 1:
+        keep = keep & (y % 2 == offsets[0])
+    return matrix(keep)
+
+
+def spread_matrix(coarse, fine_index, parent, partner, valid):
+    j = iota((coarse, fine_index.shape[1]), 0)
+    weights = jnp.where(j == parent, 0.75, jnp.where(j == partner, 0.25, 0.0))
+    return jnp.where(valid, weights, 0.0).astype(BF16)
+
+
+def pack_kernel(f, kappa, cx, cy, cz, x_head, x_tail, y_head, y_tail):
+    group = iota((8, 128), 1) // 8
+    refs = (f, kappa, cx, cy, cz)
+    for a, ref in enumerate(refs):
+        cells = ref[...].reshape(NZ, TX, TY)
+        x_head[pl.ds(a * NZ * HALO, NZ * HALO), :] = cells[:, :HALO].reshape(NZ * HALO, TY)
+        x_tail[pl.ds(a * NZ * HALO, NZ * HALO), :] = cells[:, TX - HALO :].reshape(NZ * HALO, TY)
+    for half in range(2):
+        for a, ref in enumerate(refs):
+            for zo in range(2):
+                head = jnp.zeros((8, 128), F32)
+                tail = jnp.zeros((8, 128), F32)
+                for zi in range(16):
+                    cells = ref[pl.ds((zo * 16 + zi) * TX + 8 * half, 8), :]
+                    cells = shift(cells, 8 * zi, 1)
+                    head = jnp.where(group == zi, cells, head)
+                    tail = jnp.where(group == (zi - 1) % 16, cells, tail)
+                at = ((half * 5 + a) * 2 + zo) * 8
+                y_head[pl.ds(at, 8), :] = head
+                y_tail[pl.ds(at, 8), :] = tail
+
+
+def coarse_rows(ref, row, rows):
+    return ref[pl.ds(row, NZ, stride=rows), :]
+
+
+def coeff_kernel(kappa, cx, cy, cz, out):
+    iy = lax.axis_index("gy")
+    y, lane = iota((128, 128), 0), iota((128, 128), 1)
+    first = jnp.zeros((4 * NZ, 128), F32)
+    second = jnp.zeros((NZ, 256), F32)
+    for xi in range(4):
+        place = (lane // 32 == (xi + iy) % 4) & (lane % 32 == y // 4)
+        rows = [4 * xi + a for a in range(4)]
+        total = lambda ref: sum(coarse_rows(ref, r, TX) for r in rows)
+        stack = [coarse_rows(cx, rows[0], TX), coarse_rows(cx, rows[3], TX), total(kappa), total(cz)]
+        first = first + mix(jnp.concatenate(stack, axis=0), matrix(place))
+        ends = [matrix(place & (y % 4 == 0)), matrix(place & (y % 4 == 3))]
+        second = second + mix(total(cy), jnp.concatenate(ends, axis=1))
+    out[pl.ds(0, 2 * NZ), :] = first[: 2 * NZ] * (1 / 128)
+    out[pl.ds(2 * NZ, NZ), :] = second[:, :128] * (1 / 128)
+    out[pl.ds(3 * NZ, NZ), :] = second[:, 128:] * (1 / 128)
+    out[pl.ds(4 * NZ, 2 * NZ), :] = first[2 * NZ :] * (1 / 16)
+
+
+def assemble(gathered, kinds, kind, dest, gx, gy):
+    group = iota((NZ, 128), 1) // 32
+    for ix in range(gx):
+        blocks = [gathered[pl.ds(((ix * gy + iy) * kinds + kind) * NZ, NZ), :] for iy in range(gy)]
+        for xi in range(4):
+            cells = blocks[0]
+            for iy in range(1, gy):
+                cells = jnp.where(group == (iy + xi) % 4, blocks[iy], cells)
+            dest[pl.ds(4 * ix + xi, NZ, stride=4 * gx), :] = shift(cells, -32 * xi, 1)
+
+
+def factor_global(rows, cols, xl, xu, yl, yu, kappa, cz, out):
+    x, y = iota((rows, 128), 0), iota((rows, 128), 1)
+    masks = [(x > 0).astype(F32), (x < rows - 1).astype(F32), (y > 0).astype(F32), (y < cols - 1).astype(F32)]
+    size = NZ * rows
+
+    def step(k, carry, last=False):
+        c_prev, cz_k, z_low = carry
+        at = plane(k, rows)
+        cz_next = jnp.zeros_like(cz_k) if last else cz[plane(k + 1, rows), :]
+        z_up = 0.5 * (cz_k + cz_next)
+        diag = jnp.where(y < cols, kappa[at, :], 1.0) + z_up + z_low
+        for n, ref in enumerate((xl, xu, yl, yu)):
+            face = ref[at, :]
+            diag = diag + face
+            out[pl.ds(pl.multiple_of(n * size + k * rows, rows), rows), :] = face * masks[n]
+        inv = 1.0 / (diag + z_low * c_prev)
+        c = jnp.zeros_like(inv) if last else -z_up * inv
+        for n, value in ((4, inv), (5, z_low * inv), (6, c)):
+            out[pl.ds(pl.multiple_of(n * size + k * rows, rows), rows), :] = value
+        return c, cz_next, z_up
+
+    cz_0 = cz[pl.ds(0, rows), :]
+    carry = lax.fori_loop(0, NZ - 1, step, (jnp.zeros_like(cz_0), cz_0, 0.5 * cz_0))
+    step(NZ - 1, carry, last=True)
+
+
+def global_kernel(gx, gy, gathered, out2, out3, out4, *scratch):
+    fine, mid, low = scratch[:8], scratch[8:14], scratch[14:20]
+    rows, cols = 4 * gx, 32 * gy
+    for kind in range(6):
+        assemble(gathered, 6, kind, fine[kind], gx, gy)
+    a_ref, b_ref, c_ref, d_ref, kappa, cz, xl, yl = fine
+    x, y = iota((1, rows, 128), 1), iota((1, rows, 128), 2)
+    cube = lambda ref: ref[...].reshape(NZ, rows, 128)
+    a, b = cube(a_ref), cube(b_ref)
+    xl[...] = (a + jnp.where(x > 0, shift(b, 1, 1), 0.0)).reshape(NZ * rows, 128)
+    b_ref[...] = (b + jnp.where(x < rows - 1, shift(a, -1, 1), 0.0)).reshape(NZ * rows, 128)
+    c, d = cube(c_ref), cube(d_ref)
+    yl[...] = (c + jnp.where(y > 0, shift(d, 1, 2), 0.0)).reshape(NZ * rows, 128)
+    d_ref[...] = (d + jnp.where(y < cols - 1, shift(c, -1, 2), 0.0)).reshape(NZ * rows, 128)
+    level = (xl, b_ref, yl, d_ref, kappa, cz)
+    factor_global(rows, cols, *level, out2)
+    pair, even, odd = pair_matrix(128, 128), pair_matrix(128, 128, (0,)), pair_matrix(128, 128, (1,))
+    for coarse, out in ((mid, out3), (low, out4)):
+        rows, cols = rows // 2, cols // 2
+        size = NZ * rows
+        first = lambda ref: ref[pl.ds(0, size, stride=2), :]
+        second = lambda ref: ref[pl.ds(1, size, stride=2), :]
+        xl, xu, yl, yu, kappa, cz = level
+        coarse[0][...] = 0.125 * mix(first(xl), pair)
+        coarse[1][...] = 0.125 * mix(second(xu), pair)
+        coarse[2][...] = 0.125 * mix(first(yl) + second(yl), even)
+        coarse[3][...] = 0.125 * mix(first(yu) + second(yu), odd)
+        coarse[4][...] = 0.25 * mix(first(kappa) + second(kappa), pair)
+        coarse[5][...] = 0.25 * mix(first(cz) + second(cz), pair)
+        level = coarse
+        factor_global(rows, cols, *level, out)
+
+
+def neighbours(cells, xl, xu, yl, yu):
+    out = xl * shift(cells, 1, 0) + xu * shift(cells, -1, 0)
+    return out + yl * shift(cells, 1, 1) + yu * shift(cells, -1, 1)
+
+
+def back_down(rows, f, u, r, coeffs, c):
+    def step(n, after):
+        k = NZ - 1 - n
+        at = plane(k, rows)
+        value = u[at, :] - c(k) * after
+        field = OMEGA * value
+        u[at, :] = field
+        r[at, :] = (1.0 - OMEGA) * f[at, :] + neighbours(field, *[get(k) for get in coeffs])
+        return value
+
+    lax.fori_loop(0, NZ, step, jnp.zeros((rows, u.shape[1]), F32))
+
+
+def forward_down(rows, f, u, inv, g):
+    def step(k, prev):
+        at = plane(k, rows)
+        value = f[at, :] * inv(k) + g(k) * prev
+        u[at, :] = value
+        return value
+
+    lax.fori_loop(0, NZ, step, jnp.zeros((rows, u.shape[1]), F32))
+
+
+def sweep_up(rows, f, u, w, e, coeffs, inv, g, c, mask):
+    def forward(k, prev):
+        at = plane(k, rows)
+        field = u[at, :] + e[at, :]
+        if mask is not None:
+            field = field * mask
+        u[at, :] = field
+        value = (f(k) + neighbours(field, *[get(k) for get in coeffs])) * inv(k) + g(k) * prev
+        w[at, :] = value
+        return value
+
+    def backward(n, after):
+        k = NZ - 1 - n
+        at = plane(k, rows)
+        value = w[at, :] - c(k) * after
+        u[at, :] = (1.0 - OMEGA) * u[at, :] + OMEGA * value
+        return value
+
+    start = jnp.zeros((rows, u.shape[1]), F32)
+    lax.fori_loop(0, NZ, forward, start)
+    lax.fori_loop(0, NZ, backward, start)
+
+
+def getter(ref, n, rows):
+    return lambda k: ref[pl.ds(pl.multiple_of(n * NZ * rows + k * rows, rows), rows), :]
+
+
+def window_mask(rows, cols, halo, ix, iy, nx, ny):
+    tile_x, tile_y = rows // 2, cols // 2
+    x, y = iota((rows, cols), 0), iota((rows, cols), 1)
+    x = jnp.where(x < tile_x + halo, x, x - rows)
+    y = jnp.where(y < tile_y + tile_y // 2, y, y - cols)
+    valid = (y >= -halo) & (y < tile_y + halo)
+    x, y = x + ix * tile_x, y + iy * tile_y
+    return (valid & (x >= 0) & (x < nx) & (y >= 0) & (y < ny)).astype(F32)
+
+
+SAVED = 9
+
+
+def window_down(rows, cols, mask, f, kappa, faces, cz, out, r, diag_out=None):
+    size = NZ * rows
+
+    def put(n, k, value):
+        out[pl.ds(pl.multiple_of(n * size + k * rows, rows), rows), :] = value
+
+    def step(k, carry, last=False):
+        c_prev, w_prev, cz_k, z_low = carry
+        at = plane(k, rows)
+        x_face, y_face = faces(k)
+        xl, xu = x_face * mask, shift(x_face, -1, 0) * mask
+        yl, yu = y_face * mask, shift(y_face, -1, 1) * mask
+        cz_next = jnp.zeros_like(cz_k) if last else cz[plane(k + 1, rows), :]
+        z_up = 0.5 * (cz_k + cz_next)
+        diag = jnp.where(mask > 0, kappa[at, :], 1.0) + xl + xu + yl + yu + z_up + z_low
+        if diag_out is not None:
+            diag_out[plane(k, TX), :] = diag[:TX, :TY]
+        inv = 1.0 / (diag + z_low * c_prev)
+        c = jnp.zeros_like(inv) if last else -z_up * inv
+        g = z_low * inv
+        f_k = f[at, :]
+        w = f_k * inv + g * w_prev
+        for n, value in enumerate((xl, xu, yl, yu, inv, g, c, w, f_k)):
+            put(n, k, value)
+        return c, w, cz_next, z_up
+
+    cz_0 = cz[pl.ds(0, rows), :]
+    zero = jnp.zeros((rows, cols), F32)
+    carry = lax.fori_loop(0, NZ - 1, step, (zero, zero, cz_0, 0.5 * cz_0))
+    step(NZ - 1, carry, last=True)
+    u, kept = out.at[pl.ds(7 * size, size), :], out.at[pl.ds(8 * size, size), :]
+    get = [getter(out, n, rows) for n in range(7)]
+    back_down(rows, kept, u, r, get[:4], get[6])
+
+
+def down_kernel(nx, ny, *refs):
+    f, kappa, cx, cy, cz, xr, xl, yr, yl, corner_r, corner_l = refs[:11]
+    send, saved0, saved1, diag = refs[11:15]
+    w_f, w_kappa, w_cx, w_cy, w_cz, x_face, y_face, r0 = refs[15:23]
+    f1, kappa1, cz1, x_face1, y_face1, r1 = refs[23:]
+    ix, iy = lax.axis_index("gx"), lax.axis_index("gy")
+    rows, cols = 2 * TX, 2 * TY
+    group = iota((8, 128), 1) // 8
+
+    def build(z, carry):
+        zo, zi = z // 16, z % 16
+        after, before = group == zi, group == (zi + 15) % 16
+        turn = (128 - 8 * zi) % 128
+        for a, (tile, dest) in enumerate(zip((f, kappa, cx, cy, cz), (w_f, w_kappa, w_cx, w_cy, w_cz))):
+            base = pl.multiple_of(z * rows, rows)
+            dest[pl.ds(base, TX), :TY] = tile[plane(z, TX), :]
+            slab = pl.ds(pl.multiple_of(a * NZ * HALO + z * HALO, HALO), HALO)
+            dest[pl.ds(base + TX, HALO), :TY] = xr[slab, :]
+            dest[pl.ds(base + TX + HALO, HALO), :TY] = xl[slab, :]
+            for t in range(4):
+                at = pl.ds(pl.multiple_of((((t % 2) * 5 * (t < 2) + a) * 2 + zo) * 8, 8), 8)
+                far = pl.ds(pl.multiple_of((10 + a * 2 + zo) * 8, 8), 8)
+                right, left = ((yr[at, :], yl[at, :]) if t < 2 else
+                               (corner_r[far, :], corner_r[at, :]) if t == 2 else
+                               (corner_l[far, :], corner_l[at, :]))
+                cells = jnp.where(after, right, jnp.where(before, left, 0.0))
+                dest[pl.ds(base + 8 * t, 8), TY:] = pltpu.roll(cells, turn, 1)
+        return carry
+
+    lax.fori_loop(0, NZ, build, 0)
+
+    def faces0(k):
+        at = plane(k, rows)
+        cx_k, cy_k = w_cx[at, :], w_cy[at, :]
+        x_k, y_k = 0.5 * (cx_k + shift(cx_k, 1, 0)), 0.5 * (cy_k + shift(cy_k, 1, 1))
+        x_face[at, :] = x_k
+        y_face[at, :] = y_k
+        return x_k, y_k
+
+    mask0 = window_mask(rows, cols, HALO, ix, iy, nx, ny)
+    window_down(rows, cols, mask0, w_f, w_kappa, faces0, w_cz, saved0, r0, diag)
+    rows, cols = rows // 2, cols // 2
+    pair, even = pair_matrix(256, 128), pair_matrix(256, 128, (0,))
+    part = 128
+    for at in range(0, NZ * rows, part):
+        here = pl.ds(at, part)
+        first = lambda ref: ref[pl.ds(2 * at, 2 * part), :].reshape(part, 2, 256)[:, 0, :]
+        both = lambda ref: ref[pl.ds(2 * at, 2 * part), :].reshape(part, 2, 256).sum(axis=1)
+        f1[here, :] = 0.25 * mix(both(r0), pair)
+        kappa1[here, :] = 0.25 * mix(both(w_kappa), pair)
+        cz1[here, :] = 0.25 * mix(both(w_cz), pair)
+        x_face1[here, :] = 0.125 * mix(first(x_face), pair)
+        y_face1[here, :] = 0.125 * mix(both(y_face), even)
+    mask1 = window_mask(rows, cols, HALO // 2, ix, iy, nx // 2, ny // 2)
+    faces1 = lambda k: (x_face1[plane(k, rows), :], y_face1[plane(k, rows), :])
+    window_down(rows, cols, mask1, f1, kappa1, faces1, cz1, saved1, r1)
+    y, lane = iota((128, 128), 0), iota((128, 128), 1)
+    total = jnp.zeros((NZ, 128), F32)
+    for xi in range(4):
+        place = (lane // 32 == (xi + iy) % 4) & (lane % 32 == y // 2) & (y < 64)
+        cells = coarse_rows(r1, 2 * xi, rows) + coarse_rows(r1, 2 * xi + 1, rows)
+        total = total + mix(cells, matrix(place))
+    send[...] = 0.25 * total
+
+
+def spread_rows(cells, x_before, x_after, dest, planes, rows):
+    size = planes * rows
+    even = 0.75 * cells + 0.25 * x_before
+    odd = 0.75 * cells + 0.25 * x_after
+    dest[pl.ds(0, size, stride=2), :] = even.reshape(size, 128)
+    dest[pl.ds(1, size, stride=2), :] = odd.reshape(size, 128)
+
+
+def up_kernel(gx, gy, *refs):
+    gathered, k2, k3, k4, saved0, saved1, diag, cz, solution_out, residual_out = refs[:10]
+    f2, u2, r2, f3, u3, r3, f4, u4, wide, e, w0, e0, s0, s1, sems = refs[10:]
+    ix, iy = lax.axis_index("gx"), lax.axis_index("gy")
+    copy1 = pltpu.make_async_copy(saved1, s1, sems.at[0])
+    copy0 = pltpu.make_async_copy(saved0, s0, sems.at[1])
+    copy1.start()
+    copy0.start()
+    assemble(gathered, 1, 0, f2, gx, gy)
+    pair = pair_matrix(128, 128)
+    rows2, cols2 = 4 * gx, 32 * gy
+
+    rows = rows2
+    for f, u, r, k, coarse in ((f2, u2, r2, k2, f3), (f3, u3, r3, k3, f4)):
+        get = [getter(k, n, rows) for n in range(7)]
+        forward_down(rows, f, u, get[4], get[5])
+        back_down(rows, f, u, r, get[:4], get[6])
+        rows = rows // 2
+        size = NZ * rows
+        cells = r[pl.ds(0, size, stride=2), :] + r[pl.ds(1, size, stride=2), :]
+        coarse[...] = 0.25 * mix(cells, pair)
+
+    get = [getter(k4, n, rows) for n in range(7)]
+
+    def coarse_solve(rhs, damped):
+        prev = jnp.zeros((rows, 128), F32)
+        forward = []
+        for k in range(NZ):
+            prev = rhs[k] * get[4](k) + get[5](k) * prev
+            forward.append(prev)
+        out = [None] * NZ
+        after = jnp.zeros((rows, 128), F32)
+        for k in reversed(range(NZ)):
+            after = forward[k] - get[6](k) * after
+            out[k] = damped[k] + OMEGA * after
+        return out
+
+    f_at = lambda k: f4[pl.ds(k * rows, rows), :]
+    field = coarse_solve([f_at(k) for k in range(NZ)], [0.0] * NZ)
+    for k in range(NZ):
+        u4[pl.ds(k * rows, rows), :] = field[k]
+
+    def relax(sweep, carry):
+        old = [u4[pl.ds(k * rows, rows), :] for k in range(NZ)]
+        rhs = [f_at(k) + neighbours(old[k], *[g(k) for g in get[:4]]) for k in range(NZ)]
+        new = coarse_solve(rhs, [(1.0 - OMEGA) * v for v in old])
+        for k in range(NZ):
+            u4[pl.ds(k * rows, rows), :] = new[k]
+        return carry
+
+    lax.fori_loop(0, COARSE_SWEEPS - 1, relax, 0)
+
+    coarse, cols = u4, cols2 // 4
+    for f, u, w, k in ((f3, u3, r3, k3), (f2, u2, r2, k2)):
+        cells = coarse[...].reshape(NZ, rows, 128)
+        x = iota((1, rows, 128), 1)
+        before = jnp.where(x > 0, shift(cells, 1, 1), 0.0)
+        after = jnp.where(x < rows - 1, shift(cells, -1, 1), 0.0)
+        spread_rows(cells, before, after, wide, NZ, rows)
+        y = iota((128, 128), 1)
+        partner = y // 2 + 2 * (y % 2) - 1
+        weights = spread_matrix(128, y, y // 2, jnp.where(partner < cols, partner, -1), y < 2 * cols)
+        rows, cols = 2 * rows, 2 * cols
+        size = NZ * rows
+        e[pl.ds(0, size), :] = mix(wide[pl.ds(0, size), :], weights)
+        get = [getter(k, n, rows) for n in range(7)]
+        f_of = functools.partial(lambda ref, count, n: ref[plane(n, count), :], f, rows)
+        sweep_up(rows, f_of, u, w, e, get[:4], get[4], get[5], get[6], None)
+        coarse = u
+
+    cells = pltpu.roll(u2[...].reshape(NZ, rows2, 128), (rows2 - 4 * ix) % rows2, 1)
+    q = iota((1, 8, 128), 1)
+    place = 4 * ix + jnp.where(q < 6, q, q - 8)
+    cells = jnp.where(q < 6, cells[:, :8], cells[:, rows2 - 8 :])
+    cells = jnp.where((place >= 0) & (place < rows2), cells, 0.0)
+    spread_rows(cells, shift(cells, 1, 1), shift(cells, -1, 1), wide, NZ, 8)
+    y = iota((128, 128), 1)
+    y = jnp.where(y < 96, y, y - 128) + 64 * iy
+    partner = (y + 128) // 2 - 64 + 2 * (y % 2) - 1
+    weights = spread_matrix(128, y, (y + 128) // 2 - 64, partner, (y >= 0) & (y < 2 * cols2))
+    size = NZ * TX
+    e[pl.ds(0, size), :] = mix(wide[pl.ds(0, size), :], weights)
+    copy1.wait()
+    get = [getter(s1, n, TX) for n in range(SAVED)]
+    mask1 = window_mask(TX, TY, HALO // 2, ix, iy, 2 * rows2, 2 * cols2)
+    u1 = s1.at[pl.ds(7 * size, size), :]
+    sweep_up(TX, get[8], u1, r2, e, get[:4], get[4], get[5], get[6], mask1)
+
+    cells = u1[...].reshape(NZ, TX, 128)
+    spread_rows(cells, shift(cells, 1, 1), shift(cells, -1, 1), wide, NZ, TX)
+    y = iota((128, 256), 1)
+    partner = (y // 2 + 2 * (y % 2) - 1 + 128) % 128
+    weights = spread_matrix(128, y, y // 2, partner, y >= 0)
+    for at in range(0, NZ * 2 * TX, 256):
+        e0[pl.ds(at, 256), :] = mix(wide[pl.ds(at, 256), :], weights)
+    copy0.wait()
+    rows = 2 * TX
+    size = NZ * rows
+    get = [getter(s0, n, rows) for n in range(SAVED)]
+    mask0 = window_mask(rows, 2 * TY, HALO, ix, iy, 4 * rows2, 4 * cols2)
+    u0 = s0.at[pl.ds(7 * size, size), :]
+    sweep_up(rows, get[8], u0, w0, e0, get[:4], get[4], get[5], get[6], mask0)
+
+    def residual(k, carry, last=False):
+        below, cz_k, z_low = carry
+        field = u0[plane(k, rows), :]
+        tile = field[:TX, :TY]
+        side = neighbours(field, *[g(k) for g in get[:4]])[:TX, :TY]
+        cz_next = jnp.zeros_like(cz_k) if last else cz[plane(k + 1, TX), :]
+        above = jnp.zeros_like(cz_k) if last else u0[plane(k + 1, rows), :][:TX, :TY]
+        z_up = 0.5 * (cz_k + cz_next)
+        out = get[8](k)[:TX, :TY] + side - diag[plane(k, TX), :] * tile + z_up * above + z_low * below
+        solution_out[plane(k, TX), :] = tile
+        residual_out[plane(k, TX), :] = out
+        return tile, cz_next, z_up
+
+    cz_0 = cz[pl.ds(0, TX), :]
+    carry = lax.fori_loop(0, NZ - 1, residual, (jnp.zeros_like(cz_0), cz_0, 0.5 * cz_0))
+    residual(NZ - 1, carry, last=True)
+
+
+def call(kernel, name, outs, ins, scratch=(), specs=None, flops=1000000):
+    shapes = [jax.ShapeDtypeStruct(s, F32) for s in outs]
+    return pl.pallas_call(
+        kernel,
+        name=name,
+        out_shape=shapes,
+        in_specs=specs or [VMEM] * len(ins),
+        out_specs=[VMEM] * len(outs),
+        scratch_shapes=list(scratch),
+        compiler_params=pltpu.CompilerParams(vmem_limit_bytes=56 * 1024 * 1024),
+        cost_estimate=pl.CostEstimate(flops=flops, bytes_accessed=4 * sum(x.size for x in ins), transcendentals=0),
+    )(*ins)
+
+
+def body(right_side, kappa_sq, cond_x, cond_y, cond_z):
+    gx, gy = lax.axis_size("gx"), lax.axis_size("gy")
+    tiles = [v.reshape(NZ * TX, TY) for v in (right_side, kappa_sq, cond_x, cond_y, cond_z)]
+    slab, strip = (5 * NZ * HALO, 128), (160, 128)
+    x_head, x_tail, y_head, y_tail = call(pack_kernel, "pack", [slab, slab, strip, strip], tiles)
+    share = call(coeff_kernel, "coeff_share", [(6 * NZ, 128)], tiles[1:])[0]
+    up = lambda n: [(i, i + 1) for i in range(n - 1)]
+    down = lambda n: [(i + 1, i) for i in range(n - 1)]
+    yr = lax.ppermute(y_head, "gy", down(gy))
+    yl = lax.ppermute(y_tail, "gy", up(gy))
+    xr = lax.ppermute(x_head, "gx", down(gx))
+    xl = lax.ppermute(x_tail, "gx", up(gx))
+    shares = lax.all_gather(share, ("gx", "gy")).reshape(gx * gy * 6 * NZ, 128)
+    corner_r = lax.ppermute(jnp.concatenate([yl[:80], yr[:80]]), "gx", down(gx))
+    corner_l = lax.ppermute(jnp.concatenate([yl[80:], yr[80:]]), "gx", up(gx))
+    vm = lambda *shape: pltpu.VMEM(shape, F32)
+    big, mid, low = NZ * 4 * gx, NZ * 2 * gx, NZ * gx
+    k2, k3, k4 = call(
+        functools.partial(global_kernel, gx, gy),
+        "global_coeffs",
+        [(7 * big, 128), (7 * mid, 128), (7 * low, 128)],
+        [shares],
+        [vm(big, 128)] * 8 + [vm(mid, 128)] * 6 + [vm(low, 128)] * 6,
+    )
+    size0, size1 = NZ * 2 * TX, NZ * TX
+    send, saved0, saved1, diag = call(
+        functools.partial(down_kernel, gx * TX, gy * TY),
+        "down",
+        [(NZ, 128), (SAVED * size0, 2 * TY), (SAVED * size1, TY), (NZ * TX, TY)],
+        [*tiles, xr, xl, yr, yl, corner_r, corner_l],
+        [vm(size0, 256)] * 8 + [vm(size1, 128)] * 6,
+    )
+    gathered = lax.all_gather(send, ("gx", "gy")).reshape(gx * gy * NZ, 128)
+    field, residual = call(
+        functools.partial(up_kernel, gx, gy),
+        "up",
+        [(NZ * TX, TY)] * 2,
+        [gathered, k2, k3, k4, saved0, saved1, diag, tiles[4]],
+        [vm(big, 128)] * 3 + [vm(mid, 128)] * 3 + [vm(low, 128)] * 2
+        + [vm(size0, 128), vm(size0, 128), vm(size0, 256), vm(size0, 256)]
+        + [vm(SAVED * size0, 256), vm(SAVED * size1, 128), pltpu.SemaphoreType.DMA((2,))],
+        [VMEM] * 4 + [ANY] * 2 + [VMEM] * 2,
+    )
+    return field.reshape(right_side.shape), residual.reshape(right_side.shape)
+
+
 def solution(mesh):
-    in_specs = (
-        P(None, "gx", "gy"),
-        P(None, "gx", "gy"),
-        P(None, "gx", "gy"),
-        P(None, "gx", "gy"),
-        P(None, "gx", "gy"),
-    )
-    out_specs = (P(None, "gx", "gy"), P(None, "gx", "gy"))
-    return jax.shard_map(body, mesh=mesh, in_specs=in_specs, out_specs=out_specs, check_vma=False)
+    spec = P(None, "gx", "gy")
+    fits = (mesh.shape["gx"], mesh.shape["gy"]) == (8, 4)
+    plan = body if fits else spread_body
+    return jax.shard_map(plan, mesh=mesh, in_specs=(spec,) * 5, out_specs=(spec, spec), check_vma=False)

time: 997 us -> 195 us (0.20)
  the two profiles are of different devices: /device:TPU:14 before, /device:TPU:0 now
where the time goes in v1:
time: 195 us; the launch traced here: 194 us
  Pallas kernels  86 us (44%)
  blocking collectives  74.7 us (38%)
  starting transfers between devices  16.7 us (9%)
  between operations  14.2 us (7%)
    pallas_call x5, Pallas kernels, call(): pl.pallas_call(kernel, name=name, out_shape=shapes, in_specs=specs or [VM...  86 us
    all_gather x1, blocking collectives, body(): gathered = lax.all_gather(send, ('gx', 'gy')).reshape(gx * gy * NZ, 128)  74.7 us
    ppermute x1, starting transfers between devices, body(): yl = lax.ppermute(y_tail, 'gy', up(gy))  5.47 us
    ppermute x1, starting transfers between devices, body(): corner_l = lax.ppermute(jnp.concatenate([yl[80:], yr[80:]]), 'gx', up(gx))  4.22 us
  transfers between devices with their start and end apart: 7, of which 1 were waited for; matrix products, arithmetic and copies ran while one was open for 0% of the time, Pallas kernels for 22%

profile of v1, /device:TPU:0, one launch (start us, length us, event | category | flops | bytes accessed | tf_op | source)
XLA Modules:
  0.0 194.2 jit_solution(1161388278484025067)
XLA Ops:
  7.2 0.0 all-gather.4.cloned.1.call-start
  7.2 2.3 %coeff_share.1 = f32[192,128]{1,0:T(8,128)} custom-call(f32[512,128]{1,0:T(8,128)} %bitcast.11, f32[512,128]{1,0:T(8,128)} %bitcast.14, f32[512,128]{1,0:T(8,128)} %bitcast.17, f32[512,128]{1,0:T(8,128)} %bitcast.7), custom_call_target="tpu_custom_call" | custom-call | flops 1000000 | bytes 1048576 | tf_op jit(solution)/shard_map/coeff_share/pallas_call | solution.py:622
  9.5 0.0 all-gather.4.cloned.1.call-update
  9.6 2.7 %pack.1 = (f32[1280,128]{1,0:T(8,128)}, f32[1280,128]{1,0:T(8,128)}, f32[160,128]{1,0:T(8,128)}, f32[160,128]{1,0:T(8,128)}) custom-call(f32[512,128]{1,0:T(8,128)} %bitcast.20, f32[512,128]{1,0:T(8,128)} %bitcast.12, f32[512,128]{1,0:T(8,128)} %bitcast.15, f32[512,128]{1,0:T(8,128)} %bitcast.18, f32[512,128]{1,0:T(8,128)} %bitcast.8), custom_call_target="tpu_custom_call" | custom-call | flops 1000000 | bytes 1310720 | tf_op jit(solution)/shard_map/pack/pallas_call | solution.py:622
  12.3 1.3 collective-permute-start.2
  13.6 5.5 %collective-permute-start.3 = (f32[160,128]{1,0:T(8,128)}, f32[160,128]{1,0:T(8,128)S(1)}, u32[]{:S(2)}, u32[]{:S(2)}) collective-permute-start(f32[160,128]{1,0:T(8,128)} %get-tuple-element.18), channel_id=1, source_target_pairs={{0,1},{1,2},{2,3},{4,5},{5,6},{6,7},{8,9},{9,10},{10,11},{12,13},{... | collective-permute-start | bytes 245768 | tf_op jit(solution)/shard_map/ppermute | solution.py:643
  19.0 1.3 collective-permute-start
  20.3 3.1 %collective-permute-start.1 = (f32[1280,128]{1,0:T(8,128)}, f32[1280,128]{1,0:T(8,128)S(1)}, u32[]{:S(2)}, u32[]{:S(2)}) collective-permute-start(f32[1280,128]{1,0:T(8,128)} %get-tuple-element.16), channel_id=1, source_target_pairs={{0,4},{4,8},{8,12},{12,16},{16,20},{20,24},{24,28},{1,5},{5,9},{9,... | collective-permute-start | bytes 1966088 | tf_op jit(solution)/shard_map/ppermute | solution.py:645
  23.4 0.0 collective-permute-done.2.refs_7_
  23.4 0.0 copy-start.2
  23.5 0.0 collective-permute-done.3.refs_8_
  23.5 0.0 copy-start.3
  23.5 1.3 collective-permute-start.4
  24.8 4.2 %collective-permute-start.5 = (f32[160,128]{1,0:T(8,128)S(1)}, f32[160,128]{1,0:T(8,128)S(1)}, u32[]{:S(2)}, u32[]{:S(2)}) collective-permute-start(f32[160,128]{1,0:T(8,128)S(1)} %pad_maximum_fusion.1), channel_id=1, source_target_pairs={{0,4},{4,8},{8,12},{12,16},{16,20},{20,24},{24,28},{1,5},{5,9},{9,... | collective-permute-start | bytes 245768 | tf_op jit(solution)/shard_map/ppermute | solution.py:648
  29.1 0.0 collective-permute-done.4.refs_9_
  29.1 0.0 copy-start.4
  29.1 0.9 collective-permute-done.5.refs_10_
  30.0 0.0 copy-start.5
  30.0 0.0 collective-permute-done.refs_5_
  30.0 0.0 copy-start
  30.0 0.0 collective-permute-done.1.refs_6_
  30.0 0.0 copy-done.2
  30.0 0.0 copy-done.3
  30.0 0.0 copy-done.4
  30.0 0.6 copy-done.5
  30.6 0.2 copy-done
  30.8 0.0 copy-start.1
  30.8 0.8 copy-done.1
  31.7 39.6 %down.1 = (f32[32,128]{1,0:T(8,128)}, f32[9216,256]{1,0:T(8,128)}, f32[4608,128]{1,0:T(8,128)}, f32[512,128]{1,0:T(8,128)}) custom-call(f32[512,128]{1,0:T(8,128)} %bitcast.21, f32[512,128]{1,0:T(8,128)} %bitcast.13, f32[512,128]{1,0:T(8,128)} %bitcast.16, f32[512,128]{1,0:T(8,128)} %bitcast.19, f32[512,128]{1,0:T(8,128)} %bitcast.9, f32[1280,128]{1,0:T(8,128)} %copy-done, ...), custom_call_target="tpu_custom_call" | custom-call | flops 1000000 | bytes 2949120 | tf_op jit(solution)/shard_map/down/pallas_call | solution.py:622
  71.3 74.7 %all-gather.refs_0_ = f32[1024,128]{1,0:T(8,128)} all-gather(f32[32,128]{1,0:T(8,128)} %get-tuple-element.19), channel_id=2, replica_groups=mesh['gx'=8,'gy'=4] {'gx','gy'}, dimensions={0}, use_global_device_ids=true | all-gather | bytes 540672 | tf_op jit(solution)/shard_map/all_gather | solution.py:666
  146.0 0.0 all-gather.4.cloned.1.call-done.gathered
  146.0 11.0 %global_coeffs.1 = (f32[7168,128]{1,0:T(8,128)}, f32[3584,128]{1,0:T(8,128)}, f32[1792,128]{1,0:T(8,128)}) custom-call(f32[6144,128]{1,0:T(8,128)} %all-gather.4.cloned.1.call-done.gathered), custom_call_target="tpu_custom_call" | custom-call | flops 1000000 | bytes 3145728 | tf_op jit(solution)/shard_map/global_coeffs/pallas_call | solution.py:622
  157.0 30.4 %up.1 = (f32[512,128]{1,0:T(8,128)}, f32[512,128]{1,0:T(8,128)}) custom-call(f32[1024,128]{1,0:T(8,128)} %all-gather.refs_0_, f32[7168,128]{1,0:T(8,128)} %get-tuple-element.20.refs_1_, f32[3584,128]{1,0:T(8,128)} %get-tuple-element.21.refs_2_, f32[1792,128]{1,0:T(8,128)} %get-tuple-element.22.refs_3_, f32[9216,256]{1,0:T(8,128)} %get-tuple-element.23.refs_4_, ...), custom_call_target="tpu_custom_call" | custom-call | flops 1000000 | bytes 19267584 | tf_op jit(solution)/shard_map/up/pallas_call | solution.py:622
  (4 shorter events, 0.0 us)
Async XLA Ops:
  7.2 138.8 %all-gather.4.cloned.1.call-start = ((), (), s32[]{:S(2)}) async-start(), calls=%async_computation | async-start | bytes 3244032 | tf_op jit(solution)/shard_map/all_gather | solution.py:646
  12.3 11.2 %collective-permute-start.2 = (f32[160,128]{1,0:T(8,128)}, f32[160,128]{1,0:T(8,128)S(1)}, u32[]{:S(2)}, u32[]{:S(2)}) collective-permute-start(f32[160,128]{1,0:T(8,128)} %get-tuple-element.17), channel_id=1, source_target_pairs={{1,0},{2,1},{3,2},{5,4},{6,5},{7,6},{9,8},{10,9},{11,10},{13,12},{... | collective-permute-start | bytes 245768 | tf_op jit(solution)/shard_map/ppermute | solution.py:642
  13.6 9.9 %collective-permute-start.3 = (f32[160,128]{1,0:T(8,128)}, f32[160,128]{1,0:T(8,128)S(1)}, u32[]{:S(2)}, u32[]{:S(2)}) collective-permute-start(f32[160,128]{1,0:T(8,128)} %get-tuple-element.18), channel_id=1, source_target_pairs={{0,1},{1,2},{2,3},{4,5},{5,6},{6,7},{8,9},{9,10},{10,11},{12,13},{... | collective-permute-start | bytes 245768 | tf_op jit(solution)/shard_map/ppermute | solution.py:643
  19.0 10.9 %collective-permute-start = (f32[1280,128]{1,0:T(8,128)}, f32[1280,128]{1,0:T(8,128)S(1)}, u32[]{:S(2)}, u32[]{:S(2)}) collective-permute-start(f32[1280,128]{1,0:T(8,128)} %get-tuple-element.15), channel_id=1, source_target_pairs={{4,0},{8,4},{12,8},{16,12},{20,16},{24,20},{28,24},{5,1},{9,5},{13... | collective-permute-start | bytes 1966088 | tf_op jit(solution)/shard_map/ppermute | solution.py:644
  20.3 9.6 %collective-permute-start.1 = (f32[1280,128]{1,0:T(8,128)}, f32[1280,128]{1,0:T(8,128)S(1)}, u32[]{:S(2)}, u32[]{:S(2)}) collective-permute-start(f32[1280,128]{1,0:T(8,128)} %get-tuple-element.16), channel_id=1, source_target_pairs={{0,4},{4,8},{8,12},{12,16},{16,20},{20,24},{24,28},{1,5},{5,9},{9,... | collective-permute-start | bytes 1966088 | tf_op jit(solution)/shard_map/ppermute | solution.py:645
  23.4 6.5 %copy-start.2 = (f32[160,128]{1,0:T(8,128)}, f32[160,128]{1,0:T(8,128)S(1)}, u32[]{:S(2)}) copy-start(f32[160,128]{1,0:T(8,128)S(1)} %collective-permute-done.2.refs_7_) | copy-start | bytes 245764
  23.5 6.5 %copy-start.3 = (f32[160,128]{1,0:T(8,128)}, f32[160,128]{1,0:T(8,128)S(1)}, u32[]{:S(2)}) copy-start(f32[160,128]{1,0:T(8,128)S(1)} %collective-permute-done.3.refs_8_) | copy-start | bytes 245764
  23.5 5.5 %collective-permute-start.4 = (f32[160,128]{1,0:T(8,128)S(1)}, f32[160,128]{1,0:T(8,128)S(1)}, u32[]{:S(2)}, u32[]{:S(2)}) collective-permute-start(f32[160,128]{1,0:T(8,128)S(1)} %pad_maximum_fusion), channel_id=1, source_target_pairs={{4,0},{8,4},{12,8},{16,12},{20,16},{24,20},{28,24},{5,1},{9,5},{13... | collective-permute-start | bytes 245768 | tf_op jit(solution)/shard_map/ppermute | solution.py:647
  24.8 5.1 %collective-permute-start.5 = (f32[160,128]{1,0:T(8,128)S(1)}, f32[160,128]{1,0:T(8,128)S(1)}, u32[]{:S(2)}, u32[]{:S(2)}) collective-permute-start(f32[160,128]{1,0:T(8,128)S(1)} %pad_maximum_fusion.1), channel_id=1, source_target_pairs={{0,4},{4,8},{8,12},{12,16},{16,20},{20,24},{24,28},{1,5},{5,9},{9,... | collective-permute-start | bytes 245768 | tf_op jit(solution)/shard_map/ppermute | solution.py:648
  29.1 0.9 copy-start.4
  30.0 0.6 copy-start.5
  30.0 0.9 copy-start
  30.8 0.9 copy-start.1
Sparse Core Ops, SparseCore 0:
  11.5 62.1 all-gather.3

commit v2 on v0

--- a/solution.py
+++ b/solution.py
@@ -1,6 +1,10 @@
+import functools
+
 import jax
 import jax.numpy as jnp
 from jax import lax
+from jax.experimental import pallas as pl
+from jax.experimental.pallas import tpu as pltpu
 from jax.sharding import PartitionSpec as P
 
 LEVELS = 4
@@ -137,7 +141,7 @@
     return field + OMEGA * line_solve(defect, factors, coeffs[6])
 
 
-def body(right_side, kappa_sq, cond_x, cond_y, cond_z):
+def spread_body(right_side, kappa_sq, cond_x, cond_y, cond_z):
     padded_x = with_halo(cond_x, (("gx", 1),), 1)
     padded_y = with_halo(cond_y, (("gy", 2),), 1)
     padded_z = jnp.pad(cond_z, ((1, 1), (0, 0), (0, 0)))
@@ -153,13 +157,761 @@
     return (solution_field, residual)
 
 
+F32 = jnp.float32
+BF16 = jnp.bfloat16
+NZ = 32
+HALF = NZ // 2
+TX, TY = 16, 128
+HALO = 8
+SLAB = 5 * NZ * HALO
+STRIP = 160
+VMEM = pl.BlockSpec(memory_space=pltpu.VMEM)
+ANY = pl.BlockSpec(memory_space=pl.ANY)
+
+
+def iota(shape, dim):
+    return lax.broadcasted_iota(jnp.int32, shape, dim)
+
+
+def shift(x, by, axis):
+    by = by % x.shape[axis]
+    return pltpu.roll(x, by, axis) if by else x
+
+
+def mix(x, weights):
+    high = x.astype(BF16)
+    rest = x - high.astype(F32)
+    mid = rest.astype(BF16)
+    low = (rest - mid.astype(F32)).astype(BF16)
+    dot = functools.partial(jnp.dot, preferred_element_type=F32)
+    return dot(low, weights) + dot(mid, weights) + dot(high, weights)
+
+
+def matrix(mask, weight=1.0):
+    return jnp.where(mask, weight, 0.0).astype(BF16)
+
+
+def span(start, size):
+    if not isinstance(start, int):
+        start = pl.multiple_of(start, 8)
+    return pl.ds(start, size)
+
+
+class Field:
+    def __init__(self, ref, rows, tiles=1, planes=NZ):
+        self.ref, self.rows, self.tiles, self.planes = ref, rows, tiles, planes
+
+    def base(self, tile, k):
+        return tile * self.planes * self.rows + k * self.rows
+
+    def part(self, tile, k):
+        return self.ref[span(self.base(tile, k), self.rows), :]
+
+    def __getitem__(self, k):
+        parts = [self.part(t, k) for t in range(self.tiles)]
+        return parts[0] if self.tiles == 1 else jnp.concatenate(parts, axis=1)
+
+    def __setitem__(self, k, value):
+        for t in range(self.tiles):
+            self.put(t, k, value[:, 128 * t : 128 * (t + 1)])
+
+    def put(self, tile, k, value):
+        self.ref[span(self.base(tile, k), self.rows), :] = value
+
+    def every_second(self, at, count, odd):
+        parts = []
+        for t in range(self.tiles):
+            first = t * self.planes * self.rows + 2 * at + odd
+            parts.append(self.ref[pl.ds(first, count, stride=2), :])
+        return parts[0] if self.tiles == 1 else jnp.concatenate(parts, axis=1)
+
+    def row(self, row):
+        return self.ref[pl.ds(row, self.planes, stride=self.rows), :]
+
+
+def loop(count, step, carry, unroll=None):
+    if unroll is None or unroll >= count:
+        for i in range(count):
+            carry = step(i, carry)
+        return carry
+    return lax.fori_loop(0, count, step, carry, unroll=unroll)
+
+
+def neighbours(field, x_face, y_face):
+    out = x_face * shift(field, 1, 0) + shift(x_face * field, -1, 0)
+    return out + (y_face * shift(field, 1, 1) + shift(y_face * field, -1, 1))
+
+
+class Line:
+    def __init__(self, inv, z_face):
+        self.inv, self.z_face = inv, z_face
+
+    def inward(self, k, upper):
+        return self.z_face[k + 1 if upper else k] * self.inv[k]
+
+    def outward(self, k, upper):
+        return self.z_face[k if upper else k + 1] * self.inv[k]
+
+
+class StoredLine:
+    def __init__(self, inv, g, c):
+        self.inv, self.g, self.c = inv, g, c
+
+    def inward(self, k, upper):
+        return self.g[k]
+
+    def outward(self, k, upper):
+        return self.c[k]
+
+
+def sweep_in(rhs, line, keep, start, unroll):
+    def step(i, carry):
+        low, high = carry
+        k, m = i, NZ - 1 - i
+        low = rhs(k) * line.inv[k] + line.inward(k, False) * low
+        high = rhs(m) * line.inv[m] + line.inward(m, True) * high
+        keep[k] = low
+        keep[m] = high
+        return low, high
+
+    return loop(HALF, step, (start, start), unroll)
+
+
+def sweep_out(ends, kept, line, emit, unroll):
+    low, high = ends
+    a, b = line.outward(HALF - 1, False), line.outward(HALF, True)
+    low = (low + a * high) * (1.0 / (1.0 - a * b))
+    high = high + b * low
+
+    def step(i, carry):
+        low, high = carry
+        k, m = HALF - 1 - i, HALF + i
+        emit(k, low)
+        emit(m, high)
+        low = kept[k - 1] + line.outward(k - 1, False) * low
+        high = kept[m + 1] + line.outward(m + 1, True) * high
+        return low, high
+
+    low, high = loop(HALF - 1, step, (low, high), unroll)
+    emit(0, low)
+    emit(NZ - 1, high)
+
+
+def factor(diag, z_face, tiles, inv_out, unroll, rhs=None, keep=None, g_out=None, c_out=None):
+    ends = []
+    for t in range(tiles):
+        zero = jnp.zeros((diag.rows, 128), F32)
+
+        def one(k, upper, inv_prev, prev):
+            below, above = z_face.part(t, k), z_face.part(t, k + 1)
+            inner, outer = (above, below) if upper else (below, above)
+            inv = 1.0 / (diag.part(t, k) + below + above - inner * inner * inv_prev)
+            inv_out.put(t, k, inv)
+            if g_out is not None:
+                g_out.put(t, k, inner * inv)
+                c_out.put(t, k, outer * inv)
+            if rhs is None:
+                return inv, prev
+            value = (rhs.part(t, k) + inner * prev) * inv
+            keep.put(t, k, value)
+            return inv, value
+
+        def step(i, carry):
+            low, high = carry
+            return one(i, False, *low), one(NZ - 1 - i, True, *high)
+
+        low, high = loop(HALF, step, ((zero, zero), (zero, zero)), unroll)
+        ends.append((low[1], high[1]))
+    join = lambda n: ends[0][n] if tiles == 1 else jnp.concatenate([e[n] for e in ends], axis=1)
+    return join(0), join(1)
+
+
+def z_faces(cz, out, tiles=1):
+    for t in range(tiles):
+        before = None
+        for k in range(NZ + 1):
+            here = cz.part(t, k) if k < NZ else None
+            both = here if before is None else before if here is None else here + before
+            out.put(t, k, 0.5 * both)
+            before = here
+
+
+def base_diag(kappa, x_face, y_face):
+    return kappa + (x_face + shift(x_face, -1, 0)) + (y_face + shift(y_face, -1, 1))
+
+
+def window_mask(rows, lanes, tile_x, tile_y, halo, ix, iy, nx, ny):
+    x, y = iota((rows, lanes), 0), iota((rows, lanes), 1)
+    x = jnp.where(x < (rows + tile_x) // 2, x, x - rows)
+    y = jnp.where(y < (lanes + tile_y) // 2, y, y - lanes)
+    valid = (y >= -halo) & (y < tile_y + halo) & (x >= -halo) & (x < tile_x + halo)
+    x, y = x + ix * tile_x, y + iy * tile_y
+    return (valid & (x >= 0) & (x < nx) & (y >= 0) & (y < ny)).astype(F32)
+
+
+def smooth_down(f, x_face, y_face, line, ends, kept, u, r, unroll):
+    def emit(k, value):
+        field = OMEGA * value
+        u[k] = field
+        r[k] = (1.0 - OMEGA) * f[k] + neighbours(field, x_face[k], y_face[k])
+
+    sweep_out(ends, kept, line, emit, unroll)
+
+
+def smooth_up(f, x_face, y_face, line, u, e, kept, mask, unroll):
+    masked = (lambda v: v) if mask is None else (lambda v: v * mask)
+
+    def rhs(k):
+        field = masked(u[k] + e[k])
+        u[k] = field
+        return masked(f[k] + neighbours(field, x_face[k], y_face[k]))
+
+    def emit(k, value):
+        u[k] = (1.0 - OMEGA) * u[k] + OMEGA * value
+
+    zero = jnp.zeros((u.rows, 128 * u.tiles), F32)
+    ends = sweep_in(rhs, line, kept, zero, unroll)
+    sweep_out(ends, kept, line, emit, unroll)
+
+
+def spread_rows(cells, before, after, dest, size):
+    dest[pl.ds(0, size, stride=2), :] = (0.75 * cells + 0.25 * before).reshape(size, 128)
+    dest[pl.ds(1, size, stride=2), :] = (0.75 * cells + 0.25 * after).reshape(size, 128)
+
+
+def spread_matrix(fine, base, coarse_count, circular=False):
+    j = iota((128, fine.shape[1]), 0) + base
+    parent = (fine + 2048) // 2 - 1024
+    partner = parent + 2 * ((fine + 2048) % 2) - 1
+    if circular:
+        j, parent, partner = j % 128, parent % 128, partner % 128
+    weights = jnp.where(j == parent, 0.75, jnp.where(j == partner, 0.25, 0.0))
+    if not circular:
+        inside = (j >= 0) & (j < coarse_count) & (fine >= 0) & (fine < 2 * coarse_count)
+        weights = jnp.where(inside, weights, 0.0)
+    return weights.astype(BF16)
+
+
+def lane_group(rows, width):
+    return iota((rows, 128), 1) // width
+
+
+def fold_planes(cells, turn):
+    group = lane_group(8, 32)
+    out = cells[:8]
+    for n in range(1, 4):
+        out = jnp.where(group == n, cells[8 * n : 8 * n + 8], out)
+    return pltpu.roll(out, turn, 1)
+
+
+def pack_kernel(f, kappa, cx, cy, cz, x_head, x_tail, y_head, y_tail, share3):
+    iy = lax.axis_index("gy")
+    y, lane = iota((128, 128), 0), iota((128, 128), 1)
+    fourth = y // 4 == lane % 32
+    rows = lambda ref: [Field(ref, TX).row(r) for r in range(TX)]
+    cx_rows, cy_rows, kappa_rows, cz_rows = rows(cx), rows(cy), rows(kappa), rows(cz)
+    totals = lambda v: [(v[4 * i] + v[4 * i + 1]) + (v[4 * i + 2] + v[4 * i + 3]) for i in range(4)]
+    stack = [cx_rows[4 * i] for i in range(4)] + [cx_rows[4 * i + 3] for i in range(4)]
+    stack = mix(jnp.concatenate(stack + totals(kappa_rows) + totals(cz_rows), axis=0), matrix(fourth))
+    ends = [matrix(fourth & (y % 4 == 0)), matrix(fourth & (y % 4 == 3))]
+    sides = mix(jnp.concatenate(totals(cy_rows), axis=0), jnp.concatenate(ends, axis=1))
+    group = lane_group(NZ, 32)
+
+    def merge(cells, scale):
+        out = cells[:NZ]
+        for xi in range(1, 4):
+            out = jnp.where(group == xi, cells[NZ * xi : NZ * (xi + 1)], out)
+        return out * scale
+
+    kinds = [merge(stack[:128], 1 / 128), merge(stack[128:256], 1 / 128)]
+    kinds += [merge(sides[:, :128], 1 / 128), merge(sides[:, 128:], 1 / 128)]
+    kinds += [merge(stack[256:384], 1 / 16), merge(stack[384:], 1 / 16)]
+    head = [jnp.zeros((8, 128), F32)] * 3
+    tail = [jnp.zeros((8, 128), F32)] * 3
+    slot = iota((8, 128), 1) % 32 // 4
+    for t, cells in enumerate(kinds):
+        at = pl.ds(SLAB + t * NZ, NZ)
+        x_head[at, :] = cells
+        x_tail[at, :] = cells
+        for zv in range(4):
+            n = 4 * t + zv
+            piece = cells[8 * zv : 8 * zv + 8]
+            head[n // 8] = jnp.where(slot == n % 8, shift(piece, 4 * (n % 8), 1), head[n // 8])
+            tail[n // 8] = jnp.where(slot == n % 8, shift(piece, 4 * (n % 8) + 4, 1), tail[n // 8])
+    for n in range(3):
+        y_head[pl.ds(STRIP + 8 * n, 8), :] = head[n]
+        y_tail[pl.ds(STRIP + 8 * n, 8), :] = tail[n]
+
+    x_in, y_in = y // 32, y % 32
+    x_out, y_out = lane % 32 // 16, lane % 16
+    pair_y, pair_x = y_in // 2 == y_out, x_in // 2 == x_out
+    folds = [
+        matrix(pair_y & (x_in == 2 * x_out), 0.125),
+        matrix(pair_y & (x_in == 2 * x_out + 1), 0.125),
+        matrix(pair_x & (y_in == 2 * y_out), 0.125),
+        matrix(pair_x & (y_in == 2 * y_out + 1), 0.125),
+        matrix(pair_x & pair_y, 0.25),
+    ]
+    for t, cells in enumerate(kinds):
+        share3[pl.ds(8 * t, 8), :] = fold_planes(mix(cells, folds[min(t, 4)]), 16 * iy)
+
+    group = lane_group(8, 8)
+    for a, ref in enumerate((f, kappa, cx, cy, cz)):
+        cells = ref[...].reshape(NZ, TX, TY)
+        at = pl.ds(a * NZ * HALO, NZ * HALO)
+        x_head[at, :] = cells[:, :HALO].reshape(NZ * HALO, TY)
+        x_tail[at, :] = cells[:, TX - HALO :].reshape(NZ * HALO, TY)
+        for half in range(2):
+            for zo in range(2):
+                head = jnp.zeros((8, 128), F32)
+                tail = jnp.zeros((8, 128), F32)
+                for zi in range(16):
+                    cells = ref[pl.ds((zo * 16 + zi) * TX + 8 * half, 8), :]
+                    cells = shift(cells, 8 * zi, 1)
+                    head = jnp.where(group == zi, cells, head)
+                    tail = jnp.where(group == (zi - 1) % 16, cells, tail)
+                at = pl.ds(((half * 5 + a) * 2 + zo) * 8, 8)
+                y_head[at, :] = head
+                y_tail[at, :] = tail
+
+
+def window2(tile, after, before, dest, first):
+    lane = iota((NZ, 128), 1)
+    for xi in range(4):
+        turned = (lane - 32 * xi + 128) % 128
+        cells = jnp.where(turned < 32, tile, jnp.where(turned < 36, after, jnp.where(turned >= 124, before, 0.0)))
+        dest[pl.ds(first + xi, NZ, stride=TX), :] = shift(cells, -32 * xi, 1)
+
+
+def window_kernel(x_head, xr, xl, yr, yl, cr, cl, x_face, y_face, inv, z_face, a, b, c, d, kappa, cz, diag):
+    ix, iy = lax.axis_index("gx"), lax.axis_index("gy")
+    nx, ny = lax.axis_size("gx") * 4, lax.axis_size("gy") * 32
+    refs = (a, b, c, d, kappa, cz)
+
+    def unpack(ref, first, t, turn):
+        pieces = []
+        for zv in range(4):
+            n = 4 * t + zv
+            pieces.append(shift(ref[pl.ds(first + 8 * (n // 8), 8), :], turn - 4 * (n % 8), 1))
+        return jnp.concatenate(pieces, axis=0)
+
+    half = STRIP // 2
+    for t, dest in enumerate(refs):
+        at = pl.ds(SLAB + t * NZ, NZ)
+        for first, tile, right, left, r_at, l_at in (
+            (0, x_head, yr, yl, STRIP, STRIP),
+            (4, xr, cr, cr, half + 24 + half, half),
+            (12, xl, cl, cl, half + 24 + half, half),
+        ):
+            window2(tile[at, :], unpack(right, r_at, t, 32), unpack(left, l_at, t, 92), dest, first)
+        for x in range(8, 12):
+            dest[pl.ds(x, NZ, stride=TX), :] = jnp.zeros((NZ, 128), F32)
+    mask = window_mask(TX, 128, 4, 32, 4, ix, iy, nx, ny)
+    fields = [Field(ref, TX) for ref in (*refs, x_face, y_face, diag, inv)]
+    a, b, c, d, kappa, cz, x_face, y_face, diag, inv = fields
+    for k in range(NZ):
+        x_k = a[k] + shift(b[k], 1, 0)
+        y_k = c[k] + shift(d[k], 1, 1)
+        x_face[k] = x_k
+        y_face[k] = y_k
+        diag[k] = base_diag(jnp.where(mask > 0, kappa[k], 1.0), x_k, y_k)
+    z_face = Field(z_face, TX, 1, NZ + 1)
+    z_faces(cz, z_face)
+    factor(diag, z_face, 1, inv, None)
+
+
+def assemble3(gathered, stride, first, dest, gx, gy, rows):
+    group = lane_group(8, 16)
+    for ix in range(gx):
+        blocks = [gathered[pl.ds((ix * gy + iy) * stride + first, 8), :] for iy in range(gy)]
+        for zo in range(4):
+            for xi in range(2):
+                q = 2 * zo + xi
+                cells = blocks[0]
+                for iy in range(1, gy):
+                    cells = jnp.where(group == (iy + q) % 8, blocks[iy], cells)
+                dest[pl.ds(8 * zo * rows + 2 * ix + xi, 8, stride=rows), :] = shift(cells, -16 * q, 1)
+
+
+def global_kernel(gx, gy, gathered, *refs):
+    outs3, outs4 = refs[:5], refs[5:10]
+    raw3, raw4 = refs[10:18], refs[18:26]
+    rows, cols = 2 * gx, 16 * gy
+    for t in range(6):
+        assemble3(gathered, 48, 8 * t, raw3[t], gx, gy, rows)
+    a, b, c, d = (Field(ref, rows) for ref in raw3[:4])
+    x, y = iota((rows, 128), 0), iota((rows, 128), 1)
+    for k in range(NZ):
+        a_k, b_k, c_k, d_k = a[k], b[k], c[k], d[k]
+        a[k] = a_k + jnp.where(x > 0, shift(b_k, 1, 0), 0.0)
+        b[k] = b_k + jnp.where(x < rows - 1, shift(a_k, -1, 0), 0.0)
+        c[k] = jnp.where(y < cols, c_k + jnp.where(y > 0, shift(d_k, 1, 1), 0.0), 0.0)
+        d[k] = jnp.where(y < cols, d_k + jnp.where(y < cols - 1, shift(c_k, -1, 1), 0.0), 0.0)
+    yy, jj = iota((128, 128), 0), iota((128, 128), 1)
+    keep = yy // 2 == jj
+    pair, even, odd = matrix(keep), matrix(keep & (yy % 2 == 0)), matrix(keep & (yy % 2 == 1))
+    size = NZ * rows // 2
+    lows = [Field(ref, rows) for ref in raw3]
+    first = lambda n: lows[n].every_second(0, size, 0)
+    second = lambda n: lows[n].every_second(0, size, 1)
+    raw4[0][...] = 0.125 * mix(first(0), pair)
+    raw4[1][...] = 0.125 * mix(second(1), pair)
+    raw4[2][...] = 0.125 * mix(first(2) + second(2), even)
+    raw4[3][...] = 0.125 * mix(first(3) + second(3), odd)
+    raw4[4][...] = 0.25 * mix(first(4) + second(4), pair)
+    raw4[5][...] = 0.25 * mix(first(5) + second(5), pair)
+    for raw, outs in ((raw3, outs3), (raw4, outs4)):
+        x, y = iota((rows, 128), 0), iota((rows, 128), 1)
+        xl, xu, yl, yu, kappa, cz = (Field(ref, rows) for ref in raw[:6])
+        z_face, diag = Field(raw[6], rows, 1, NZ + 1), Field(raw[7], rows)
+        x_face, y_face, inv, g, c = (Field(ref, rows) for ref in outs)
+        inside_x, inside_y = (x > 0).astype(F32), ((y > 0) & (y < cols)).astype(F32)
+        for k in range(NZ):
+            xl_k, yl_k = xl[k], yl[k]
+            diag[k] = jnp.where(y < cols, kappa[k], 1.0) + (xl_k + xu[k]) + (yl_k + yu[k])
+            x_face[k] = xl_k * inside_x
+            y_face[k] = yl_k * inside_y
+        z_faces(cz, z_face)
+        factor(diag, z_face, 1, inv, None, g_out=g, c_out=c)
+        rows, cols = rows // 2, cols // 2
+
+
+def down_kernel(nx, ny, *refs):
+    f, kappa, cx, cy, cz, xr, xl, yr, yl, corner_r, corner_l = refs[:11]
+    send, outs0, outs1 = refs[11], refs[12:18], refs[18:24]
+    scratch = list(refs[24:-1])
+    sems = refs[-1]
+    take = lambda n: [scratch.pop(0) for _ in range(n)]
+    ix, iy = lax.axis_index("gx"), lax.axis_index("gy")
+    rows, tiles = 2 * TX, 2
+    whole = take(11)
+    names = [Field(ref, rows, tiles) for ref in whole[:10]]
+    x_face, y_face, inv, u, f0, kappa0, cz0, diag, kept, r = names
+    z_face = Field(whole[10], rows, tiles, NZ + 1)
+    group = lane_group(8, 8)
+
+    def window(a, tile, z, after, before, turn):
+        zo = z // 16
+        slab = span(a * NZ * HALO + z * HALO, HALO)
+        main = jnp.concatenate([tile[span(z * TX, TX), :], xr[slab, :], xl[slab, :]], axis=0)
+        at = lambda first: span(first + (a * 2 + zo) * 8, 8)
+        half = STRIP // 2
+        sides = []
+        for right, left in (
+            (yr[at(0), :], yl[at(0), :]),
+            (yr[at(half), :], yl[at(half), :]),
+            (corner_r[at(half + 24), :], corner_r[at(0), :]),
+            (corner_l[at(half + 24), :], corner_l[at(0), :]),
+        ):
+            cells = jnp.where(after, right, jnp.where(before, left, 0.0))
+            sides.append(pltpu.roll(cells, turn, 1))
+        return jnp.concatenate([main, jnp.concatenate(sides, axis=0)], axis=1)
+
+    mask0 = window_mask(rows, 256, TX, TY, HALO, ix, iy, nx, ny)
+
+    def prepare(z, cz_prev):
+        zi = z % 16
+        after, before = group == zi, group == (zi + 15) % 16
+        turn = (128 - 8 * zi) % 128
+        f_k, kappa_k, cx_k, cy_k, cz_k = (
+            window(a, tile, z, after, before, turn) for a, tile in enumerate((f, kappa, cx, cy, cz))
+        )
+        f0[z] = f_k
+        kappa0[z] = kappa_k
+        cz0[z] = cz_k
+        z_face[z] = 0.5 * (cz_k + cz_prev)
+        x_k, y_k = 0.5 * (cx_k + shift(cx_k, 1, 0)), 0.5 * (cy_k + shift(cy_k, 1, 1))
+        x_face[z] = x_k
+        y_face[z] = y_k
+        diag[z] = base_diag(jnp.where(mask0 > 0, kappa_k, 1.0), x_k, y_k)
+        return cz_k
+
+    last = loop(NZ, prepare, jnp.zeros((rows, 256), F32), 2)
+    z_face[NZ] = 0.5 * last
+    ends = factor(diag, z_face, tiles, inv, 4, f0, kept)
+    sources = [x_face, y_face, inv, z_face, u, f0]
+    copies = [pltpu.make_async_copy(s.ref, o, sems.at[n]) for n, (s, o) in enumerate(zip(sources, outs0))]
+    for n in (0, 1, 2, 3, 5):
+        copies[n].start()
+    smooth_down(f0, x_face, y_face, Line(inv, z_face), ends, kept, u, r, 2)
+    copies[4].start()
+
+    fine = (r, kappa0, cz0, x_face, y_face)
+    lanes, tile_x, tile_y, halo, outs = 256, TX, TY, HALO, outs1
+    for level in (1, 2):
+        rows, tile_x, tile_y, halo = rows // 2, tile_x // 2, tile_y // 2, halo // 2
+        nx, ny = nx // 2, ny // 2
+        whole = take(11)
+        names = [Field(ref, rows) for ref in whole[:10]]
+        x_face, y_face, inv, u, f1, kappa1, cz1, diag, kept, r = names
+        z_face = Field(whole[10], rows, 1, NZ + 1)
+        mask = window_mask(rows, 128, tile_x, tile_y, halo, ix, iy, nx, ny)
+        y, j = iota((lanes, 128), 0), iota((lanes, 128), 1)
+        if lanes == 128:
+            j = jnp.where(j < 48, j, jnp.where(j >= 80, j - 64, -1))
+        pair, even = matrix(y // 2 == j), matrix(y == 2 * j)
+        part = min(128, NZ * rows)
+        for at in range(0, NZ * rows, part):
+            here = pl.ds(at, part)
+            both = lambda n: fine[n].every_second(at, part, 0) + fine[n].every_second(at, part, 1)
+            f1.ref[here, :] = 0.25 * mix(both(0), pair)
+            kappa1.ref[here, :] = 0.25 * mix(both(1), pair)
+            cz1.ref[here, :] = 0.25 * mix(both(2), pair)
+            x_face.ref[here, :] = 0.125 * mix(fine[3].every_second(at, part, 0), pair)
+            y_face.ref[here, :] = 0.125 * mix(both(4), even)
+        for k in range(NZ):
+            f1[k] = f1[k] * mask
+            diag[k] = base_diag(jnp.where(mask > 0, kappa1[k], 1.0), x_face[k], y_face[k])
+        z_faces(cz1, z_face)
+        ends = factor(diag, z_face, 1, inv, None, f1, kept)
+        smooth_down(f1, x_face, y_face, Line(inv, z_face), ends, kept, u, r, None)
+        if level == 1:
+            sources = [x_face, y_face, inv, z_face, u, f1]
+            more = [pltpu.make_async_copy(s.ref, o, sems.at[6 + n]) for n, (s, o) in enumerate(zip(sources, outs1))]
+            for copy in more:
+                copy.start()
+            copies += more
+        fine, lanes = (r, kappa1, cz1, x_face, y_face), 128
+
+    group = lane_group(NZ, 32)
+    out = f1.row(0)
+    for xi in range(1, 4):
+        out = jnp.where(group == xi, shift(f1.row(xi), 32 * xi, 1), out)
+    send[pl.ds(0, NZ), :] = out
+    y, lane = iota((128, 128), 0), iota((128, 128), 1)
+    total = jnp.zeros((NZ, 128), F32)
+    for xi in range(2):
+        place = (lane % 32 // 16 == xi) & (y // 2 == lane % 16) & (y < 32)
+        total = total + mix(r.row(2 * xi) + r.row(2 * xi + 1), matrix(place, 0.25))
+    send[pl.ds(NZ, 8), :] = fold_planes(total, 16 * iy)
+    for copy in copies:
+        copy.wait()
+
+
+def up_kernel(gx, gy, *refs):
+    gathered, kappa = refs[:2]
+    k3, k4, k2 = refs[2:7], refs[7:12], refs[12:16]
+    saved0, saved1 = refs[16:22], refs[22:28]
+    solution_out, residual_out = refs[28:30]
+    scratch = list(refs[30:-1])
+    sems = refs[-1]
+    take = lambda n: [scratch.pop(0) for _ in range(n)]
+    ix, iy = lax.axis_index("gx"), lax.axis_index("gy")
+    held0, held1 = take(6), take(6)
+    copies = []
+    for n, (source, dest) in enumerate(zip((*saved1, *saved0), (*held1, *held0))):
+        copies.append(pltpu.make_async_copy(source, dest, sems.at[n]))
+        copies[-1].start()
+    f3, u3, r3, f2, u2, kept2, f4, u4, wide, e_ref, e0_ref, kept0 = take(12)
+
+    rows, cols = 2 * gx, 16 * gy
+    assemble3(gathered, NZ + 8, NZ, f3, gx, gy, rows)
+    y, lane = iota((128, 128), 0), iota((128, 128), 1)
+    f3, u3, r3 = (Field(ref, rows) for ref in (f3, u3, r3))
+    y = iota((rows, 128), 1)
+    x_face3, y_face3, inv3, g3, c3 = (Field(ref, rows) for ref in k3)
+    line3 = StoredLine(inv3, g3, c3)
+    clean = (y < cols).astype(F32)
+    for k in range(NZ):
+        f3[k] = f3[k] * clean
+    zero = jnp.zeros((rows, 128), F32)
+    ends = sweep_in(lambda k: f3[k], line3, r3, zero, None)
+    smooth_down(f3, x_face3, y_face3, line3, ends, r3, u3, Field(e_ref, rows), None)
+    fine = Field(e_ref, rows)
+    rows, cols = rows // 2, cols // 2
+    size = NZ * rows
+    yy, jj = iota((128, 128), 0), iota((128, 128), 1)
+    f4[...] = 0.25 * mix(fine.every_second(0, size, 0) + fine.every_second(0, size, 1), matrix(yy // 2 == jj))
+    f4, u4 = Field(f4, rows), Field(u4, rows)
+    x_face4, y_face4, inv4, g4, c4 = (Field(ref, rows) for ref in k4)
+    line4 = StoredLine(inv4, g4, c4)
+    zero = jnp.zeros((rows, 128), F32)
+
+    def solve4(rhs, old):
+        kept, out = {}, {}
+        ends = sweep_in(rhs, line4, kept, zero, None)
+
+        def emit(k, value):
+            out[k] = OMEGA * value if old is None else (1.0 - OMEGA) * old[k] + OMEGA * value
+
+        sweep_out(ends, kept, line4, emit, None)
+        for k in range(NZ):
+            u4[k] = out[k]
+
+    solve4(lambda k: f4[k], None)
+
+    def relax(sweep, carry):
+        old = [u4[k] for k in range(NZ)]
+        solve4(lambda k: f4[k] + neighbours(old[k], x_face4[k], y_face4[k]), old)
+        return carry
+
+    lax.fori_loop(0, COARSE_SWEEPS - 1, relax, 0)
+
+    cells = u4.ref[...].reshape(NZ, rows, 128)
+    x = iota((1, rows, 128), 1)
+    before = jnp.where(x > 0, shift(cells, 1, 1), 0.0)
+    after = jnp.where(x < rows - 1, shift(cells, -1, 1), 0.0)
+    spread_rows(cells, before, after, wide, size)
+    e_ref[...] = mix(wide[pl.ds(0, 2 * size), :], spread_matrix(iota((128, 128), 1), 0, cols))
+    rows, cols = 2 * rows, 2 * cols
+    smooth_up(f3, x_face3, y_face3, line3, u3, Field(e_ref, rows), r3, None, None)
+
+    def block(dx, dy):
+        jx, jy = ix + dx, iy + dy
+        inside = ((jx >= 0) & (jx < gx) & (jy >= 0) & (jy < gy)).astype(F32)
+        device = jnp.clip(jx, 0, gx - 1) * gy + jnp.clip(jy, 0, gy - 1)
+        return gathered[span(device * (NZ + 8), NZ), :] * inside
+
+    for first, dx in ((0, 0), (4, 1), (12, -1)):
+        window2(block(dx, 0), shift(block(dx, 1), 32, 1), shift(block(dx, -1), 96, 1), f2, first)
+    for x in range(8, 12):
+        f2[pl.ds(x, NZ, stride=TX), :] = jnp.zeros((NZ, 128), F32)
+    f2, u2, kept2 = (Field(ref, TX) for ref in (f2, u2, kept2))
+    x_face2, y_face2, inv2 = (Field(ref, TX) for ref in k2[:3])
+    line2 = Line(inv2, Field(k2[3], TX, 1, NZ + 1))
+    zero = jnp.zeros((TX, 128), F32)
+    ends = sweep_in(lambda k: f2[k], line2, kept2, zero, None)
+
+    def emit2(k, value):
+        u2[k] = OMEGA * value
+
+    sweep_out(ends, kept2, line2, emit2, None)
+
+    cells = pltpu.roll(u3.ref[...].reshape(NZ, rows, 128), (rows - 2 * ix) % rows, 1)
+    x = iota((1, rows, 128), 1)
+    place = 2 * ix + jnp.where(x < rows // 2, x, x - rows)
+    cells = jnp.where((place >= 0) & (place < rows), cells, 0.0)
+    ring = lambda v, first: jnp.where(iota((1, 8, 128), 1) < first, v[:, :8], v[:, rows - 8 :])
+    spread_rows(ring(cells, 4), ring(shift(cells, 1, 1), 4), ring(shift(cells, -1, 1), 4), wide, NZ * 8)
+    lane = iota((128, 128), 1)
+    fine_y = jnp.where(lane < 80, lane, lane - 128) + 32 * iy
+    e_ref[...] = mix(wide[pl.ds(0, NZ * TX), :], spread_matrix(fine_y, 0, cols))
+    mask2 = window_mask(TX, 128, 4, 32, 4, ix, iy, 4 * gx, 32 * gy)
+    smooth_up(f2, x_face2, y_face2, line2, u2, Field(e_ref, TX), kept2, mask2, None)
+
+    cells = u2.ref[...].reshape(NZ, TX, 128)
+    ring = lambda v: jnp.where(iota((1, 8, 128), 1) < 6, v[:, :8], v[:, 8:])
+    spread_rows(ring(cells), ring(shift(cells, 1, 1)), ring(shift(cells, -1, 1)), wide, NZ * 8)
+    fine_y = jnp.where(lane < 96, lane, lane - 128)
+    e_ref[...] = mix(wide[pl.ds(0, NZ * TX), :], spread_matrix(fine_y, 0, 0, circular=True))
+    for copy in copies[:6]:
+        copy.wait()
+    x_face1, y_face1, inv1, z_face1, u1, f1 = held1
+    x_face1, y_face1, inv1, u1, f1 = (Field(ref, TX) for ref in (x_face1, y_face1, inv1, u1, f1))
+    line1 = Line(inv1, Field(z_face1, TX, 1, NZ + 1))
+    mask1 = window_mask(TX, 128, 8, 64, 4, ix, iy, 8 * gx, 64 * gy)
+    smooth_up(f1, x_face1, y_face1, line1, u1, Field(e_ref, TX), kept2, mask1, None)
+
+    cells = u1.ref[...].reshape(NZ, TX, 128)
+    spread_rows(cells, shift(cells, 1, 1), shift(cells, -1, 1), wide, NZ * TX)
+    rows = 2 * TX
+    weights = spread_matrix(iota((128, 256), 1), 0, 0, circular=True)
+    e0 = Field(e0_ref, rows, 2)
+    for k in range(0, NZ, 8):
+        cells = mix(wide[pl.ds(k * rows, 8 * rows), :], weights)
+        for t in range(2):
+            e0_ref[pl.ds(e0.base(t, k), 8 * rows), :] = cells[:, 128 * t : 128 * (t + 1)]
+    for copy in copies[6:]:
+        copy.wait()
+    x_face0, y_face0, inv0, z_face0, u0, f0 = held0
+    x_face0, y_face0, inv0, u0, f0 = (Field(ref, rows, 2) for ref in (x_face0, y_face0, inv0, u0, f0))
+    z_face0 = Field(z_face0, rows, 2, NZ + 1)
+    mask0 = window_mask(rows, 256, TX, TY, HALO, ix, iy, TX * gx, TY * gy)
+    smooth_up(f0, x_face0, y_face0, Line(inv0, z_face0), u0, e0, Field(kept0, rows, 2), mask0, 2)
+
+    kappa = Field(kappa, TX)
+    tile = lambda v: v[:TX, :TY]
+
+    def residual(k, carry):
+        below, flux_z = carry
+        field = u0[k]
+        flux_x = x_face0[k] * (field - shift(field, 1, 0))
+        flux_y = y_face0[k] * (field - shift(field, 1, 1))
+        side = (flux_x - shift(flux_x, -1, 0)) + (flux_y - shift(flux_y, -1, 1))
+        here = tile(field)
+        above = u0.part(0, k + 1)[:TX] if k is not NZ - 1 else jnp.zeros((TX, TY), F32)
+        flux_up = z_face0.part(0, k + 1)[:TX] * (above - here)
+        solution_out[span(k * TX, TX), :] = here
+        out = f0.part(0, k)[:TX] - kappa[k] * here - tile(side) - flux_z + flux_up
+        residual_out[span(k * TX, TX), :] = out
+        return here, flux_up
+
+    start = z_face0.part(0, 0)[:TX] * tile(u0[0])
+    carry = loop(NZ - 1, residual, (start, start), 2)
+    residual(NZ - 1, carry)
+
+
+def call(kernel, name, outs, ins, scratch=(), in_specs=None, out_specs=None, flops=1000000):
+    shapes = [jax.ShapeDtypeStruct(s, F32) for s in outs]
+    return pl.pallas_call(
+        kernel,
+        name=name,
+        out_shape=shapes,
+        in_specs=in_specs or [VMEM] * len(ins),
+        out_specs=out_specs or [VMEM] * len(outs),
+        scratch_shapes=list(scratch),
+        compiler_params=pltpu.CompilerParams(vmem_limit_bytes=56 * 1024 * 1024),
+        cost_estimate=pl.CostEstimate(flops=flops, bytes_accessed=4 * sum(x.size for x in ins), transcendentals=0),
+    )(*ins)
+
+
+def body(right_side, kappa_sq, cond_x, cond_y, cond_z):
+    gx, gy = lax.axis_size("gx"), lax.axis_size("gy")
+    tiles = [v.reshape(NZ * TX, TY) for v in (right_side, kappa_sq, cond_x, cond_y, cond_z)]
+    slab, strip = (SLAB + 6 * NZ, 128), (STRIP + 24, 128)
+    x_head, x_tail, y_head, y_tail, share3 = call(pack_kernel, "pack", [slab, slab, strip, strip, (48, 128)], tiles)
+    up = lambda n: [(i, i + 1) for i in range(n - 1)]
+    down = lambda n: [(i + 1, i) for i in range(n - 1)]
+    yr = lax.ppermute(y_head, "gy", down(gy))
+    yl = lax.ppermute(y_tail, "gy", up(gy))
+    xr = lax.ppermute(x_head, "gx", down(gx))
+    xl = lax.ppermute(x_tail, "gx", up(gx))
+    shares = lax.all_gather(lax.all_gather(share3, "gy"), "gx").reshape(gx * gy * 48, 128)
+    half = STRIP // 2
+    corner_r = lax.ppermute(jnp.concatenate([yl[:half], yl[STRIP:], yr[:half], yr[STRIP:]]), "gx", down(gx))
+    corner_l = lax.ppermute(jnp.concatenate([yl[half:STRIP], yl[STRIP:], yr[half:STRIP], yr[STRIP:]]), "gx", up(gx))
+    vm = lambda *shape: pltpu.VMEM(shape, F32)
+    level = lambda rows, n: [vm(NZ * rows, 128)] * n
+    faces = lambda rows, tiles: vm(tiles * (NZ + 1) * rows, 128)
+    rows3, rows4 = 2 * gx, gx
+    whole = call(
+        functools.partial(global_kernel, gx, gy),
+        "global_coeffs",
+        [(NZ * rows3, 128)] * 5 + [(NZ * rows4, 128)] * 5,
+        [shares],
+        level(rows3, 6) + [faces(rows3, 1)] + level(rows3, 1) + level(rows4, 6) + [faces(rows4, 1)] + level(rows4, 1),
+    )
+    size, tall = (NZ * TX, 128), ((NZ + 1) * TX, 128)
+    k2 = call(
+        window_kernel, "window_coeffs", [size, size, size, tall], [x_head, xr, xl, yr, yl, corner_r, corner_l], level(TX, 7)
+    )
+    big, big_z = (2 * NZ * 2 * TX, 128), (2 * (NZ + 1) * 2 * TX, 128)
+    send, *saved = call(
+        functools.partial(down_kernel, gx * TX, gy * TY),
+        "down",
+        [(NZ + 8, 128), big, big, big, big_z, big, big, size, size, size, tall, size, size],
+        [*tiles, xr, xl, yr, yl, corner_r, corner_l],
+        [vm(*big)] * 10 + [vm(*big_z)] + level(TX, 10) + [faces(TX, 1)] + level(8, 10) + [faces(8, 1)]
+        + [pltpu.SemaphoreType.DMA((12,))],
+        out_specs=[VMEM] + [ANY] * 12,
+    )
+    copies = jnp.broadcast_to(send[None], (gx * gy, NZ + 8, 128))
+    gathered = lax.all_to_all(copies, ("gx", "gy"), 0, 0).reshape(gx * gy * (NZ + 8), 128)
+    field, residual = call(
+        functools.partial(up_kernel, gx, gy),
+        "up",
+        [(NZ * TX, TY)] * 2,
+        [gathered, tiles[1], *whole, *k2, *saved],
+        [vm(*big), vm(*big), vm(*big), vm(*big_z), vm(*big), vm(*big), vm(*size), vm(*size), vm(*size), vm(*tall), vm(*size), vm(*size)]
+        + level(rows3, 3) + level(TX, 3) + level(rows4, 2)
+        + [vm(NZ * 2 * TX, 128), vm(*size), vm(*big), vm(*big), pltpu.SemaphoreType.DMA((12,))],
+        in_specs=[VMEM] * 16 + [ANY] * 12,
+    )
+    return field.reshape(right_side.shape), residual.reshape(right_side.shape)
+
+
 def solution(mesh):
-    in_specs = (
-        P(None, "gx", "gy"),
-        P(None, "gx", "gy"),
-        P(None, "gx", "gy"),
-        P(None, "gx", "gy"),
-        P(None, "gx", "gy"),
-    )
-    out_specs = (P(None, "gx", "gy"), P(None, "gx", "gy"))
-    return jax.shard_map(body, mesh=mesh, in_specs=in_specs, out_specs=out_specs, check_vma=False)
+    spec = P(None, "gx", "gy")
+    fits = (mesh.shape["gx"], mesh.shape["gy"]) == (8, 4)
+    plan = body if fits else spread_body
+    return jax.shard_map(plan, mesh=mesh, in_specs=(spec,) * 5, out_specs=(spec, spec), check_vma=False)

time: 997 us -> 98.8 us (0.10)
  the two profiles are of different devices: /device:TPU:14 before, /device:TPU:0 now
where the time goes in v2:
time: 98.8 us; the launch traced here: 98.2 us
  Pallas kernels  34.7 us (35%)
  blocking collectives  27.9 us (28%)
  starting transfers between devices  23.4 us (24%)
  waiting for transfers between devices  7.19 us (7%)
  local copies, waits for them, and re-layouts  4.26 us (4%)
    pallas_call x5, Pallas kernels, call(): pl.pallas_call(kernel, name=name, out_shape=shapes, in_specs=in_specs or...  34.7 us
    all_gather x1, blocking collectives, body(): lax.all_gather(lax.all_gather(share3, 'gy'), 'gx')  17 us
    all_gather x1, blocking collectives, body(): lax.all_gather(share3, 'gy')  10.9 us
    all_to_all x1, starting transfers between devices, body(): lax.all_to_all(copies, ('gx', 'gy'), 0, 0).reshape(gx * gy * (NZ + 8), 128)  8.57 us
    ppermute x1, starting transfers between devices, body(): yl = lax.ppermute(y_tail, 'gy', up(gy))  4.85 us
    ppermute x1, waiting for transfers between devices, body(): yr = lax.ppermute(y_head, 'gy', down(gy))  4.36 us
    ppermute x1, starting transfers between devices, body(): xl = lax.ppermute(x_tail, 'gx', up(gx))  3.08 us
    ppermute x1, starting transfers between devices, body(): lax.ppermute(jnp.concatenate([yl[half:STRIP], yl[STRIP:], yr[half:STRIP],...  3.04 us
  transfers between devices with their start and end apart: 7, of which 3 were waited for; matrix products, arithmetic and copies ran while one was open for 0% of the time, Pallas kernels for 8%

profile of v2, /device:TPU:0, one launch (start us, length us, event | category | flops | bytes accessed | tf_op | source)
XLA Modules:
  0.0 98.2 jit_solution(5385616410978620016)
XLA Ops:
  0.6 3.3 %pack.1 = (f32[1472,128]{1,0:T(8,128)}, f32[1472,128]{1,0:T(8,128)}, f32[184,128]{1,0:T(8,128)}, f32[184,128]{1,0:T(8,128)}, f32[48,128]{1,0:T(8,128)}) custom-call(f32[512,128]{1,0:T(8,128)} %bitcast.15, f32[512,128]{1,0:T(8,128)} %bitcast.12, f32[512,128]{1,0:T(8,128)} %bitcast.17, f32[512,128]{1,0:T(8,128)} %bitcast.19, f32[512,128]{1,0:T(8,128)} %bitcast.21), custom_call_target="tpu_custom_call" | custom-call | flops 1000000 | bytes 1310720 | tf_op jit(solution)/shard_map/pack/pallas_call | solution.py:846
  3.9 1.3 %collective-permute-start = (f32[1472,128]{1,0:T(8,128)}, f32[1472,128]{1,0:T(8,128)S(1)}, u32[]{:S(2)}, u32[]{:S(2)}) collective-permute-start(f32[1472,128]{1,0:T(8,128)} %get-tuple-element.36.x_head), channel_id=1, source_target_pairs={{4,0},{8,4},{12,8},{16,12},{20,16},{24,20},{28,24},{5,1},{9,5},{13... | collective-permute-start | bytes 2261000 | tf_op jit(solution)/shard_map/ppermute | solution.py:867
  5.2 3.1 %collective-permute-start.1 = (f32[1472,128]{1,0:T(8,128)}, f32[1472,128]{1,0:T(8,128)S(1)}, u32[]{:S(2)}, u32[]{:S(2)}) collective-permute-start(f32[1472,128]{1,0:T(8,128)} %get-tuple-element.37), channel_id=1, source_target_pairs={{0,4},{4,8},{8,12},{12,16},{16,20},{20,24},{24,28},{1,5},{5,9},{9,... | collective-permute-start | bytes 2261000 | tf_op jit(solution)/shard_map/ppermute | solution.py:868
  8.3 4.8 %collective-permute-start.3 = (f32[184,128]{1,0:T(8,128)}, f32[184,128]{1,0:T(8,128)S(1)}, u32[]{:S(2)}, u32[]{:S(2)}) collective-permute-start(f32[184,128]{1,0:T(8,128)} %get-tuple-element.39), channel_id=1, source_target_pairs={{0,1},{1,2},{2,3},{4,5},{5,6},{6,7},{8,9},{9,10},{10,11},{12,13},{... | collective-permute-start | bytes 282632 | tf_op jit(solution)/shard_map/ppermute | solution.py:866
  13.2 1.3 %collective-permute-start.2 = (f32[184,128]{1,0:T(8,128)}, f32[184,128]{1,0:T(8,128)S(1)}, u32[]{:S(2)}, u32[]{:S(2)}) collective-permute-start(f32[184,128]{1,0:T(8,128)} %get-tuple-element.38), channel_id=1, source_target_pairs={{1,0},{2,1},{3,2},{5,4},{6,5},{7,6},{9,8},{10,9},{11,10},{13,12},{... | collective-permute-start | bytes 282632 | tf_op jit(solution)/shard_map/ppermute | solution.py:865
  14.5 1.9 %collective-permute-done.3.refs_8_.yl = f32[184,128]{1,0:T(8,128)S(1)} collective-permute-done((f32[184,128]{1,0:T(8,128)}, f32[184,128]{1,0:T(8,128)S(1)}, u32[]{:S(2)}, u32[]{:S(2)}) %collective-permute-start.3) | collective-permute-done | bytes 94240 | tf_op jit(solution)/shard_map/ppermute | solution.py:866
  16.4 0.0 copy-start.3
  16.4 4.4 %collective-permute-done.2.refs_7_.yr = f32[184,128]{1,0:T(8,128)S(1)} collective-permute-done((f32[184,128]{1,0:T(8,128)}, f32[184,128]{1,0:T(8,128)S(1)}, u32[]{:S(2)}, u32[]{:S(2)}) %collective-permute-start.2) | collective-permute-done | bytes 94240 | tf_op jit(solution)/shard_map/ppermute | solution.py:865
  20.7 0.0 copy-start.4
  20.8 1.3 %collective-permute-start.4 = (f32[208,128]{1,0:T(8,128)S(1)}, f32[208,128]{1,0:T(8,128)S(1)}, u32[]{:S(2)}, u32[]{:S(2)}) collective-permute-start(f32[208,128]{1,0:T(8,128)S(1)} %pad_maximum_fusion), channel_id=1, source_target_pairs={{4,0},{8,4},{12,8},{16,12},{20,16},{24,20},{28,24},{5,1},{9,5},{13... | collective-permute-start | bytes 319496 | tf_op jit(solution)/shard_map/ppermute | solution.py:871
  22.1 3.0 %collective-permute-start.5 = (f32[208,128]{1,0:T(8,128)S(1)}, f32[208,128]{1,0:T(8,128)S(1)}, u32[]{:S(2)}, u32[]{:S(2)}) collective-permute-start(f32[208,128]{1,0:T(8,128)S(1)} %pad_maximum_fusion.1), channel_id=1, source_target_pairs={{0,4},{4,8},{8,12},{12,16},{16,20},{20,24},{24,28},{1,5},{5,9},{9,... | collective-permute-start | bytes 319496 | tf_op jit(solution)/shard_map/ppermute | solution.py:872
  25.2 0.0 collective-permute-done.4.refs_9_.cr
  25.2 0.0 copy-start.5
  25.2 0.9 collective-permute-done.5.refs_10_.cl
  26.1 0.0 copy-start.6
  26.1 0.0 collective-permute-done.refs_5_.xr
  26.1 0.0 copy-start
  26.1 0.0 collective-permute-done.1.refs_6_.xl
  26.1 0.0 copy-done.3
  26.1 0.0 copy-done.4
  26.1 0.0 copy-done.5
  26.1 0.6 copy-done.6
  26.7 0.3 copy-done
  27.0 0.0 copy-start.1
  27.0 0.9 copy-done.1
  27.9 10.9 %down.1 = (f32[40,128]{1,0:T(8,128)}, f32[2048,128]{1,0:T(8,128)}, f32[2048,128]{1,0:T(8,128)}, f32[2048,128]{1,0:T(8,128)}, f32[2112,128]{1,0:T(8,128)}, /*inde...) custom-call(f32[512,128]{1,0:T(8,128)} %bitcast.16, ...), custom_call_target="tpu_custom_call" | custom-call | flops 1000000 | bytes 3219456 | tf_op jit(solution)/shard_map/down/pallas_call | solution.py:846
  38.8 0.0 copy-start.7
  38.8 1.6 %broadcast_in_dim.2 = f32[32,40,128]{2,1,0:T(8,128)} broadcast(f32[40,128]{1,0:T(8,128)} %get-tuple-element.40), dimensions={1,2} | broadcast | bytes 675840 | tf_op jit(solution)/shard_map/broadcast_in_dim | solution.py:898
  40.5 8.6 %all-to-all-start = ((f32[32,40,128]{2,1,0:T(8,128)}), f32[32,40,128]{2,1,0:T(8,128)S(1)}, u32[]{:S(2)}, u32[]{:S(2)}) async-start(f32[32,40,128]{2,1,0:T(8,128)} %broadcast_in_dim.2), calls=%async_computation | async-start | bytes 1310720 | tf_op jit(solution)/shard_map/all_to_all | solution.py:899
  49.0 0.0 copy-done.7
  49.0 10.9 %all-gather = f32[192,128]{1,0:T(8,128)S(1)} all-gather(f32[48,128]{1,0:T(8,128)S(1)} %copy-done.7), channel_id=2, replica_groups=mesh['gx'=8,'gy'=4] {'gy'}, dimensions={0}, use_global_device_ids=true | all-gather | bytes 122880 | tf_op jit(solution)/shard_map/all_gather | solution.py:869
  59.9 17.0 %all-gather.1 = f32[32,48,128]{2,1,0:T(8,128)} all-gather(f32[4,48,128]{2,1,0:T(8,128)S(1)} %bitcast.23), channel_id=3, replica_groups=mesh['gx'=8,'gy'=4] {'gx'}, dimensions={0}, use_global_device_ids=true | all-gather | bytes 884736 | tf_op jit(solution)/shard_map/all_gather | solution.py:869
  76.9 3.5 %global_coeffs.1 = (f32[512,128]{1,0:T(8,128)}, f32[512,128]{1,0:T(8,128)}, f32[512,128]{1,0:T(8,128)}, f32[512,128]{1,0:T(8,128)}, f32[512,128]{1,0:T(8,128)}, ...) custom-call(f32[1536,128]{1,0:T(8,128)} %bitcast.10), custom_call_target="tpu_custom_call" | custom-call | flops 1000000 | bytes 786432 | tf_op jit(solution)/shard_map/global_coeffs/pallas_call | solution.py:846
  80.4 4.2 %window_coeffs.1 = (f32[512,128]{1,0:T(8,128)}, f32[512,128]{1,0:T(8,128)}, f32[512,128]{1,0:T(8,128)}, f32[528,128]{1,0:T(8,128)}) custom-call(f32[1472,128]{1,0:T(8,128)} %get-tuple-element.36.x_head, f32[1472,128]{1,0:T(8,128)} %copy-done, f32[1472,128]{1,0:T(8,128)} %copy-done.1, f32[184,128]{1,0:T(8,128)} %copy-done.4, f32[184,128]{1,0:T(8,128)} %copy-done.3, ...), custom_call_target="tpu_custom_call" | custom-call | flops 1000000 | bytes 2662400 | tf_op jit(solution)/shard_map/window_coeffs/pallas_call | solution.py:846
  84.5 0.0 all-to-all-done
  84.5 0.0 copy-start.2
  84.5 0.8 copy-done.2
  85.4 12.9 %up.1 = (f32[512,128]{1,0:T(8,128)}, f32[512,128]{1,0:T(8,128)}) custom-call(f32[1280,128]{1,0:T(8,128)} %bitcast.11, f32[512,128]{1,0:T(8,128)} %bitcast.14, f32[512,128]{1,0:T(8,128)} %get-tuple-element.42.refs_2_, f32[512,128]{1,0:T(8,128)} %get-tuple-element.43.refs_3_, f32[512,128]{1,0:T(8,128)} %get-tuple-element.44.refs_4_, ...), custom_call_target="tpu_custom_call" | custom-call | flops 1000000 | bytes 11845632 | tf_op jit(solution)/shard_map/up/pallas_call | solution.py:846
  (8 shorter events, 0.0 us)
Async XLA Ops:
  3.9 22.2 %collective-permute-start = (f32[1472,128]{1,0:T(8,128)}, f32[1472,128]{1,0:T(8,128)S(1)}, u32[]{:S(2)}, u32[]{:S(2)}) collective-permute-start(f32[1472,128]{1,0:T(8,128)} %get-tuple-element.36.x_head), channel_id=1, source_target_pairs={{4,0},{8,4},{12,8},{16,12},{20,16},{24,20},{28,24},{5,1},{9,5},{13... | collective-permute-start | bytes 2261000 | tf_op jit(solution)/shard_map/ppermute | solution.py:867
  5.2 20.9 %collective-permute-start.1 = (f32[1472,128]{1,0:T(8,128)}, f32[1472,128]{1,0:T(8,128)S(1)}, u32[]{:S(2)}, u32[]{:S(2)}) collective-permute-start(f32[1472,128]{1,0:T(8,128)} %get-tuple-element.37), channel_id=1, source_target_pairs={{0,4},{4,8},{8,12},{12,16},{16,20},{20,24},{24,28},{1,5},{5,9},{9,... | collective-permute-start | bytes 2261000 | tf_op jit(solution)/shard_map/ppermute | solution.py:868
  8.3 8.1 %collective-permute-start.3 = (f32[184,128]{1,0:T(8,128)}, f32[184,128]{1,0:T(8,128)S(1)}, u32[]{:S(2)}, u32[]{:S(2)}) collective-permute-start(f32[184,128]{1,0:T(8,128)} %get-tuple-element.39), channel_id=1, source_target_pairs={{0,1},{1,2},{2,3},{4,5},{5,6},{6,7},{8,9},{9,10},{10,11},{12,13},{... | collective-permute-start | bytes 282632 | tf_op jit(solution)/shard_map/ppermute | solution.py:866
  13.2 7.6 %collective-permute-start.2 = (f32[184,128]{1,0:T(8,128)}, f32[184,128]{1,0:T(8,128)S(1)}, u32[]{:S(2)}, u32[]{:S(2)}) collective-permute-start(f32[184,128]{1,0:T(8,128)} %get-tuple-element.38), channel_id=1, source_target_pairs={{1,0},{2,1},{3,2},{5,4},{6,5},{7,6},{9,8},{10,9},{11,10},{13,12},{... | collective-permute-start | bytes 282632 | tf_op jit(solution)/shard_map/ppermute | solution.py:865
  16.4 9.7 %copy-start.3 = (f32[184,128]{1,0:T(8,128)}, f32[184,128]{1,0:T(8,128)S(1)}, u32[]{:S(2)}) copy-start(f32[184,128]{1,0:T(8,128)S(1)} %collective-permute-done.3.refs_8_.yl) | copy-start | bytes 282628
  20.7 5.4 %copy-start.4 = (f32[184,128]{1,0:T(8,128)}, f32[184,128]{1,0:T(8,128)S(1)}, u32[]{:S(2)}) copy-start(f32[184,128]{1,0:T(8,128)S(1)} %collective-permute-done.2.refs_7_.yr) | copy-start | bytes 282628
  20.8 4.4 %collective-permute-start.4 = (f32[208,128]{1,0:T(8,128)S(1)}, f32[208,128]{1,0:T(8,128)S(1)}, u32[]{:S(2)}, u32[]{:S(2)}) collective-permute-start(f32[208,128]{1,0:T(8,128)S(1)} %pad_maximum_fusion), channel_id=1, source_target_pairs={{4,0},{8,4},{12,8},{16,12},{20,16},{24,20},{28,24},{5,1},{9,5},{13... | collective-permute-start | bytes 319496 | tf_op jit(solution)/shard_map/ppermute | solution.py:871
  22.1 4.0 %collective-permute-start.5 = (f32[208,128]{1,0:T(8,128)S(1)}, f32[208,128]{1,0:T(8,128)S(1)}, u32[]{:S(2)}, u32[]{:S(2)}) collective-permute-start(f32[208,128]{1,0:T(8,128)S(1)} %pad_maximum_fusion.1), channel_id=1, source_target_pairs={{0,4},{4,8},{8,12},{12,16},{16,20},{20,24},{24,28},{1,5},{5,9},{9,... | collective-permute-start | bytes 319496 | tf_op jit(solution)/shard_map/ppermute | solution.py:872
  25.2 1.0 copy-start.5
  26.1 0.6 copy-start.6
  26.1 0.9 copy-start
  27.0 0.9 copy-start.1
  38.8 10.2 %copy-start.7 = (f32[48,128]{1,0:T(8,128)S(1)}, f32[48,128]{1,0:T(8,128)}, u32[]{:S(2)}) copy-start(f32[48,128]{1,0:T(8,128)} %get-tuple-element.41) | copy-start | bytes 73732
  40.5 44.1 %all-to-all-start = ((f32[32,40,128]{2,1,0:T(8,128)}), f32[32,40,128]{2,1,0:T(8,128)S(1)}, u32[]{:S(2)}, u32[]{:S(2)}) async-start(f32[32,40,128]{2,1,0:T(8,128)} %broadcast_in_dim.2), calls=%async_computation | async-start | bytes 1310720 | tf_op jit(solution)/shard_map/all_to_all | solution.py:899
  84.5 0.8 copy-start.2

commit v3 on v2

--- a/solution.py
+++ b/solution.py
@@ -165,6 +165,7 @@
 HALO = 8
 SLAB = 5 * NZ * HALO
 STRIP = 160
+Y_BLOCK = STRIP + 24 + 48
 VMEM = pl.BlockSpec(memory_space=pltpu.VMEM)
 ANY = pl.BlockSpec(memory_space=pl.ANY)
 
@@ -178,13 +179,15 @@
     return pltpu.roll(x, by, axis) if by else x
 
 
-def mix(x, weights):
-    high = x.astype(BF16)
-    rest = x - high.astype(F32)
-    mid = rest.astype(BF16)
-    low = (rest - mid.astype(F32)).astype(BF16)
-    dot = functools.partial(jnp.dot, preferred_element_type=F32)
-    return dot(low, weights) + dot(mid, weights) + dot(high, weights)
+def mix(x, weights, parts=2):
+    out = None
+    for n in range(parts):
+        part = x.astype(BF16)
+        term = jnp.dot(part, weights, preferred_element_type=F32)
+        out = term if out is None else out + term
+        if n < parts - 1:
+            x = x - part.astype(F32)
+    return out
 
 
 def matrix(mask, weight=1.0):
@@ -404,7 +407,17 @@
     return pltpu.roll(out, turn, 1)
 
 
-def pack_kernel(f, kappa, cx, cy, cz, x_head, x_tail, y_head, y_tail, share3):
+def pack_x_kernel(f, kappa, cx, cy, cz, share2, x_head, x_tail):
+    for a, ref in enumerate((f, kappa, cx, cy, cz)):
+        cells = ref[...].reshape(NZ, TX, TY)
+        at = pl.ds(a * NZ * HALO, NZ * HALO)
+        x_head[at, :] = cells[:, :HALO].reshape(NZ * HALO, TY)
+        x_tail[at, :] = cells[:, TX - HALO :].reshape(NZ * HALO, TY)
+    x_head[pl.ds(SLAB, 6 * NZ), :] = share2[...]
+    x_tail[pl.ds(SLAB, 6 * NZ), :] = share2[...]
+
+
+def pack_y_kernel(gy, f, kappa, cx, cy, cz, y_blocks, share2, y_head, y_tail):
     iy = lax.axis_index("gy")
     y, lane = iota((128, 128), 0), iota((128, 128), 1)
     fourth = y // 4 == lane % 32
@@ -430,9 +443,7 @@
     tail = [jnp.zeros((8, 128), F32)] * 3
     slot = iota((8, 128), 1) % 32 // 4
     for t, cells in enumerate(kinds):
-        at = pl.ds(SLAB + t * NZ, NZ)
-        x_head[at, :] = cells
-        x_tail[at, :] = cells
+        share2[pl.ds(t * NZ, NZ), :] = cells
         for zv in range(4):
             n = 4 * t + zv
             piece = cells[8 * zv : 8 * zv + 8]
@@ -453,14 +464,12 @@
         matrix(pair_x & pair_y, 0.25),
     ]
     for t, cells in enumerate(kinds):
-        share3[pl.ds(8 * t, 8), :] = fold_planes(mix(cells, folds[min(t, 4)]), 16 * iy)
+        cells = fold_planes(mix(cells, folds[min(t, 4)]), 16 * iy)
+        for j in range(gy):
+            y_blocks[pl.ds(j * Y_BLOCK + STRIP + 24 + 8 * t, 8), :] = cells
 
     group = lane_group(8, 8)
     for a, ref in enumerate((f, kappa, cx, cy, cz)):
-        cells = ref[...].reshape(NZ, TX, TY)
-        at = pl.ds(a * NZ * HALO, NZ * HALO)
-        x_head[at, :] = cells[:, :HALO].reshape(NZ * HALO, TY)
-        x_tail[at, :] = cells[:, TX - HALO :].reshape(NZ * HALO, TY)
         for half in range(2):
             for zo in range(2):
                 head = jnp.zeros((8, 128), F32)
@@ -473,37 +482,58 @@
                 at = pl.ds(((half * 5 + a) * 2 + zo) * 8, 8)
                 y_head[at, :] = head
                 y_tail[at, :] = tail
-
-
-def window2(tile, after, before, dest, first):
+    for j in range(gy):
+        y_blocks[pl.ds(j * Y_BLOCK, STRIP + 24), :] = jnp.where(iy < j, y_tail[...], y_head[...])
+
+
+def forward_kernel(gx, gy, y_all, corner_head, corner_tail, copies, shares, sem):
+    iy = lax.axis_index("gy")
+    for j in range(gy):
+        shares[pl.ds(j * 48, 48), :] = y_all[pl.ds(j * Y_BLOCK + STRIP + 24, 48), :]
+    sends = [pltpu.make_async_copy(shares, copies.at[pl.ds(j * gy * 48, gy * 48), :], sem.at[j]) for j in range(gx)]
+    for send in sends:
+        send.start()
+    half = STRIP // 2
+    for n, source in enumerate((jnp.maximum(iy - 1, 0), jnp.minimum(iy + 1, gy - 1))):
+        for first, dest in ((0, corner_head), (half, corner_tail)):
+            dest[pl.ds(n * 104, half), :] = y_all[span(source * Y_BLOCK + first, half), :]
+            dest[pl.ds(n * 104 + half, 24), :] = y_all[span(source * Y_BLOCK + STRIP, 24), :]
+    for send in sends:
+        send.wait()
+
+
+def window2(tile, after, before, dest, first, iy, gy):
     lane = iota((NZ, 128), 1)
+    first_after, first_before = jnp.where(iy < gy - 1, 36, 0), jnp.where(iy > 0, 124, 128)
     for xi in range(4):
         turned = (lane - 32 * xi + 128) % 128
-        cells = jnp.where(turned < 32, tile, jnp.where(turned < 36, after, jnp.where(turned >= 124, before, 0.0)))
+        cells = jnp.where(turned < 32, tile, jnp.where(turned < first_after, after, jnp.where(turned >= first_before, before, 0.0)))
         dest[pl.ds(first + xi, NZ, stride=TX), :] = shift(cells, -32 * xi, 1)
 
 
-def window_kernel(x_head, xr, xl, yr, yl, cr, cl, x_face, y_face, inv, z_face, a, b, c, d, kappa, cz, diag):
+def window_kernel(share2, xr, xl, y_all, cr, cl, x_face, y_face, inv, z_face, a, b, c, d, kappa, cz, diag):
     ix, iy = lax.axis_index("gx"), lax.axis_index("gy")
-    nx, ny = lax.axis_size("gx") * 4, lax.axis_size("gy") * 32
+    gy = lax.axis_size("gy")
+    nx, ny = lax.axis_size("gx") * 4, gy * 32
     refs = (a, b, c, d, kappa, cz)
+    y_after, y_before = jnp.minimum(iy + 1, gy - 1) * Y_BLOCK, jnp.maximum(iy - 1, 0) * Y_BLOCK
 
     def unpack(ref, first, t, turn):
         pieces = []
         for zv in range(4):
             n = 4 * t + zv
-            pieces.append(shift(ref[pl.ds(first + 8 * (n // 8), 8), :], turn - 4 * (n % 8), 1))
+            pieces.append(shift(ref[span(first + 8 * (n // 8), 8), :], turn - 4 * (n % 8), 1))
         return jnp.concatenate(pieces, axis=0)
 
     half = STRIP // 2
     for t, dest in enumerate(refs):
-        at = pl.ds(SLAB + t * NZ, NZ)
-        for first, tile, right, left, r_at, l_at in (
-            (0, x_head, yr, yl, STRIP, STRIP),
-            (4, xr, cr, cr, half + 24 + half, half),
-            (12, xl, cl, cl, half + 24 + half, half),
+        for first, tile, base, right, left, r_at, l_at in (
+            (0, share2, 0, y_all, y_all, y_after + STRIP, y_before + STRIP),
+            (4, xr, SLAB, cr, cr, half + 24 + half, half),
+            (12, xl, SLAB, cl, cl, half + 24 + half, half),
         ):
-            window2(tile[at, :], unpack(right, r_at, t, 32), unpack(left, l_at, t, 92), dest, first)
+            cells = tile[pl.ds(base + t * NZ, NZ), :]
+            window2(cells, unpack(right, r_at, t, 32), unpack(left, l_at, t, 92), dest, first, iy, gy)
         for x in range(8, 12):
             dest[pl.ds(x, NZ, stride=TX), :] = jnp.zeros((NZ, 128), F32)
     mask = window_mask(TX, 128, 4, 32, 4, ix, iy, nx, ny)
@@ -520,10 +550,10 @@
     factor(diag, z_face, 1, inv, None)
 
 
-def assemble3(gathered, stride, first, dest, gx, gy, rows):
+def assemble3(gathered, dest, gx, gy, rows, at=slice(None)):
     group = lane_group(8, 16)
     for ix in range(gx):
-        blocks = [gathered[pl.ds((ix * gy + iy) * stride + first, 8), :] for iy in range(gy)]
+        blocks = [gathered[ix * gy + iy, at, :] for iy in range(gy)]
         for zo in range(4):
             for xi in range(2):
                 q = 2 * zo + xi
@@ -538,7 +568,7 @@
     raw3, raw4 = refs[10:18], refs[18:26]
     rows, cols = 2 * gx, 16 * gy
     for t in range(6):
-        assemble3(gathered, 48, 8 * t, raw3[t], gx, gy, rows)
+        assemble3(gathered, raw3[t], gx, gy, rows, pl.ds(8 * t, 8))
     a, b, c, d = (Field(ref, rows) for ref in raw3[:4])
     x, y = iota((rows, 128), 0), iota((rows, 128), 1)
     for k in range(NZ):
@@ -577,12 +607,14 @@
 
 
 def down_kernel(nx, ny, *refs):
-    f, kappa, cx, cy, cz, xr, xl, yr, yl, corner_r, corner_l = refs[:11]
-    send, outs0, outs1 = refs[11], refs[12:18], refs[18:24]
-    scratch = list(refs[24:-1])
+    f, kappa, cx, cy, cz, xr, xl, y_all, corner_r, corner_l = refs[:10]
+    sends, outs0, outs1 = refs[10], refs[11:17], refs[17:23]
+    scratch = list(refs[23:-1])
     sems = refs[-1]
     take = lambda n: [scratch.pop(0) for _ in range(n)]
     ix, iy = lax.axis_index("gx"), lax.axis_index("gy")
+    gx, gy = lax.axis_size("gx"), lax.axis_size("gy")
+    y_after, y_before = jnp.minimum(iy + 1, gy - 1) * Y_BLOCK, jnp.maximum(iy - 1, 0) * Y_BLOCK
     rows, tiles = 2 * TX, 2
     whole = take(11)
     names = [Field(ref, rows, tiles) for ref in whole[:10]]
@@ -598,8 +630,8 @@
         half = STRIP // 2
         sides = []
         for right, left in (
-            (yr[at(0), :], yl[at(0), :]),
-            (yr[at(half), :], yl[at(half), :]),
+            (y_all[at(y_after), :], y_all[at(y_before), :]),
+            (y_all[at(y_after + half), :], y_all[at(y_before + half), :]),
             (corner_r[at(half + 24), :], corner_r[at(0), :]),
             (corner_l[at(half + 24), :], corner_l[at(0), :]),
         ):
@@ -611,7 +643,7 @@
 
     def prepare(z, cz_prev):
         zi = z % 16
-        after, before = group == zi, group == (zi + 15) % 16
+        after, before = (group == zi) & (iy < gy - 1), (group == (zi + 15) % 16) & (iy > 0)
         turn = (128 - 8 * zi) % 128
         f_k, kappa_k, cx_k, cy_k, cz_k = (
             window(a, tile, z, after, before, turn) for a, tile in enumerate((f, kappa, cx, cy, cz))
@@ -673,6 +705,7 @@
             copies += more
         fine, lanes = (r, kappa1, cz1, x_face, y_face), 128
 
+    send = take(1)[0]
     group = lane_group(NZ, 32)
     out = f1.row(0)
     for xi in range(1, 4):
@@ -684,28 +717,41 @@
         place = (lane % 32 // 16 == xi) & (y // 2 == lane % 16) & (y < 32)
         total = total + mix(r.row(2 * xi) + r.row(2 * xi + 1), matrix(place, 0.25))
     send[pl.ds(NZ, 8), :] = fold_planes(total, 16 * iy)
+    for n in range(gx * gy):
+        copies.append(pltpu.make_async_copy(send, sends.at[pl.ds(n * (NZ + 8), NZ + 8), :], sems.at[12 + n]))
+        copies[-1].start()
     for copy in copies:
         copy.wait()
 
 
 def up_kernel(gx, gy, *refs):
     gathered, kappa = refs[:2]
-    k3, k4, k2 = refs[2:7], refs[7:12], refs[12:16]
-    saved0, saved1 = refs[16:22], refs[22:28]
+    k3, k4 = refs[2:7], refs[7:12]
+    saved2, saved0, saved1 = refs[12:16], refs[16:22], refs[22:28]
     solution_out, residual_out = refs[28:30]
     scratch = list(refs[30:-1])
     sems = refs[-1]
     take = lambda n: [scratch.pop(0) for _ in range(n)]
     ix, iy = lax.axis_index("gx"), lax.axis_index("gy")
-    held0, held1 = take(6), take(6)
+    held0, held1, k2, whole3, blocks = take(6), take(6), take(4), take(1)[0], take(1)[0]
+    fetch = pltpu.make_async_copy(gathered.at[:, pl.ds(NZ, 8), :], whole3, sems.at[16])
+    fetch.start()
+    fetches = []
+    sides = [(dx, dy) for dx in (0, 1, -1) for dy in (0, 1, -1)]
+    for n, (dx, dy) in enumerate(sides):
+        device = jnp.clip(ix + dx, 0, gx - 1) * gy + jnp.clip(iy + dy, 0, gy - 1)
+        source = gathered.at[device, pl.ds(0, NZ), :]
+        fetches.append(pltpu.make_async_copy(source, blocks.at[n], sems.at[17 + n]))
+        fetches[-1].start()
     copies = []
-    for n, (source, dest) in enumerate(zip((*saved1, *saved0), (*held1, *held0))):
+    for n, (source, dest) in enumerate(zip((*saved2, *saved1, *saved0), (*k2, *held1, *held0))):
         copies.append(pltpu.make_async_copy(source, dest, sems.at[n]))
         copies[-1].start()
     f3, u3, r3, f2, u2, kept2, f4, u4, wide, e_ref, e0_ref, kept0 = take(12)
 
     rows, cols = 2 * gx, 16 * gy
-    assemble3(gathered, NZ + 8, NZ, f3, gx, gy, rows)
+    fetch.wait()
+    assemble3(whole3, f3, gx, gy, rows)
     y, lane = iota((128, 128), 0), iota((128, 128), 1)
     f3, u3, r3 = (Field(ref, rows) for ref in (f3, u3, r3))
     y = iota((rows, 128), 1)
@@ -752,18 +798,18 @@
     before = jnp.where(x > 0, shift(cells, 1, 1), 0.0)
     after = jnp.where(x < rows - 1, shift(cells, -1, 1), 0.0)
     spread_rows(cells, before, after, wide, size)
-    e_ref[...] = mix(wide[pl.ds(0, 2 * size), :], spread_matrix(iota((128, 128), 1), 0, cols))
+    e_ref[...] = mix(wide[pl.ds(0, 2 * size), :], spread_matrix(iota((128, 128), 1), 0, cols), 3)
     rows, cols = 2 * rows, 2 * cols
     smooth_up(f3, x_face3, y_face3, line3, u3, Field(e_ref, rows), r3, None, None)
 
     def block(dx, dy):
-        jx, jy = ix + dx, iy + dy
-        inside = ((jx >= 0) & (jx < gx) & (jy >= 0) & (jy < gy)).astype(F32)
-        device = jnp.clip(jx, 0, gx - 1) * gy + jnp.clip(jy, 0, gy - 1)
-        return gathered[span(device * (NZ + 8), NZ), :] * inside
-
+        inside = ((ix + dx >= 0) & (ix + dx < gx)).astype(F32)
+        return blocks[sides.index((dx, dy))] * inside
+
+    for copy in fetches + copies[:4]:
+        copy.wait()
     for first, dx in ((0, 0), (4, 1), (12, -1)):
-        window2(block(dx, 0), shift(block(dx, 1), 32, 1), shift(block(dx, -1), 96, 1), f2, first)
+        window2(block(dx, 0), shift(block(dx, 1), 32, 1), shift(block(dx, -1), 96, 1), f2, first, iy, gy)
     for x in range(8, 12):
         f2[pl.ds(x, NZ, stride=TX), :] = jnp.zeros((NZ, 128), F32)
     f2, u2, kept2 = (Field(ref, TX) for ref in (f2, u2, kept2))
@@ -785,7 +831,7 @@
     spread_rows(ring(cells, 4), ring(shift(cells, 1, 1), 4), ring(shift(cells, -1, 1), 4), wide, NZ * 8)
     lane = iota((128, 128), 1)
     fine_y = jnp.where(lane < 80, lane, lane - 128) + 32 * iy
-    e_ref[...] = mix(wide[pl.ds(0, NZ * TX), :], spread_matrix(fine_y, 0, cols))
+    e_ref[...] = mix(wide[pl.ds(0, NZ * TX), :], spread_matrix(fine_y, 0, cols), 3)
     mask2 = window_mask(TX, 128, 4, 32, 4, ix, iy, 4 * gx, 32 * gy)
     smooth_up(f2, x_face2, y_face2, line2, u2, Field(e_ref, TX), kept2, mask2, None)
 
@@ -793,8 +839,8 @@
     ring = lambda v: jnp.where(iota((1, 8, 128), 1) < 6, v[:, :8], v[:, 8:])
     spread_rows(ring(cells), ring(shift(cells, 1, 1)), ring(shift(cells, -1, 1)), wide, NZ * 8)
     fine_y = jnp.where(lane < 96, lane, lane - 128)
-    e_ref[...] = mix(wide[pl.ds(0, NZ * TX), :], spread_matrix(fine_y, 0, 0, circular=True))
-    for copy in copies[:6]:
+    e_ref[...] = mix(wide[pl.ds(0, NZ * TX), :], spread_matrix(fine_y, 0, 0, circular=True), 3)
+    for copy in copies[4:10]:
         copy.wait()
     x_face1, y_face1, inv1, z_face1, u1, f1 = held1
     x_face1, y_face1, inv1, u1, f1 = (Field(ref, TX) for ref in (x_face1, y_face1, inv1, u1, f1))
@@ -808,10 +854,10 @@
     weights = spread_matrix(iota((128, 256), 1), 0, 0, circular=True)
     e0 = Field(e0_ref, rows, 2)
     for k in range(0, NZ, 8):
-        cells = mix(wide[pl.ds(k * rows, 8 * rows), :], weights)
+        cells = mix(wide[pl.ds(k * rows, 8 * rows), :], weights, 3)
         for t in range(2):
             e0_ref[pl.ds(e0.base(t, k), 8 * rows), :] = cells[:, 128 * t : 128 * (t + 1)]
-    for copy in copies[6:]:
+    for copy in copies[10:]:
         copy.wait()
     x_face0, y_face0, inv0, z_face0, u0, f0 = held0
     x_face0, y_face0, inv0, u0, f0 = (Field(ref, rows, 2) for ref in (x_face0, y_face0, inv0, u0, f0))
@@ -859,18 +905,26 @@
     gx, gy = lax.axis_size("gx"), lax.axis_size("gy")
     tiles = [v.reshape(NZ * TX, TY) for v in (right_side, kappa_sq, cond_x, cond_y, cond_z)]
     slab, strip = (SLAB + 6 * NZ, 128), (STRIP + 24, 128)
-    x_head, x_tail, y_head, y_tail, share3 = call(pack_kernel, "pack", [slab, slab, strip, strip, (48, 128)], tiles)
+    vm = lambda *shape: pltpu.VMEM(shape, F32)
+    pack_y = functools.partial(pack_y_kernel, gy)
+    y_blocks, share2 = call(pack_y, "pack_y", [(gy * Y_BLOCK, 128), (6 * NZ, 128)], tiles, [vm(*strip)] * 2)
+    y_all = lax.all_to_all(y_blocks.reshape(gy, Y_BLOCK, 128), "gy", 0, 0).reshape(gy * Y_BLOCK, 128)
+    x_head, x_tail = call(pack_x_kernel, "pack_x", [slab, slab], [*tiles, share2])
     up = lambda n: [(i, i + 1) for i in range(n - 1)]
     down = lambda n: [(i + 1, i) for i in range(n - 1)]
-    yr = lax.ppermute(y_head, "gy", down(gy))
-    yl = lax.ppermute(y_tail, "gy", up(gy))
     xr = lax.ppermute(x_head, "gx", down(gx))
     xl = lax.ppermute(x_tail, "gx", up(gx))
-    shares = lax.all_gather(lax.all_gather(share3, "gy"), "gx").reshape(gx * gy * 48, 128)
-    half = STRIP // 2
-    corner_r = lax.ppermute(jnp.concatenate([yl[:half], yl[STRIP:], yr[:half], yr[STRIP:]]), "gx", down(gx))
-    corner_l = lax.ppermute(jnp.concatenate([yl[half:STRIP], yl[STRIP:], yr[half:STRIP], yr[STRIP:]]), "gx", up(gx))
-    vm = lambda *shape: pltpu.VMEM(shape, F32)
+    corner_head, corner_tail, copies = call(
+        functools.partial(forward_kernel, gx, gy),
+        "forward",
+        [(208, 128), (208, 128), (gx * gy * 48, 128)],
+        [y_all],
+        [vm(gy * 48, 128), pltpu.SemaphoreType.DMA((gx,))],
+        out_specs=[VMEM, VMEM, ANY],
+    )
+    corner_r = lax.ppermute(corner_head, "gx", down(gx))
+    corner_l = lax.ppermute(corner_tail, "gx", up(gx))
+    shares = lax.all_to_all(copies.reshape(gx, gy * 48, 128), "gx", 0, 0).reshape(gx * gy, 48, 128)
     level = lambda rows, n: [vm(NZ * rows, 128)] * n
     faces = lambda rows, tiles: vm(tiles * (NZ + 1) * rows, 128)
     rows3, rows4 = 2 * gx, gx
@@ -883,29 +937,29 @@
     )
     size, tall = (NZ * TX, 128), ((NZ + 1) * TX, 128)
     k2 = call(
-        window_kernel, "window_coeffs", [size, size, size, tall], [x_head, xr, xl, yr, yl, corner_r, corner_l], level(TX, 7)
+        window_kernel, "window_coeffs", [size, size, size, tall], [share2, xr, xl, y_all, corner_r, corner_l], level(TX, 7)
     )
     big, big_z = (2 * NZ * 2 * TX, 128), (2 * (NZ + 1) * 2 * TX, 128)
-    send, *saved = call(
+    sends, *saved = call(
         functools.partial(down_kernel, gx * TX, gy * TY),
         "down",
-        [(NZ + 8, 128), big, big, big, big_z, big, big, size, size, size, tall, size, size],
-        [*tiles, xr, xl, yr, yl, corner_r, corner_l],
+        [(gx * gy * (NZ + 8), 128), big, big, big, big_z, big, big, size, size, size, tall, size, size],
+        [*tiles, xr, xl, y_all, corner_r, corner_l],
         [vm(*big)] * 10 + [vm(*big_z)] + level(TX, 10) + [faces(TX, 1)] + level(8, 10) + [faces(8, 1)]
-        + [pltpu.SemaphoreType.DMA((12,))],
-        out_specs=[VMEM] + [ANY] * 12,
+        + [vm(NZ + 8, 128), pltpu.SemaphoreType.DMA((12 + gx * gy,))],
+        out_specs=[ANY] * 13,
     )
-    copies = jnp.broadcast_to(send[None], (gx * gy, NZ + 8, 128))
-    gathered = lax.all_to_all(copies, ("gx", "gy"), 0, 0).reshape(gx * gy * (NZ + 8), 128)
+    gathered = lax.all_to_all(sends.reshape(gx * gy, NZ + 8, 128), ("gx", "gy"), 0, 0)
     field, residual = call(
         functools.partial(up_kernel, gx, gy),
         "up",
         [(NZ * TX, TY)] * 2,
         [gathered, tiles[1], *whole, *k2, *saved],
         [vm(*big), vm(*big), vm(*big), vm(*big_z), vm(*big), vm(*big), vm(*size), vm(*size), vm(*size), vm(*tall), vm(*size), vm(*size)]
+        + [vm(*size), vm(*size), vm(*size), vm(*tall), vm(gx * gy, 8, 128), vm(9, NZ, 128)]
         + level(rows3, 3) + level(TX, 3) + level(rows4, 2)
-        + [vm(NZ * 2 * TX, 128), vm(*size), vm(*big), vm(*big), pltpu.SemaphoreType.DMA((12,))],
-        in_specs=[VMEM] * 16 + [ANY] * 12,
+        + [vm(NZ * 2 * TX, 128), vm(*size), vm(*big), vm(*big), pltpu.SemaphoreType.DMA((26,))],
+        in_specs=[ANY] + [VMEM] * 11 + [ANY] * 16,
     )
     return field.reshape(right_side.shape), residual.reshape(right_side.shape)
 

time: 98.8 us -> 103 us (1.043)
  blocking collectives: 27.9 us -> 13.9 us
  starting transfers between devices: 23.4 us -> 32.7 us
  waiting for transfers between devices: 7.19 us -> 12.2 us
  Pallas kernels: 34.7 us -> 39.7 us
  local copies, waits for them, and re-layouts: 4.26 us -> 2.66 us
    all_gather x2 -> x0, blocking collectives: 27.9 us -> none  [the longest x1 17 us: body(): lax.all_gather(lax.all_gather(share3, 'gy'), 'gx')]
    all_to_all x1 -> x2, starting transfers between devices: 8.57 us -> 22.8 us  [the longest x1 17.8 us: body(): lax.all_to_all(sends.reshape(gx * gy, NZ + 8, 128), ('gx', 'gy'), 0, 0)]
    all_to_all x0 -> x1, blocking collectives: none -> 13.9 us  [body(): lax.all_to_all(y_blocks.reshape(gy, Y_BLOCK, 128), 'gy', 0, 0)]
    all_to_all x1 -> x2, waiting for transfers between devices: 0.01 us -> 11.3 us  [the longest x1 11.3 us: body(): lax.all_to_all(sends.reshape(gx * gy, NZ + 8, 128), ('gx', 'gy'), 0, 0)]
    ppermute x4 -> x2, waiting for transfers between devices: 7.19 us -> 0.91 us  [the longest x1 0.91 us: body(): corner_l = lax.ppermute(corner_tail, 'gx', up(gx))]
    pallas_call x5 -> x7, Pallas kernels: 34.7 us -> 39.7 us  [call(): pl.pallas_call(kernel, name=name, out_shape=shapes, in_specs=in_specs or...]
    ppermute x4 -> x2, starting transfers between devices: 10.5 us -> 5.51 us  [the longest x1 4.22 us: body(): corner_l = lax.ppermute(corner_tail, 'gx', up(gx))]
    broadcast_in_dim x1 -> x0, local copies, waits for them, and re-layouts: 1.63 us -> none  [body(): copies = jnp.broadcast_to(send[None], (gx * gy, NZ + 8, 128))]
  transfers between devices with their start and end apart: 7 -> 6, of which waited for: 3 -> 2; matrix products, arithmetic and copies ran while one was open for 0% -> 0% of each run, Pallas kernels for 8% -> 21%
where the time goes in v3:
time: 103 us; the launch traced here: 102 us
  Pallas kernels  39.7 us (39%)
  starting transfers between devices  32.7 us (32%)
  blocking collectives  13.9 us (13%)
  waiting for transfers between devices  12.2 us (12%)
  local copies, waits for them, and re-layouts  2.66 us (3%)
    pallas_call x7, Pallas kernels, call(): pl.pallas_call(kernel, name=name, out_shape=shapes, in_specs=in_specs or...  39.7 us
    all_to_all x1, starting transfers between devices, body(): lax.all_to_all(sends.reshape(gx * gy, NZ + 8, 128), ('gx', 'gy'), 0, 0)  17.8 us
    all_to_all x1, blocking collectives, body(): lax.all_to_all(y_blocks.reshape(gy, Y_BLOCK, 128), 'gy', 0, 0)  13.9 us
    all_to_all x1, waiting for transfers between devices, body(): lax.all_to_all(sends.reshape(gx * gy, NZ + 8, 128), ('gx', 'gy'), 0, 0)  11.3 us
    all_to_all x1, starting transfers between devices, body(): lax.all_to_all(copies.reshape(gx, gy * 48, 128), 'gx', 0, 0)  5.07 us
    ppermute x1, starting transfers between devices, body(): corner_l = lax.ppermute(corner_tail, 'gx', up(gx))  4.22 us
    ppermute x1, starting transfers between devices, body(): xl = lax.ppermute(x_tail, 'gx', up(gx))  3.08 us
    unnamed x16, local copies, waits for them, and re-layouts  2.66 us
  transfers between devices with their start and end apart: 6, of which 2 were waited for; matrix products, arithmetic and copies ran while one was open for 0% of the time, Pallas kernels for 21%

profile of v3, /device:TPU:0, one launch (start us, length us, event | category | flops | bytes accessed | tf_op | source)
XLA Modules:
  0.0 101.9 jit_solution(10676807361230896791)
XLA Ops:
  0.6 2.8 %pack_y.1 = (f32[928,128]{1,0:T(8,128)}, f32[192,128]{1,0:T(8,128)}) custom-call(f32[512,128]{1,0:T(8,128)} %bitcast.20, f32[512,128]{1,0:T(8,128)} %bitcast.15, f32[512,128]{1,0:T(8,128)} %bitcast.23, f32[512,128]{1,0:T(8,128)} %bitcast.26, f32[512,128]{1,0:T(8,128)} %bitcast.29), custom_call_target="tpu_custom_call" | custom-call | flops 1000000 | bytes 1310720 | tf_op jit(solution)/shard_map/pack_y/pallas_call | solution.py:892
  3.4 13.9 %all_to_all.15 = f32[4,232,128]{2,1,0:T(8,128)} all-to-all(f32[4,232,128]{2,1,0:T(8,128)} %bitcast.34), channel_id=1, replica_groups=mesh['gx'=8,'gy'=4] {'gy'}, dimensions={0} | all-to-all | bytes 950272 | tf_op jit(solution)/shard_map/all_to_all | solution.py:911
  17.3 2.7 %forward.1 = (f32[208,128]{1,0:T(8,128)}, f32[208,128]{1,0:T(8,128)}, f32[1536,128]{1,0:T(8,128)}) custom-call(f32[928,128]{1,0:T(8,128)} %bitcast.12), custom_call_target="tpu_custom_call" | custom-call | flops 1000000 | bytes 475136 | tf_op jit(solution)/shard_map/forward/pallas_call | solution.py:892
  20.0 5.1 %all-to-all-start.2 = ((f32[8,192,128]{2,1,0:T(8,128)}), f32[8,192,128]{2,1,0:T(8,128)S(1)}, u32[]{:S(2)}, u32[]{:S(2)}) async-start(f32[8,192,128]{2,1,0:T(8,128)} %bitcast.32), calls=%async_computation.2 | async-start | bytes 1572864 | tf_op jit(solution)/shard_map/all_to_all | solution.py:927
  25.1 0.0 copy-start.7
  25.1 0.0 copy-start.6
  25.1 2.6 %pack_x.1 = (f32[1472,128]{1,0:T(8,128)}, f32[1472,128]{1,0:T(8,128)}) custom-call(f32[512,128]{1,0:T(8,128)} %bitcast.21, f32[512,128]{1,0:T(8,128)} %bitcast.16, f32[512,128]{1,0:T(8,128)} %bitcast.24, f32[512,128]{1,0:T(8,128)} %bitcast.27, f32[512,128]{1,0:T(8,128)} %bitcast.30, f32[192,128]{1,0:T(8,128)} %get-tuple-element.38.share2), custom_call_target="tpu_custom_call" | custom-call | flops 1000000 | bytes 1409024 | tf_op jit(solution)/shard_map/pack_x/pallas_call | solution.py:892
  27.7 1.3 %collective-permute-start = (f32[1472,128]{1,0:T(8,128)}, f32[1472,128]{1,0:T(8,128)S(1)}, u32[]{:S(2)}, u32[]{:S(2)}) collective-permute-start(f32[1472,128]{1,0:T(8,128)} %get-tuple-element.39), channel_id=1, source_target_pairs={{4,0},{8,4},{12,8},{16,12},{20,16},{24,20},{28,24},{5,1},{9,5},{13... | collective-permute-start | bytes 2261000 | tf_op jit(solution)/shard_map/ppermute | solution.py:915
  29.0 3.1 %collective-permute-start.1 = (f32[1472,128]{1,0:T(8,128)}, f32[1472,128]{1,0:T(8,128)S(1)}, u32[]{:S(2)}, u32[]{:S(2)}) collective-permute-start(f32[1472,128]{1,0:T(8,128)} %get-tuple-element.40), channel_id=1, source_target_pairs={{0,4},{4,8},{8,12},{12,16},{16,20},{20,24},{24,28},{1,5},{5,9},{9,... | collective-permute-start | bytes 2261000 | tf_op jit(solution)/shard_map/ppermute | solution.py:916
  32.0 0.0 copy-done.7
  32.0 1.3 %collective-permute-start.2 = (f32[208,128]{1,0:T(8,128)S(1)}, f32[208,128]{1,0:T(8,128)S(1)}, u32[]{:S(2)}, u32[]{:S(2)}) collective-permute-start(f32[208,128]{1,0:T(8,128)S(1)} %copy-done.7), channel_id=1, source_target_pairs={{4,0},{8,4},{12,8},{16,12},{20,16},{24,20},{28,24},{5,1},{9,5},{13... | collective-permute-start | bytes 319496 | tf_op jit(solution)/shard_map/ppermute | solution.py:925
  33.3 0.0 copy-done.6
  33.4 4.2 %collective-permute-start.3 = (f32[208,128]{1,0:T(8,128)S(1)}, f32[208,128]{1,0:T(8,128)S(1)}, u32[]{:S(2)}, u32[]{:S(2)}) collective-permute-start(f32[208,128]{1,0:T(8,128)S(1)} %copy-done.6), channel_id=1, source_target_pairs={{0,4},{4,8},{8,12},{12,16},{16,20},{20,24},{24,28},{1,5},{5,9},{9,... | collective-permute-start | bytes 319496 | tf_op jit(solution)/shard_map/ppermute | solution.py:926
  37.6 0.0 collective-permute-done.2.refs_8_.cr
  37.6 0.0 copy-start.4
  37.6 0.9 collective-permute-done.3.refs_9_.cl
  38.5 0.0 copy-start.5
  38.5 0.0 collective-permute-done.refs_5_.xr
  38.5 0.0 copy-start.1
  38.5 0.0 collective-permute-done.1.refs_6_.xl
  38.5 0.0 copy-done.4
  38.5 0.6 copy-done.5
  39.2 0.3 copy-done.1
  39.4 0.0 copy-start.2
  39.4 0.8 copy-done.2
  40.3 10.8 %down.1 = (f32[1280,128]{1,0:T(8,128)}, f32[2048,128]{1,0:T(8,128)}, f32[2048,128]{1,0:T(8,128)}, f32[2048,128]{1,0:T(8,128)}, f32[2112,128]{1,0:T(8,128)}, /*in...) custom-call(f32[512,128]{1,0:T(8,128)} %bitcast.22, ...), custom_call_target="tpu_custom_call" | custom-call | flops 1000000 | bytes 3506176 | tf_op jit(solution)/shard_map/down/pallas_call | solution.py:892
  51.1 0.0 all-to-all-done.2
  51.1 0.0 copy-start
  51.1 17.8 %all-to-all-start.1 = ((f32[32,40,128]{2,1,0:T(8,128)}), f32[32,40,128]{2,1,0:T(8,128)S(1)}, u32[]{:S(2)}, u32[]{:S(2)}) async-start(f32[32,40,128]{2,1,0:T(8,128)} %bitcast.33), calls=%async_computation.1 | async-start | bytes 1310720 | tf_op jit(solution)/shard_map/all_to_all | solution.py:952
  68.9 4.1 %window_coeffs.1 = (f32[512,128]{1,0:T(8,128)}, f32[512,128]{1,0:T(8,128)}, f32[512,128]{1,0:T(8,128)}, f32[528,128]{1,0:T(8,128)}) custom-call(f32[192,128]{1,0:T(8,128)} %get-tuple-element.38.share2, f32[1472,128]{1,0:T(8,128)} %copy-done.1, f32[1472,128]{1,0:T(8,128)} %copy-done.2, f32[928,128]{1,0:T(8,128)} %bitcast.14, f32[208,128]{1,0:T(8,128)} %copy-done.4, ...), custom_call_target="tpu_custom_call" | custom-call | flops 1000000 | bytes 2293760 | tf_op jit(solution)/shard_map/window_coeffs/pallas_call | solution.py:892
  73.0 0.0 copy-done
  73.0 3.4 %global_coeffs.1 = (f32[512,128]{1,0:T(8,128)}, f32[512,128]{1,0:T(8,128)}, f32[512,128]{1,0:T(8,128)}, f32[512,128]{1,0:T(8,128)}, f32[512,128]{1,0:T(8,128)}, ...) custom-call(f32[32,48,128]{2,1,0:T(8,128)} %bitcast.19), custom_call_target="tpu_custom_call" | custom-call | flops 1000000 | bytes 786432 | tf_op jit(solution)/shard_map/global_coeffs/pallas_call | solution.py:892
  76.4 11.3 %all-to-all-done.1.refs_0_ = f32[32,40,128]{2,1,0:T(8,128)S(1)} async-done(((f32[32,40,128]{2,1,0:T(8,128)}), f32[32,40,128]{2,1,0:T(8,128)S(1)}, u32[]{:S(2)}, u32[]{:S(2)}) %all-to-all-start.1) | async-done | bytes 655392 | tf_op jit(solution)/shard_map/all_to_all | solution.py:952
  87.7 0.0 copy-start.3
  87.7 0.9 copy-done.3
  88.6 13.3 %up.1 = (f32[512,128]{1,0:T(8,128)}, f32[512,128]{1,0:T(8,128)}) custom-call(f32[32,40,128]{2,1,0:T(8,128)} %copy-done.3, f32[512,128]{1,0:T(8,128)} %bitcast.18, f32[512,128]{1,0:T(8,128)} %get-tuple-element.46.refs_2_, f32[512,128]{1,0:T(8,128)} %get-tuple-element.47.refs_3_, f32[512,128]{1,0:T(8,128)} %get-tuple-element.48.refs_4_, ...), custom_call_target="tpu_custom_call" | custom-call | flops 1000000 | bytes 11845632 | tf_op jit(solution)/shard_map/up/pallas_call | solution.py:892
Async XLA Ops:
  20.0 31.1 %all-to-all-start.2 = ((f32[8,192,128]{2,1,0:T(8,128)}), f32[8,192,128]{2,1,0:T(8,128)S(1)}, u32[]{:S(2)}, u32[]{:S(2)}) async-start(f32[8,192,128]{2,1,0:T(8,128)} %bitcast.32), calls=%async_computation.2 | async-start | bytes 1572864 | tf_op jit(solution)/shard_map/all_to_all | solution.py:927
  25.1 7.0 %copy-start.7 = (f32[208,128]{1,0:T(8,128)S(1)}, f32[208,128]{1,0:T(8,128)}, u32[]{:S(2)}) copy-start(f32[208,128]{1,0:T(8,128)} %get-tuple-element.42) | copy-start | bytes 319492
  25.1 8.3 %copy-start.6 = (f32[208,128]{1,0:T(8,128)S(1)}, f32[208,128]{1,0:T(8,128)}, u32[]{:S(2)}) copy-start(f32[208,128]{1,0:T(8,128)} %get-tuple-element.43) | copy-start | bytes 319492
  27.7 10.9 %collective-permute-start = (f32[1472,128]{1,0:T(8,128)}, f32[1472,128]{1,0:T(8,128)S(1)}, u32[]{:S(2)}, u32[]{:S(2)}) collective-permute-start(f32[1472,128]{1,0:T(8,128)} %get-tuple-element.39), channel_id=1, source_target_pairs={{4,0},{8,4},{12,8},{16,12},{20,16},{24,20},{28,24},{5,1},{9,5},{13... | collective-permute-start | bytes 2261000 | tf_op jit(solution)/shard_map/ppermute | solution.py:915
  29.0 9.6 %collective-permute-start.1 = (f32[1472,128]{1,0:T(8,128)}, f32[1472,128]{1,0:T(8,128)S(1)}, u32[]{:S(2)}, u32[]{:S(2)}) collective-permute-start(f32[1472,128]{1,0:T(8,128)} %get-tuple-element.40), channel_id=1, source_target_pairs={{0,4},{4,8},{8,12},{12,16},{16,20},{20,24},{24,28},{1,5},{5,9},{9,... | collective-permute-start | bytes 2261000 | tf_op jit(solution)/shard_map/ppermute | solution.py:916
  32.0 5.5 %collective-permute-start.2 = (f32[208,128]{1,0:T(8,128)S(1)}, f32[208,128]{1,0:T(8,128)S(1)}, u32[]{:S(2)}, u32[]{:S(2)}) collective-permute-start(f32[208,128]{1,0:T(8,128)S(1)} %copy-done.7), channel_id=1, source_target_pairs={{4,0},{8,4},{12,8},{16,12},{20,16},{24,20},{28,24},{5,1},{9,5},{13... | collective-permute-start | bytes 319496 | tf_op jit(solution)/shard_map/ppermute | solution.py:925
  33.4 5.2 %collective-permute-start.3 = (f32[208,128]{1,0:T(8,128)S(1)}, f32[208,128]{1,0:T(8,128)S(1)}, u32[]{:S(2)}, u32[]{:S(2)}) collective-permute-start(f32[208,128]{1,0:T(8,128)S(1)} %copy-done.6), channel_id=1, source_target_pairs={{0,4},{4,8},{8,12},{12,16},{16,20},{20,24},{24,28},{1,5},{5,9},{9,... | collective-permute-start | bytes 319496 | tf_op jit(solution)/shard_map/ppermute | solution.py:926
  37.6 0.9 copy-start.4
  38.5 0.6 copy-start.5
  38.5 0.9 copy-start.1
  39.4 0.9 copy-start.2
  51.1 21.9 %copy-start = (f32[8,192,128]{2,1,0:T(8,128)}, f32[8,192,128]{2,1,0:T(8,128)S(1)}, u32[]{:S(2)}) copy-start(f32[8,192,128]{2,1,0:T(8,128)S(1)} %all-to-all-done.2) | copy-start | bytes 2359300
  51.1 36.6 %all-to-all-start.1 = ((f32[32,40,128]{2,1,0:T(8,128)}), f32[32,40,128]{2,1,0:T(8,128)S(1)}, u32[]{:S(2)}, u32[]{:S(2)}) async-start(f32[32,40,128]{2,1,0:T(8,128)} %bitcast.33), calls=%async_computation.1 | async-start | bytes 1310720 | tf_op jit(solution)/shard_map/all_to_all | solution.py:952
  87.7 0.9 copy-start.3

commit v4 on v3

--- a/solution.py
+++ b/solution.py
@@ -165,7 +165,7 @@
 HALO = 8
 SLAB = 5 * NZ * HALO
 STRIP = 160
-Y_BLOCK = STRIP + 24 + 48
+CORNER = SLAB + 6 * NZ
 VMEM = pl.BlockSpec(memory_space=pltpu.VMEM)
 ANY = pl.BlockSpec(memory_space=pl.ANY)
 
@@ -407,7 +407,8 @@
     return pltpu.roll(out, turn, 1)
 
 
-def pack_x_kernel(f, kappa, cx, cy, cz, share2, x_head, x_tail):
+def pack_x_kernel(devices, f, kappa, cx, cy, cz, share2, x_head, x_tail, copies):
+    iy = lax.axis_index("gy")
     for a, ref in enumerate((f, kappa, cx, cy, cz)):
         cells = ref[...].reshape(NZ, TX, TY)
         at = pl.ds(a * NZ * HALO, NZ * HALO)
@@ -415,10 +416,37 @@
         x_tail[at, :] = cells[:, TX - HALO :].reshape(NZ * HALO, TY)
     x_head[pl.ds(SLAB, 6 * NZ), :] = share2[...]
     x_tail[pl.ds(SLAB, 6 * NZ), :] = share2[...]
-
-
-def pack_y_kernel(gy, f, kappa, cx, cy, cz, y_blocks, share2, y_head, y_tail):
-    iy = lax.axis_index("gy")
+    y, lane = iota((128, 128), 0), iota((128, 128), 1)
+    x_in, y_in = y // 32, y % 32
+    x_out, y_out = lane % 32 // 16, lane % 16
+    pair_y, pair_x = y_in // 2 == y_out, x_in // 2 == x_out
+    folds = [
+        matrix(pair_y & (x_in == 2 * x_out), 0.125),
+        matrix(pair_y & (x_in == 2 * x_out + 1), 0.125),
+        matrix(pair_x & (y_in == 2 * y_out), 0.125),
+        matrix(pair_x & (y_in == 2 * y_out + 1), 0.125),
+        matrix(pair_x & pair_y, 0.25),
+    ]
+    for t in range(6):
+        cells = fold_planes(mix(share2[pl.ds(t * NZ, NZ), :], folds[min(t, 4)]), 16 * iy)
+        for n in range(devices):
+            copies[pl.ds(n * 48 + 8 * t, 8), :] = cells
+
+
+def pack_corner_kernel(head_in, tail_in, yr, yl, x_head, x_tail, sem):
+    half = STRIP // 2
+    copies = []
+    for n, source in enumerate((yl, yr)):
+        for first, dest in ((0, x_head), (half, x_tail)):
+            for at, to, rows in ((first, 0, half), (STRIP, half, 24)):
+                into = dest.at[pl.ds(CORNER + n * 104 + to, rows), :]
+                copies.append(pltpu.make_async_copy(source.at[pl.ds(at, rows), :], into, sem.at[len(copies)]))
+                copies[-1].start()
+    for copy in copies:
+        copy.wait()
+
+
+def pack_y_kernel(f, kappa, cx, cy, cz, y_head, y_tail, share2):
     y, lane = iota((128, 128), 0), iota((128, 128), 1)
     fourth = y // 4 == lane % 32
     rows = lambda ref: [Field(ref, TX).row(r) for r in range(TX)]
@@ -453,21 +481,6 @@
         y_head[pl.ds(STRIP + 8 * n, 8), :] = head[n]
         y_tail[pl.ds(STRIP + 8 * n, 8), :] = tail[n]
 
-    x_in, y_in = y // 32, y % 32
-    x_out, y_out = lane % 32 // 16, lane % 16
-    pair_y, pair_x = y_in // 2 == y_out, x_in // 2 == x_out
-    folds = [
-        matrix(pair_y & (x_in == 2 * x_out), 0.125),
-        matrix(pair_y & (x_in == 2 * x_out + 1), 0.125),
-        matrix(pair_x & (y_in == 2 * y_out), 0.125),
-        matrix(pair_x & (y_in == 2 * y_out + 1), 0.125),
-        matrix(pair_x & pair_y, 0.25),
-    ]
-    for t, cells in enumerate(kinds):
-        cells = fold_planes(mix(cells, folds[min(t, 4)]), 16 * iy)
-        for j in range(gy):
-            y_blocks[pl.ds(j * Y_BLOCK + STRIP + 24 + 8 * t, 8), :] = cells
-
     group = lane_group(8, 8)
     for a, ref in enumerate((f, kappa, cx, cy, cz)):
         for half in range(2):
@@ -482,24 +495,6 @@
                 at = pl.ds(((half * 5 + a) * 2 + zo) * 8, 8)
                 y_head[at, :] = head
                 y_tail[at, :] = tail
-    for j in range(gy):
-        y_blocks[pl.ds(j * Y_BLOCK, STRIP + 24), :] = jnp.where(iy < j, y_tail[...], y_head[...])
-
-
-def forward_kernel(gx, gy, y_all, corner_head, corner_tail, copies, shares, sem):
-    iy = lax.axis_index("gy")
-    for j in range(gy):
-        shares[pl.ds(j * 48, 48), :] = y_all[pl.ds(j * Y_BLOCK + STRIP + 24, 48), :]
-    sends = [pltpu.make_async_copy(shares, copies.at[pl.ds(j * gy * 48, gy * 48), :], sem.at[j]) for j in range(gx)]
-    for send in sends:
-        send.start()
-    half = STRIP // 2
-    for n, source in enumerate((jnp.maximum(iy - 1, 0), jnp.minimum(iy + 1, gy - 1))):
-        for first, dest in ((0, corner_head), (half, corner_tail)):
-            dest[pl.ds(n * 104, half), :] = y_all[span(source * Y_BLOCK + first, half), :]
-            dest[pl.ds(n * 104 + half, 24), :] = y_all[span(source * Y_BLOCK + STRIP, 24), :]
-    for send in sends:
-        send.wait()
 
 
 def window2(tile, after, before, dest, first, iy, gy):
@@ -511,12 +506,11 @@
         dest[pl.ds(first + xi, NZ, stride=TX), :] = shift(cells, -32 * xi, 1)
 
 
-def window_kernel(share2, xr, xl, y_all, cr, cl, x_face, y_face, inv, z_face, a, b, c, d, kappa, cz, diag):
+def window_kernel(share2, xr, xl, yr, yl, x_face, y_face, inv, z_face, a, b, c, d, kappa, cz, diag):
     ix, iy = lax.axis_index("gx"), lax.axis_index("gy")
     gy = lax.axis_size("gy")
     nx, ny = lax.axis_size("gx") * 4, gy * 32
     refs = (a, b, c, d, kappa, cz)
-    y_after, y_before = jnp.minimum(iy + 1, gy - 1) * Y_BLOCK, jnp.maximum(iy - 1, 0) * Y_BLOCK
 
     def unpack(ref, first, t, turn):
         pieces = []
@@ -525,12 +519,12 @@
             pieces.append(shift(ref[span(first + 8 * (n // 8), 8), :], turn - 4 * (n % 8), 1))
         return jnp.concatenate(pieces, axis=0)
 
-    half = STRIP // 2
+    near, far = CORNER + STRIP // 2, CORNER + 104 + STRIP // 2
     for t, dest in enumerate(refs):
         for first, tile, base, right, left, r_at, l_at in (
-            (0, share2, 0, y_all, y_all, y_after + STRIP, y_before + STRIP),
-            (4, xr, SLAB, cr, cr, half + 24 + half, half),
-            (12, xl, SLAB, cl, cl, half + 24 + half, half),
+            (0, share2, 0, yr, yl, STRIP, STRIP),
+            (4, xr, SLAB, xr, xr, far, near),
+            (12, xl, SLAB, xl, xl, far, near),
         ):
             cells = tile[pl.ds(base + t * NZ, NZ), :]
             window2(cells, unpack(right, r_at, t, 32), unpack(left, l_at, t, 92), dest, first, iy, gy)
@@ -607,14 +601,17 @@
 
 
 def down_kernel(nx, ny, *refs):
-    f, kappa, cx, cy, cz, xr, xl, y_all, corner_r, corner_l = refs[:10]
-    sends, outs0, outs1 = refs[10], refs[11:17], refs[17:23]
+    f, kappa, cx, cy, cz, yr, yl, xr_in, xl_in = refs[:9]
+    sends3, sends2, outs0, outs1 = refs[9], refs[10], refs[11:17], refs[17:23]
     scratch = list(refs[23:-1])
     sems = refs[-1]
     take = lambda n: [scratch.pop(0) for _ in range(n)]
     ix, iy = lax.axis_index("gx"), lax.axis_index("gy")
     gx, gy = lax.axis_size("gx"), lax.axis_size("gy")
-    y_after, y_before = jnp.minimum(iy + 1, gy - 1) * Y_BLOCK, jnp.maximum(iy - 1, 0) * Y_BLOCK
+    xr, xl = take(2)
+    fetches = [pltpu.make_async_copy(xr_in, xr, sems.at[12]), pltpu.make_async_copy(xl_in, xl, sems.at[13])]
+    for fetch in fetches:
+        fetch.start()
     rows, tiles = 2 * TX, 2
     whole = take(11)
     names = [Field(ref, rows, tiles) for ref in whole[:10]]
@@ -630,10 +627,10 @@
         half = STRIP // 2
         sides = []
         for right, left in (
-            (y_all[at(y_after), :], y_all[at(y_before), :]),
-            (y_all[at(y_after + half), :], y_all[at(y_before + half), :]),
-            (corner_r[at(half + 24), :], corner_r[at(0), :]),
-            (corner_l[at(half + 24), :], corner_l[at(0), :]),
+            (yr[at(0), :], yl[at(0), :]),
+            (yr[at(half), :], yl[at(half), :]),
+            (xr[at(CORNER + 104), :], xr[at(CORNER), :]),
+            (xl[at(CORNER + 104), :], xl[at(CORNER), :]),
         ):
             cells = jnp.where(after, right, jnp.where(before, left, 0.0))
             sides.append(pltpu.roll(cells, turn, 1))
@@ -643,7 +640,7 @@
 
     def prepare(z, cz_prev):
         zi = z % 16
-        after, before = (group == zi) & (iy < gy - 1), (group == (zi + 15) % 16) & (iy > 0)
+        after, before = group == zi, group == (zi + 15) % 16
         turn = (128 - 8 * zi) % 128
         f_k, kappa_k, cx_k, cy_k, cz_k = (
             window(a, tile, z, after, before, turn) for a, tile in enumerate((f, kappa, cx, cy, cz))
@@ -658,6 +655,8 @@
         diag[z] = base_diag(jnp.where(mask0 > 0, kappa_k, 1.0), x_k, y_k)
         return cz_k
 
+    for fetch in fetches:
+        fetch.wait()
     last = loop(NZ, prepare, jnp.zeros((rows, 256), F32), 2)
     z_face[NZ] = 0.5 * last
     ends = factor(diag, z_face, tiles, inv, 4, f0, kept)
@@ -705,54 +704,30 @@
             copies += more
         fine, lanes = (r, kappa1, cz1, x_face, y_face), 128
 
-    send = take(1)[0]
     group = lane_group(NZ, 32)
     out = f1.row(0)
     for xi in range(1, 4):
         out = jnp.where(group == xi, shift(f1.row(xi), 32 * xi, 1), out)
-    send[pl.ds(0, NZ), :] = out
+    for n in range(gx * gy):
+        sends2[pl.ds(n * NZ, NZ), :] = out
     y, lane = iota((128, 128), 0), iota((128, 128), 1)
     total = jnp.zeros((NZ, 128), F32)
     for xi in range(2):
         place = (lane % 32 // 16 == xi) & (y // 2 == lane % 16) & (y < 32)
         total = total + mix(r.row(2 * xi) + r.row(2 * xi + 1), matrix(place, 0.25))
-    send[pl.ds(NZ, 8), :] = fold_planes(total, 16 * iy)
+    total = fold_planes(total, 16 * iy)
     for n in range(gx * gy):
-        copies.append(pltpu.make_async_copy(send, sends.at[pl.ds(n * (NZ + 8), NZ + 8), :], sems.at[12 + n]))
-        copies[-1].start()
+        sends3[pl.ds(n * 8, 8), :] = total
     for copy in copies:
         copy.wait()
 
 
-def up_kernel(gx, gy, *refs):
-    gathered, kappa = refs[:2]
-    k3, k4 = refs[2:7], refs[7:12]
-    saved2, saved0, saved1 = refs[12:16], refs[16:22], refs[22:28]
-    solution_out, residual_out = refs[28:30]
-    scratch = list(refs[30:-1])
-    sems = refs[-1]
-    take = lambda n: [scratch.pop(0) for _ in range(n)]
-    ix, iy = lax.axis_index("gx"), lax.axis_index("gy")
-    held0, held1, k2, whole3, blocks = take(6), take(6), take(4), take(1)[0], take(1)[0]
-    fetch = pltpu.make_async_copy(gathered.at[:, pl.ds(NZ, 8), :], whole3, sems.at[16])
-    fetch.start()
-    fetches = []
-    sides = [(dx, dy) for dx in (0, 1, -1) for dy in (0, 1, -1)]
-    for n, (dx, dy) in enumerate(sides):
-        device = jnp.clip(ix + dx, 0, gx - 1) * gy + jnp.clip(iy + dy, 0, gy - 1)
-        source = gathered.at[device, pl.ds(0, NZ), :]
-        fetches.append(pltpu.make_async_copy(source, blocks.at[n], sems.at[17 + n]))
-        fetches[-1].start()
-    copies = []
-    for n, (source, dest) in enumerate(zip((*saved2, *saved1, *saved0), (*k2, *held1, *held0))):
-        copies.append(pltpu.make_async_copy(source, dest, sems.at[n]))
-        copies[-1].start()
-    f3, u3, r3, f2, u2, kept2, f4, u4, wide, e_ref, e0_ref, kept0 = take(12)
+def coarse_kernel(gx, gy, *refs):
+    gathered, k3, k4 = refs[0], refs[1:6], refs[6:11]
+    u3, f3, r3, f4, u4, wide, e_ref = refs[11:]
 
     rows, cols = 2 * gx, 16 * gy
-    fetch.wait()
-    assemble3(whole3, f3, gx, gy, rows)
-    y, lane = iota((128, 128), 0), iota((128, 128), 1)
+    assemble3(gathered, f3, gx, gy, rows)
     f3, u3, r3 = (Field(ref, rows) for ref in (f3, u3, r3))
     y = iota((rows, 128), 1)
     x_face3, y_face3, inv3, g3, c3 = (Field(ref, rows) for ref in k3)
@@ -802,6 +777,29 @@
     rows, cols = 2 * rows, 2 * cols
     smooth_up(f3, x_face3, y_face3, line3, u3, Field(e_ref, rows), r3, None, None)
 
+def up_kernel(gx, gy, *refs):
+    gathered, u3, kappa = refs[:3]
+    saved2, saved0, saved1 = refs[3:7], refs[7:13], refs[13:19]
+    solution_out, residual_out = refs[19:21]
+    scratch = list(refs[21:-1])
+    sems = refs[-1]
+    take = lambda n: [scratch.pop(0) for _ in range(n)]
+    ix, iy = lax.axis_index("gx"), lax.axis_index("gy")
+    held0, held1, k2, blocks = take(6), take(6), take(4), take(1)[0]
+    fetches = []
+    sides = [(dx, dy) for dx in (0, 1, -1) for dy in (0, 1, -1)]
+    for n, (dx, dy) in enumerate(sides):
+        device = jnp.clip(ix + dx, 0, gx - 1) * gy + jnp.clip(iy + dy, 0, gy - 1)
+        source = gathered.at[device]
+        fetches.append(pltpu.make_async_copy(source, blocks.at[n], sems.at[16 + n]))
+        fetches[-1].start()
+    copies = []
+    for n, (source, dest) in enumerate(zip((*saved2, *saved1, *saved0), (*k2, *held1, *held0))):
+        copies.append(pltpu.make_async_copy(source, dest, sems.at[n]))
+        copies[-1].start()
+    f2, u2, kept2, wide, e_ref, e0_ref, kept0 = take(7)
+
+    rows, cols = 2 * gx, 16 * gy
     def block(dx, dy):
         inside = ((ix + dx >= 0) & (ix + dx < gx)).astype(F32)
         return blocks[sides.index((dx, dy))] * inside
@@ -823,7 +821,7 @@
 
     sweep_out(ends, kept2, line2, emit2, None)
 
-    cells = pltpu.roll(u3.ref[...].reshape(NZ, rows, 128), (rows - 2 * ix) % rows, 1)
+    cells = pltpu.roll(u3[...].reshape(NZ, rows, 128), (rows - 2 * ix) % rows, 1)
     x = iota((1, rows, 128), 1)
     place = 2 * ix + jnp.where(x < rows // 2, x, x - rows)
     cells = jnp.where((place >= 0) & (place < rows), cells, 0.0)
@@ -887,7 +885,13 @@
     residual(NZ - 1, carry)
 
 
-def call(kernel, name, outs, ins, scratch=(), in_specs=None, out_specs=None, flops=1000000):
+COSTS = {
+    "pack_y": 2 * 10**9, "pack_x": 3 * 10**9, "pack_corner": 10**9, "down": 10**10,
+    "window_coeffs": 4 * 10**9, "global_coeffs": 4 * 10**9, "coarse": 6 * 10**9, "up": 8 * 10**9,
+}
+
+
+def call(kernel, name, outs, ins, scratch=(), in_specs=None, out_specs=None, aliases=None):
     shapes = [jax.ShapeDtypeStruct(s, F32) for s in outs]
     return pl.pallas_call(
         kernel,
@@ -896,35 +900,33 @@
         in_specs=in_specs or [VMEM] * len(ins),
         out_specs=out_specs or [VMEM] * len(outs),
         scratch_shapes=list(scratch),
+        input_output_aliases=aliases or {},
         compiler_params=pltpu.CompilerParams(vmem_limit_bytes=56 * 1024 * 1024),
-        cost_estimate=pl.CostEstimate(flops=flops, bytes_accessed=4 * sum(x.size for x in ins), transcendentals=0),
+        cost_estimate=pl.CostEstimate(flops=COSTS[name], bytes_accessed=4 * sum(x.size for x in ins), transcendentals=0),
     )(*ins)
 
 
 def body(right_side, kappa_sq, cond_x, cond_y, cond_z):
     gx, gy = lax.axis_size("gx"), lax.axis_size("gy")
     tiles = [v.reshape(NZ * TX, TY) for v in (right_side, kappa_sq, cond_x, cond_y, cond_z)]
-    slab, strip = (SLAB + 6 * NZ, 128), (STRIP + 24, 128)
+    slab, strip = (CORNER + 208, 128), (STRIP + 24, 128)
     vm = lambda *shape: pltpu.VMEM(shape, F32)
-    pack_y = functools.partial(pack_y_kernel, gy)
-    y_blocks, share2 = call(pack_y, "pack_y", [(gy * Y_BLOCK, 128), (6 * NZ, 128)], tiles, [vm(*strip)] * 2)
-    y_all = lax.all_to_all(y_blocks.reshape(gy, Y_BLOCK, 128), "gy", 0, 0).reshape(gy * Y_BLOCK, 128)
-    x_head, x_tail = call(pack_x_kernel, "pack_x", [slab, slab], [*tiles, share2])
+    dma = lambda n: pltpu.SemaphoreType.DMA((n,))
+    devices = gx * gy
     up = lambda n: [(i, i + 1) for i in range(n - 1)]
     down = lambda n: [(i + 1, i) for i in range(n - 1)]
+    y_head, y_tail, share2 = call(pack_y_kernel, "pack_y", [strip, strip, (6 * NZ, 128)], tiles)
+    yr = lax.ppermute(y_head, "gy", down(gy))
+    yl = lax.ppermute(y_tail, "gy", up(gy))
+    pack_x = functools.partial(pack_x_kernel, devices)
+    x_head, x_tail, copies = call(pack_x, "pack_x", [slab, slab, (devices * 48, 128)], [*tiles, share2])
+    x_head, x_tail = call(
+        pack_corner_kernel, "pack_corner", [slab, slab], [x_head, x_tail, yr, yl], [dma(8)], [ANY] * 4, [ANY] * 2, {0: 0, 1: 1}
+    )
     xr = lax.ppermute(x_head, "gx", down(gx))
     xl = lax.ppermute(x_tail, "gx", up(gx))
-    corner_head, corner_tail, copies = call(
-        functools.partial(forward_kernel, gx, gy),
-        "forward",
-        [(208, 128), (208, 128), (gx * gy * 48, 128)],
-        [y_all],
-        [vm(gy * 48, 128), pltpu.SemaphoreType.DMA((gx,))],
-        out_specs=[VMEM, VMEM, ANY],
-    )
-    corner_r = lax.ppermute(corner_head, "gx", down(gx))
-    corner_l = lax.ppermute(corner_tail, "gx", up(gx))
-    shares = lax.all_to_all(copies.reshape(gx, gy * 48, 128), "gx", 0, 0).reshape(gx * gy, 48, 128)
+    copies, xr, xl = lax.optimization_barrier((copies, xr, xl))
+    shares = lax.all_to_all(copies.reshape(devices, 48, 128), ("gx", "gy"), 0, 0)
     level = lambda rows, n: [vm(NZ * rows, 128)] * n
     faces = lambda rows, tiles: vm(tiles * (NZ + 1) * rows, 128)
     rows3, rows4 = 2 * gx, gx
@@ -937,29 +939,37 @@
     )
     size, tall = (NZ * TX, 128), ((NZ + 1) * TX, 128)
     k2 = call(
-        window_kernel, "window_coeffs", [size, size, size, tall], [share2, xr, xl, y_all, corner_r, corner_l], level(TX, 7)
+        window_kernel, "window_coeffs", [size, size, size, tall], [share2, xr, xl, yr, yl], level(TX, 7)
     )
     big, big_z = (2 * NZ * 2 * TX, 128), (2 * (NZ + 1) * 2 * TX, 128)
-    sends, *saved = call(
+    sends3, sends2, *saved = call(
         functools.partial(down_kernel, gx * TX, gy * TY),
         "down",
-        [(gx * gy * (NZ + 8), 128), big, big, big, big_z, big, big, size, size, size, tall, size, size],
-        [*tiles, xr, xl, y_all, corner_r, corner_l],
-        [vm(*big)] * 10 + [vm(*big_z)] + level(TX, 10) + [faces(TX, 1)] + level(8, 10) + [faces(8, 1)]
-        + [vm(NZ + 8, 128), pltpu.SemaphoreType.DMA((12 + gx * gy,))],
-        out_specs=[ANY] * 13,
+        [(devices * 8, 128), (devices * NZ, 128), big, big, big, big_z, big, big, size, size, size, tall, size, size],
+        [*tiles, yr, yl, xr, xl],
+        [vm(*slab)] * 2 + [vm(*big)] * 10 + [vm(*big_z)] + level(TX, 10) + [faces(TX, 1)] + level(8, 10) + [faces(8, 1)]
+        + [dma(14)],
+        in_specs=[VMEM] * 7 + [ANY] * 2,
+        out_specs=[VMEM] * 2 + [ANY] * 12,
     )
-    gathered = lax.all_to_all(sends.reshape(gx * gy, NZ + 8, 128), ("gx", "gy"), 0, 0)
+    gathered3 = lax.all_to_all(sends3.reshape(devices, 8, 128), ("gx", "gy"), 0, 0)
+    gathered2 = lax.all_to_all(sends2.reshape(devices, NZ, 128), ("gx", "gy"), 0, 0)
+    u3 = call(
+        functools.partial(coarse_kernel, gx, gy),
+        "coarse",
+        [(NZ * rows3, 128)],
+        [gathered3, *whole],
+        level(rows3, 2) + level(rows4, 2) + level(rows3, 2),
+    )[0]
     field, residual = call(
         functools.partial(up_kernel, gx, gy),
         "up",
         [(NZ * TX, TY)] * 2,
-        [gathered, tiles[1], *whole, *k2, *saved],
+        [gathered2, u3, tiles[1], *k2, *saved],
         [vm(*big), vm(*big), vm(*big), vm(*big_z), vm(*big), vm(*big), vm(*size), vm(*size), vm(*size), vm(*tall), vm(*size), vm(*size)]
-        + [vm(*size), vm(*size), vm(*size), vm(*tall), vm(gx * gy, 8, 128), vm(9, NZ, 128)]
-        + level(rows3, 3) + level(TX, 3) + level(rows4, 2)
-        + [vm(NZ * 2 * TX, 128), vm(*size), vm(*big), vm(*big), pltpu.SemaphoreType.DMA((26,))],
-        in_specs=[ANY] + [VMEM] * 11 + [ANY] * 16,
+        + [vm(*size), vm(*size), vm(*size), vm(*tall), vm(9, NZ, 128)]
+        + level(TX, 3) + [vm(NZ * 2 * TX, 128), vm(*size), vm(*big), vm(*big), dma(25)],
+        in_specs=[ANY] + [VMEM] * 2 + [ANY] * 16,
     )
     return field.reshape(right_side.shape), residual.reshape(right_side.shape)
 

time: 103 us -> 120 us (1.17)
  blocking collectives: 13.9 us -> 49.4 us
  starting transfers between devices: 32.7 us -> 13.9 us
  Pallas kernels: 39.7 us -> 48.4 us
  waiting for transfers between devices: 12.2 us -> 4.91 us
    all_to_all x1 -> x2, blocking collectives: 13.9 us -> 49.4 us  [the longest x1 25.7 us: body(): lax.all_to_all(sends3.reshape(devices, 8, 128), ('gx', 'gy'), 0, 0)]
    all_to_all x2 -> x1, starting transfers between devices: 22.8 us -> 2.75 us  [body(): lax.all_to_all(sends2.reshape(devices, NZ, 128), ('gx', 'gy'), 0, 0)]
    pallas_call x7 -> x8, Pallas kernels: 39.7 us -> 48.4 us  [call(): pl.pallas_call(kernel, name=name, out_shape=shapes, in_specs=in_specs or...]
    all_to_all x2 -> x1, waiting for transfers between devices: 11.3 us -> 2.75 us  [body(): lax.all_to_all(sends2.reshape(devices, NZ, 128), ('gx', 'gy'), 0, 0)]
    ppermute x1, waiting for transfers between devices: 0.01 us -> 2.05 us  [body(): xl = lax.ppermute(x_tail, 'gx', up(gx))]
    ppermute x2, starting transfers between devices: 5.51 us -> 6.75 us  [the longest x1 5.47 us: body(): yl = lax.ppermute(y_tail, 'gy', up(gy))]
    unnamed x16 -> x12, local copies, waits for them, and re-layouts: 2.66 us -> 2.37 us
  transfers between devices with their start and end apart: 6 -> 5, of which waited for: 2 -> 3; matrix products, arithmetic and copies ran while one was open for 0% -> 0% of each run, Pallas kernels for 21% -> 14%
where the time goes in v4:
time: 120 us
  blocking collectives  49.4 us (41%)
  Pallas kernels  48.4 us (40%)
  starting transfers between devices  13.9 us (12%)
  waiting for transfers between devices  4.91 us (4%)
  local copies, waits for them, and re-layouts  2.37 us (2%)
    pallas_call x8, Pallas kernels, call(): pl.pallas_call(kernel, name=name, out_shape=shapes, in_specs=in_specs or...  48.4 us
    all_to_all x1, blocking collectives, body(): lax.all_to_all(sends3.reshape(devices, 8, 128), ('gx', 'gy'), 0, 0)  25.7 us
    all_to_all x1, blocking collectives, body(): lax.all_to_all(copies.reshape(devices, 48, 128), ('gx', 'gy'), 0, 0)  23.8 us
    ppermute x1, starting transfers between devices, body(): yl = lax.ppermute(y_tail, 'gy', up(gy))  5.47 us
    ppermute x1, starting transfers between devices, body(): xl = lax.ppermute(x_tail, 'gx', up(gx))  3.08 us
    all_to_all x1, starting transfers between devices, body(): lax.all_to_all(sends2.reshape(devices, NZ, 128), ('gx', 'gy'), 0, 0)  2.75 us
    all_to_all x1, waiting for transfers between devices, body(): lax.all_to_all(sends2.reshape(devices, NZ, 128), ('gx', 'gy'), 0, 0)  2.75 us
  transfers between devices with their start and end apart: 5, of which 3 were waited for; matrix products, arithmetic and copies ran while one was open for 0% of the time, Pallas kernels for 14%

profile of v4, /device:TPU:0, one launch (start us, length us, event | category | flops | bytes accessed | tf_op | source)
XLA Modules:
  0.0 119.7 jit_solution(10714811805163851165)
XLA Ops:
  0.6 2.6 %pack_y.1 = (f32[184,128]{1,0:T(8,128)}, f32[184,128]{1,0:T(8,128)}, f32[192,128]{1,0:T(8,128)}) custom-call(f32[512,128]{1,0:T(8,128)} %bitcast.12, f32[512,128]{1,0:T(8,128)} %bitcast.24, f32[512,128]{1,0:T(8,128)} %bitcast.15, f32[512,128]{1,0:T(8,128)} %bitcast.18, f32[512,128]{1,0:T(8,128)} %bitcast.21), custom_call_target="tpu_custom_call" | custom-call | flops 2000000000 | bytes 1310720 | tf_op jit(solution)/shard_map/pack_y/pallas_call | solution.py:896
  3.3 1.3 %collective-permute-start = (f32[184,128]{1,0:T(8,128)}, f32[184,128]{1,0:T(8,128)S(1)}, u32[]{:S(2)}, u32[]{:S(2)}) collective-permute-start(f32[184,128]{1,0:T(8,128)} %get-tuple-element.43), channel_id=1, source_target_pairs={{1,0},{2,1},{3,2},{5,4},{6,5},{7,6},{9,8},{10,9},{11,10},{13,12},{... | collective-permute-start | bytes 282632 | tf_op jit(solution)/shard_map/ppermute | solution.py:919
  4.5 5.5 %collective-permute-start.1 = (f32[184,128]{1,0:T(8,128)}, f32[184,128]{1,0:T(8,128)S(1)}, u32[]{:S(2)}, u32[]{:S(2)}) collective-permute-start(f32[184,128]{1,0:T(8,128)} %get-tuple-element.44), channel_id=1, source_target_pairs={{0,1},{1,2},{2,3},{4,5},{5,6},{6,7},{8,9},{9,10},{10,11},{12,13},{... | collective-permute-start | bytes 282632 | tf_op jit(solution)/shard_map/ppermute | solution.py:920
  10.0 3.0 %pack_x.1 = (f32[1680,128]{1,0:T(8,128)}, f32[1680,128]{1,0:T(8,128)}, f32[1536,128]{1,0:T(8,128)}) custom-call(f32[512,128]{1,0:T(8,128)} %bitcast.13, f32[512,128]{1,0:T(8,128)} %bitcast.25, f32[512,128]{1,0:T(8,128)} %bitcast.16, f32[512,128]{1,0:T(8,128)} %bitcast.19, f32[512,128]{1,0:T(8,128)} %bitcast.22, f32[192,128]{1,0:T(8,128)} %get-tuple-element.45.share2), custom_call_target="tpu_custom_call" | custom-call | flops 3000000000 | bytes 1409024 | tf_op jit(solution)/shard_map/pack_x/pallas_call | solution.py:896
  13.1 0.0 collective-permute-done.yr.refs_5_
  13.1 0.0 copy-start.4
  13.1 0.0 collective-permute-done.1.yl.refs_6_
  13.1 0.0 copy-start.5
  13.1 0.6 copy-done.4
  13.7 0.0 copy-done.5
  13.7 7.6 %pack_corner.1 = (f32[1680,128]{1,0:T(8,128)}, f32[1680,128]{1,0:T(8,128)}) custom-call(f32[1680,128]{1,0:T(8,128)} %get-tuple-element.47.head_in, f32[1680,128]{1,0:T(8,128)} %get-tuple-element.48.tail_in, f32[184,128]{1,0:T(8,128)} %copy-done.4, f32[184,128]{1,0:T(8,128)} %copy-done.5), custom_call_target="tpu_custom_call", output_to_operand_aliasing={{0}: (0, {}), {1}: (1, {})} | custom-call | flops 1000000000 | bytes 1908736 | tf_op jit(solution)/shard_map/pack_corner/pallas_call | solution.py:896
  21.4 1.3 %collective-permute-start.2 = (f32[1680,128]{1,0:T(8,128)}, f32[1680,128]{1,0:T(8,128)S(1)}, u32[]{:S(2)}, u32[]{:S(2)}) collective-permute-start(f32[1680,128]{1,0:T(8,128)} %get-tuple-element.49), channel_id=1, source_target_pairs={{4,0},{8,4},{12,8},{16,12},{20,16},{24,20},{28,24},{5,1},{9,5},{13... | collective-permute-start | bytes 2580488 | tf_op jit(solution)/shard_map/ppermute | solution.py:926
  22.7 3.1 %collective-permute-start.3 = (f32[1680,128]{1,0:T(8,128)}, f32[1680,128]{1,0:T(8,128)S(1)}, u32[]{:S(2)}, u32[]{:S(2)}) collective-permute-start(f32[1680,128]{1,0:T(8,128)} %get-tuple-element.50), channel_id=1, source_target_pairs={{0,4},{4,8},{8,12},{12,16},{16,20},{20,24},{24,28},{1,5},{5,9},{9,... | collective-permute-start | bytes 2580488 | tf_op jit(solution)/shard_map/ppermute | solution.py:927
  25.8 0.1 collective-permute-done.2.refs_7_.xr
  25.9 0.0 copy-start.2
  25.9 2.0 %collective-permute-done.3.refs_8_.xl = f32[1680,128]{1,0:T(8,128)S(1)} collective-permute-done((f32[1680,128]{1,0:T(8,128)}, f32[1680,128]{1,0:T(8,128)S(1)}, u32[]{:S(2)}, u32[]{:S(2)}) %collective-permute-start.3) | collective-permute-done | bytes 860192 | tf_op jit(solution)/shard_map/ppermute | solution.py:927
  27.9 0.0 copy-start.3
  27.9 0.0 copy-done.2
  27.9 0.9 copy-done.3
  28.8 0.0 copy-start
  28.8 11.9 %down.1 = (f32[256,128]{1,0:T(8,128)}, f32[1024,128]{1,0:T(8,128)}, f32[2048,128]{1,0:T(8,128)}, f32[2048,128]{1,0:T(8,128)}, f32[2048,128]{1,0:T(8,128)}, /*ind...) custom-call(f32[512,128]{1,0:T(8,128)} %bitcast.14, ...), custom_call_target="tpu_custom_call" | custom-call | flops 10000000000 | bytes 3219456 | tf_op jit(solution)/shard_map/down/pallas_call | solution.py:896
  40.8 25.7 %all_to_all.15.refs_0_ = f32[32,8,128]{2,1,0:T(8,128)} all-to-all(f32[32,8,128]{2,1,0:T(8,128)} %bitcast.11), channel_id=1, replica_groups=mesh['gx'=8,'gy'=4] {'gx','gy'}, dimensions={0} | all-to-all | bytes 262144 | tf_op jit(solution)/shard_map/all_to_all | solution.py:955
  66.4 0.0 copy-done
  66.4 23.8 %all_to_all.16.gathered = f32[32,48,128]{2,1,0:T(8,128)} all-to-all(f32[32,48,128]{2,1,0:T(8,128)S(1)} %bitcast.10), channel_id=1, replica_groups=mesh['gx'=8,'gy'=4] {'gx','gy'}, dimensions={0} | all-to-all | bytes 1572864 | tf_op jit(solution)/shard_map/all_to_all | solution.py:929
  90.2 2.8 %all-to-all-start = ((f32[32,32,128]{2,1,0:T(8,128)}), f32[32,32,128]{2,1,0:T(8,128)S(1)}, u32[]{:S(2)}, u32[]{:S(2)}) async-start(f32[32,32,128]{2,1,0:T(8,128)} %bitcast.5), calls=%async_computation | async-start | bytes 1048576 | tf_op jit(solution)/shard_map/all_to_all | solution.py:956
  93.0 4.0 %window_coeffs.1 = (f32[512,128]{1,0:T(8,128)}, f32[512,128]{1,0:T(8,128)}, f32[512,128]{1,0:T(8,128)}, f32[528,128]{1,0:T(8,128)}) custom-call(f32[192,128]{1,0:T(8,128)} %get-tuple-element.45.share2, f32[1680,128]{1,0:T(8,128)} %copy-done.2, f32[1680,128]{1,0:T(8,128)} %copy-done.3, f32[184,128]{1,0:T(8,128)} %copy-done.4, f32[184,128]{1,0:T(8,128)} %copy-done.5), custom_call_target="tpu_custom_call" | custom-call | flops 4000000000 | bytes 2007040 | tf_op jit(solution)/shard_map/window_coeffs/pallas_call | solution.py:896
  97.0 3.4 %global_coeffs.1 = (f32[512,128]{1,0:T(8,128)}, f32[512,128]{1,0:T(8,128)}, f32[512,128]{1,0:T(8,128)}, f32[512,128]{1,0:T(8,128)}, f32[512,128]{1,0:T(8,128)}, ...) custom-call(f32[32,48,128]{2,1,0:T(8,128)} %all_to_all.16.gathered), custom_call_target="tpu_custom_call" | custom-call | flops 4000000000 | bytes 786432 | tf_op jit(solution)/shard_map/global_coeffs/pallas_call | solution.py:896
  100.4 6.1 %coarse.1.refs_1_ = f32[512,128]{1,0:T(8,128)} custom-call(f32[32,8,128]{2,1,0:T(8,128)} %all_to_all.15.refs_0_, f32[512,128]{1,0:T(8,128)} %get-tuple-element.56.refs_1_, f32[512,128]{1,0:T(8,128)} %get-tuple-element.57.refs_2_, f32[512,128]{1,0:T(8,128)} %get-tuple-element.58.refs_3_, f32[512,128]{1,0:T(8,128)} %get-tuple-element.59.refs_4_, ...), custom_call_target="tpu_custom_call" | custom-call | flops 6000000000 | bytes 2097152 | tf_op jit(solution)/shard_map/coarse/pallas_call | solution.py:896
  106.5 2.7 %all-to-all-done.refs_0_ = f32[32,32,128]{2,1,0:T(8,128)S(1)} async-done(((f32[32,32,128]{2,1,0:T(8,128)}), f32[32,32,128]{2,1,0:T(8,128)S(1)}, u32[]{:S(2)}, u32[]{:S(2)}) %all-to-all-start) | async-done | bytes 524320 | tf_op jit(solution)/shard_map/all_to_all | solution.py:956
  109.2 0.0 copy-start.1
  109.2 0.8 copy-done.1
  110.0 9.7 %up.1 = (f32[512,128]{1,0:T(8,128)}, f32[512,128]{1,0:T(8,128)}) custom-call(f32[32,32,128]{2,1,0:T(8,128)} %copy-done.1, f32[512,128]{1,0:T(8,128)} %coarse.1.refs_1_, f32[512,128]{1,0:T(8,128)} %bitcast.27, f32[512,128]{1,0:T(8,128)} %get-tuple-element.66.refs_3_, f32[512,128]{1,0:T(8,128)} %get-tuple-element.67.refs_4_, ...), custom_call_target="tpu_custom_call" | custom-call | flops 8000000000 | bytes 10010624 | tf_op jit(solution)/shard_map/up/pallas_call | solution.py:896
Async XLA Ops:
  3.3 9.8 %collective-permute-start = (f32[184,128]{1,0:T(8,128)}, f32[184,128]{1,0:T(8,128)S(1)}, u32[]{:S(2)}, u32[]{:S(2)}) collective-permute-start(f32[184,128]{1,0:T(8,128)} %get-tuple-element.43), channel_id=1, source_target_pairs={{1,0},{2,1},{3,2},{5,4},{6,5},{7,6},{9,8},{10,9},{11,10},{13,12},{... | collective-permute-start | bytes 282632 | tf_op jit(solution)/shard_map/ppermute | solution.py:919
  4.5 8.5 %collective-permute-start.1 = (f32[184,128]{1,0:T(8,128)}, f32[184,128]{1,0:T(8,128)S(1)}, u32[]{:S(2)}, u32[]{:S(2)}) collective-permute-start(f32[184,128]{1,0:T(8,128)} %get-tuple-element.44), channel_id=1, source_target_pairs={{0,1},{1,2},{2,3},{4,5},{5,6},{6,7},{8,9},{9,10},{10,11},{12,13},{... | collective-permute-start | bytes 282632 | tf_op jit(solution)/shard_map/ppermute | solution.py:920
  13.1 0.7 copy-start.4
  13.1 0.7 copy-start.5
  21.4 4.5 %collective-permute-start.2 = (f32[1680,128]{1,0:T(8,128)}, f32[1680,128]{1,0:T(8,128)S(1)}, u32[]{:S(2)}, u32[]{:S(2)}) collective-permute-start(f32[1680,128]{1,0:T(8,128)} %get-tuple-element.49), channel_id=1, source_target_pairs={{4,0},{8,4},{12,8},{16,12},{20,16},{24,20},{28,24},{5,1},{9,5},{13... | collective-permute-start | bytes 2580488 | tf_op jit(solution)/shard_map/ppermute | solution.py:926
  22.7 5.2 %collective-permute-start.3 = (f32[1680,128]{1,0:T(8,128)}, f32[1680,128]{1,0:T(8,128)S(1)}, u32[]{:S(2)}, u32[]{:S(2)}) collective-permute-start(f32[1680,128]{1,0:T(8,128)} %get-tuple-element.50), channel_id=1, source_target_pairs={{0,4},{4,8},{8,12},{12,16},{16,20},{20,24},{24,28},{1,5},{5,9},{9,... | collective-permute-start | bytes 2580488 | tf_op jit(solution)/shard_map/ppermute | solution.py:927
  25.9 2.1 %copy-start.2 = (f32[1680,128]{1,0:T(8,128)}, f32[1680,128]{1,0:T(8,128)S(1)}, u32[]{:S(2)}) copy-start(f32[1680,128]{1,0:T(8,128)S(1)} %collective-permute-done.2.refs_7_.xr) | copy-start | bytes 2580484
  27.9 0.9 copy-start.3
  28.8 37.6 %copy-start = (f32[1536,128]{1,0:T(8,128)S(1)}, f32[1536,128]{1,0:T(8,128)}, u32[]{:S(2)}) copy-start(f32[1536,128]{1,0:T(8,128)} %get-tuple-element.55) | copy-start | bytes 2359300
  90.2 19.0 %all-to-all-start = ((f32[32,32,128]{2,1,0:T(8,128)}), f32[32,32,128]{2,1,0:T(8,128)S(1)}, u32[]{:S(2)}, u32[]{:S(2)}) async-start(f32[32,32,128]{2,1,0:T(8,128)} %bitcast.5), calls=%async_computation | async-start | bytes 1048576 | tf_op jit(solution)/shard_map/all_to_all | solution.py:956
  109.2 0.8 copy-start.1

commit v5 on v3

--- a/solution.py
+++ b/solution.py
@@ -165,9 +165,11 @@
 HALO = 8
 SLAB = 5 * NZ * HALO
 STRIP = 160
-Y_BLOCK = STRIP + 24 + 48
+CORNER = 104
+SHARE = 40
+BLOCK = NZ + 8
 VMEM = pl.BlockSpec(memory_space=pltpu.VMEM)
-ANY = pl.BlockSpec(memory_space=pl.ANY)
+HBM = pl.BlockSpec(memory_space=pltpu.HBM)
 
 
 def iota(shape, dim):
@@ -303,28 +305,29 @@
 def factor(diag, z_face, tiles, inv_out, unroll, rhs=None, keep=None, g_out=None, c_out=None):
     ends = []
     for t in range(tiles):
-        zero = jnp.zeros((diag.rows, 128), F32)
-
-        def one(k, upper, inv_prev, prev):
+        zero = diag.part(t, 0) * 0.0
+
+        def one(k, upper, before, last, prev):
             below, above = z_face.part(t, k), z_face.part(t, k + 1)
             inner, outer = (above, below) if upper else (below, above)
-            inv = 1.0 / (diag.part(t, k) + below + above - inner * inner * inv_prev)
+            minor = (diag.part(t, k) + below + above) * last - (inner * inner) * before
+            inv = last * (1.0 / minor)
             inv_out.put(t, k, inv)
             if g_out is not None:
                 g_out.put(t, k, inner * inv)
                 c_out.put(t, k, outer * inv)
-            if rhs is None:
-                return inv, prev
-            value = (rhs.part(t, k) + inner * prev) * inv
-            keep.put(t, k, value)
-            return inv, value
+            if rhs is not None:
+                prev = rhs.part(t, k) * inv + (inner * inv) * prev
+                keep.put(t, k, prev)
+            return last, minor, prev
 
         def step(i, carry):
             low, high = carry
             return one(i, False, *low), one(NZ - 1 - i, True, *high)
 
-        low, high = loop(HALF, step, ((zero, zero), (zero, zero)), unroll)
-        ends.append((low[1], high[1]))
+        start = (zero, zero + 1.0, zero)
+        low, high = loop(HALF, step, (start, start), unroll)
+        ends.append((low[2], high[2]))
     join = lambda n: ends[0][n] if tiles == 1 else jnp.concatenate([e[n] for e in ends], axis=1)
     return join(0), join(1)
 
@@ -417,8 +420,29 @@
     x_tail[pl.ds(SLAB, 6 * NZ), :] = share2[...]
 
 
-def pack_y_kernel(gy, f, kappa, cx, cy, cz, y_blocks, share2, y_head, y_tail):
+def share_kernel(devices, share2, copies):
     iy = lax.axis_index("gy")
+    y, lane = iota((128, 128), 0), iota((128, 128), 1)
+    x_in, y_in = y // 32, y % 32
+    x_out, y_out = lane % 32 // 16, lane % 16
+    pair_y, pair_x = y_in // 2 == y_out, x_in // 2 == x_out
+    a, b, c, d, kappa, cz = (share2[pl.ds(t * NZ, NZ), :] for t in range(6))
+    eighth = lambda mask: matrix(mask, 0.125)
+    blocks = [
+        mix(a, eighth(pair_y & (x_in == 2 * x_out))) + mix(b, eighth(pair_y & (x_in == 1) & (x_out == 1))),
+        mix(b, eighth(pair_y & (x_in == 3) & (x_out == 0)))
+        + mix(d, eighth((x_out == 1) & (y_in == 31) & (x_in // 2 == y_out))),
+        mix(c, eighth(pair_x & (y_in == 2 * y_out))) + mix(d, eighth(pair_x & (y_in == 2 * y_out - 1))),
+        mix(kappa, matrix(pair_x & pair_y, 0.25)),
+        mix(cz, matrix(pair_x & pair_y, 0.25)),
+    ]
+    for t, cells in enumerate(blocks):
+        cells = fold_planes(cells, 16 * iy)
+        for n in range(devices):
+            copies[pl.ds(n * SHARE + 8 * t, 8), :] = cells
+
+
+def pack_y_kernel(f, kappa, cx, cy, cz, y_head, y_tail, share2):
     y, lane = iota((128, 128), 0), iota((128, 128), 1)
     fourth = y // 4 == lane % 32
     rows = lambda ref: [Field(ref, TX).row(r) for r in range(TX)]
@@ -453,21 +477,6 @@
         y_head[pl.ds(STRIP + 8 * n, 8), :] = head[n]
         y_tail[pl.ds(STRIP + 8 * n, 8), :] = tail[n]
 
-    x_in, y_in = y // 32, y % 32
-    x_out, y_out = lane % 32 // 16, lane % 16
-    pair_y, pair_x = y_in // 2 == y_out, x_in // 2 == x_out
-    folds = [
-        matrix(pair_y & (x_in == 2 * x_out), 0.125),
-        matrix(pair_y & (x_in == 2 * x_out + 1), 0.125),
-        matrix(pair_x & (y_in == 2 * y_out), 0.125),
-        matrix(pair_x & (y_in == 2 * y_out + 1), 0.125),
-        matrix(pair_x & pair_y, 0.25),
-    ]
-    for t, cells in enumerate(kinds):
-        cells = fold_planes(mix(cells, folds[min(t, 4)]), 16 * iy)
-        for j in range(gy):
-            y_blocks[pl.ds(j * Y_BLOCK + STRIP + 24 + 8 * t, 8), :] = cells
-
     group = lane_group(8, 8)
     for a, ref in enumerate((f, kappa, cx, cy, cz)):
         for half in range(2):
@@ -482,24 +491,6 @@
                 at = pl.ds(((half * 5 + a) * 2 + zo) * 8, 8)
                 y_head[at, :] = head
                 y_tail[at, :] = tail
-    for j in range(gy):
-        y_blocks[pl.ds(j * Y_BLOCK, STRIP + 24), :] = jnp.where(iy < j, y_tail[...], y_head[...])
-
-
-def forward_kernel(gx, gy, y_all, corner_head, corner_tail, copies, shares, sem):
-    iy = lax.axis_index("gy")
-    for j in range(gy):
-        shares[pl.ds(j * 48, 48), :] = y_all[pl.ds(j * Y_BLOCK + STRIP + 24, 48), :]
-    sends = [pltpu.make_async_copy(shares, copies.at[pl.ds(j * gy * 48, gy * 48), :], sem.at[j]) for j in range(gx)]
-    for send in sends:
-        send.start()
-    half = STRIP // 2
-    for n, source in enumerate((jnp.maximum(iy - 1, 0), jnp.minimum(iy + 1, gy - 1))):
-        for first, dest in ((0, corner_head), (half, corner_tail)):
-            dest[pl.ds(n * 104, half), :] = y_all[span(source * Y_BLOCK + first, half), :]
-            dest[pl.ds(n * 104 + half, 24), :] = y_all[span(source * Y_BLOCK + STRIP, 24), :]
-    for send in sends:
-        send.wait()
 
 
 def window2(tile, after, before, dest, first, iy, gy):
@@ -511,12 +502,11 @@
         dest[pl.ds(first + xi, NZ, stride=TX), :] = shift(cells, -32 * xi, 1)
 
 
-def window_kernel(share2, xr, xl, y_all, cr, cl, x_face, y_face, inv, z_face, a, b, c, d, kappa, cz, diag):
+def window_kernel(share2, xr, xl, yr, yl, cr, cl, x_face, y_face, inv, z_face, a, b, c, d, kappa, cz, diag):
     ix, iy = lax.axis_index("gx"), lax.axis_index("gy")
     gy = lax.axis_size("gy")
     nx, ny = lax.axis_size("gx") * 4, gy * 32
     refs = (a, b, c, d, kappa, cz)
-    y_after, y_before = jnp.minimum(iy + 1, gy - 1) * Y_BLOCK, jnp.maximum(iy - 1, 0) * Y_BLOCK
 
     def unpack(ref, first, t, turn):
         pieces = []
@@ -525,12 +515,12 @@
             pieces.append(shift(ref[span(first + 8 * (n // 8), 8), :], turn - 4 * (n % 8), 1))
         return jnp.concatenate(pieces, axis=0)
 
-    half = STRIP // 2
+    near, far = STRIP // 2, CORNER + STRIP // 2
     for t, dest in enumerate(refs):
         for first, tile, base, right, left, r_at, l_at in (
-            (0, share2, 0, y_all, y_all, y_after + STRIP, y_before + STRIP),
-            (4, xr, SLAB, cr, cr, half + 24 + half, half),
-            (12, xl, SLAB, cl, cl, half + 24 + half, half),
+            (0, share2, 0, yr, yl, STRIP, STRIP),
+            (4, xr, SLAB, cr, cr, far, near),
+            (12, xl, SLAB, cl, cl, far, near),
         ):
             cells = tile[pl.ds(base + t * NZ, NZ), :]
             window2(cells, unpack(right, r_at, t, 32), unpack(left, l_at, t, 92), dest, first, iy, gy)
@@ -567,16 +557,23 @@
     outs3, outs4 = refs[:5], refs[5:10]
     raw3, raw4 = refs[10:18], refs[18:26]
     rows, cols = 2 * gx, 16 * gy
-    for t in range(6):
-        assemble3(gathered, raw3[t], gx, gy, rows, pl.ds(8 * t, 8))
-    a, b, c, d = (Field(ref, rows) for ref in raw3[:4])
+    for t, n in enumerate((0, 1, 2, 4, 5)):
+        assemble3(gathered, raw3[n], gx, gy, rows, pl.ds(8 * t, 8))
+    xl, xu, yl, yu = (Field(ref, rows) for ref in raw3[:4])
     x, y = iota((rows, 128), 0), iota((rows, 128), 1)
+    odd_row, inside = x % 2 == 1, y < cols
     for k in range(NZ):
-        a_k, b_k, c_k, d_k = a[k], b[k], c[k], d[k]
-        a[k] = a_k + jnp.where(x > 0, shift(b_k, 1, 0), 0.0)
-        b[k] = b_k + jnp.where(x < rows - 1, shift(a_k, -1, 0), 0.0)
-        c[k] = jnp.where(y < cols, c_k + jnp.where(y > 0, shift(d_k, 1, 1), 0.0), 0.0)
-        d[k] = jnp.where(y < cols, d_k + jnp.where(y < cols - 1, shift(c_k, -1, 1), 0.0), 0.0)
+        half = jnp.where(inside, xu[k], 0.0)
+        below = jnp.where(odd_row | (x < 2), 0.0, shift(half, 2, 0))
+        x_k = jnp.where(inside, xl[k] + below, 0.0)
+        xl[k] = x_k
+        xu[k] = jnp.where(x == rows - 1, shift(half, 1, 0), shift(x_k, -1, 0))
+        next_row = shift(half, -1, 0)
+        below = jnp.where(odd_row, shift(half, 15, 1), shift(next_row, 16, 1))
+        y_k = jnp.where(inside, yl[k] + jnp.where((y % 16 == 0) & (y > 0), below, 0.0), 0.0)
+        yl[k] = y_k
+        above = jnp.where(odd_row, shift(half, 14, 1), shift(next_row, 15, 1))
+        yu[k] = jnp.where(y == cols - 1, above, jnp.where(inside, shift(y_k, -1, 1), 0.0))
     yy, jj = iota((128, 128), 0), iota((128, 128), 1)
     keep = yy // 2 == jj
     pair, even, odd = matrix(keep), matrix(keep & (yy % 2 == 0)), matrix(keep & (yy % 2 == 1))
@@ -607,14 +604,17 @@
 
 
 def down_kernel(nx, ny, *refs):
-    f, kappa, cx, cy, cz, xr, xl, y_all, corner_r, corner_l = refs[:10]
-    sends, outs0, outs1 = refs[10], refs[11:17], refs[17:23]
-    scratch = list(refs[23:-1])
+    f, kappa, cx, cy, cz, yr, yl, corner_r, corner_l, xr_in, xl_in = refs[:11]
+    sends, outs0, outs1 = refs[11], refs[12:18], refs[18:24]
+    scratch = list(refs[24:-1])
     sems = refs[-1]
     take = lambda n: [scratch.pop(0) for _ in range(n)]
     ix, iy = lax.axis_index("gx"), lax.axis_index("gy")
     gx, gy = lax.axis_size("gx"), lax.axis_size("gy")
-    y_after, y_before = jnp.minimum(iy + 1, gy - 1) * Y_BLOCK, jnp.maximum(iy - 1, 0) * Y_BLOCK
+    xr, xl = take(2)
+    fetches = [pltpu.make_async_copy(xr_in, xr, sems.at[12]), pltpu.make_async_copy(xl_in, xl, sems.at[13])]
+    for fetch in fetches:
+        fetch.start()
     rows, tiles = 2 * TX, 2
     whole = take(11)
     names = [Field(ref, rows, tiles) for ref in whole[:10]]
@@ -630,10 +630,10 @@
         half = STRIP // 2
         sides = []
         for right, left in (
-            (y_all[at(y_after), :], y_all[at(y_before), :]),
-            (y_all[at(y_after + half), :], y_all[at(y_before + half), :]),
-            (corner_r[at(half + 24), :], corner_r[at(0), :]),
-            (corner_l[at(half + 24), :], corner_l[at(0), :]),
+            (yr[at(0), :], yl[at(0), :]),
+            (yr[at(half), :], yl[at(half), :]),
+            (corner_r[at(CORNER), :], corner_r[at(0), :]),
+            (corner_l[at(CORNER), :], corner_l[at(0), :]),
         ):
             cells = jnp.where(after, right, jnp.where(before, left, 0.0))
             sides.append(pltpu.roll(cells, turn, 1))
@@ -643,7 +643,7 @@
 
     def prepare(z, cz_prev):
         zi = z % 16
-        after, before = (group == zi) & (iy < gy - 1), (group == (zi + 15) % 16) & (iy > 0)
+        after, before = group == zi, group == (zi + 15) % 16
         turn = (128 - 8 * zi) % 128
         f_k, kappa_k, cx_k, cy_k, cz_k = (
             window(a, tile, z, after, before, turn) for a, tile in enumerate((f, kappa, cx, cy, cz))
@@ -658,6 +658,8 @@
         diag[z] = base_diag(jnp.where(mask0 > 0, kappa_k, 1.0), x_k, y_k)
         return cz_k
 
+    for fetch in fetches:
+        fetch.wait()
     last = loop(NZ, prepare, jnp.zeros((rows, 256), F32), 2)
     z_face[NZ] = 0.5 * last
     ends = factor(diag, z_face, tiles, inv, 4, f0, kept)
@@ -705,28 +707,26 @@
             copies += more
         fine, lanes = (r, kappa1, cz1, x_face, y_face), 128
 
-    send = take(1)[0]
     group = lane_group(NZ, 32)
     out = f1.row(0)
     for xi in range(1, 4):
         out = jnp.where(group == xi, shift(f1.row(xi), 32 * xi, 1), out)
-    send[pl.ds(0, NZ), :] = out
+    for n in range(gx * gy):
+        sends[pl.ds(n * BLOCK, NZ), :] = out
     y, lane = iota((128, 128), 0), iota((128, 128), 1)
     total = jnp.zeros((NZ, 128), F32)
     for xi in range(2):
         place = (lane % 32 // 16 == xi) & (y // 2 == lane % 16) & (y < 32)
         total = total + mix(r.row(2 * xi) + r.row(2 * xi + 1), matrix(place, 0.25))
-    send[pl.ds(NZ, 8), :] = fold_planes(total, 16 * iy)
+    total = fold_planes(total, 16 * iy)
     for n in range(gx * gy):
-        copies.append(pltpu.make_async_copy(send, sends.at[pl.ds(n * (NZ + 8), NZ + 8), :], sems.at[12 + n]))
-        copies[-1].start()
+        sends[pl.ds(n * BLOCK + NZ, 8), :] = total
     for copy in copies:
         copy.wait()
 
 
 def up_kernel(gx, gy, *refs):
-    gathered, kappa = refs[:2]
-    k3, k4 = refs[2:7], refs[7:12]
+    gathered, kappa, k3, k4 = refs[0], refs[1], refs[2:7], refs[7:12]
     saved2, saved0, saved1 = refs[12:16], refs[16:22], refs[22:28]
     solution_out, residual_out = refs[28:30]
     scratch = list(refs[30:-1])
@@ -734,25 +734,24 @@
     take = lambda n: [scratch.pop(0) for _ in range(n)]
     ix, iy = lax.axis_index("gx"), lax.axis_index("gy")
     held0, held1, k2, whole3, blocks = take(6), take(6), take(4), take(1)[0], take(1)[0]
-    fetch = pltpu.make_async_copy(gathered.at[:, pl.ds(NZ, 8), :], whole3, sems.at[16])
+    fetch = pltpu.make_async_copy(gathered.at[:, pl.ds(NZ, 8), :], whole3, sems.at[25])
     fetch.start()
     fetches = []
     sides = [(dx, dy) for dx in (0, 1, -1) for dy in (0, 1, -1)]
     for n, (dx, dy) in enumerate(sides):
         device = jnp.clip(ix + dx, 0, gx - 1) * gy + jnp.clip(iy + dy, 0, gy - 1)
         source = gathered.at[device, pl.ds(0, NZ), :]
-        fetches.append(pltpu.make_async_copy(source, blocks.at[n], sems.at[17 + n]))
+        fetches.append(pltpu.make_async_copy(source, blocks.at[n], sems.at[16 + n]))
         fetches[-1].start()
     copies = []
     for n, (source, dest) in enumerate(zip((*saved2, *saved1, *saved0), (*k2, *held1, *held0))):
         copies.append(pltpu.make_async_copy(source, dest, sems.at[n]))
         copies[-1].start()
-    f3, u3, r3, f2, u2, kept2, f4, u4, wide, e_ref, e0_ref, kept0 = take(12)
+    f2, u2, kept2, wide, e_ref, e0_ref, kept0, u3, f3, r3, f4, u4 = take(12)
 
     rows, cols = 2 * gx, 16 * gy
     fetch.wait()
     assemble3(whole3, f3, gx, gy, rows)
-    y, lane = iota((128, 128), 0), iota((128, 128), 1)
     f3, u3, r3 = (Field(ref, rows) for ref in (f3, u3, r3))
     y = iota((rows, 128), 1)
     x_face3, y_face3, inv3, g3, c3 = (Field(ref, rows) for ref in k3)
@@ -866,28 +865,34 @@
     smooth_up(f0, x_face0, y_face0, Line(inv0, z_face0), u0, e0, Field(kept0, rows, 2), mask0, 2)
 
     kappa = Field(kappa, TX)
-    tile = lambda v: v[:TX, :TY]
 
     def residual(k, carry):
         below, flux_z = carry
-        field = u0[k]
-        flux_x = x_face0[k] * (field - shift(field, 1, 0))
-        flux_y = y_face0[k] * (field - shift(field, 1, 1))
-        side = (flux_x - shift(flux_x, -1, 0)) + (flux_y - shift(flux_y, -1, 1))
-        here = tile(field)
+        column = u0.part(0, k)
+        here = column[:TX]
+        flux_x = (x_face0.part(0, k) * (column - shift(column, 1, 0)))[: TX + 8]
+        row = u0[k][:TX]
+        flux_y = y_face0[k][:TX] * (row - shift(row, 1, 1))
+        side = (flux_x - shift(flux_x, -1, 0))[:TX] + (flux_y - shift(flux_y, -1, 1))[:, :TY]
         above = u0.part(0, k + 1)[:TX] if k is not NZ - 1 else jnp.zeros((TX, TY), F32)
         flux_up = z_face0.part(0, k + 1)[:TX] * (above - here)
         solution_out[span(k * TX, TX), :] = here
-        out = f0.part(0, k)[:TX] - kappa[k] * here - tile(side) - flux_z + flux_up
+        out = f0.part(0, k)[:TX] - kappa[k] * here - side - flux_z + flux_up
         residual_out[span(k * TX, TX), :] = out
         return here, flux_up
 
-    start = z_face0.part(0, 0)[:TX] * tile(u0[0])
-    carry = loop(NZ - 1, residual, (start, start), 2)
+    start = z_face0.part(0, 0)[:TX] * u0.part(0, 0)[:TX]
+    carry = loop(NZ - 1, residual, (start, start), 4)
     residual(NZ - 1, carry)
 
 
-def call(kernel, name, outs, ins, scratch=(), in_specs=None, out_specs=None, flops=1000000):
+COSTS = {
+    "pack_y": 2 * 10**9, "pack_x": 2 * 10**9, "share": 10**9, "down": 10**10,
+    "window_coeffs": 4 * 10**9, "global_coeffs": 4 * 10**9, "up": 12 * 10**9,
+}
+
+
+def call(kernel, name, outs, ins, scratch=(), in_specs=None, out_specs=None, aliases=None):
     shapes = [jax.ShapeDtypeStruct(s, F32) for s in outs]
     return pl.pallas_call(
         kernel,
@@ -896,8 +901,9 @@
         in_specs=in_specs or [VMEM] * len(ins),
         out_specs=out_specs or [VMEM] * len(outs),
         scratch_shapes=list(scratch),
+        input_output_aliases=aliases or {},
         compiler_params=pltpu.CompilerParams(vmem_limit_bytes=56 * 1024 * 1024),
-        cost_estimate=pl.CostEstimate(flops=flops, bytes_accessed=4 * sum(x.size for x in ins), transcendentals=0),
+        cost_estimate=pl.CostEstimate(flops=COSTS[name], bytes_accessed=4 * sum(x.size for x in ins), transcendentals=0),
     )(*ins)
 
 
@@ -906,28 +912,42 @@
     tiles = [v.reshape(NZ * TX, TY) for v in (right_side, kappa_sq, cond_x, cond_y, cond_z)]
     slab, strip = (SLAB + 6 * NZ, 128), (STRIP + 24, 128)
     vm = lambda *shape: pltpu.VMEM(shape, F32)
-    pack_y = functools.partial(pack_y_kernel, gy)
-    y_blocks, share2 = call(pack_y, "pack_y", [(gy * Y_BLOCK, 128), (6 * NZ, 128)], tiles, [vm(*strip)] * 2)
-    y_all = lax.all_to_all(y_blocks.reshape(gy, Y_BLOCK, 128), "gy", 0, 0).reshape(gy * Y_BLOCK, 128)
-    x_head, x_tail = call(pack_x_kernel, "pack_x", [slab, slab], [*tiles, share2])
+    dma = lambda n: pltpu.SemaphoreType.DMA((n,))
+    devices = gx * gy
     up = lambda n: [(i, i + 1) for i in range(n - 1)]
     down = lambda n: [(i + 1, i) for i in range(n - 1)]
+    y_head, y_tail, share2 = call(pack_y_kernel, "pack_y", [strip, strip, (6 * NZ, 128)], tiles)
+    yr = lax.ppermute(y_head, "gy", down(gy))
+    yl = lax.ppermute(y_tail, "gy", up(gy))
+    x_head, x_tail = call(pack_x_kernel, "pack_x", [slab, slab], [*tiles, share2])
     xr = lax.ppermute(x_head, "gx", down(gx))
     xl = lax.ppermute(x_tail, "gx", up(gx))
-    corner_head, corner_tail, copies = call(
-        functools.partial(forward_kernel, gx, gy),
-        "forward",
-        [(208, 128), (208, 128), (gx * gy * 48, 128)],
-        [y_all],
-        [vm(gy * 48, 128), pltpu.SemaphoreType.DMA((gx,))],
-        out_specs=[VMEM, VMEM, ANY],
-    )
-    corner_r = lax.ppermute(corner_head, "gx", down(gx))
-    corner_l = lax.ppermute(corner_tail, "gx", up(gx))
-    shares = lax.all_to_all(copies.reshape(gx, gy * 48, 128), "gx", 0, 0).reshape(gx * gy, 48, 128)
+    copies = call(functools.partial(share_kernel, devices), "share", [(devices * SHARE, 128)], [share2])[0]
+    copies, yr, yl = lax.optimization_barrier((copies, yr, yl))
+    half = STRIP // 2
+    corner_r = lax.ppermute(jnp.concatenate([yl[:half], yl[STRIP:], yr[:half], yr[STRIP:]]), "gx", down(gx))
+    corner_l = lax.ppermute(jnp.concatenate([yl[half:], yr[half:]]), "gx", up(gx))
+    shares = lax.all_to_all(copies.reshape(devices, SHARE, 128), ("gx", "gy"), 0, 0)
     level = lambda rows, n: [vm(NZ * rows, 128)] * n
     faces = lambda rows, tiles: vm(tiles * (NZ + 1) * rows, 128)
     rows3, rows4 = 2 * gx, gx
+    size, tall = (NZ * TX, 128), ((NZ + 1) * TX, 128)
+    k2 = call(
+        window_kernel, "window_coeffs", [size, size, size, tall], [share2, xr, xl, yr, yl, corner_r, corner_l], level(TX, 7)
+    )
+    big, big_z = (2 * NZ * 2 * TX, 128), (2 * (NZ + 1) * 2 * TX, 128)
+    sends, *saved = call(
+        functools.partial(down_kernel, gx * TX, gy * TY),
+        "down",
+        [(devices * BLOCK, 128), big, big, big, big_z, big, big, size, size, size, tall, size, size],
+        [*tiles, yr, yl, corner_r, corner_l, xr, xl],
+        [vm(*slab)] * 2 + [vm(*big)] * 10 + [vm(*big_z)] + level(TX, 10) + [faces(TX, 1)] + level(8, 10) + [faces(8, 1)]
+        + [dma(14)],
+        in_specs=[VMEM] * 9 + [HBM] * 2,
+        out_specs=[VMEM] + [HBM] * 12,
+    )
+    sends, shares = lax.optimization_barrier((sends, shares))
+    gathered = lax.all_to_all(sends.reshape(devices, BLOCK, 128), ("gx", "gy"), 0, 0)
     whole = call(
         functools.partial(global_kernel, gx, gy),
         "global_coeffs",
@@ -935,31 +955,16 @@
         [shares],
         level(rows3, 6) + [faces(rows3, 1)] + level(rows3, 1) + level(rows4, 6) + [faces(rows4, 1)] + level(rows4, 1),
     )
-    size, tall = (NZ * TX, 128), ((NZ + 1) * TX, 128)
-    k2 = call(
-        window_kernel, "window_coeffs", [size, size, size, tall], [share2, xr, xl, y_all, corner_r, corner_l], level(TX, 7)
-    )
-    big, big_z = (2 * NZ * 2 * TX, 128), (2 * (NZ + 1) * 2 * TX, 128)
-    sends, *saved = call(
-        functools.partial(down_kernel, gx * TX, gy * TY),
-        "down",
-        [(gx * gy * (NZ + 8), 128), big, big, big, big_z, big, big, size, size, size, tall, size, size],
-        [*tiles, xr, xl, y_all, corner_r, corner_l],
-        [vm(*big)] * 10 + [vm(*big_z)] + level(TX, 10) + [faces(TX, 1)] + level(8, 10) + [faces(8, 1)]
-        + [vm(NZ + 8, 128), pltpu.SemaphoreType.DMA((12 + gx * gy,))],
-        out_specs=[ANY] * 13,
-    )
-    gathered = lax.all_to_all(sends.reshape(gx * gy, NZ + 8, 128), ("gx", "gy"), 0, 0)
     field, residual = call(
         functools.partial(up_kernel, gx, gy),
         "up",
         [(NZ * TX, TY)] * 2,
         [gathered, tiles[1], *whole, *k2, *saved],
         [vm(*big), vm(*big), vm(*big), vm(*big_z), vm(*big), vm(*big), vm(*size), vm(*size), vm(*size), vm(*tall), vm(*size), vm(*size)]
-        + [vm(*size), vm(*size), vm(*size), vm(*tall), vm(gx * gy, 8, 128), vm(9, NZ, 128)]
-        + level(rows3, 3) + level(TX, 3) + level(rows4, 2)
-        + [vm(NZ * 2 * TX, 128), vm(*size), vm(*big), vm(*big), pltpu.SemaphoreType.DMA((26,))],
-        in_specs=[ANY] + [VMEM] * 11 + [ANY] * 16,
+        + [vm(*size), vm(*size), vm(*size), vm(*tall), vm(devices, 8, 128), vm(9, NZ, 128)]
+        + level(TX, 3) + [vm(NZ * 2 * TX, 128), vm(*size), vm(*big), vm(*big)]
+        + level(rows3, 3) + level(rows4, 2) + [dma(26)],
+        in_specs=[HBM] + [VMEM] * 11 + [HBM] * 16,
     )
     return field.reshape(right_side.shape), residual.reshape(right_side.shape)
 

time: 103 us -> 95.7 us (0.929)
  blocking collectives: 13.9 us -> 0 us
  starting transfers between devices: 32.7 us -> 37.3 us
  waiting for transfers between devices: 12.2 us -> 14.5 us
    all_to_all x1 -> x0, blocking collectives: 13.9 us -> none  [body(): lax.all_to_all(y_blocks.reshape(gy, Y_BLOCK, 128), 'gy', 0, 0)]
    ppermute x2 -> x4, starting transfers between devices: 5.51 us -> 10.2 us  [the longest x1 5.48 us: body(): yl = lax.ppermute(y_tail, 'gy', up(gy))]
    ppermute x2 -> x4, waiting for transfers between devices: 0.91 us -> 3.62 us  [the longest x1 3.02 us: body(): lax.ppermute(jnp.concatenate([yl[:half], yl[STRIP:], yr[:half], yr[STRIP:...]
    unnamed x16 -> x20, local copies, waits for them, and re-layouts: 2.66 us -> 2.7 us
  transfers between devices with their start and end apart: 6 -> 8, of which waited for: 2 -> 3; matrix products, arithmetic and copies ran while one was open for 0% -> 0% of each run, Pallas kernels for 21% -> 23%
where the time goes in v5:
time: 95.7 us; the launch traced here: 95 us
  Pallas kernels  39.6 us (41%)
  starting transfers between devices  37.3 us (39%)
  waiting for transfers between devices  14.5 us (15%)
  local copies, waits for them, and re-layouts  2.72 us (3%)
    pallas_call x7, Pallas kernels, call(): pl.pallas_call(kernel, name=name, out_shape=shapes, in_specs=in_specs or...  39.6 us
    all_to_all x1, starting transfers between devices, body(): lax.all_to_all(sends.reshape(devices, BLOCK, 128), ('gx', 'gy'), 0, 0)  15.1 us
    all_to_all x1, waiting for transfers between devices, body(): lax.all_to_all(sends.reshape(devices, BLOCK, 128), ('gx', 'gy'), 0, 0)  10.9 us
    all_to_all x1, starting transfers between devices, body(): lax.all_to_all(copies.reshape(devices, SHARE, 128), ('gx', 'gy'), 0, 0)  7.58 us
    ppermute x1, starting transfers between devices, body(): yl = lax.ppermute(y_tail, 'gy', up(gy))  5.48 us
    ppermute x1, starting transfers between devices, body(): xl = lax.ppermute(x_tail, 'gx', up(gx))  3.08 us
    ppermute x1, waiting for transfers between devices, body(): lax.ppermute(jnp.concatenate([yl[:half], yl[STRIP:], yr[:half], yr[STRIP:...  3.02 us
    unnamed x20, local copies, waits for them, and re-layouts  2.7 us
  transfers between devices with their start and end apart: 8, of which 3 were waited for; matrix products, arithmetic and copies ran while one was open for 0% of the time, Pallas kernels for 23%

profile of v5, /device:TPU:0, one launch (start us, length us, event | category | flops | bytes accessed | tf_op | source)
XLA Modules:
  0.0 95.0 jit_solution(10632764506636636745)
XLA Ops:
  0.6 2.6 %pack_y.1 = (f32[184,128]{1,0:T(8,128)}, f32[184,128]{1,0:T(8,128)}, f32[192,128]{1,0:T(8,128)}) custom-call(f32[512,128]{1,0:T(8,128)} %bitcast.11, f32[512,128]{1,0:T(8,128)} %bitcast.23, f32[512,128]{1,0:T(8,128)} %bitcast.14, f32[512,128]{1,0:T(8,128)} %bitcast.17, f32[512,128]{1,0:T(8,128)} %bitcast.20), custom_call_target="tpu_custom_call" | custom-call | flops 2000000000 | bytes 1310720 | tf_op jit(solution)/shard_map/pack_y/pallas_call | solution.py:897
  3.3 0.0 copy-start.9
  3.3 0.0 copy-start.8
  3.3 2.6 %pack_x.1 = (f32[1472,128]{1,0:T(8,128)}, f32[1472,128]{1,0:T(8,128)}) custom-call(f32[512,128]{1,0:T(8,128)} %bitcast.12, f32[512,128]{1,0:T(8,128)} %bitcast.24, f32[512,128]{1,0:T(8,128)} %bitcast.15, f32[512,128]{1,0:T(8,128)} %bitcast.18, f32[512,128]{1,0:T(8,128)} %bitcast.21, f32[192,128]{1,0:T(8,128)} %get-tuple-element.41.share2), custom_call_target="tpu_custom_call" | custom-call | flops 2000000000 | bytes 1409024 | tf_op jit(solution)/shard_map/pack_x/pallas_call | solution.py:897
  5.8 1.3 %collective-permute-start.4 = (f32[1472,128]{1,0:T(8,128)}, f32[1472,128]{1,0:T(8,128)S(1)}, u32[]{:S(2)}, u32[]{:S(2)}) collective-permute-start(f32[1472,128]{1,0:T(8,128)} %get-tuple-element.46), channel_id=1, source_target_pairs={{4,0},{8,4},{12,8},{16,12},{20,16},{24,20},{28,24},{5,1},{9,5},{13... | collective-permute-start | bytes 2261000 | tf_op jit(solution)/shard_map/ppermute | solution.py:923
  7.1 3.1 %collective-permute-start.5 = (f32[1472,128]{1,0:T(8,128)}, f32[1472,128]{1,0:T(8,128)S(1)}, u32[]{:S(2)}, u32[]{:S(2)}) collective-permute-start(f32[1472,128]{1,0:T(8,128)} %get-tuple-element.47), channel_id=1, source_target_pairs={{0,4},{4,8},{8,12},{12,16},{16,20},{20,24},{24,28},{1,5},{5,9},{9,... | collective-permute-start | bytes 2261000 | tf_op jit(solution)/shard_map/ppermute | solution.py:924
  10.2 0.0 copy-done.9
  10.2 1.3 %collective-permute-start = (f32[184,128]{1,0:T(8,128)S(1)}, f32[184,128]{1,0:T(8,128)S(1)}, u32[]{:S(2)}, u32[]{:S(2)}) collective-permute-start(f32[184,128]{1,0:T(8,128)S(1)} %copy-done.9), channel_id=1, source_target_pairs={{1,0},{2,1},{3,2},{5,4},{6,5},{7,6},{9,8},{10,9},{11,10},{13,12},{... | collective-permute-start | bytes 282632 | tf_op jit(solution)/shard_map/ppermute | solution.py:920
  11.5 0.0 copy-done.8
  11.5 5.5 %collective-permute-start.1 = (f32[184,128]{1,0:T(8,128)S(1)}, f32[184,128]{1,0:T(8,128)S(1)}, u32[]{:S(2)}, u32[]{:S(2)}) collective-permute-start(f32[184,128]{1,0:T(8,128)S(1)} %copy-done.8), channel_id=1, source_target_pairs={{0,1},{1,2},{2,3},{4,5},{5,6},{6,7},{8,9},{9,10},{10,11},{12,13},{... | collective-permute-start | bytes 282632 | tf_op jit(solution)/shard_map/ppermute | solution.py:921
  17.0 2.1 %share.1 = f32[1280,128]{1,0:T(8,128)} custom-call(f32[192,128]{1,0:T(8,128)} %get-tuple-element.41.share2), custom_call_target="tpu_custom_call" | custom-call | flops 1000000000 | bytes 98304 | tf_op jit(solution)/shard_map/share/pallas_call | solution.py:897
  19.1 0.0 collective-permute-done.refs_5_.yr
  19.1 0.0 copy-start.2
  19.1 0.6 collective-permute-done.1.refs_6_.yl
  19.7 0.0 copy-start.3
  19.8 7.6 %all-to-all-start = ((f32[32,40,128]{2,1,0:T(8,128)}), f32[32,40,128]{2,1,0:T(8,128)S(1)}, u32[]{:S(2)}, u32[]{:S(2)}) async-start(f32[32,40,128]{2,1,0:T(8,128)} %bitcast.9), calls=%async_computation | async-start | bytes 1310720 | tf_op jit(solution)/shard_map/all_to_all | solution.py:930
  27.4 2.2 %collective-permute-start.3 = (f32[208,128]{1,0:T(8,128)S(1)}, f32[208,128]{1,0:T(8,128)S(1)}, u32[]{:S(2)}, u32[]{:S(2)}) collective-permute-start(f32[208,128]{1,0:T(8,128)S(1)} %pad_maximum_fusion.1), channel_id=1, source_target_pairs={{0,4},{4,8},{8,12},{12,16},{16,20},{20,24},{24,28},{1,5},{5,9},{9,... | collective-permute-start | bytes 319496 | tf_op jit(solution)/shard_map/ppermute | solution.py:929
  29.6 0.0 copy-done.2
  29.6 0.0 copy-done.3
  29.6 1.3 %collective-permute-start.2 = (f32[208,128]{1,0:T(8,128)S(1)}, f32[208,128]{1,0:T(8,128)S(1)}, u32[]{:S(2)}, u32[]{:S(2)}) collective-permute-start(f32[208,128]{1,0:T(8,128)S(1)} %pad_maximum_fusion), channel_id=1, source_target_pairs={{4,0},{8,4},{12,8},{16,12},{20,16},{24,20},{28,24},{5,1},{9,5},{13... | collective-permute-start | bytes 319496 | tf_op jit(solution)/shard_map/ppermute | solution.py:928
  30.9 0.0 collective-permute-done.3.refs_8_.cl
  30.9 0.0 copy-start.6
  30.9 3.0 %collective-permute-done.2.refs_7_.cr = f32[208,128]{1,0:T(8,128)S(1)} collective-permute-done((f32[208,128]{1,0:T(8,128)S(1)}, f32[208,128]{1,0:T(8,128)S(1)}, u32[]{:S(2)}, u32[]{:S(2)}) %collective-permute-start.2) | collective-permute-done | bytes 106528 | tf_op jit(solution)/shard_map/ppermute | solution.py:928
  34.0 0.0 copy-start.7
  34.0 0.0 collective-permute-done.4.refs_9_.xr
  34.0 0.0 copy-start.4
  34.0 0.0 collective-permute-done.5.refs_10_.xl
  34.0 0.0 copy-done.6
  34.0 0.6 copy-done.7
  34.6 0.3 copy-done.4
  34.9 0.0 copy-start.5
  34.9 0.9 copy-done.5
  35.8 11.9 %down.1 = (f32[1280,128]{1,0:T(8,128)}, f32[2048,128]{1,0:T(8,128)}, f32[2048,128]{1,0:T(8,128)}, f32[2048,128]{1,0:T(8,128)}, f32[2112,128]{1,0:T(8,128)}, /*in...) custom-call(f32[512,128]{1,0:T(8,128)} %bitcast.13, ...), custom_call_target="tpu_custom_call" | custom-call | flops 10000000000 | bytes 3219456 | tf_op jit(solution)/shard_map/down/pallas_call | solution.py:897
  47.6 0.0 all-to-all-done.gathered
  47.6 0.0 copy-start
  47.6 15.1 %all-to-all-start.1 = ((f32[32,40,128]{2,1,0:T(8,128)}), f32[32,40,128]{2,1,0:T(8,128)S(1)}, u32[]{:S(2)}, u32[]{:S(2)}) async-start(f32[32,40,128]{2,1,0:T(8,128)} %bitcast.10), calls=%async_computation.1 | async-start | bytes 1310720 | tf_op jit(solution)/shard_map/all_to_all | solution.py:950
  62.8 4.5 %window_coeffs.1 = (f32[512,128]{1,0:T(8,128)}, f32[512,128]{1,0:T(8,128)}, f32[512,128]{1,0:T(8,128)}, f32[528,128]{1,0:T(8,128)}) custom-call(f32[192,128]{1,0:T(8,128)} %get-tuple-element.41.share2, f32[1472,128]{1,0:T(8,128)} %copy-done.4, f32[1472,128]{1,0:T(8,128)} %copy-done.5, f32[184,128]{1,0:T(8,128)} %copy-done.2, f32[184,128]{1,0:T(8,128)} %copy-done.3, ...), custom_call_target="tpu_custom_call" | custom-call | flops 4000000000 | bytes 2007040 | tf_op jit(solution)/shard_map/window_coeffs/pallas_call | solution.py:897
  67.2 0.0 copy-done
  67.2 3.4 %global_coeffs.1 = (f32[512,128]{1,0:T(8,128)}, f32[512,128]{1,0:T(8,128)}, f32[512,128]{1,0:T(8,128)}, f32[512,128]{1,0:T(8,128)}, f32[512,128]{1,0:T(8,128)}, ...) custom-call(f32[32,40,128]{2,1,0:T(8,128)} %copy-done), custom_call_target="tpu_custom_call" | custom-call | flops 4000000000 | bytes 655360 | tf_op jit(solution)/shard_map/global_coeffs/pallas_call | solution.py:897
  70.7 10.9 %all-to-all-done.1.refs_0_ = f32[32,40,128]{2,1,0:T(8,128)S(1)} async-done(((f32[32,40,128]{2,1,0:T(8,128)}), f32[32,40,128]{2,1,0:T(8,128)S(1)}, u32[]{:S(2)}, u32[]{:S(2)}) %all-to-all-start.1) | async-done | bytes 655392 | tf_op jit(solution)/shard_map/all_to_all | solution.py:950
  81.6 0.0 copy-start.1
  81.6 0.9 copy-done.1
  82.5 12.5 %up.1 = (f32[512,128]{1,0:T(8,128)}, f32[512,128]{1,0:T(8,128)}) custom-call(f32[32,40,128]{2,1,0:T(8,128)} %copy-done.1, f32[512,128]{1,0:T(8,128)} %bitcast.26, f32[512,128]{1,0:T(8,128)} %get-tuple-element.52.refs_2_, f32[512,128]{1,0:T(8,128)} %get-tuple-element.53.refs_3_, f32[512,128]{1,0:T(8,128)} %get-tuple-element.54.refs_4_, ...), custom_call_target="tpu_custom_call" | custom-call | flops 12000000000 | bytes 11845632 | tf_op jit(solution)/shard_map/up/pallas_call | solution.py:897
  (8 shorter events, 0.0 us)
Async XLA Ops:
  3.3 7.0 %copy-start.9 = (f32[184,128]{1,0:T(8,128)S(1)}, f32[184,128]{1,0:T(8,128)}, u32[]{:S(2)}) copy-start(f32[184,128]{1,0:T(8,128)} %get-tuple-element.42) | copy-start | bytes 282628
  3.3 8.3 %copy-start.8 = (f32[184,128]{1,0:T(8,128)S(1)}, f32[184,128]{1,0:T(8,128)}, u32[]{:S(2)}) copy-start(f32[184,128]{1,0:T(8,128)} %get-tuple-element.43) | copy-start | bytes 282628
  5.8 28.1 %collective-permute-start.4 = (f32[1472,128]{1,0:T(8,128)}, f32[1472,128]{1,0:T(8,128)S(1)}, u32[]{:S(2)}, u32[]{:S(2)}) collective-permute-start(f32[1472,128]{1,0:T(8,128)} %get-tuple-element.46), channel_id=1, source_target_pairs={{4,0},{8,4},{12,8},{16,12},{20,16},{24,20},{28,24},{5,1},{9,5},{13... | collective-permute-start | bytes 2261000 | tf_op jit(solution)/shard_map/ppermute | solution.py:923
  7.1 26.8 %collective-permute-start.5 = (f32[1472,128]{1,0:T(8,128)}, f32[1472,128]{1,0:T(8,128)S(1)}, u32[]{:S(2)}, u32[]{:S(2)}) collective-permute-start(f32[1472,128]{1,0:T(8,128)} %get-tuple-element.47), channel_id=1, source_target_pairs={{0,4},{4,8},{8,12},{12,16},{16,20},{20,24},{24,28},{1,5},{5,9},{9,... | collective-permute-start | bytes 2261000 | tf_op jit(solution)/shard_map/ppermute | solution.py:924
  10.2 8.9 %collective-permute-start = (f32[184,128]{1,0:T(8,128)S(1)}, f32[184,128]{1,0:T(8,128)S(1)}, u32[]{:S(2)}, u32[]{:S(2)}) collective-permute-start(f32[184,128]{1,0:T(8,128)S(1)} %copy-done.9), channel_id=1, source_target_pairs={{1,0},{2,1},{3,2},{5,4},{6,5},{7,6},{9,8},{10,9},{11,10},{13,12},{... | collective-permute-start | bytes 282632 | tf_op jit(solution)/shard_map/ppermute | solution.py:920
  11.5 8.2 %collective-permute-start.1 = (f32[184,128]{1,0:T(8,128)S(1)}, f32[184,128]{1,0:T(8,128)S(1)}, u32[]{:S(2)}, u32[]{:S(2)}) collective-permute-start(f32[184,128]{1,0:T(8,128)S(1)} %copy-done.8), channel_id=1, source_target_pairs={{0,1},{1,2},{2,3},{4,5},{5,6},{6,7},{8,9},{9,10},{10,11},{12,13},{... | collective-permute-start | bytes 282632 | tf_op jit(solution)/shard_map/ppermute | solution.py:921
  19.1 10.5 %copy-start.2 = (f32[184,128]{1,0:T(8,128)}, f32[184,128]{1,0:T(8,128)S(1)}, u32[]{:S(2)}) copy-start(f32[184,128]{1,0:T(8,128)S(1)} %collective-permute-done.refs_5_.yr) | copy-start | bytes 282628
  19.7 9.9 %copy-start.3 = (f32[184,128]{1,0:T(8,128)}, f32[184,128]{1,0:T(8,128)S(1)}, u32[]{:S(2)}) copy-start(f32[184,128]{1,0:T(8,128)S(1)} %collective-permute-done.1.refs_6_.yl) | copy-start | bytes 282628
  19.8 27.8 %all-to-all-start = ((f32[32,40,128]{2,1,0:T(8,128)}), f32[32,40,128]{2,1,0:T(8,128)S(1)}, u32[]{:S(2)}, u32[]{:S(2)}) async-start(f32[32,40,128]{2,1,0:T(8,128)} %bitcast.9), calls=%async_computation | async-start | bytes 1310720 | tf_op jit(solution)/shard_map/all_to_all | solution.py:930
  27.4 3.5 %collective-permute-start.3 = (f32[208,128]{1,0:T(8,128)S(1)}, f32[208,128]{1,0:T(8,128)S(1)}, u32[]{:S(2)}, u32[]{:S(2)}) collective-permute-start(f32[208,128]{1,0:T(8,128)S(1)} %pad_maximum_fusion.1), channel_id=1, source_target_pairs={{0,4},{4,8},{8,12},{12,16},{16,20},{20,24},{24,28},{1,5},{5,9},{9,... | collective-permute-start | bytes 319496 | tf_op jit(solution)/shard_map/ppermute | solution.py:929
  29.6 4.3 %collective-permute-start.2 = (f32[208,128]{1,0:T(8,128)S(1)}, f32[208,128]{1,0:T(8,128)S(1)}, u32[]{:S(2)}, u32[]{:S(2)}) collective-permute-start(f32[208,128]{1,0:T(8,128)S(1)} %pad_maximum_fusion), channel_id=1, source_target_pairs={{4,0},{8,4},{12,8},{16,12},{20,16},{24,20},{28,24},{5,1},{9,5},{13... | collective-permute-start | bytes 319496 | tf_op jit(solution)/shard_map/ppermute | solution.py:928
  30.9 3.0 %copy-start.6 = (f32[208,128]{1,0:T(8,128)}, f32[208,128]{1,0:T(8,128)S(1)}, u32[]{:S(2)}) copy-start(f32[208,128]{1,0:T(8,128)S(1)} %collective-permute-done.3.refs_8_.cl) | copy-start | bytes 319492
  34.0 0.6 copy-start.7
  34.0 0.9 copy-start.4
  34.9 0.9 copy-start.5
  47.6 19.6 %copy-start = (f32[32,40,128]{2,1,0:T(8,128)}, f32[32,40,128]{2,1,0:T(8,128)S(1)}, u32[]{:S(2)}) copy-start(f32[32,40,128]{2,1,0:T(8,128)S(1)} %all-to-all-done.gathered) | copy-start | bytes 1966084
  47.6 33.9 %all-to-all-start.1 = ((f32[32,40,128]{2,1,0:T(8,128)}), f32[32,40,128]{2,1,0:T(8,128)S(1)}, u32[]{:S(2)}, u32[]{:S(2)}) async-start(f32[32,40,128]{2,1,0:T(8,128)} %bitcast.10), calls=%async_computation.1 | async-start | bytes 1310720 | tf_op jit(solution)/shard_map/all_to_all | solution.py:950
  81.6 0.9 copy-start.1

commit v6 on v5

--- a/solution.py
+++ b/solution.py
@@ -169,7 +169,7 @@
 SHARE = 40
 BLOCK = NZ + 8
 VMEM = pl.BlockSpec(memory_space=pltpu.VMEM)
-HBM = pl.BlockSpec(memory_space=pltpu.HBM)
+ANY = pl.BlockSpec(memory_space=pl.ANY)
 
 
 def iota(shape, dim):
@@ -182,14 +182,15 @@
 
 
 def mix(x, weights, parts=2):
-    out = None
+    pieces = []
     for n in range(parts):
-        part = x.astype(BF16)
-        term = jnp.dot(part, weights, preferred_element_type=F32)
-        out = term if out is None else out + term
+        piece = x.astype(BF16)
+        pieces.append(piece)
         if n < parts - 1:
-            x = x - part.astype(F32)
-    return out
+            x = x - piece.astype(F32)
+    out = jnp.dot(jnp.concatenate(pieces, axis=0), weights, preferred_element_type=F32)
+    rows = x.shape[0]
+    return sum(out[n * rows : (n + 1) * rows] for n in reversed(range(parts)))
 
 
 def matrix(mask, weight=1.0):
@@ -540,10 +541,10 @@
     factor(diag, z_face, 1, inv, None)
 
 
-def assemble3(gathered, dest, gx, gy, rows, at=slice(None)):
+def assemble3(block, dest, gx, gy, rows):
     group = lane_group(8, 16)
     for ix in range(gx):
-        blocks = [gathered[ix * gy + iy, at, :] for iy in range(gy)]
+        blocks = [block(ix, iy) for iy in range(gy)]
         for zo in range(4):
             for xi in range(2):
                 q = 2 * zo + xi
@@ -553,12 +554,22 @@
                 dest[pl.ds(8 * zo * rows + 2 * ix + xi, 8, stride=rows), :] = shift(cells, -16 * q, 1)
 
 
-def global_kernel(gx, gy, gathered, *refs):
+def global_kernel(gx, gy, own, other, *refs):
     outs3, outs4 = refs[:5], refs[5:10]
-    raw3, raw4 = refs[10:18], refs[18:26]
+    raw3, raw4, shares, sems = refs[10:18], refs[18:26], refs[26], refs[27]
+    core = lax.axis_index("gx") % 2
+    copies = [
+        pltpu.make_async_copy(own, shares.at[:, core], sems.at[0]),
+        pltpu.make_async_copy(other, shares.at[:, 1 - core], sems.at[1]),
+    ]
+    for copy in copies:
+        copy.start()
+    for copy in copies:
+        copy.wait()
     rows, cols = 2 * gx, 16 * gy
     for t, n in enumerate((0, 1, 2, 4, 5)):
-        assemble3(gathered, raw3[n], gx, gy, rows, pl.ds(8 * t, 8))
+        block = lambda jx, jy: shares[jx // 2, jx % 2, pl.ds(jy * SHARE + 8 * t, 8), :]
+        assemble3(block, raw3[n], gx, gy, rows)
     xl, xu, yl, yu = (Field(ref, rows) for ref in raw3[:4])
     x, y = iota((rows, 128), 0), iota((rows, 128), 1)
     odd_row, inside = x % 2 == 1, y < cols
@@ -683,16 +694,16 @@
         y, j = iota((lanes, 128), 0), iota((lanes, 128), 1)
         if lanes == 128:
             j = jnp.where(j < 48, j, jnp.where(j >= 80, j - 64, -1))
-        pair, even = matrix(y // 2 == j), matrix(y == 2 * j)
-        part = min(128, NZ * rows)
+        pair = matrix(y // 2 == j)
+        even = (iota((1, lanes), 1) % 2 == 0).astype(F32)
+        part = 128
         for at in range(0, NZ * rows, part):
             here = pl.ds(at, part)
             both = lambda n: fine[n].every_second(at, part, 0) + fine[n].every_second(at, part, 1)
-            f1.ref[here, :] = 0.25 * mix(both(0), pair)
-            kappa1.ref[here, :] = 0.25 * mix(both(1), pair)
-            cz1.ref[here, :] = 0.25 * mix(both(2), pair)
-            x_face.ref[here, :] = 0.125 * mix(fine[3].every_second(at, part, 0), pair)
-            y_face.ref[here, :] = 0.125 * mix(both(4), even)
+            below = fine[3].every_second(at, part, 0)
+            out = mix(jnp.concatenate([both(0), both(1), both(2), below, both(4) * even], axis=0), pair)
+            for n, (dest, weight) in enumerate(((f1, 0.25), (kappa1, 0.25), (cz1, 0.25), (x_face, 0.125), (y_face, 0.125))):
+                dest.ref[here, :] = weight * out[n * part : (n + 1) * part]
         for k in range(NZ):
             f1[k] = f1[k] * mask
             diag[k] = base_diag(jnp.where(mask > 0, kappa1[k], 1.0), x_face[k], y_face[k])
@@ -751,7 +762,7 @@
 
     rows, cols = 2 * gx, 16 * gy
     fetch.wait()
-    assemble3(whole3, f3, gx, gy, rows)
+    assemble3(lambda jx, jy: whole3[jx * gy + jy], f3, gx, gy, rows)
     f3, u3, r3 = (Field(ref, rows) for ref in (f3, u3, r3))
     y = iota((rows, 128), 1)
     x_face3, y_face3, inv3, g3, c3 = (Field(ref, rows) for ref in k3)
@@ -902,7 +913,7 @@
         out_specs=out_specs or [VMEM] * len(outs),
         scratch_shapes=list(scratch),
         input_output_aliases=aliases or {},
-        compiler_params=pltpu.CompilerParams(vmem_limit_bytes=56 * 1024 * 1024),
+        compiler_params=pltpu.CompilerParams(vmem_limit_bytes=(32 if name in ("down", "up") else 16) * 1024 * 1024),
         cost_estimate=pl.CostEstimate(flops=COSTS[name], bytes_accessed=4 * sum(x.size for x in ins), transcendentals=0),
     )(*ins)
 
@@ -922,12 +933,14 @@
     x_head, x_tail = call(pack_x_kernel, "pack_x", [slab, slab], [*tiles, share2])
     xr = lax.ppermute(x_head, "gx", down(gx))
     xl = lax.ppermute(x_tail, "gx", up(gx))
-    copies = call(functools.partial(share_kernel, devices), "share", [(devices * SHARE, 128)], [share2])[0]
-    copies, yr, yl = lax.optimization_barrier((copies, yr, yl))
+    copies = call(functools.partial(share_kernel, devices // 2), "share", [(devices // 2 * SHARE, 128)], [share2])[0]
     half = STRIP // 2
     corner_r = lax.ppermute(jnp.concatenate([yl[:half], yl[STRIP:], yr[:half], yr[STRIP:]]), "gx", down(gx))
     corner_l = lax.ppermute(jnp.concatenate([yl[half:], yr[half:]]), "gx", up(gx))
-    shares = lax.all_to_all(copies.reshape(devices, SHARE, 128), ("gx", "gy"), 0, 0)
+    copies, corner_r, corner_l = lax.optimization_barrier((copies, corner_r, corner_l))
+    cores = [[x * gy + y for x in range(core, gx, 2) for y in range(gy)] for core in range(2)]
+    blocks = copies.reshape(devices // 2, SHARE, 128)
+    own = lax.all_to_all(blocks, ("gx", "gy"), 0, 0, axis_index_groups=cores).reshape(gx // 2, gy * SHARE, 128)
     level = lambda rows, n: [vm(NZ * rows, 128)] * n
     faces = lambda rows, tiles: vm(tiles * (NZ + 1) * rows, 128)
     rows3, rows4 = 2 * gx, gx
@@ -943,17 +956,20 @@
         [*tiles, yr, yl, corner_r, corner_l, xr, xl],
         [vm(*slab)] * 2 + [vm(*big)] * 10 + [vm(*big_z)] + level(TX, 10) + [faces(TX, 1)] + level(8, 10) + [faces(8, 1)]
         + [dma(14)],
-        in_specs=[VMEM] * 9 + [HBM] * 2,
-        out_specs=[VMEM] + [HBM] * 12,
+        in_specs=[VMEM] * 9 + [ANY] * 2,
+        out_specs=[VMEM] + [ANY] * 12,
     )
-    sends, shares = lax.optimization_barrier((sends, shares))
+    sends, own = lax.optimization_barrier((sends, own))
+    other = lax.ppermute(own, "gx", [(i, i ^ 1) for i in range(gx)])
     gathered = lax.all_to_all(sends.reshape(devices, BLOCK, 128), ("gx", "gy"), 0, 0)
     whole = call(
         functools.partial(global_kernel, gx, gy),
         "global_coeffs",
         [(NZ * rows3, 128)] * 5 + [(NZ * rows4, 128)] * 5,
-        [shares],
-        level(rows3, 6) + [faces(rows3, 1)] + level(rows3, 1) + level(rows4, 6) + [faces(rows4, 1)] + level(rows4, 1),
+        [own, other],
+        level(rows3, 6) + [faces(rows3, 1)] + level(rows3, 1) + level(rows4, 6) + [faces(rows4, 1)] + level(rows4, 1)
+        + [vm(gx // 2, 2, gy * SHARE, 128), dma(2)],
+        in_specs=[ANY] * 2,
     )
     field, residual = call(
         functools.partial(up_kernel, gx, gy),
@@ -964,7 +980,7 @@
         + [vm(*size), vm(*size), vm(*size), vm(*tall), vm(devices, 8, 128), vm(9, NZ, 128)]
         + level(TX, 3) + [vm(NZ * 2 * TX, 128), vm(*size), vm(*big), vm(*big)]
         + level(rows3, 3) + level(rows4, 2) + [dma(26)],
-        in_specs=[HBM] + [VMEM] * 11 + [HBM] * 16,
+        in_specs=[ANY] + [VMEM] * 11 + [ANY] * 16,
     )
     return field.reshape(right_side.shape), residual.reshape(right_side.shape)
 

time: 95.7 us -> 116 us (1.21)
  local copies, waits for them, and re-layouts: 2.72 us -> 40.3 us
  Pallas kernels: 39.6 us -> 27.5 us
  starting transfers between devices: 37.3 us -> 30.5 us
    unnamed x20 -> x106, local copies, waits for them, and re-layouts: 2.7 us -> 40.2 us
    pallas_call x7, Pallas kernels: 39.6 us -> 27.5 us  [call(): pl.pallas_call(kernel, name=name, out_shape=shapes, in_specs=in_specs or...]
    all_to_all x1, starting transfers between devices: 15.1 us -> 5.91 us  [body(): lax.all_to_all(sends.reshape(devices, BLOCK, 128), ('gx', 'gy'), 0, 0)]
    all_to_all x1, starting transfers between devices: 7.58 us -> 9.32 us  [body(): lax.all_to_all(blocks, ('gx', 'gy'), 0, 0, axis_index_groups=cores)]
    ppermute x1, waiting for transfers between devices: 0.6 us -> 1.77 us  [body(): yl = lax.ppermute(y_tail, 'gy', up(gy))]
  transfers between devices with their start and end apart: 8 -> 9, of which waited for: 3 -> 4; matrix products, arithmetic and copies ran while one was open for 0% -> 0% of each run, Pallas kernels for 23% -> 13%
where the time goes in v6:
time: 116 us; the launch traced here: 114 us
  local copies, waits for them, and re-layouts  40.3 us (35%)
  starting transfers between devices  30.5 us (26%)
  Pallas kernels  27.5 us (24%)
  waiting for transfers between devices  15.1 us (13%)
    unnamed x106, local copies, waits for them, and re-layouts  40.2 us
    pallas_call x7, Pallas kernels, call(): pl.pallas_call(kernel, name=name, out_shape=shapes, in_specs=in_specs or...  27.5 us
    all_to_all x1, waiting for transfers between devices, body(): lax.all_to_all(sends.reshape(devices, BLOCK, 128), ('gx', 'gy'), 0, 0)  9.99 us
    all_to_all x1, starting transfers between devices, body(): lax.all_to_all(blocks, ('gx', 'gy'), 0, 0, axis_index_groups=cores)  9.32 us
    all_to_all x1, starting transfers between devices, body(): lax.all_to_all(sends.reshape(devices, BLOCK, 128), ('gx', 'gy'), 0, 0)  5.91 us
    ppermute x1, starting transfers between devices, body(): yl = lax.ppermute(y_tail, 'gy', up(gy))  5.48 us
    ppermute x1, starting transfers between devices, body(): xl = lax.ppermute(x_tail, 'gx', up(gx))  3.08 us
    ppermute x1, waiting for transfers between devices, body(): lax.ppermute(jnp.concatenate([yl[:half], yl[STRIP:], yr[:half], yr[STRIP:...  2.4 us
  transfers between devices with their start and end apart: 9, of which 4 were waited for; matrix products, arithmetic and copies ran while one was open for 0% of the time, Pallas kernels for 13%

profile of v6, /device:TPU:0, one launch (start us, length us, event | category | flops | bytes accessed | tf_op | source)
XLA Modules:
  0.0 114.3 jit_solution(1105116354197829398)
XLA Ops:
  0.6 0.9 copy-done
  1.6 0.9 copy-done.2
  2.5 0.9 copy-done.4
  3.5 0.9 copy-done.6
  4.4 0.9 copy-done.8
  5.4 0.7 pack_y.1
  6.1 1.0 pack_x.1
  7.1 1.3 %collective-permute-start.4 = (f32[1472,128]{1,0:T(8,128)}, f32[1472,128]{1,0:T(8,128)S(1)}, u32[]{:S(2)}, u32[]{:S(2)}) collective-permute-start(f32[1472,128]{1,0:T(8,128)} %get-tuple-element.46), channel_id=1, source_target_pairs={{4,0},{8,4},{12,8},{16,12},{20,16},{24,20},{28,24},{5,1},{9,5},{13... | collective-permute-start | bytes 2261000 | tf_op jit(solution)/shard_map/ppermute | solution.py:934
  8.3 3.1 %collective-permute-start.5 = (f32[1472,128]{1,0:T(8,128)S(1)}, f32[1472,128]{1,0:T(8,128)S(1)}, u32[]{:S(2)}, u32[]{:S(2)}) collective-permute-start(f32[1472,128]{1,0:T(8,128)S(1)} %get-tuple-element.47), channel_id=1, source_target_pairs={{0,4},{4,8},{8,12},{12,16},{16,20},{20,24},{24,28},{1,5},{5,9},{9,... | collective-permute-start | bytes 2261000 | tf_op jit(solution)/shard_map/ppermute | solution.py:935
  11.4 1.3 %collective-permute-start = (f32[184,128]{1,0:T(8,128)S(1)}, f32[184,128]{1,0:T(8,128)S(1)}, u32[]{:S(2)}, u32[]{:S(2)}) collective-permute-start(f32[184,128]{1,0:T(8,128)S(1)} %get-tuple-element.41), channel_id=1, source_target_pairs={{1,0},{2,1},{3,2},{5,4},{6,5},{7,6},{9,8},{10,9},{11,10},{13,12},{... | collective-permute-start | bytes 282632 | tf_op jit(solution)/shard_map/ppermute | solution.py:931
  12.7 5.5 %collective-permute-start.1 = (f32[184,128]{1,0:T(8,128)S(1)}, f32[184,128]{1,0:T(8,128)S(1)}, u32[]{:S(2)}, u32[]{:S(2)}) collective-permute-start(f32[184,128]{1,0:T(8,128)S(1)} %get-tuple-element.42), channel_id=1, source_target_pairs={{0,1},{1,2},{2,3},{4,5},{5,6},{6,7},{8,9},{9,10},{10,11},{12,13},{... | collective-permute-start | bytes 282632 | tf_op jit(solution)/shard_map/ppermute | solution.py:932
  18.2 1.0 collective-permute-done.refs_5_.yr
  19.2 1.8 %collective-permute-done.1.refs_6_.yl = f32[184,128]{1,0:T(8,128)S(1)} collective-permute-done((f32[184,128]{1,0:T(8,128)S(1)}, f32[184,128]{1,0:T(8,128)S(1)}, u32[]{:S(2)}, u32[]{:S(2)}) %collective-permute-start.1) | collective-permute-done | bytes 94240 | tf_op jit(solution)/shard_map/ppermute | solution.py:932
  21.0 2.4 %collective-permute-start.3 = (f32[208,128]{1,0:T(8,128)S(1)}, f32[208,128]{1,0:T(8,128)S(1)}, u32[]{:S(2)}, u32[]{:S(2)}) collective-permute-start(f32[208,128]{1,0:T(8,128)S(1)} %pad_maximum_fusion.1), channel_id=1, source_target_pairs={{0,4},{4,8},{8,12},{12,16},{16,20},{20,24},{24,28},{1,5},{5,9},{9,... | collective-permute-start | bytes 319496 | tf_op jit(solution)/shard_map/ppermute | solution.py:939
  23.4 1.4 %collective-permute-start.2 = (f32[208,128]{1,0:T(8,128)S(1)}, f32[208,128]{1,0:T(8,128)S(1)}, u32[]{:S(2)}, u32[]{:S(2)}) collective-permute-start(f32[208,128]{1,0:T(8,128)S(1)} %pad_maximum_fusion), channel_id=1, source_target_pairs={{4,0},{8,4},{12,8},{16,12},{20,16},{24,20},{28,24},{5,1},{9,5},{13... | collective-permute-start | bytes 319496 | tf_op jit(solution)/shard_map/ppermute | solution.py:938
  24.9 1.0 share.1
  25.9 2.4 %collective-permute-done.2.refs_7_.cr = f32[208,128]{1,0:T(8,128)S(1)} collective-permute-done((f32[208,128]{1,0:T(8,128)S(1)}, f32[208,128]{1,0:T(8,128)S(1)}, u32[]{:S(2)}, u32[]{:S(2)}) %collective-permute-start.2) | collective-permute-done | bytes 106528 | tf_op jit(solution)/shard_map/ppermute | solution.py:938
  28.3 9.3 %all-to-all-start = ((f32[16,40,128]{2,1,0:T(8,128)}), f32[16,40,128]{2,1,0:T(8,128)S(1)}, u32[]{:S(2)}, u32[]{:S(2)}) async-start(f32[16,40,128]{2,1,0:T(8,128)} %bitcast.5), calls=%async_computation | async-start | bytes 655360 | tf_op jit(solution)/shard_map/all_to_all | solution.py:943
  37.7 0.9 copy-done.5
  38.6 0.9 copy-done.7
  39.6 0.9 copy-done.9
  40.5 10.0 %down.1 = (f32[1280,128]{1,0:T(8,128)}, f32[2048,128]{1,0:T(8,128)S(1)}, f32[2048,128]{1,0:T(8,128)S(1)}, f32[2048,128]{1,0:T(8,128)S(1)}, f32[2112,128]{1,0:T(8...) custom-call(f32[512,128]{1,0:T(8,128)S(1)} %bitcast.14, ...), custom_call_target="tpu_custom_call" | custom-call | flops 10000000000 | bytes 3219456 | tf_op jit(solution)/shard_map/down/pallas_call | solution.py:908
  50.6 1.0 copy-done.21
  51.5 1.0 copy-done.23
  52.5 1.0 copy-done.25
  53.6 1.0 copy-done.27
  54.6 1.0 copy-done.29
  55.5 1.1 copy-done.31
  56.6 0.7 copy-done.41
  57.3 0.7 copy-done.43
  58.0 0.7 copy-done.45
  58.7 0.7 copy-done.47
  59.4 0.7 copy-done.49
  60.1 0.7 copy-done.51
  60.8 5.9 %all-to-all-start.1 = ((f32[32,40,128]{2,1,0:T(8,128)}), f32[32,40,128]{2,1,0:T(8,128)S(1)}, u32[]{:S(2)}, u32[]{:S(2)}) async-start(f32[32,40,128]{2,1,0:T(8,128)} %bitcast.7), calls=%async_computation.1 | async-start | bytes 1310720 | tf_op jit(solution)/shard_map/all_to_all | solution.py:964
  66.8 0.3 collective-permute-start.6
  67.1 2.2 %window_coeffs.1 = (f32[512,128]{1,0:T(8,128)S(1)}, f32[512,128]{1,0:T(8,128)S(1)}, f32[512,128]{1,0:T(8,128)S(1)}, f32[528,128]{1,0:T(8,128)S(1)}) custom-call(f32[192,128]{1,0:T(8,128)S(1)} %copy-done.14, f32[1472,128]{1,0:T(8,128)S(1)} %collective-permute-done.4.refs_9_.xr, f32[1472,128]{1,0:T(8,128)S(1)} %collective-permute-done.5.refs_10_.xl, ...), custom_call_target="tpu_custom_call" | custom-call | flops 4000000000 | bytes 2007040 | tf_op jit(solution)/shard_map/window_coeffs/pallas_call | solution.py:908
  69.3 0.7 copy-done.15
  70.0 0.7 copy-done.17
  70.7 1.5 %global_coeffs.1 = (f32[512,128]{1,0:T(8,128)S(1)}, f32[512,128]{1,0:T(8,128)S(1)}, f32[512,128]{1,0:T(8,128)S(1)}, f32[512,128]{1,0:T(8,128)S(1)}, f32[512,128]...) custom-call(f32[4,160,128]{2,1,0:T(8,128)S(1)} %bitcast.11, ...), custom_call_target="tpu_custom_call" | custom-call | flops 4000000000 | bytes 655360 | tf_op jit(solution)/shard_map/global_coeffs/pallas_call | solution.py:908
  72.2 0.7 copy-done.19
  72.9 0.7 copy-done.33
  73.6 0.7 copy-done.35
  74.3 0.7 copy-done.37
  74.9 0.6 copy-done.39
  75.6 10.0 %all-to-all-done.1.refs_0_ = f32[32,40,128]{2,1,0:T(8,128)S(1)} async-done(((f32[32,40,128]{2,1,0:T(8,128)}), f32[32,40,128]{2,1,0:T(8,128)S(1)}, u32[]{:S(2)}, u32[]{:S(2)}) %all-to-all-start.1) | async-done | bytes 655392 | tf_op jit(solution)/shard_map/all_to_all | solution.py:964
  85.6 0.9 copy-done.20
  86.5 1.2 %copy-done.22 = f32[2112,128]{1,0:T(8,128)S(1)} copy-done((f32[2112,128]{1,0:T(8,128)S(1)}, f32[2112,128]{1,0:T(8,128)}, u32[]{:S(2)}) %copy-start.22) | copy-done | bytes 1081368
  87.8 1.2 %copy-done.24 = f32[2048,128]{1,0:T(8,128)S(1)} copy-done((f32[2048,128]{1,0:T(8,128)S(1)}, f32[2048,128]{1,0:T(8,128)}, u32[]{:S(2)}) %copy-start.24) | copy-done | bytes 1048600
  89.0 1.2 %copy-done.26 = f32[2048,128]{1,0:T(8,128)S(1)} copy-done((f32[2048,128]{1,0:T(8,128)S(1)}, f32[2048,128]{1,0:T(8,128)}, u32[]{:S(2)}) %copy-start.26) | copy-done | bytes 1048600
  90.2 1.2 %copy-done.28 = f32[2048,128]{1,0:T(8,128)S(1)} copy-done((f32[2048,128]{1,0:T(8,128)S(1)}, f32[2048,128]{1,0:T(8,128)}, u32[]{:S(2)}) %copy-start.28) | copy-done | bytes 1048600
  91.4 1.2 %copy-done.30 = f32[2048,128]{1,0:T(8,128)S(1)} copy-done((f32[2048,128]{1,0:T(8,128)S(1)}, f32[2048,128]{1,0:T(8,128)}, u32[]{:S(2)}) %copy-start.30) | copy-done | bytes 1048600
  92.7 1.2 %copy-done.32 = f32[2048,128]{1,0:T(8,128)S(1)} copy-done((f32[2048,128]{1,0:T(8,128)S(1)}, f32[2048,128]{1,0:T(8,128)}, u32[]{:S(2)}) %copy-start.32) | copy-done | bytes 1048600
  93.9 0.9 copy-done.34
  94.8 0.9 copy-done.36
  95.7 0.9 copy-done.38
  96.6 0.9 copy-done.40
  97.5 1.0 copy-done.42
  98.4 0.9 copy-done.44
  99.4 0.9 copy-done.46
  100.3 0.9 copy-done.48
  101.3 0.9 copy-done.50
  102.3 0.9 copy-done.52
  103.2 11.1 %up.1 = (f32[512,128]{1,0:T(8,128)}, f32[512,128]{1,0:T(8,128)}) custom-call(f32[32,40,128]{2,1,0:T(8,128)S(1)} %all-to-all-done.1.refs_0_, f32[512,128]{1,0:T(8,128)S(1)} %bitcast.27, f32[512,128]{1,0:T(8,128)S(1)} %get-tuple-element.52.refs_2_, f32[512,128]{1,0:T(8,128)S(1)} %get-tuple-element.53.refs_3_, f32[512,128]{1,0:T(8,128)S(1)} %get-tuple-element.54.refs_4_, ...), custom_call_target="tpu_custom_call" | custom-call | flops 12000000000 | bytes 11845632 | tf_op jit(solution)/shard_map/up/pallas_call | solution.py:908
  (75 shorter events, 0.2 us)
Async XLA Ops:
  0.6 1.0 copy-start
  1.6 0.9 copy-start.2
  2.5 0.9 copy-start.4
  3.5 0.9 copy-start.6
  4.4 0.9 copy-start.8
  6.0 18.8 %copy-start.13 = (f32[192,128]{1,0:T(8,128)}, f32[192,128]{1,0:T(8,128)S(1)}, u32[]{:S(2)}) copy-start(f32[192,128]{1,0:T(8,128)S(1)} %get-tuple-element.43.share2) | copy-start | bytes 294916
  7.1 30.6 %collective-permute-start.4 = (f32[1472,128]{1,0:T(8,128)}, f32[1472,128]{1,0:T(8,128)S(1)}, u32[]{:S(2)}, u32[]{:S(2)}) collective-permute-start(f32[1472,128]{1,0:T(8,128)} %get-tuple-element.46), channel_id=1, source_target_pairs={{4,0},{8,4},{12,8},{16,12},{20,16},{24,20},{28,24},{5,1},{9,5},{13... | collective-permute-start | bytes 2261000 | tf_op jit(solution)/shard_map/ppermute | solution.py:934
  8.3 29.3 %collective-permute-start.5 = (f32[1472,128]{1,0:T(8,128)S(1)}, f32[1472,128]{1,0:T(8,128)S(1)}, u32[]{:S(2)}, u32[]{:S(2)}) collective-permute-start(f32[1472,128]{1,0:T(8,128)S(1)} %get-tuple-element.47), channel_id=1, source_target_pairs={{0,4},{4,8},{8,12},{12,16},{16,20},{20,24},{24,28},{1,5},{5,9},{9,... | collective-permute-start | bytes 2261000 | tf_op jit(solution)/shard_map/ppermute | solution.py:935
  11.4 7.7 %collective-permute-start = (f32[184,128]{1,0:T(8,128)S(1)}, f32[184,128]{1,0:T(8,128)S(1)}, u32[]{:S(2)}, u32[]{:S(2)}) collective-permute-start(f32[184,128]{1,0:T(8,128)S(1)} %get-tuple-element.41), channel_id=1, source_target_pairs={{1,0},{2,1},{3,2},{5,4},{6,5},{7,6},{9,8},{10,9},{11,10},{13,12},{... | collective-permute-start | bytes 282632 | tf_op jit(solution)/shard_map/ppermute | solution.py:931
  12.7 8.2 %collective-permute-start.1 = (f32[184,128]{1,0:T(8,128)S(1)}, f32[184,128]{1,0:T(8,128)S(1)}, u32[]{:S(2)}, u32[]{:S(2)}) collective-permute-start(f32[184,128]{1,0:T(8,128)S(1)} %get-tuple-element.42), channel_id=1, source_target_pairs={{0,1},{1,2},{2,3},{4,5},{5,6},{6,7},{8,9},{9,10},{10,11},{12,13},{... | collective-permute-start | bytes 282632 | tf_op jit(solution)/shard_map/ppermute | solution.py:932
  21.0 4.9 %collective-permute-start.3 = (f32[208,128]{1,0:T(8,128)S(1)}, f32[208,128]{1,0:T(8,128)S(1)}, u32[]{:S(2)}, u32[]{:S(2)}) collective-permute-start(f32[208,128]{1,0:T(8,128)S(1)} %pad_maximum_fusion.1), channel_id=1, source_target_pairs={{0,4},{4,8},{8,12},{12,16},{16,20},{20,24},{24,28},{1,5},{5,9},{9,... | collective-permute-start | bytes 319496 | tf_op jit(solution)/shard_map/ppermute | solution.py:939
  23.4 14.2 %copy-start.1 = (f32[32,16,128]{2,1,0:T(8,128)S(1)}, f32[32,16,128]{2,1,0:T(8,128)}, u32[]{:S(2)}) copy-start(f32[32,16,128]{2,1,0:T(8,128)} %param.5) | copy-start | bytes 786436
  23.4 14.2 %copy-start.3 = (f32[32,16,128]{2,1,0:T(8,128)S(1)}, f32[32,16,128]{2,1,0:T(8,128)}, u32[]{:S(2)}) copy-start(f32[32,16,128]{2,1,0:T(8,128)} %param.7) | copy-start | bytes 786436
  23.4 4.9 %collective-permute-start.2 = (f32[208,128]{1,0:T(8,128)S(1)}, f32[208,128]{1,0:T(8,128)S(1)}, u32[]{:S(2)}, u32[]{:S(2)}) collective-permute-start(f32[208,128]{1,0:T(8,128)S(1)} %pad_maximum_fusion), channel_id=1, source_target_pairs={{4,0},{8,4},{12,8},{16,12},{20,16},{24,20},{28,24},{5,1},{9,5},{13... | collective-permute-start | bytes 319496 | tf_op jit(solution)/shard_map/ppermute | solution.py:938
  28.3 22.2 %copy-start.11 = (f32[208,128]{1,0:T(8,128)}, f32[208,128]{1,0:T(8,128)S(1)}, u32[]{:S(2)}) copy-start(f32[208,128]{1,0:T(8,128)S(1)} %collective-permute-done.2.refs_7_.cr) | copy-start | bytes 319492
  28.3 32.5 %all-to-all-start = ((f32[16,40,128]{2,1,0:T(8,128)}), f32[16,40,128]{2,1,0:T(8,128)S(1)}, u32[]{:S(2)}, u32[]{:S(2)}) async-start(f32[16,40,128]{2,1,0:T(8,128)} %bitcast.5), calls=%async_computation | async-start | bytes 655360 | tf_op jit(solution)/shard_map/all_to_all | solution.py:943
  37.7 1.0 copy-start.5
  38.6 0.9 copy-start.7
  39.6 0.9 copy-start.9
  50.5 1.0 copy-start.21
  51.5 1.0 copy-start.23
  52.5 1.0 copy-start.25
  53.6 1.0 copy-start.27
  54.6 1.0 copy-start.29
  55.5 1.1 copy-start.31
  56.6 0.7 copy-start.41
  57.3 0.7 copy-start.43
  58.0 0.7 copy-start.45
  58.7 0.7 copy-start.47
  59.4 0.7 copy-start.49
  60.1 0.7 copy-start.51
  60.8 6.2 %copy-start.14 = (f32[192,128]{1,0:T(8,128)S(1)}, f32[192,128]{1,0:T(8,128)}, u32[]{:S(2)}) copy-start(f32[192,128]{1,0:T(8,128)} %copy-done.13) | copy-start | bytes 294916
  60.8 6.2 %copy-start.12 = (f32[208,128]{1,0:T(8,128)S(1)}, f32[208,128]{1,0:T(8,128)}, u32[]{:S(2)}) copy-start(f32[208,128]{1,0:T(8,128)} %copy-done.11) | copy-start | bytes 319492
  60.8 24.7 %all-to-all-start.1 = ((f32[32,40,128]{2,1,0:T(8,128)}), f32[32,40,128]{2,1,0:T(8,128)S(1)}, u32[]{:S(2)}, u32[]{:S(2)}) async-start(f32[32,40,128]{2,1,0:T(8,128)} %bitcast.7), calls=%async_computation.1 | async-start | bytes 1310720 | tf_op jit(solution)/shard_map/all_to_all | solution.py:964
  66.8 3.9 %collective-permute-start.6 = (f32[4,160,128]{2,1,0:T(8,128)S(1)}, f32[4,160,128]{2,1,0:T(8,128)S(1)}, u32[]{:S(2)}, u32[]{:S(2)}) collective-permute-start(f32[4,160,128]{2,1,0:T(8,128)S(1)} %bitcast.10), channel_id=1, source_target_pairs={{0,4},{4,0},{8,12},{12,8},{16,20},{20,16},{24,28},{28,24},{1,5},{5... | collective-permute-start | bytes 983048 | tf_op jit(solution)/shard_map/ppermute | solution.py:963
  69.3 0.7 copy-start.15
  70.0 0.7 copy-start.17
  70.7 14.9 %copy-start.10 = (f32[32,16,128]{2,1,0:T(8,128)S(1)}, f32[32,16,128]{2,1,0:T(8,128)}, u32[]{:S(2)}) copy-start(f32[32,16,128]{2,1,0:T(8,128)} %param.6) | copy-start | bytes 786436
  70.7 14.9 %copy-start.16 = (f32[512,128]{1,0:T(8,128)S(1)}, f32[512,128]{1,0:T(8,128)}, u32[]{:S(2)}) copy-start(f32[512,128]{1,0:T(8,128)} %copy-done.15) | copy-start | bytes 786436
  70.7 14.9 %copy-start.18 = (f32[512,128]{1,0:T(8,128)S(1)}, f32[512,128]{1,0:T(8,128)}, u32[]{:S(2)}) copy-start(f32[512,128]{1,0:T(8,128)} %copy-done.17) | copy-start | bytes 786436
  72.2 0.7 copy-start.19
  72.9 0.7 copy-start.33
  73.6 0.7 copy-start.35
  74.3 0.7 copy-start.37
  74.9 0.6 copy-start.39
  85.6 1.0 copy-start.20
  86.5 1.2 %copy-start.22 = (f32[2112,128]{1,0:T(8,128)S(1)}, f32[2112,128]{1,0:T(8,128)}, u32[]{:S(2)}) copy-start(f32[2112,128]{1,0:T(8,128)} %copy-done.21) | copy-start | bytes 3244036
  87.7 1.2 %copy-start.24 = (f32[2048,128]{1,0:T(8,128)S(1)}, f32[2048,128]{1,0:T(8,128)}, u32[]{:S(2)}) copy-start(f32[2048,128]{1,0:T(8,128)} %copy-done.23) | copy-start | bytes 3145732
  89.0 1.2 %copy-start.26 = (f32[2048,128]{1,0:T(8,128)S(1)}, f32[2048,128]{1,0:T(8,128)}, u32[]{:S(2)}) copy-start(f32[2048,128]{1,0:T(8,128)} %copy-done.25) | copy-start | bytes 3145732
  90.2 1.2 %copy-start.28 = (f32[2048,128]{1,0:T(8,128)S(1)}, f32[2048,128]{1,0:T(8,128)}, u32[]{:S(2)}) copy-start(f32[2048,128]{1,0:T(8,128)} %copy-done.27) | copy-start | bytes 3145732
  91.4 1.2 %copy-start.30 = (f32[2048,128]{1,0:T(8,128)S(1)}, f32[2048,128]{1,0:T(8,128)}, u32[]{:S(2)}) copy-start(f32[2048,128]{1,0:T(8,128)} %copy-done.29) | copy-start | bytes 3145732
  92.6 1.2 %copy-start.32 = (f32[2048,128]{1,0:T(8,128)S(1)}, f32[2048,128]{1,0:T(8,128)}, u32[]{:S(2)}) copy-start(f32[2048,128]{1,0:T(8,128)} %copy-done.31) | copy-start | bytes 3145732
  93.9 0.9 copy-start.34
  94.8 0.9 copy-start.36
  95.7 0.9 copy-start.38
  96.6 0.9 copy-start.40
  97.5 1.0 copy-start.42
  98.4 0.9 copy-start.44
  99.4 0.9 copy-start.46
  100.3 0.9 copy-start.48
  101.3 0.9 copy-start.50
  102.2 0.9 copy-start.52

commit v7 on v6

--- a/solution.py
+++ b/solution.py
@@ -170,6 +170,7 @@
 BLOCK = NZ + 8
 VMEM = pl.BlockSpec(memory_space=pltpu.VMEM)
 ANY = pl.BlockSpec(memory_space=pl.ANY)
+HBM = pl.BlockSpec(memory_space=pltpu.HBM)
 
 
 def iota(shape, dim):
@@ -204,11 +205,11 @@
 
 
 class Field:
-    def __init__(self, ref, rows, tiles=1, planes=NZ):
-        self.ref, self.rows, self.tiles, self.planes = ref, rows, tiles, planes
+    def __init__(self, ref, rows, tiles=1, planes=NZ, start=0):
+        self.ref, self.rows, self.tiles, self.planes, self.start = ref, rows, tiles, planes, start
 
     def base(self, tile, k):
-        return tile * self.planes * self.rows + k * self.rows
+        return self.start + tile * self.planes * self.rows + k * self.rows
 
     def part(self, tile, k):
         return self.ref[span(self.base(tile, k), self.rows), :]
@@ -227,12 +228,18 @@
     def every_second(self, at, count, odd):
         parts = []
         for t in range(self.tiles):
-            first = t * self.planes * self.rows + 2 * at + odd
+            first = self.base(t, 0) + 2 * at + odd
             parts.append(self.ref[pl.ds(first, count, stride=2), :])
         return parts[0] if self.tiles == 1 else jnp.concatenate(parts, axis=1)
 
     def row(self, row):
-        return self.ref[pl.ds(row, self.planes, stride=self.rows), :]
+        return self.ref[pl.ds(self.start + row, self.planes, stride=self.rows), :]
+
+
+def stack_fields(ref, rows, count, tiles=1, z_face=True, start=0):
+    size = tiles * NZ * rows
+    out = [Field(ref, rows, tiles, NZ, start + n * size) for n in range(count)]
+    return out + [Field(ref, rows, tiles, NZ + 1, start + count * size)] if z_face else out
 
 
 def loop(count, step, carry, unroll=None):
@@ -409,16 +416,6 @@
     for n in range(1, 4):
         out = jnp.where(group == n, cells[8 * n : 8 * n + 8], out)
     return pltpu.roll(out, turn, 1)
-
-
-def pack_x_kernel(f, kappa, cx, cy, cz, share2, x_head, x_tail):
-    for a, ref in enumerate((f, kappa, cx, cy, cz)):
-        cells = ref[...].reshape(NZ, TX, TY)
-        at = pl.ds(a * NZ * HALO, NZ * HALO)
-        x_head[at, :] = cells[:, :HALO].reshape(NZ * HALO, TY)
-        x_tail[at, :] = cells[:, TX - HALO :].reshape(NZ * HALO, TY)
-    x_head[pl.ds(SLAB, 6 * NZ), :] = share2[...]
-    x_tail[pl.ds(SLAB, 6 * NZ), :] = share2[...]
 
 
 def share_kernel(devices, share2, copies):
@@ -443,7 +440,26 @@
             copies[pl.ds(n * SHARE + 8 * t, 8), :] = cells
 
 
-def pack_y_kernel(f, kappa, cx, cy, cz, y_head, y_tail, share2):
+def fetch_all(sources, dests, sems, first=0):
+    copies = [pltpu.make_async_copy(a, b, sems.at[first + n]) for n, (a, b) in enumerate(zip(sources, dests))]
+    for copy in copies:
+        copy.start()
+    return copies
+
+
+def pack_kernel(f_in, kappa_in, cx_in, cy_in, cz_in, x_near, x_far, y_near, y_far, share2, stack, sems):
+    even_x, even_y = lax.axis_index("gx") % 2 == 0, lax.axis_index("gy") % 2 == 0
+    tiles = [stack.at[pl.ds(a * NZ * TX, NZ * TX), :] for a in range(5)]
+    for copy in fetch_all((f_in, kappa_in, cx_in, cy_in, cz_in), tiles, sems):
+        copy.wait()
+    f, kappa, cx, cy, cz = tiles
+    for a, ref in enumerate(tiles):
+        cells = ref[...].reshape(NZ, TX, TY)
+        at = pl.ds(a * NZ * HALO, NZ * HALO)
+        head = cells[:, :HALO].reshape(NZ * HALO, TY)
+        tail = cells[:, TX - HALO :].reshape(NZ * HALO, TY)
+        x_near[at, :] = jnp.where(even_x, tail, head)
+        x_far[at, :] = jnp.where(even_x, head, tail)
     y, lane = iota((128, 128), 0), iota((128, 128), 1)
     fourth = y // 4 == lane % 32
     rows = lambda ref: [Field(ref, TX).row(r) for r in range(TX)]
@@ -468,15 +484,16 @@
     tail = [jnp.zeros((8, 128), F32)] * 3
     slot = iota((8, 128), 1) % 32 // 4
     for t, cells in enumerate(kinds):
-        share2[pl.ds(t * NZ, NZ), :] = cells
+        for dest, first in ((share2, 0), (x_near, SLAB), (x_far, SLAB)):
+            dest[pl.ds(first + t * NZ, NZ), :] = cells
         for zv in range(4):
             n = 4 * t + zv
             piece = cells[8 * zv : 8 * zv + 8]
             head[n // 8] = jnp.where(slot == n % 8, shift(piece, 4 * (n % 8), 1), head[n // 8])
             tail[n // 8] = jnp.where(slot == n % 8, shift(piece, 4 * (n % 8) + 4, 1), tail[n // 8])
     for n in range(3):
-        y_head[pl.ds(STRIP + 8 * n, 8), :] = head[n]
-        y_tail[pl.ds(STRIP + 8 * n, 8), :] = tail[n]
+        y_near[pl.ds(STRIP + 8 * n, 8), :] = jnp.where(even_y, tail[n], head[n])
+        y_far[pl.ds(STRIP + 8 * n, 8), :] = jnp.where(even_y, head[n], tail[n])
 
     group = lane_group(8, 8)
     for a, ref in enumerate((f, kappa, cx, cy, cz)):
@@ -490,8 +507,8 @@
                     head = jnp.where(group == zi, cells, head)
                     tail = jnp.where(group == (zi - 1) % 16, cells, tail)
                 at = pl.ds(((half * 5 + a) * 2 + zo) * 8, 8)
-                y_head[at, :] = head
-                y_tail[at, :] = tail
+                y_near[at, :] = jnp.where(even_y, tail, head)
+                y_far[at, :] = jnp.where(even_y, head, tail)
 
 
 def window2(tile, after, before, dest, first, iy, gy):
@@ -503,7 +520,7 @@
         dest[pl.ds(first + xi, NZ, stride=TX), :] = shift(cells, -32 * xi, 1)
 
 
-def window_kernel(share2, xr, xl, yr, yl, cr, cl, x_face, y_face, inv, z_face, a, b, c, d, kappa, cz, diag):
+def window_kernel(share2, x_near, x_far, yr, yl, cr, cl, out, a, b, c, d, kappa, cz, diag):
     ix, iy = lax.axis_index("gx"), lax.axis_index("gy")
     gy = lax.axis_size("gy")
     nx, ny = lax.axis_size("gx") * 4, gy * 32
@@ -517,26 +534,26 @@
         return jnp.concatenate(pieces, axis=0)
 
     near, far = STRIP // 2, CORNER + STRIP // 2
+    even_x = ix % 2 == 0
     for t, dest in enumerate(refs):
-        for first, tile, base, right, left, r_at, l_at in (
-            (0, share2, 0, yr, yl, STRIP, STRIP),
-            (4, xr, SLAB, cr, cr, far, near),
-            (12, xl, SLAB, cl, cl, far, near),
+        beside = x_near[pl.ds(SLAB + t * NZ, NZ), :], x_far[pl.ds(SLAB + t * NZ, NZ), :]
+        for first, cells, right, left, r_at, l_at in (
+            (0, share2[pl.ds(t * NZ, NZ), :], yr, yl, STRIP, STRIP),
+            (4, jnp.where(even_x, *beside), cr, cr, far, near),
+            (12, jnp.where(even_x, *beside[::-1]), cl, cl, far, near),
         ):
-            cells = tile[pl.ds(base + t * NZ, NZ), :]
             window2(cells, unpack(right, r_at, t, 32), unpack(left, l_at, t, 92), dest, first, iy, gy)
         for x in range(8, 12):
             dest[pl.ds(x, NZ, stride=TX), :] = jnp.zeros((NZ, 128), F32)
     mask = window_mask(TX, 128, 4, 32, 4, ix, iy, nx, ny)
-    fields = [Field(ref, TX) for ref in (*refs, x_face, y_face, diag, inv)]
-    a, b, c, d, kappa, cz, x_face, y_face, diag, inv = fields
+    a, b, c, d, kappa, cz, diag = (Field(ref, TX) for ref in (*refs, diag))
+    x_face, y_face, inv, z_face = stack_fields(out, TX, 3)
     for k in range(NZ):
         x_k = a[k] + shift(b[k], 1, 0)
         y_k = c[k] + shift(d[k], 1, 1)
         x_face[k] = x_k
         y_face[k] = y_k
         diag[k] = base_diag(jnp.where(mask > 0, kappa[k], 1.0), x_k, y_k)
-    z_face = Field(z_face, TX, 1, NZ + 1)
     z_faces(cz, z_face)
     factor(diag, z_face, 1, inv, None)
 
@@ -555,8 +572,9 @@
 
 
 def global_kernel(gx, gy, own, other, *refs):
-    outs3, outs4 = refs[:5], refs[5:10]
-    raw3, raw4, shares, sems = refs[10:18], refs[18:26], refs[26], refs[27]
+    out, raw3, raw4, shares, sems = refs[0], refs[1:9], refs[9:17], refs[17], refs[18]
+    outs3 = stack_fields(out, 2 * gx, 5, z_face=False)
+    outs4 = stack_fields(out, gx, 5, z_face=False, start=5 * NZ * 2 * gx)
     core = lax.axis_index("gx") % 2
     copies = [
         pltpu.make_async_copy(own, shares.at[:, core], sems.at[0]),
@@ -602,7 +620,7 @@
         x, y = iota((rows, 128), 0), iota((rows, 128), 1)
         xl, xu, yl, yu, kappa, cz = (Field(ref, rows) for ref in raw[:6])
         z_face, diag = Field(raw[6], rows, 1, NZ + 1), Field(raw[7], rows)
-        x_face, y_face, inv, g, c = (Field(ref, rows) for ref in outs)
+        x_face, y_face, inv, g, c = outs
         inside_x, inside_y = (x > 0).astype(F32), ((y > 0) & (y < cols)).astype(F32)
         for k in range(NZ):
             xl_k, yl_k = xl[k], yl[k]
@@ -615,17 +633,15 @@
 
 
 def down_kernel(nx, ny, *refs):
-    f, kappa, cx, cy, cz, yr, yl, corner_r, corner_l, xr_in, xl_in = refs[:11]
-    sends, outs0, outs1 = refs[11], refs[12:18], refs[18:24]
-    scratch = list(refs[24:-1])
+    stack, yr, yl, corner_r, corner_l, x_near, x_far = refs[:7]
+    sends, saved = refs[7:9]
+    scratch = list(refs[9:-1])
     sems = refs[-1]
     take = lambda n: [scratch.pop(0) for _ in range(n)]
     ix, iy = lax.axis_index("gx"), lax.axis_index("gy")
     gx, gy = lax.axis_size("gx"), lax.axis_size("gy")
-    xr, xl = take(2)
-    fetches = [pltpu.make_async_copy(xr_in, xr, sems.at[12]), pltpu.make_async_copy(xl_in, xl, sems.at[13])]
-    for fetch in fetches:
-        fetch.start()
+    f, kappa, cx, cy, cz = (stack.at[pl.ds(a * NZ * TX, NZ * TX), :] for a in range(5))
+    even_x = ix % 2 == 0
     rows, tiles = 2 * TX, 2
     whole = take(11)
     names = [Field(ref, rows, tiles) for ref in whole[:10]]
@@ -636,7 +652,9 @@
     def window(a, tile, z, after, before, turn):
         zo = z // 16
         slab = span(a * NZ * HALO + z * HALO, HALO)
-        main = jnp.concatenate([tile[span(z * TX, TX), :], xr[slab, :], xl[slab, :]], axis=0)
+        near, far = x_near[slab, :], x_far[slab, :]
+        sides = [jnp.where(even_x, near, far), jnp.where(even_x, far, near)]
+        main = jnp.concatenate([tile[span(z * TX, TX), :], *sides], axis=0)
         at = lambda first: span(first + (a * 2 + zo) * 8, 8)
         half = STRIP // 2
         sides = []
@@ -669,20 +687,26 @@
         diag[z] = base_diag(jnp.where(mask0 > 0, kappa_k, 1.0), x_k, y_k)
         return cz_k
 
-    for fetch in fetches:
-        fetch.wait()
     last = loop(NZ, prepare, jnp.zeros((rows, 256), F32), 2)
     z_face[NZ] = 0.5 * last
     ends = factor(diag, z_face, tiles, inv, 4, f0, kept)
-    sources = [x_face, y_face, inv, z_face, u, f0]
-    copies = [pltpu.make_async_copy(s.ref, o, sems.at[n]) for n, (s, o) in enumerate(zip(sources, outs0))]
-    for n in (0, 1, 2, 3, 5):
-        copies[n].start()
+    copies = []
+
+    def save(field):
+        at = sum(copy[1] for copy in copies)
+        count = field.ref.shape[0]
+        copy = pltpu.make_async_copy(field.ref, saved.at[pl.ds(at, count), :], sems.at[len(copies)])
+        copy.start()
+        copies.append((copy, count))
+
+    for field in (x_face, y_face, inv, f0):
+        save(field)
     smooth_down(f0, x_face, y_face, Line(inv, z_face), ends, kept, u, r, 2)
-    copies[4].start()
+    save(u)
+    save(z_face)
 
     fine = (r, kappa0, cz0, x_face, y_face)
-    lanes, tile_x, tile_y, halo, outs = 256, TX, TY, HALO, outs1
+    lanes, tile_x, tile_y, halo = 256, TX, TY, HALO
     for level in (1, 2):
         rows, tile_x, tile_y, halo = rows // 2, tile_x // 2, tile_y // 2, halo // 2
         nx, ny = nx // 2, ny // 2
@@ -711,11 +735,8 @@
         ends = factor(diag, z_face, 1, inv, None, f1, kept)
         smooth_down(f1, x_face, y_face, Line(inv, z_face), ends, kept, u, r, None)
         if level == 1:
-            sources = [x_face, y_face, inv, z_face, u, f1]
-            more = [pltpu.make_async_copy(s.ref, o, sems.at[6 + n]) for n, (s, o) in enumerate(zip(sources, outs1))]
-            for copy in more:
-                copy.start()
-            copies += more
+            for field in (x_face, y_face, inv, f1, u, z_face):
+                save(field)
         fine, lanes = (r, kappa1, cz1, x_face, y_face), 128
 
     group = lane_group(NZ, 32)
@@ -732,40 +753,27 @@
     total = fold_planes(total, 16 * iy)
     for n in range(gx * gy):
         sends[pl.ds(n * BLOCK + NZ, 8), :] = total
-    for copy in copies:
+    for copy, _ in copies:
         copy.wait()
 
 
 def up_kernel(gx, gy, *refs):
-    gathered, kappa, k3, k4 = refs[0], refs[1], refs[2:7], refs[7:12]
-    saved2, saved0, saved1 = refs[12:16], refs[16:22], refs[22:28]
-    solution_out, residual_out = refs[28:30]
-    scratch = list(refs[30:-1])
+    gathered, whole, k2, stack, saved, solution_out, residual_out = refs[:7]
+    scratch = list(refs[7:-1])
     sems = refs[-1]
     take = lambda n: [scratch.pop(0) for _ in range(n)]
     ix, iy = lax.axis_index("gx"), lax.axis_index("gy")
-    held0, held1, k2, whole3, blocks = take(6), take(6), take(4), take(1)[0], take(1)[0]
-    fetch = pltpu.make_async_copy(gathered.at[:, pl.ds(NZ, 8), :], whole3, sems.at[25])
-    fetch.start()
-    fetches = []
-    sides = [(dx, dy) for dx in (0, 1, -1) for dy in (0, 1, -1)]
-    for n, (dx, dy) in enumerate(sides):
-        device = jnp.clip(ix + dx, 0, gx - 1) * gy + jnp.clip(iy + dy, 0, gy - 1)
-        source = gathered.at[device, pl.ds(0, NZ), :]
-        fetches.append(pltpu.make_async_copy(source, blocks.at[n], sems.at[16 + n]))
-        fetches[-1].start()
-    copies = []
-    for n, (source, dest) in enumerate(zip((*saved2, *saved1, *saved0), (*k2, *held1, *held0))):
-        copies.append(pltpu.make_async_copy(source, dest, sems.at[n]))
-        copies[-1].start()
+    held0, held1 = take(2)
+    split = held0.shape[0]
+    parts = [saved.at[pl.ds(split, held1.shape[0]), :], saved.at[pl.ds(0, split), :]]
+    copy1, copy0 = fetch_all(parts, (held1, held0), sems)
     f2, u2, kept2, wide, e_ref, e0_ref, kept0, u3, f3, r3, f4, u4 = take(12)
 
     rows, cols = 2 * gx, 16 * gy
-    fetch.wait()
-    assemble3(lambda jx, jy: whole3[jx * gy + jy], f3, gx, gy, rows)
+    assemble3(lambda jx, jy: gathered[jx * gy + jy, pl.ds(NZ, 8), :], f3, gx, gy, rows)
     f3, u3, r3 = (Field(ref, rows) for ref in (f3, u3, r3))
     y = iota((rows, 128), 1)
-    x_face3, y_face3, inv3, g3, c3 = (Field(ref, rows) for ref in k3)
+    x_face3, y_face3, inv3, g3, c3 = stack_fields(whole, rows, 5, z_face=False)
     line3 = StoredLine(inv3, g3, c3)
     clean = (y < cols).astype(F32)
     for k in range(NZ):
@@ -779,7 +787,7 @@
     yy, jj = iota((128, 128), 0), iota((128, 128), 1)
     f4[...] = 0.25 * mix(fine.every_second(0, size, 0) + fine.every_second(0, size, 1), matrix(yy // 2 == jj))
     f4, u4 = Field(f4, rows), Field(u4, rows)
-    x_face4, y_face4, inv4, g4, c4 = (Field(ref, rows) for ref in k4)
+    x_face4, y_face4, inv4, g4, c4 = stack_fields(whole, rows, 5, z_face=False, start=5 * NZ * 2 * rows)
     line4 = StoredLine(inv4, g4, c4)
     zero = jnp.zeros((rows, 128), F32)
 
@@ -814,17 +822,16 @@
 
     def block(dx, dy):
         inside = ((ix + dx >= 0) & (ix + dx < gx)).astype(F32)
-        return blocks[sides.index((dx, dy))] * inside
-
-    for copy in fetches + copies[:4]:
-        copy.wait()
+        device = jnp.clip(ix + dx, 0, gx - 1) * gy + jnp.clip(iy + dy, 0, gy - 1)
+        return gathered[device, pl.ds(0, NZ), :] * inside
+
     for first, dx in ((0, 0), (4, 1), (12, -1)):
         window2(block(dx, 0), shift(block(dx, 1), 32, 1), shift(block(dx, -1), 96, 1), f2, first, iy, gy)
     for x in range(8, 12):
         f2[pl.ds(x, NZ, stride=TX), :] = jnp.zeros((NZ, 128), F32)
     f2, u2, kept2 = (Field(ref, TX) for ref in (f2, u2, kept2))
-    x_face2, y_face2, inv2 = (Field(ref, TX) for ref in k2[:3])
-    line2 = Line(inv2, Field(k2[3], TX, 1, NZ + 1))
+    x_face2, y_face2, inv2, z_face2 = stack_fields(k2, TX, 3)
+    line2 = Line(inv2, z_face2)
     zero = jnp.zeros((TX, 128), F32)
     ends = sweep_in(lambda k: f2[k], line2, kept2, zero, None)
 
@@ -850,15 +857,13 @@
     spread_rows(ring(cells), ring(shift(cells, 1, 1)), ring(shift(cells, -1, 1)), wide, NZ * 8)
     fine_y = jnp.where(lane < 96, lane, lane - 128)
     e_ref[...] = mix(wide[pl.ds(0, NZ * TX), :], spread_matrix(fine_y, 0, 0, circular=True), 3)
-    for copy in copies[4:10]:
-        copy.wait()
-    x_face1, y_face1, inv1, z_face1, u1, f1 = held1
-    x_face1, y_face1, inv1, u1, f1 = (Field(ref, TX) for ref in (x_face1, y_face1, inv1, u1, f1))
-    line1 = Line(inv1, Field(z_face1, TX, 1, NZ + 1))
+    copy1.wait()
+    x_face1, y_face1, inv1, f1, u1, z_face1 = stack_fields(held1, TX, 5)
+    line1 = Line(inv1, z_face1)
     mask1 = window_mask(TX, 128, 8, 64, 4, ix, iy, 8 * gx, 64 * gy)
     smooth_up(f1, x_face1, y_face1, line1, u1, Field(e_ref, TX), kept2, mask1, None)
 
-    cells = u1.ref[...].reshape(NZ, TX, 128)
+    cells = held1[pl.ds(u1.start, NZ * TX), :].reshape(NZ, TX, 128)
     spread_rows(cells, shift(cells, 1, 1), shift(cells, -1, 1), wide, NZ * TX)
     rows = 2 * TX
     weights = spread_matrix(iota((128, 256), 1), 0, 0, circular=True)
@@ -867,15 +872,12 @@
         cells = mix(wide[pl.ds(k * rows, 8 * rows), :], weights, 3)
         for t in range(2):
             e0_ref[pl.ds(e0.base(t, k), 8 * rows), :] = cells[:, 128 * t : 128 * (t + 1)]
-    for copy in copies[10:]:
-        copy.wait()
-    x_face0, y_face0, inv0, z_face0, u0, f0 = held0
-    x_face0, y_face0, inv0, u0, f0 = (Field(ref, rows, 2) for ref in (x_face0, y_face0, inv0, u0, f0))
-    z_face0 = Field(z_face0, rows, 2, NZ + 1)
+    copy0.wait()
+    x_face0, y_face0, inv0, f0, u0, z_face0 = stack_fields(held0, rows, 5, 2)
     mask0 = window_mask(rows, 256, TX, TY, HALO, ix, iy, TX * gx, TY * gy)
     smooth_up(f0, x_face0, y_face0, Line(inv0, z_face0), u0, e0, Field(kept0, rows, 2), mask0, 2)
 
-    kappa = Field(kappa, TX)
+    kappa = Field(stack, TX, start=NZ * TX)
 
     def residual(k, carry):
         below, flux_z = carry
@@ -897,8 +899,9 @@
     residual(NZ - 1, carry)
 
 
+MEBIBYTES = {"pack": 56, "down": 32, "up": 32}
 COSTS = {
-    "pack_y": 2 * 10**9, "pack_x": 2 * 10**9, "share": 10**9, "down": 10**10,
+    "pack": 3 * 10**9, "share": 10**9, "down": 10**10,
     "window_coeffs": 4 * 10**9, "global_coeffs": 4 * 10**9, "up": 12 * 10**9,
 }
 
@@ -913,7 +916,7 @@
         out_specs=out_specs or [VMEM] * len(outs),
         scratch_shapes=list(scratch),
         input_output_aliases=aliases or {},
-        compiler_params=pltpu.CompilerParams(vmem_limit_bytes=(32 if name in ("down", "up") else 16) * 1024 * 1024),
+        compiler_params=pltpu.CompilerParams(vmem_limit_bytes=MEBIBYTES.get(name, 16) * 1024 * 1024),
         cost_estimate=pl.CostEstimate(flops=COSTS[name], bytes_accessed=4 * sum(x.size for x in ins), transcendentals=0),
     )(*ins)
 
@@ -925,19 +928,25 @@
     vm = lambda *shape: pltpu.VMEM(shape, F32)
     dma = lambda n: pltpu.SemaphoreType.DMA((n,))
     devices = gx * gy
-    up = lambda n: [(i, i + 1) for i in range(n - 1)]
-    down = lambda n: [(i + 1, i) for i in range(n - 1)]
-    y_head, y_tail, share2 = call(pack_y_kernel, "pack_y", [strip, strip, (6 * NZ, 128)], tiles)
-    yr = lax.ppermute(y_head, "gy", down(gy))
-    yl = lax.ppermute(y_tail, "gy", up(gy))
-    x_head, x_tail = call(pack_x_kernel, "pack_x", [slab, slab], [*tiles, share2])
-    xr = lax.ppermute(x_head, "gx", down(gx))
-    xl = lax.ppermute(x_tail, "gx", up(gx))
+    near = lambda n: [(i, i ^ 1) for i in range(n)]
+    far = lambda n: [(i, (i + 1 ^ 1) - 1) for i in range(1, n - 1)]
+    even_x, even_y = lax.axis_index("gx") % 2 == 0, lax.axis_index("gy") % 2 == 0
+    x_near, x_far, y_near, y_far, share2, stack = call(
+        pack_kernel, "pack", [slab, slab, strip, strip, (6 * NZ, 128), (5 * NZ * TX, TY)], tiles, [dma(5)], [HBM] * 5
+    )
+    y_near = lax.ppermute(y_near, "gy", near(gy))
+    y_far = lax.ppermute(y_far, "gy", far(gy))
+    x_near = lax.ppermute(x_near, "gx", near(gx))
+    x_far = lax.ppermute(x_far, "gx", far(gx))
+    yr, yl = jnp.where(even_y, y_near, y_far), jnp.where(even_y, y_far, y_near)
     copies = call(functools.partial(share_kernel, devices // 2), "share", [(devices // 2 * SHARE, 128)], [share2])[0]
     half = STRIP // 2
-    corner_r = lax.ppermute(jnp.concatenate([yl[:half], yl[STRIP:], yr[:half], yr[STRIP:]]), "gx", down(gx))
-    corner_l = lax.ppermute(jnp.concatenate([yl[half:], yr[half:]]), "gx", up(gx))
-    copies, corner_r, corner_l = lax.optimization_barrier((copies, corner_r, corner_l))
+    head = jnp.concatenate([yl[:half], yl[STRIP:], yr[:half], yr[STRIP:]])
+    tail = jnp.concatenate([yl[half:], yr[half:]])
+    c_near = lax.ppermute(jnp.where(even_x, tail, head), "gx", near(gx))
+    c_far = lax.ppermute(jnp.where(even_x, head, tail), "gx", far(gx))
+    copies, c_near, c_far = lax.optimization_barrier((copies, c_near, c_far))
+    corner_r, corner_l = jnp.where(even_x, c_near, c_far), jnp.where(even_x, c_far, c_near)
     cores = [[x * gy + y for x in range(core, gx, 2) for y in range(gy)] for core in range(2)]
     blocks = copies.reshape(devices // 2, SHARE, 128)
     own = lax.all_to_all(blocks, ("gx", "gy"), 0, 0, axis_index_groups=cores).reshape(gx // 2, gy * SHARE, 128)
@@ -946,41 +955,38 @@
     rows3, rows4 = 2 * gx, gx
     size, tall = (NZ * TX, 128), ((NZ + 1) * TX, 128)
     k2 = call(
-        window_kernel, "window_coeffs", [size, size, size, tall], [share2, xr, xl, yr, yl, corner_r, corner_l], level(TX, 7)
-    )
+        window_kernel, "window_coeffs", [(NZ * TX * 4 + TX, 128)], [share2, x_near, x_far, yr, yl, corner_r, corner_l], level(TX, 7)
+    )[0]
     big, big_z = (2 * NZ * 2 * TX, 128), (2 * (NZ + 1) * 2 * TX, 128)
-    sends, *saved = call(
+    total0, total1 = 2 * (NZ * 6 + 1) * 2 * TX, (NZ * 6 + 1) * TX
+    sends, saved = call(
         functools.partial(down_kernel, gx * TX, gy * TY),
         "down",
-        [(devices * BLOCK, 128), big, big, big, big_z, big, big, size, size, size, tall, size, size],
-        [*tiles, yr, yl, corner_r, corner_l, xr, xl],
-        [vm(*slab)] * 2 + [vm(*big)] * 10 + [vm(*big_z)] + level(TX, 10) + [faces(TX, 1)] + level(8, 10) + [faces(8, 1)]
-        + [dma(14)],
-        in_specs=[VMEM] * 9 + [ANY] * 2,
-        out_specs=[VMEM] + [ANY] * 12,
+        [(devices * BLOCK, 128), (total0 + total1, 128)],
+        [stack, yr, yl, corner_r, corner_l, x_near, x_far],
+        [vm(*big)] * 10 + [vm(*big_z)] + level(TX, 10) + [faces(TX, 1)] + level(8, 10) + [faces(8, 1)] + [dma(12)],
+        out_specs=[VMEM, ANY],
     )
     sends, own = lax.optimization_barrier((sends, own))
-    other = lax.ppermute(own, "gx", [(i, i ^ 1) for i in range(gx)])
+    other = lax.ppermute(own, "gx", near(gx))
     gathered = lax.all_to_all(sends.reshape(devices, BLOCK, 128), ("gx", "gy"), 0, 0)
     whole = call(
         functools.partial(global_kernel, gx, gy),
         "global_coeffs",
-        [(NZ * rows3, 128)] * 5 + [(NZ * rows4, 128)] * 5,
+        [(5 * NZ * (rows3 + rows4), 128)],
         [own, other],
         level(rows3, 6) + [faces(rows3, 1)] + level(rows3, 1) + level(rows4, 6) + [faces(rows4, 1)] + level(rows4, 1)
         + [vm(gx // 2, 2, gy * SHARE, 128), dma(2)],
         in_specs=[ANY] * 2,
-    )
+    )[0]
     field, residual = call(
         functools.partial(up_kernel, gx, gy),
         "up",
         [(NZ * TX, TY)] * 2,
-        [gathered, tiles[1], *whole, *k2, *saved],
-        [vm(*big), vm(*big), vm(*big), vm(*big_z), vm(*big), vm(*big), vm(*size), vm(*size), vm(*size), vm(*tall), vm(*size), vm(*size)]
-        + [vm(*size), vm(*size), vm(*size), vm(*tall), vm(devices, 8, 128), vm(9, NZ, 128)]
-        + level(TX, 3) + [vm(NZ * 2 * TX, 128), vm(*size), vm(*big), vm(*big)]
-        + level(rows3, 3) + level(rows4, 2) + [dma(26)],
-        in_specs=[ANY] + [VMEM] * 11 + [ANY] * 16,
+        [gathered, whole, k2, stack, saved],
+        [vm(total0, 128), vm(total1, 128)] + level(TX, 3) + [vm(NZ * 2 * TX, 128), vm(*size), vm(*big), vm(*big)]
+        + level(rows3, 3) + level(rows4, 2) + [dma(2)],
+        in_specs=[VMEM] * 4 + [ANY],
     )
     return field.reshape(right_side.shape), residual.reshape(right_side.shape)
 

time: 116 us -> 85.2 us (0.73); the launches traced: 114 us -> 84.8 us
  local copies, waits for them, and re-layouts: 40.3 us -> 12.5 us
  waiting for transfers between devices: 15.1 us -> 13.9 us
    unnamed x106 -> x20, local copies, waits for them, and re-layouts: 40.2 us -> 12.5 us
    ppermute x7, starting transfers between devices: 15.2 us -> 8.79 us  [the longest x1 3.37 us: body(): c_near = lax.ppermute(jnp.where(even_x, tail, head), 'gx', near(gx))]
    all_to_all x1, starting transfers between devices: 9.32 us -> 14.7 us  [body(): lax.all_to_all(blocks, ('gx', 'gy'), 0, 0, axis_index_groups=cores)]
    ppermute x7, waiting for transfers between devices: 5.13 us -> 1.45 us  [the longest x1 1.44 us: body(): y_near = lax.ppermute(y_near, 'gy', near(gy))]
    all_to_all x1, waiting for transfers between devices: 9.99 us -> 12.5 us  [body(): lax.all_to_all(sends.reshape(devices, BLOCK, 128), ('gx', 'gy'), 0, 0)]
    pallas_call x7 -> x6, Pallas kernels: 27.5 us -> 28 us  [call(): pl.pallas_call(kernel, name=name, out_shape=shapes, in_specs=in_specs or...]
  transfers between devices with their start and end apart: 9 -> 9, of which waited for: 4 -> 2; matrix products, arithmetic and copies ran while one was open for 0% -> 0% of each run, Pallas kernels for 13% -> 17%
where the time goes in v7:
time: 85.2 us; the launch traced here: 84.8 us
  starting transfers between devices  29.4 us (35%)
  Pallas kernels  28 us (33%)
  waiting for transfers between devices  13.9 us (16%)
  local copies, waits for them, and re-layouts  12.5 us (15%)
    pallas_call x6, Pallas kernels, call(): pl.pallas_call(kernel, name=name, out_shape=shapes, in_specs=in_specs or...  28 us
    all_to_all x1, starting transfers between devices, body(): lax.all_to_all(blocks, ('gx', 'gy'), 0, 0, axis_index_groups=cores)  14.7 us
    unnamed x20, local copies, waits for them, and re-layouts  12.5 us
    all_to_all x1, waiting for transfers between devices, body(): lax.all_to_all(sends.reshape(devices, BLOCK, 128), ('gx', 'gy'), 0, 0)  12.5 us
    all_to_all x1, starting transfers between devices, body(): lax.all_to_all(sends.reshape(devices, BLOCK, 128), ('gx', 'gy'), 0, 0)  5.9 us
    ppermute x1, starting transfers between devices, body(): c_near = lax.ppermute(jnp.where(even_x, tail, head), 'gx', near(gx))  3.37 us
    ppermute x1, starting transfers between devices, body(): y_near = lax.ppermute(y_near, 'gy', near(gy))  3 us
  transfers between devices with their start and end apart: 9, of which 2 were waited for; matrix products, arithmetic and copies ran while one was open for 0% of the time, Pallas kernels for 17%

profile of v7, /device:TPU:0, one launch (start us, length us, event | category | flops | bytes accessed | tf_op | source)
XLA Modules:
  0.0 84.8 jit_solution(12358427714132490344)
XLA Ops:
  0.6 3.2 %pack.1 = (f32[1472,128]{1,0:T(8,128)}, f32[1472,128]{1,0:T(8,128)}, f32[184,128]{1,0:T(8,128)}, f32[184,128]{1,0:T(8,128)}, f32[192,128]{1,0:T(8,128)}, /*index=5*/f32[2560,128]{1,0:T(8,128)}) custom-call(f32[512,128]{1,0:T(8,128)} %bitcast.12, f32[512,128]{1,0:T(8,128)} %bitcast.13, f32[512,128]{1,0:T(8,128)} %bitcast.14, f32[512,128]{1,0:T(8,128)} %bitcast.15, ...), custom_call_target="tpu_custom_call" | custom-call | flops 3000000000 | bytes 1310720 | tf_op jit(solution)/shard_map/pack/pallas_call | solution.py:911
  3.8 3.0 %collective-permute-start = (f32[184,128]{1,0:T(8,128)}, f32[184,128]{1,0:T(8,128)S(1)}, u32[]{:S(2)}, u32[]{:S(2)}) collective-permute-start(f32[184,128]{1,0:T(8,128)} %get-tuple-element.18), channel_id=1, source_target_pairs={{0,1},{1,0},{2,3},{3,2},{4,5},{5,4},{6,7},{7,6},{8,9},{9,8},{10,11... | collective-permute-start | bytes 282632 | tf_op jit(solution)/shard_map/ppermute | solution.py:937
  6.8 0.7 collective-permute-start.1
  7.5 0.1 collective-permute-start.4
  7.6 0.7 collective-permute-start.5
  8.3 1.4 %collective-permute-done = f32[184,128]{1,0:T(8,128)S(1)} collective-permute-done((f32[184,128]{1,0:T(8,128)}, f32[184,128]{1,0:T(8,128)S(1)}, u32[]{:S(2)}, u32[]{:S(2)}) %collective-permute-start) | collective-permute-done | bytes 94240 | tf_op jit(solution)/shard_map/ppermute | solution.py:937
  9.7 0.0 collective-permute-done.1
  9.9 0.7 collective-permute-start.3
  10.6 3.4 %collective-permute-start.2 = (f32[208,128]{1,0:T(8,128)S(1)}, f32[208,128]{1,0:T(8,128)S(1)}, u32[]{:S(2)}, u32[]{:S(2)}) collective-permute-start(f32[208,128]{1,0:T(8,128)S(1)} %get-tuple-element.35), channel_id=1, source_target_pairs={{0,4},{4,0},{8,12},{12,8},{16,20},{20,16},{24,28},{28,24},{1,5},{5... | collective-permute-start | bytes 319496 | tf_op jit(solution)/shard_map/ppermute | solution.py:946
  13.9 0.0 copy-start.4
  13.9 0.9 %copy-done.4 = f32[192,128]{1,0:T(8,128)S(1)} copy-done((f32[192,128]{1,0:T(8,128)S(1)}, f32[192,128]{1,0:T(8,128)}, u32[]{:S(2)}) %copy-start.4) | copy-done | bytes 98328
  14.8 1.0 %share.1 = f32[640,128]{1,0:T(8,128)} custom-call(f32[192,128]{1,0:T(8,128)S(1)} %copy-done.4), custom_call_target="tpu_custom_call" | custom-call | flops 1000000000 | bytes 98304 | tf_op jit(solution)/shard_map/share/pallas_call | solution.py:911
  15.8 0.0 collective-permute-done.3
  15.8 0.0 collective-permute-done.2
  15.8 14.7 %all-to-all-start = ((f32[16,40,128]{2,1,0:T(8,128)}), f32[16,40,128]{2,1,0:T(8,128)S(1)}, u32[]{:S(2)}, u32[]{:S(2)}) async-start(f32[16,40,128]{2,1,0:T(8,128)} %bitcast.5), calls=%async_computation | async-start | bytes 655360 | tf_op jit(solution)/shard_map/all_to_all | solution.py:952
  30.6 0.0 collective-permute-done.4.refs_5_.x_near
  30.6 0.0 collective-permute-done.5.refs_6_.x_far
  30.6 0.0 copy-start
  30.6 1.3 %copy-done = f32[2560,128]{1,0:T(8,128)S(1)} copy-done((f32[2560,128]{1,0:T(8,128)S(1)}, f32[2560,128]{1,0:T(8,128)}, u32[]{:S(2)}) %copy-start) | copy-done | bytes 1310744
  31.9 0.0 copy-start.5
  31.9 9.3 %down.1 = (f32[1280,128]{1,0:T(8,128)}, f32[15440,128]{1,0:T(8,128)S(1)}) custom-call(f32[2560,128]{1,0:T(8,128)S(1)} %copy-done, f32[184,128]{1,0:T(8,128)S(1)} %get-tuple-element.37.refs_1_.yr, f32[184,128]{1,0:T(8,128)S(1)} %get-tuple-element.36.refs_2_.yl, f32[208,128]{1,0:T(8,128)S(1)} %get-tuple-element.33.refs_3_.cr, ...), custom_call_target="tpu_custom_call" | custom-call | flops 10000000000 | bytes 3219456 | tf_op jit(solution)/shard_map/down/pallas_call | solution.py:911
  41.2 0.0 copy-start.6
  41.2 3.2 %copy-done.6 = f32[15440,128]{1,0:T(8,128)} copy-done((f32[15440,128]{1,0:T(8,128)}, f32[15440,128]{1,0:T(8,128)S(1)}, u32[]{:S(2)}) %copy-start.6) | copy-done | bytes 7905304
  44.4 0.0 all-to-all-done
  44.4 5.9 %all-to-all-start.1 = ((f32[32,40,128]{2,1,0:T(8,128)}), f32[32,40,128]{2,1,0:T(8,128)S(1)}, u32[]{:S(2)}, u32[]{:S(2)}) async-start(f32[32,40,128]{2,1,0:T(8,128)} %bitcast.7), calls=%async_computation.1 | async-start | bytes 1310720 | tf_op jit(solution)/shard_map/all_to_all | solution.py:972
  50.3 0.3 collective-permute-start.6
  50.6 0.0 copy-done.5
  50.6 2.2 %window_coeffs.1.refs_2_ = f32[2064,128]{1,0:T(8,128)S(1)} custom-call(f32[192,128]{1,0:T(8,128)S(1)} %copy-done.5, f32[1472,128]{1,0:T(8,128)S(1)} %collective-permute-done.4.refs_5_.x_near, f32[1472,128]{1,0:T(8,128)S(1)} %collective-permute-done.5.refs_6_.x_far, f32[184,128]{1,0:T(8,128)S(1)} %get-tuple-element.37.refs_1_.yr, ...), custom_call_target="tpu_custom_call" | custom-call | flops 4000000000 | bytes 2007040 | tf_op jit(solution)/shard_map/window_coeffs/pallas_call | solution.py:911
  52.8 0.0 copy-start.8
  52.8 1.0 %copy-done.8 = f32[2064,128]{1,0:T(8,128)} copy-done((f32[2064,128]{1,0:T(8,128)}, f32[2064,128]{1,0:T(8,128)S(1)}, u32[]{:S(2)}) %copy-start.8) | copy-done | bytes 1056792
  53.9 0.0 copy-start.1
  53.9 0.0 collective-permute-done.6.other
  53.9 0.0 copy-start.9
  53.9 1.5 %global_coeffs.1.refs_1_ = f32[3840,128]{1,0:T(8,128)S(1)} custom-call(f32[4,160,128]{2,1,0:T(8,128)S(1)} %bitcast.11, f32[4,160,128]{2,1,0:T(8,128)S(1)} %collective-permute-done.6.other), custom_call_target="tpu_custom_call" | custom-call | flops 4000000000 | bytes 655360 | tf_op jit(solution)/shard_map/global_coeffs/pallas_call | solution.py:911
  55.4 0.0 copy-start.2
  55.4 1.3 %copy-done.2 = f32[3840,128]{1,0:T(8,128)} copy-done((f32[3840,128]{1,0:T(8,128)}, f32[3840,128]{1,0:T(8,128)S(1)}, u32[]{:S(2)}) %copy-start.2) | copy-done | bytes 1966104
  56.7 12.5 %all-to-all-done.1.refs_0_ = f32[32,40,128]{2,1,0:T(8,128)S(1)} async-done(((f32[32,40,128]{2,1,0:T(8,128)}), f32[32,40,128]{2,1,0:T(8,128)S(1)}, u32[]{:S(2)}, u32[]{:S(2)}) %all-to-all-start.1) | async-done | bytes 655392 | tf_op jit(solution)/shard_map/all_to_all | solution.py:972
  69.1 0.0 copy-done.1
  69.1 0.0 copy-done.9
  69.1 0.0 copy-start.3
  69.1 1.5 %copy-done.3 = f32[3840,128]{1,0:T(8,128)S(1)} copy-done((f32[3840,128]{1,0:T(8,128)S(1)}, f32[3840,128]{1,0:T(8,128)}, u32[]{:S(2)}) %copy-start.3) | copy-done | bytes 1966104
  70.7 0.0 copy-start.7
  70.7 3.2 %copy-done.7 = f32[15440,128]{1,0:T(8,128)S(1)} copy-done((f32[15440,128]{1,0:T(8,128)S(1)}, f32[15440,128]{1,0:T(8,128)}, u32[]{:S(2)}) %copy-start.7) | copy-done | bytes 7905304
  73.9 10.8 %up.1 = (f32[512,128]{1,0:T(8,128)}, f32[512,128]{1,0:T(8,128)}) custom-call(f32[32,40,128]{2,1,0:T(8,128)S(1)} %all-to-all-done.1.refs_0_, f32[3840,128]{1,0:T(8,128)S(1)} %copy-done.3, f32[2064,128]{1,0:T(8,128)S(1)} %copy-done.9, f32[2560,128]{1,0:T(8,128)S(1)} %copy-done.1, f32[15440,128]{1,0:T(8,128)S(1)} %copy-done.7), custom_call_target="tpu_custom_call" | custom-call | flops 12000000000 | bytes 12894208 | tf_op jit(solution)/shard_map/up/pallas_call | solution.py:911
  (9 shorter events, 0.1 us)
Async XLA Ops:
  3.8 5.9 %collective-permute-start = (f32[184,128]{1,0:T(8,128)}, f32[184,128]{1,0:T(8,128)S(1)}, u32[]{:S(2)}, u32[]{:S(2)}) collective-permute-start(f32[184,128]{1,0:T(8,128)} %get-tuple-element.18), channel_id=1, source_target_pairs={{0,1},{1,0},{2,3},{3,2},{4,5},{5,4},{6,7},{7,6},{8,9},{9,8},{10,11... | collective-permute-start | bytes 282632 | tf_op jit(solution)/shard_map/ppermute | solution.py:937
  6.8 2.9 %collective-permute-start.1 = (f32[184,128]{1,0:T(8,128)}, f32[184,128]{1,0:T(8,128)S(1)}, u32[]{:S(2)}, u32[]{:S(2)}) collective-permute-start(f32[184,128]{1,0:T(8,128)} %get-tuple-element.19), channel_id=1, source_target_pairs={{1,2},{2,1},{5,6},{6,5},{9,10},{10,9},{13,14},{14,13},{17,18},{18,... | collective-permute-start | bytes 282632 | tf_op jit(solution)/shard_map/ppermute | solution.py:938
  7.5 23.1 %collective-permute-start.4 = (f32[1472,128]{1,0:T(8,128)}, f32[1472,128]{1,0:T(8,128)S(1)}, u32[]{:S(2)}, u32[]{:S(2)}) collective-permute-start(f32[1472,128]{1,0:T(8,128)} %get-tuple-element.23), channel_id=1, source_target_pairs={{0,4},{4,0},{8,12},{12,8},{16,20},{20,16},{24,28},{28,24},{1,5},{5... | collective-permute-start | bytes 2261000 | tf_op jit(solution)/shard_map/ppermute | solution.py:939
  7.6 23.0 %collective-permute-start.5 = (f32[1472,128]{1,0:T(8,128)}, f32[1472,128]{1,0:T(8,128)S(1)}, u32[]{:S(2)}, u32[]{:S(2)}) collective-permute-start(f32[1472,128]{1,0:T(8,128)} %get-tuple-element.24), channel_id=1, source_target_pairs={{4,8},{8,4},{12,16},{16,12},{20,24},{24,20},{5,9},{9,5},{13,17},{1... | collective-permute-start | bytes 2261000 | tf_op jit(solution)/shard_map/ppermute | solution.py:940
  9.9 6.0 %collective-permute-start.3 = (f32[208,128]{1,0:T(8,128)S(1)}, f32[208,128]{1,0:T(8,128)S(1)}, u32[]{:S(2)}, u32[]{:S(2)}) collective-permute-start(f32[208,128]{1,0:T(8,128)S(1)} %get-tuple-element.34), channel_id=1, source_target_pairs={{4,8},{8,4},{12,16},{16,12},{20,24},{24,20},{5,9},{9,5},{13,17},{1... | collective-permute-start | bytes 319496 | tf_op jit(solution)/shard_map/ppermute | solution.py:947
  10.6 5.3 %collective-permute-start.2 = (f32[208,128]{1,0:T(8,128)S(1)}, f32[208,128]{1,0:T(8,128)S(1)}, u32[]{:S(2)}, u32[]{:S(2)}) collective-permute-start(f32[208,128]{1,0:T(8,128)S(1)} %get-tuple-element.35), channel_id=1, source_target_pairs={{0,4},{4,0},{8,12},{12,8},{16,20},{20,16},{24,28},{28,24},{1,5},{5... | collective-permute-start | bytes 319496 | tf_op jit(solution)/shard_map/ppermute | solution.py:946
  13.9 0.9 %copy-start.4 = (f32[192,128]{1,0:T(8,128)S(1)}, f32[192,128]{1,0:T(8,128)}, u32[]{:S(2)}) copy-start(f32[192,128]{1,0:T(8,128)} %get-tuple-element.20.share2) | copy-start | bytes 294916
  15.8 28.6 %all-to-all-start = ((f32[16,40,128]{2,1,0:T(8,128)}), f32[16,40,128]{2,1,0:T(8,128)S(1)}, u32[]{:S(2)}, u32[]{:S(2)}) async-start(f32[16,40,128]{2,1,0:T(8,128)} %bitcast.5), calls=%async_computation | async-start | bytes 655360 | tf_op jit(solution)/shard_map/all_to_all | solution.py:952
  30.6 1.3 %copy-start = (f32[2560,128]{1,0:T(8,128)S(1)}, f32[2560,128]{1,0:T(8,128)}, u32[]{:S(2)}) copy-start(f32[2560,128]{1,0:T(8,128)} %get-tuple-element.17.refs_0_.refs_3_) | copy-start | bytes 3932164
  31.9 18.7 %copy-start.5 = (f32[192,128]{1,0:T(8,128)S(1)}, f32[192,128]{1,0:T(8,128)}, u32[]{:S(2)}) copy-start(f32[192,128]{1,0:T(8,128)} %get-tuple-element.20.share2) | copy-start | bytes 294916
  41.2 3.2 %copy-start.6 = (f32[15440,128]{1,0:T(8,128)}, f32[15440,128]{1,0:T(8,128)S(1)}, u32[]{:S(2)}) copy-start(f32[15440,128]{1,0:T(8,128)S(1)} %get-tuple-element.29.refs_4_) | copy-start | bytes 23715844
  44.4 24.7 %all-to-all-start.1 = ((f32[32,40,128]{2,1,0:T(8,128)}), f32[32,40,128]{2,1,0:T(8,128)S(1)}, u32[]{:S(2)}, u32[]{:S(2)}) async-start(f32[32,40,128]{2,1,0:T(8,128)} %bitcast.7), calls=%async_computation.1 | async-start | bytes 1310720 | tf_op jit(solution)/shard_map/all_to_all | solution.py:972
  50.3 3.5 %collective-permute-start.6 = (f32[4,160,128]{2,1,0:T(8,128)S(1)}, f32[4,160,128]{2,1,0:T(8,128)S(1)}, u32[]{:S(2)}, u32[]{:S(2)}) collective-permute-start(f32[4,160,128]{2,1,0:T(8,128)S(1)} %bitcast.10), channel_id=1, source_target_pairs={{0,4},{4,0},{8,12},{12,8},{16,20},{20,16},{24,28},{28,24},{1,5},{5... | collective-permute-start | bytes 983048 | tf_op jit(solution)/shard_map/ppermute | solution.py:971
  52.8 1.0 %copy-start.8 = (f32[2064,128]{1,0:T(8,128)}, f32[2064,128]{1,0:T(8,128)S(1)}, u32[]{:S(2)}) copy-start(f32[2064,128]{1,0:T(8,128)S(1)} %window_coeffs.1.refs_2_) | copy-start | bytes 3170308
  53.9 15.3 %copy-start.1 = (f32[2560,128]{1,0:T(8,128)S(1)}, f32[2560,128]{1,0:T(8,128)}, u32[]{:S(2)}) copy-start(f32[2560,128]{1,0:T(8,128)} %get-tuple-element.17.refs_0_.refs_3_) | copy-start | bytes 3932164
  53.9 15.3 %copy-start.9 = (f32[2064,128]{1,0:T(8,128)S(1)}, f32[2064,128]{1,0:T(8,128)}, u32[]{:S(2)}) copy-start(f32[2064,128]{1,0:T(8,128)} %copy-done.8) | copy-start | bytes 3170308
  55.4 1.3 %copy-start.2 = (f32[3840,128]{1,0:T(8,128)}, f32[3840,128]{1,0:T(8,128)S(1)}, u32[]{:S(2)}) copy-start(f32[3840,128]{1,0:T(8,128)S(1)} %global_coeffs.1.refs_1_) | copy-start | bytes 5898244
  69.1 1.5 %copy-start.3 = (f32[3840,128]{1,0:T(8,128)S(1)}, f32[3840,128]{1,0:T(8,128)}, u32[]{:S(2)}) copy-start(f32[3840,128]{1,0:T(8,128)} %copy-done.2) | copy-start | bytes 5898244
  70.7 3.2 %copy-start.7 = (f32[15440,128]{1,0:T(8,128)S(1)}, f32[15440,128]{1,0:T(8,128)}, u32[]{:S(2)}) copy-start(f32[15440,128]{1,0:T(8,128)} %copy-done.6) | copy-start | bytes 23715844

commit v8 on v7

--- a/solution.py
+++ b/solution.py
@@ -743,7 +743,7 @@
     out = f1.row(0)
     for xi in range(1, 4):
         out = jnp.where(group == xi, shift(f1.row(xi), 32 * xi, 1), out)
-    for n in range(gx * gy):
+    for n in range(gx * gy // 2):
         sends[pl.ds(n * BLOCK, NZ), :] = out
     y, lane = iota((128, 128), 0), iota((128, 128), 1)
     total = jnp.zeros((NZ, 128), F32)
@@ -751,26 +751,33 @@
         place = (lane % 32 // 16 == xi) & (y // 2 == lane % 16) & (y < 32)
         total = total + mix(r.row(2 * xi) + r.row(2 * xi + 1), matrix(place, 0.25))
     total = fold_planes(total, 16 * iy)
-    for n in range(gx * gy):
+    for n in range(gx * gy // 2):
         sends[pl.ds(n * BLOCK + NZ, 8), :] = total
     for copy, _ in copies:
         copy.wait()
 
 
 def up_kernel(gx, gy, *refs):
-    gathered, whole, k2, stack, saved, solution_out, residual_out = refs[:7]
-    scratch = list(refs[7:-1])
+    own, other, whole, k2, stack, saved, solution_out, residual_out = refs[:8]
+    scratch = list(refs[8:-1])
     sems = refs[-1]
     take = lambda n: [scratch.pop(0) for _ in range(n)]
     ix, iy = lax.axis_index("gx"), lax.axis_index("gy")
     held0, held1 = take(2)
     split = held0.shape[0]
     parts = [saved.at[pl.ds(split, held1.shape[0]), :], saved.at[pl.ds(0, split), :]]
-    copy1, copy0 = fetch_all(parts, (held1, held0), sems)
+    fetched = fetch_all(parts, (held1, held0), sems)
+    core = ix % 2
+
+    def gathered(jx, jy, at):
+        if isinstance(jx, int):
+            same = core == jx % 2
+            return jnp.where(same, own[jx // 2 * gy + jy, at, :], other[jx // 2 * gy + jy, at, :])
+        return jx[1][jx[0] // 2 * gy + jy, at, :]
     f2, u2, kept2, wide, e_ref, e0_ref, kept0, u3, f3, r3, f4, u4 = take(12)
 
     rows, cols = 2 * gx, 16 * gy
-    assemble3(lambda jx, jy: gathered[jx * gy + jy, pl.ds(NZ, 8), :], f3, gx, gy, rows)
+    assemble3(lambda jx, jy: gathered(jx, jy, pl.ds(NZ, 8)), f3, gx, gy, rows)
     f3, u3, r3 = (Field(ref, rows) for ref in (f3, u3, r3))
     y = iota((rows, 128), 1)
     x_face3, y_face3, inv3, g3, c3 = stack_fields(whole, rows, 5, z_face=False)
@@ -822,8 +829,8 @@
 
     def block(dx, dy):
         inside = ((ix + dx >= 0) & (ix + dx < gx)).astype(F32)
-        device = jnp.clip(ix + dx, 0, gx - 1) * gy + jnp.clip(iy + dy, 0, gy - 1)
-        return gathered[device, pl.ds(0, NZ), :] * inside
+        jx, jy = jnp.clip(ix + dx, 0, gx - 1), jnp.clip(iy + dy, 0, gy - 1)
+        return gathered((jx, other if dx else own), jy, pl.ds(0, NZ)) * inside
 
     for first, dx in ((0, 0), (4, 1), (12, -1)):
         window2(block(dx, 0), shift(block(dx, 1), 32, 1), shift(block(dx, -1), 96, 1), f2, first, iy, gy)
@@ -857,7 +864,7 @@
     spread_rows(ring(cells), ring(shift(cells, 1, 1)), ring(shift(cells, -1, 1)), wide, NZ * 8)
     fine_y = jnp.where(lane < 96, lane, lane - 128)
     e_ref[...] = mix(wide[pl.ds(0, NZ * TX), :], spread_matrix(fine_y, 0, 0, circular=True), 3)
-    copy1.wait()
+    fetched[0].wait()
     x_face1, y_face1, inv1, f1, u1, z_face1 = stack_fields(held1, TX, 5)
     line1 = Line(inv1, z_face1)
     mask1 = window_mask(TX, 128, 8, 64, 4, ix, iy, 8 * gx, 64 * gy)
@@ -872,7 +879,7 @@
         cells = mix(wide[pl.ds(k * rows, 8 * rows), :], weights, 3)
         for t in range(2):
             e0_ref[pl.ds(e0.base(t, k), 8 * rows), :] = cells[:, 128 * t : 128 * (t + 1)]
-    copy0.wait()
+    fetched[1].wait()
     x_face0, y_face0, inv0, f0, u0, z_face0 = stack_fields(held0, rows, 5, 2)
     mask0 = window_mask(rows, 256, TX, TY, HALO, ix, iy, TX * gx, TY * gy)
     smooth_up(f0, x_face0, y_face0, Line(inv0, z_face0), u0, e0, Field(kept0, rows, 2), mask0, 2)
@@ -899,7 +906,8 @@
     residual(NZ - 1, carry)
 
 
-MEBIBYTES = {"pack": 56, "down": 32, "up": 32}
+SAVED_ROWS = 72 * 1024
+MEBIBYTES = {"pack": 56}
 COSTS = {
     "pack": 3 * 10**9, "share": 10**9, "down": 10**10,
     "window_coeffs": 4 * 10**9, "global_coeffs": 4 * 10**9, "up": 12 * 10**9,
@@ -916,7 +924,7 @@
         out_specs=out_specs or [VMEM] * len(outs),
         scratch_shapes=list(scratch),
         input_output_aliases=aliases or {},
-        compiler_params=pltpu.CompilerParams(vmem_limit_bytes=MEBIBYTES.get(name, 16) * 1024 * 1024),
+        compiler_params=pltpu.CompilerParams(vmem_limit_bytes=MEBIBYTES.get(name, 32) * 1024 * 1024),
         cost_estimate=pl.CostEstimate(flops=COSTS[name], bytes_accessed=4 * sum(x.size for x in ins), transcendentals=0),
     )(*ins)
 
@@ -962,14 +970,16 @@
     sends, saved = call(
         functools.partial(down_kernel, gx * TX, gy * TY),
         "down",
-        [(devices * BLOCK, 128), (total0 + total1, 128)],
+        [(devices // 2 * BLOCK, 128), (max(total0 + total1, SAVED_ROWS), 128)],
         [stack, yr, yl, corner_r, corner_l, x_near, x_far],
         [vm(*big)] * 10 + [vm(*big_z)] + level(TX, 10) + [faces(TX, 1)] + level(8, 10) + [faces(8, 1)] + [dma(12)],
         out_specs=[VMEM, ANY],
     )
     sends, own = lax.optimization_barrier((sends, own))
     other = lax.ppermute(own, "gx", near(gx))
-    gathered = lax.all_to_all(sends.reshape(devices, BLOCK, 128), ("gx", "gy"), 0, 0)
+    blocks = sends.reshape(devices // 2, BLOCK, 128)
+    own_blocks = lax.all_to_all(blocks, ("gx", "gy"), 0, 0, axis_index_groups=cores)
+    other_blocks = lax.ppermute(own_blocks, "gx", near(gx))
     whole = call(
         functools.partial(global_kernel, gx, gy),
         "global_coeffs",
@@ -983,10 +993,10 @@
         functools.partial(up_kernel, gx, gy),
         "up",
         [(NZ * TX, TY)] * 2,
-        [gathered, whole, k2, stack, saved],
+        [own_blocks, other_blocks, whole, k2, stack, saved],
         [vm(total0, 128), vm(total1, 128)] + level(TX, 3) + [vm(NZ * 2 * TX, 128), vm(*size), vm(*big), vm(*big)]
         + level(rows3, 3) + level(rows4, 2) + [dma(2)],
-        in_specs=[VMEM] * 4 + [ANY],
+        in_specs=[VMEM] * 5 + [ANY],
     )
     return field.reshape(right_side.shape), residual.reshape(right_side.shape)
 

time: 85.2 us -> 70.5 us (0.83)
  local copies, waits for them, and re-layouts: 12.5 us -> 3.22 us
  waiting for transfers between devices: 13.9 us -> 9.06 us
  Pallas kernels: 28 us -> 27.1 us
    all_to_all x1 -> x0, waiting for transfers between devices: 12.5 us -> none  [body(): lax.all_to_all(sends.reshape(devices, BLOCK, 128), ('gx', 'gy'), 0, 0)]
    unnamed x20 -> x12, local copies, waits for them, and re-layouts: 12.5 us -> 3.19 us
    all_to_all x1 -> x2, waiting for transfers between devices: 0.01 us -> 7.52 us  [body(): lax.all_to_all(blocks, ('gx', 'gy'), 0, 0, axis_index_groups=cores)]
    all_to_all x1 -> x2, starting transfers between devices: 14.7 us -> 21.2 us  [body(): lax.all_to_all(blocks, ('gx', 'gy'), 0, 0, axis_index_groups=cores)]
    all_to_all x1 -> x0, starting transfers between devices: 5.9 us -> none  [body(): lax.all_to_all(sends.reshape(devices, BLOCK, 128), ('gx', 'gy'), 0, 0)]
    pallas_call x6, Pallas kernels: 28 us -> 27.1 us  [call(): pl.pallas_call(kernel, name=name, out_shape=shapes, in_specs=in_specs or...]
  transfers between devices with their start and end apart: 9 -> 10, of which waited for: 2 -> 4; matrix products, arithmetic and copies ran while one was open for 0% -> 0% of each run, Pallas kernels for 17% -> 20%
where the time goes in v8:
time: 70.5 us; the launch traced here: 70.1 us
  starting transfers between devices  29.8 us (42%)
  Pallas kernels  27.1 us (38%)
  waiting for transfers between devices  9.06 us (13%)
  local copies, waits for them, and re-layouts  3.22 us (5%)
  between operations  0.85 us (1%)
    pallas_call x6, Pallas kernels, call(): pl.pallas_call(kernel, name=name, out_shape=shapes, in_specs=in_specs or...  27.1 us
    all_to_all x2, starting transfers between devices, body(): lax.all_to_all(blocks, ('gx', 'gy'), 0, 0, axis_index_groups=cores)  21.2 us
    all_to_all x2, waiting for transfers between devices, body(): lax.all_to_all(blocks, ('gx', 'gy'), 0, 0, axis_index_groups=cores)  7.52 us
    ppermute x1, starting transfers between devices, body(): c_near = lax.ppermute(jnp.where(even_x, tail, head), 'gx', near(gx))  3.37 us
    unnamed x12, local copies, waits for them, and re-layouts  3.19 us
    ppermute x1, starting transfers between devices, body(): y_near = lax.ppermute(y_near, 'gy', near(gy))  3 us
    ppermute x1, waiting for transfers between devices, body(): y_near = lax.ppermute(y_near, 'gy', near(gy))  1.44 us
  transfers between devices with their start and end apart: 10, of which 4 were waited for; matrix products, arithmetic and copies ran while one was open for 0% of the time, Pallas kernels for 20%

profile of v8, /device:TPU:0, one launch (start us, length us, event | category | flops | bytes accessed | tf_op | source)
XLA Modules:
  0.0 70.1 jit_solution(18241038622531308468)
XLA Ops:
  0.6 3.2 %pack.1 = (f32[1472,128]{1,0:T(8,128)}, f32[1472,128]{1,0:T(8,128)}, f32[184,128]{1,0:T(8,128)}, f32[184,128]{1,0:T(8,128)}, f32[192,128]{1,0:T(8,128)}, /*index=5*/f32[2560,128]{1,0:T(8,128)}) custom-call(f32[512,128]{1,0:T(8,128)} %bitcast.12, f32[512,128]{1,0:T(8,128)} %bitcast.13, f32[512,128]{1,0:T(8,128)} %bitcast.14, f32[512,128]{1,0:T(8,128)} %bitcast.15, ...), custom_call_target="tpu_custom_call" | custom-call | flops 3000000000 | bytes 1310720 | tf_op jit(solution)/shard_map/pack/pallas_call | solution.py:919
  3.8 3.0 %collective-permute-start = (f32[184,128]{1,0:T(8,128)}, f32[184,128]{1,0:T(8,128)S(1)}, u32[]{:S(2)}, u32[]{:S(2)}) collective-permute-start(f32[184,128]{1,0:T(8,128)} %get-tuple-element.18), channel_id=1, source_target_pairs={{0,1},{1,0},{2,3},{3,2},{4,5},{5,4},{6,7},{7,6},{8,9},{9,8},{10,11... | collective-permute-start | bytes 282632 | tf_op jit(solution)/shard_map/ppermute | solution.py:945
  6.8 0.7 collective-permute-start.1
  7.5 0.1 collective-permute-start.4
  7.6 0.7 %collective-permute-start.5 = (f32[1472,128]{1,0:T(8,128)}, f32[1472,128]{1,0:T(8,128)S(1)}, u32[]{:S(2)}, u32[]{:S(2)}) collective-permute-start(f32[1472,128]{1,0:T(8,128)} %get-tuple-element.24), channel_id=1, source_target_pairs={{4,8},{8,4},{12,16},{16,12},{20,24},{24,20},{5,9},{9,5},{13,17},{1... | collective-permute-start | bytes 2261000 | tf_op jit(solution)/shard_map/ppermute | solution.py:948
  8.3 1.4 %collective-permute-done = f32[184,128]{1,0:T(8,128)S(1)} collective-permute-done((f32[184,128]{1,0:T(8,128)}, f32[184,128]{1,0:T(8,128)S(1)}, u32[]{:S(2)}, u32[]{:S(2)}) %collective-permute-start) | collective-permute-done | bytes 94240 | tf_op jit(solution)/shard_map/ppermute | solution.py:945
  9.7 0.0 collective-permute-done.1
  9.9 0.7 collective-permute-start.3
  10.6 3.4 %collective-permute-start.2 = (f32[208,128]{1,0:T(8,128)S(1)}, f32[208,128]{1,0:T(8,128)S(1)}, u32[]{:S(2)}, u32[]{:S(2)}) collective-permute-start(f32[208,128]{1,0:T(8,128)S(1)} %get-tuple-element.35), channel_id=1, source_target_pairs={{0,4},{4,0},{8,12},{12,8},{16,20},{20,16},{24,28},{28,24},{1,5},{5... | collective-permute-start | bytes 319496 | tf_op jit(solution)/shard_map/ppermute | solution.py:954
  13.9 0.0 copy-start.4
  13.9 0.9 %copy-done.4 = f32[192,128]{1,0:T(8,128)S(1)} copy-done((f32[192,128]{1,0:T(8,128)S(1)}, f32[192,128]{1,0:T(8,128)}, u32[]{:S(2)}) %copy-start.4) | copy-done | bytes 98328
  14.8 1.0 %share.1 = f32[640,128]{1,0:T(8,128)} custom-call(f32[192,128]{1,0:T(8,128)S(1)} %copy-done.4), custom_call_target="tpu_custom_call" | custom-call | flops 1000000000 | bytes 98304 | tf_op jit(solution)/shard_map/share/pallas_call | solution.py:919
  15.8 0.0 collective-permute-done.3
  15.8 0.0 collective-permute-done.2
  15.8 14.7 %all-to-all-start = ((f32[16,40,128]{2,1,0:T(8,128)}), f32[16,40,128]{2,1,0:T(8,128)S(1)}, u32[]{:S(2)}, u32[]{:S(2)}) async-start(f32[16,40,128]{2,1,0:T(8,128)} %bitcast.5), calls=%async_computation | async-start | bytes 655360 | tf_op jit(solution)/shard_map/all_to_all | solution.py:960
  30.6 0.0 collective-permute-done.4.refs_5_.x_near
  30.6 0.0 collective-permute-done.5.refs_6_.x_far
  30.6 0.0 copy-start
  30.6 1.3 %copy-done = f32[2560,128]{1,0:T(8,128)S(1)} copy-done((f32[2560,128]{1,0:T(8,128)S(1)}, f32[2560,128]{1,0:T(8,128)}, u32[]{:S(2)}) %copy-start) | copy-done | bytes 1310744
  31.9 0.0 copy-start.5
  31.9 9.2 %down.1 = (f32[640,128]{1,0:T(8,128)}, f32[73728,128]{1,0:T(8,128)}) custom-call(f32[2560,128]{1,0:T(8,128)S(1)} %copy-done, f32[184,128]{1,0:T(8,128)S(1)} %get-tuple-element.37.refs_1_.yr, f32[184,128]{1,0:T(8,128)S(1)} %get-tuple-element.36.refs_2_.yl, f32[208,128]{1,0:T(8,128)S(1)} %get-tuple-element.33.refs_3_.cr, ...), custom_call_target="tpu_custom_call" | custom-call | flops 10000000000 | bytes 3219456 | tf_op jit(solution)/shard_map/down/pallas_call | solution.py:919
  41.1 0.4 all-to-all-done
  41.5 6.5 %all-to-all-start.1 = ((f32[16,40,128]{2,1,0:T(8,128)}), f32[16,40,128]{2,1,0:T(8,128)S(1)}, u32[]{:S(2)}, u32[]{:S(2)}) async-start(f32[16,40,128]{2,1,0:T(8,128)} %bitcast.7), calls=%async_computation.1 | async-start | bytes 655360 | tf_op jit(solution)/shard_map/all_to_all | solution.py:981
  48.0 0.1 collective-permute-start.7
  48.1 0.0 copy-done.5
  48.1 2.2 %window_coeffs.1.refs_3_ = f32[2064,128]{1,0:T(8,128)S(1)} custom-call(f32[192,128]{1,0:T(8,128)S(1)} %copy-done.5, f32[1472,128]{1,0:T(8,128)S(1)} %collective-permute-done.4.refs_5_.x_near, f32[1472,128]{1,0:T(8,128)S(1)} %collective-permute-done.5.refs_6_.x_far, f32[184,128]{1,0:T(8,128)S(1)} %get-tuple-element.37.refs_1_.yr, ...), custom_call_target="tpu_custom_call" | custom-call | flops 4000000000 | bytes 2007040 | tf_op jit(solution)/shard_map/window_coeffs/pallas_call | solution.py:919
  50.3 0.0 copy-start.2
  50.3 1.0 %copy-done.2 = f32[2064,128]{1,0:T(8,128)} copy-done((f32[2064,128]{1,0:T(8,128)}, f32[2064,128]{1,0:T(8,128)S(1)}, u32[]{:S(2)}) %copy-start.2) | copy-done | bytes 1056792
  51.3 0.0 copy-start.1
  51.3 7.1 %all-to-all-done.1.refs_0_ = f32[16,40,128]{2,1,0:T(8,128)S(1)} async-done(((f32[16,40,128]{2,1,0:T(8,128)}), f32[16,40,128]{2,1,0:T(8,128)S(1)}, u32[]{:S(2)}, u32[]{:S(2)}) %all-to-all-start.1) | async-done | bytes 327712 | tf_op jit(solution)/shard_map/all_to_all | solution.py:981
  58.4 0.0 copy-start.3
  58.4 0.0 collective-permute-start.6
  58.4 0.0 collective-permute-done.7.other
  58.4 1.5 %global_coeffs.1.refs_2_ = f32[3840,128]{1,0:T(8,128)S(1)} custom-call(f32[4,160,128]{2,1,0:T(8,128)S(1)} %bitcast.11, f32[4,160,128]{2,1,0:T(8,128)S(1)} %collective-permute-done.7.other), custom_call_target="tpu_custom_call" | custom-call | flops 4000000000 | bytes 655360 | tf_op jit(solution)/shard_map/global_coeffs/pallas_call | solution.py:919
  60.0 0.1 collective-permute-done.6.refs_1_
  60.1 0.0 copy-done.1
  60.1 0.0 copy-done.3
  60.1 10.0 %up.1 = (f32[512,128]{1,0:T(8,128)}, f32[512,128]{1,0:T(8,128)}) custom-call(f32[16,40,128]{2,1,0:T(8,128)S(1)} %all-to-all-done.1.refs_0_, f32[16,40,128]{2,1,0:T(8,128)S(1)} %collective-permute-done.6.refs_1_, f32[3840,128]{1,0:T(8,128)S(1)} %global_coeffs.1.refs_2_, f32[2064,128]{1,0:T(8,128)S(1)} %copy-done.3, f32[2560,128]{1,0:T(8,128)S(1)} %copy-done.1, ...), custom_call_target="tpu_custom_call" | custom-call | flops 12000000000 | bytes 42737664 | tf_op jit(solution)/shard_map/up/pallas_call | solution.py:919
  (9 shorter events, 0.1 us)
Async XLA Ops:
  3.8 5.9 %collective-permute-start = (f32[184,128]{1,0:T(8,128)}, f32[184,128]{1,0:T(8,128)S(1)}, u32[]{:S(2)}, u32[]{:S(2)}) collective-permute-start(f32[184,128]{1,0:T(8,128)} %get-tuple-element.18), channel_id=1, source_target_pairs={{0,1},{1,0},{2,3},{3,2},{4,5},{5,4},{6,7},{7,6},{8,9},{9,8},{10,11... | collective-permute-start | bytes 282632 | tf_op jit(solution)/shard_map/ppermute | solution.py:945
  6.8 2.9 %collective-permute-start.1 = (f32[184,128]{1,0:T(8,128)}, f32[184,128]{1,0:T(8,128)S(1)}, u32[]{:S(2)}, u32[]{:S(2)}) collective-permute-start(f32[184,128]{1,0:T(8,128)} %get-tuple-element.19), channel_id=1, source_target_pairs={{1,2},{2,1},{5,6},{6,5},{9,10},{10,9},{13,14},{14,13},{17,18},{18,... | collective-permute-start | bytes 282632 | tf_op jit(solution)/shard_map/ppermute | solution.py:946
  7.5 23.1 %collective-permute-start.4 = (f32[1472,128]{1,0:T(8,128)}, f32[1472,128]{1,0:T(8,128)S(1)}, u32[]{:S(2)}, u32[]{:S(2)}) collective-permute-start(f32[1472,128]{1,0:T(8,128)} %get-tuple-element.23), channel_id=1, source_target_pairs={{0,4},{4,0},{8,12},{12,8},{16,20},{20,16},{24,28},{28,24},{1,5},{5... | collective-permute-start | bytes 2261000 | tf_op jit(solution)/shard_map/ppermute | solution.py:947
  7.6 23.0 %collective-permute-start.5 = (f32[1472,128]{1,0:T(8,128)}, f32[1472,128]{1,0:T(8,128)S(1)}, u32[]{:S(2)}, u32[]{:S(2)}) collective-permute-start(f32[1472,128]{1,0:T(8,128)} %get-tuple-element.24), channel_id=1, source_target_pairs={{4,8},{8,4},{12,16},{16,12},{20,24},{24,20},{5,9},{9,5},{13,17},{1... | collective-permute-start | bytes 2261000 | tf_op jit(solution)/shard_map/ppermute | solution.py:948
  9.9 5.9 %collective-permute-start.3 = (f32[208,128]{1,0:T(8,128)S(1)}, f32[208,128]{1,0:T(8,128)S(1)}, u32[]{:S(2)}, u32[]{:S(2)}) collective-permute-start(f32[208,128]{1,0:T(8,128)S(1)} %get-tuple-element.34), channel_id=1, source_target_pairs={{4,8},{8,4},{12,16},{16,12},{20,24},{24,20},{5,9},{9,5},{13,17},{1... | collective-permute-start | bytes 319496 | tf_op jit(solution)/shard_map/ppermute | solution.py:955
  10.6 5.3 %collective-permute-start.2 = (f32[208,128]{1,0:T(8,128)S(1)}, f32[208,128]{1,0:T(8,128)S(1)}, u32[]{:S(2)}, u32[]{:S(2)}) collective-permute-start(f32[208,128]{1,0:T(8,128)S(1)} %get-tuple-element.35), channel_id=1, source_target_pairs={{0,4},{4,0},{8,12},{12,8},{16,20},{20,16},{24,28},{28,24},{1,5},{5... | collective-permute-start | bytes 319496 | tf_op jit(solution)/shard_map/ppermute | solution.py:954
  13.9 0.9 %copy-start.4 = (f32[192,128]{1,0:T(8,128)S(1)}, f32[192,128]{1,0:T(8,128)}, u32[]{:S(2)}) copy-start(f32[192,128]{1,0:T(8,128)} %get-tuple-element.20.share2) | copy-start | bytes 294916
  15.8 25.7 %all-to-all-start = ((f32[16,40,128]{2,1,0:T(8,128)}), f32[16,40,128]{2,1,0:T(8,128)S(1)}, u32[]{:S(2)}, u32[]{:S(2)}) async-start(f32[16,40,128]{2,1,0:T(8,128)} %bitcast.5), calls=%async_computation | async-start | bytes 655360 | tf_op jit(solution)/shard_map/all_to_all | solution.py:960
  30.6 1.3 %copy-start = (f32[2560,128]{1,0:T(8,128)S(1)}, f32[2560,128]{1,0:T(8,128)}, u32[]{:S(2)}) copy-start(f32[2560,128]{1,0:T(8,128)} %get-tuple-element.17.refs_0_.refs_4_) | copy-start | bytes 3932164
  31.9 16.2 %copy-start.5 = (f32[192,128]{1,0:T(8,128)S(1)}, f32[192,128]{1,0:T(8,128)}, u32[]{:S(2)}) copy-start(f32[192,128]{1,0:T(8,128)} %get-tuple-element.20.share2) | copy-start | bytes 294916
  41.5 16.9 %all-to-all-start.1 = ((f32[16,40,128]{2,1,0:T(8,128)}), f32[16,40,128]{2,1,0:T(8,128)S(1)}, u32[]{:S(2)}, u32[]{:S(2)}) async-start(f32[16,40,128]{2,1,0:T(8,128)} %bitcast.7), calls=%async_computation.1 | async-start | bytes 655360 | tf_op jit(solution)/shard_map/all_to_all | solution.py:981
  48.0 10.4 %collective-permute-start.7 = (f32[4,160,128]{2,1,0:T(8,128)S(1)}, f32[4,160,128]{2,1,0:T(8,128)S(1)}, u32[]{:S(2)}, u32[]{:S(2)}) collective-permute-start(f32[4,160,128]{2,1,0:T(8,128)S(1)} %bitcast.10), channel_id=1, source_target_pairs={{0,4},{4,0},{8,12},{12,8},{16,20},{20,16},{24,28},{28,24},{1,5},{5... | collective-permute-start | bytes 983048 | tf_op jit(solution)/shard_map/ppermute | solution.py:979
  50.3 1.0 %copy-start.2 = (f32[2064,128]{1,0:T(8,128)}, f32[2064,128]{1,0:T(8,128)S(1)}, u32[]{:S(2)}) copy-start(f32[2064,128]{1,0:T(8,128)S(1)} %window_coeffs.1.refs_3_) | copy-start | bytes 3170308
  51.3 8.8 %copy-start.1 = (f32[2560,128]{1,0:T(8,128)S(1)}, f32[2560,128]{1,0:T(8,128)}, u32[]{:S(2)}) copy-start(f32[2560,128]{1,0:T(8,128)} %get-tuple-element.17.refs_0_.refs_4_) | copy-start | bytes 3932164
  58.4 1.6 %copy-start.3 = (f32[2064,128]{1,0:T(8,128)S(1)}, f32[2064,128]{1,0:T(8,128)}, u32[]{:S(2)}) copy-start(f32[2064,128]{1,0:T(8,128)} %copy-done.2) | copy-start | bytes 3170308
  58.4 1.6 %collective-permute-start.6 = (f32[16,40,128]{2,1,0:T(8,128)S(1)}, f32[16,40,128]{2,1,0:T(8,128)S(1)}, u32[]{:S(2)}, u32[]{:S(2)}) collective-permute-start(f32[16,40,128]{2,1,0:T(8,128)S(1)} %all-to-all-done.1.refs_0_), channel_id=1, source_target_pairs={{0,4},{4,0},{8,12},{12,8},{16,20},{20,16},{24,28},{28,24},{1,5},{5... | collective-permute-start | bytes 983048 | tf_op jit(solution)/shard_map/ppermute | solution.py:982

commit v9 on v8

--- a/solution.py
+++ b/solution.py
@@ -418,7 +418,7 @@
     return pltpu.roll(out, turn, 1)
 
 
-def share_kernel(devices, share2, copies):
+def share_kernel(devices, share2, stack, copies):
     iy = lax.axis_index("gy")
     y, lane = iota((128, 128), 0), iota((128, 128), 1)
     x_in, y_in = y // 32, y % 32
@@ -947,13 +947,13 @@
     x_near = lax.ppermute(x_near, "gx", near(gx))
     x_far = lax.ppermute(x_far, "gx", far(gx))
     yr, yl = jnp.where(even_y, y_near, y_far), jnp.where(even_y, y_far, y_near)
-    copies = call(functools.partial(share_kernel, devices // 2), "share", [(devices // 2 * SHARE, 128)], [share2])[0]
+    copies = call(functools.partial(share_kernel, devices // 2), "share", [(devices // 2 * SHARE, 128)], [share2, stack])[0]
     half = STRIP // 2
     head = jnp.concatenate([yl[:half], yl[STRIP:], yr[:half], yr[STRIP:]])
     tail = jnp.concatenate([yl[half:], yr[half:]])
     c_near = lax.ppermute(jnp.where(even_x, tail, head), "gx", near(gx))
     c_far = lax.ppermute(jnp.where(even_x, head, tail), "gx", far(gx))
-    copies, c_near, c_far = lax.optimization_barrier((copies, c_near, c_far))
+    copies, c_near = lax.optimization_barrier((copies, c_near))
     corner_r, corner_l = jnp.where(even_x, c_near, c_far), jnp.where(even_x, c_far, c_near)
     cores = [[x * gy + y for x in range(core, gx, 2) for y in range(gy)] for core in range(2)]
     blocks = copies.reshape(devices // 2, SHARE, 128)

time: 70.5 us -> 66.9 us (0.949)
  starting transfers between devices: 29.8 us -> 23.5 us
  waiting for transfers between devices: 9.06 us -> 10.4 us
  local copies, waits for them, and re-layouts: 3.22 us -> 4.53 us
    all_to_all x2, starting transfers between devices: 21.2 us -> 16.8 us  [body(): lax.all_to_all(blocks, ('gx', 'gy'), 0, 0, axis_index_groups=cores)]
    ppermute x1, starting transfers between devices: 3.37 us -> 1.54 us  [body(): c_near = lax.ppermute(jnp.where(even_x, tail, head), 'gx', near(gx))]
    all_to_all x2, waiting for transfers between devices: 7.52 us -> 8.87 us  [body(): lax.all_to_all(blocks, ('gx', 'gy'), 0, 0, axis_index_groups=cores)]
    unnamed x12 -> x14, local copies, waits for them, and re-layouts: 3.19 us -> 4.5 us
  transfers between devices with their start and end apart: 10 -> 10, of which waited for: 4 -> 4; matrix products, arithmetic and copies ran while one was open for 0% -> 0% of each run, Pallas kernels for 20% -> 21%
where the time goes in v9:
time: 66.9 us; the launch traced here: 66.5 us
  Pallas kernels  27.1 us (41%)
  starting transfers between devices  23.5 us (35%)
  waiting for transfers between devices  10.4 us (16%)
  local copies, waits for them, and re-layouts  4.53 us (7%)
  between operations  0.86 us (1%)
    pallas_call x6, Pallas kernels, call(): pl.pallas_call(kernel, name=name, out_shape=shapes, in_specs=in_specs or...  27.1 us
    all_to_all x2, starting transfers between devices, body(): lax.all_to_all(blocks, ('gx', 'gy'), 0, 0, axis_index_groups=cores)  16.8 us
    all_to_all x2, waiting for transfers between devices, body(): lax.all_to_all(blocks, ('gx', 'gy'), 0, 0, axis_index_groups=cores)  8.87 us
    unnamed x14, local copies, waits for them, and re-layouts  4.5 us
    ppermute x1, starting transfers between devices, body(): y_near = lax.ppermute(y_near, 'gy', near(gy))  3 us
    ppermute x1, starting transfers between devices, body(): c_near = lax.ppermute(jnp.where(even_x, tail, head), 'gx', near(gx))  1.54 us
    ppermute x1, waiting for transfers between devices, body(): y_near = lax.ppermute(y_near, 'gy', near(gy))  1.44 us
  transfers between devices with their start and end apart: 10, of which 4 were waited for; matrix products, arithmetic and copies ran while one was open for 0% of the time, Pallas kernels for 21%

profile of v9, /device:TPU:0, one launch (start us, length us, event | category | flops | bytes accessed | tf_op | source)
XLA Modules:
  0.0 66.5 jit_solution(5197984256661025288)
XLA Ops:
  0.6 3.2 %pack.1 = (f32[1472,128]{1,0:T(8,128)}, f32[1472,128]{1,0:T(8,128)}, f32[184,128]{1,0:T(8,128)}, f32[184,128]{1,0:T(8,128)}, f32[192,128]{1,0:T(8,128)}, /*index=5*/f32[2560,128]{1,0:T(8,128)}) custom-call(f32[512,128]{1,0:T(8,128)} %bitcast.12, f32[512,128]{1,0:T(8,128)} %bitcast.13, f32[512,128]{1,0:T(8,128)} %bitcast.14, f32[512,128]{1,0:T(8,128)} %bitcast.15, ...), custom_call_target="tpu_custom_call" | custom-call | flops 3000000000 | bytes 1310720 | tf_op jit(solution)/shard_map/pack/pallas_call | solution.py:919
  3.8 3.0 %collective-permute-start = (f32[184,128]{1,0:T(8,128)}, f32[184,128]{1,0:T(8,128)S(1)}, u32[]{:S(2)}, u32[]{:S(2)}) collective-permute-start(f32[184,128]{1,0:T(8,128)} %get-tuple-element.17), channel_id=1, source_target_pairs={{0,1},{1,0},{2,3},{3,2},{4,5},{5,4},{6,7},{7,6},{8,9},{9,8},{10,11... | collective-permute-start | bytes 282632 | tf_op jit(solution)/shard_map/ppermute | solution.py:945
  6.8 0.7 collective-permute-start.1
  7.5 0.1 collective-permute-start.4
  7.6 0.7 %collective-permute-start.5 = (f32[1472,128]{1,0:T(8,128)}, f32[1472,128]{1,0:T(8,128)S(1)}, u32[]{:S(2)}, u32[]{:S(2)}) collective-permute-start(f32[1472,128]{1,0:T(8,128)} %get-tuple-element.22), channel_id=1, source_target_pairs={{4,8},{8,4},{12,16},{16,12},{20,24},{24,20},{5,9},{9,5},{13,17},{1... | collective-permute-start | bytes 2261000 | tf_op jit(solution)/shard_map/ppermute | solution.py:948
  8.3 1.4 %collective-permute-done = f32[184,128]{1,0:T(8,128)S(1)} collective-permute-done((f32[184,128]{1,0:T(8,128)}, f32[184,128]{1,0:T(8,128)S(1)}, u32[]{:S(2)}, u32[]{:S(2)}) %collective-permute-start) | collective-permute-done | bytes 94240 | tf_op jit(solution)/shard_map/ppermute | solution.py:945
  9.7 0.0 collective-permute-done.1
  9.9 1.5 %collective-permute-start.2 = (f32[208,128]{1,0:T(8,128)S(1)}, f32[208,128]{1,0:T(8,128)S(1)}, u32[]{:S(2)}, u32[]{:S(2)}) collective-permute-start(f32[208,128]{1,0:T(8,128)S(1)} %get-tuple-element.33), channel_id=1, source_target_pairs={{0,4},{4,0},{8,12},{12,8},{16,20},{20,16},{24,28},{28,24},{1,5},{5... | collective-permute-start | bytes 319496 | tf_op jit(solution)/shard_map/ppermute | solution.py:954
  11.4 0.7 collective-permute-start.3
  12.1 0.0 copy-start
  12.1 1.3 %copy-done = f32[2560,128]{1,0:T(8,128)S(1)} copy-done((f32[2560,128]{1,0:T(8,128)S(1)}, f32[2560,128]{1,0:T(8,128)}, u32[]{:S(2)}) %copy-start) | copy-done | bytes 1310744
  13.4 0.0 copy-start.5
  13.4 0.9 %copy-done.5 = f32[192,128]{1,0:T(8,128)S(1)} copy-done((f32[192,128]{1,0:T(8,128)S(1)}, f32[192,128]{1,0:T(8,128)}, u32[]{:S(2)}) %copy-start.5) | copy-done | bytes 98328
  14.3 1.0 %share.1 = f32[640,128]{1,0:T(8,128)} custom-call(f32[192,128]{1,0:T(8,128)S(1)} %copy-done.5, f32[2560,128]{1,0:T(8,128)S(1)} %copy-done), custom_call_target="tpu_custom_call" | custom-call | flops 1000000000 | bytes 1409024 | tf_op jit(solution)/shard_map/share/pallas_call | solution.py:919
  15.3 0.0 collective-permute-done.2
  15.3 10.9 %all-to-all-start = ((f32[16,40,128]{2,1,0:T(8,128)}), f32[16,40,128]{2,1,0:T(8,128)S(1)}, u32[]{:S(2)}, u32[]{:S(2)}) async-start(f32[16,40,128]{2,1,0:T(8,128)} %bitcast.5), calls=%async_computation | async-start | bytes 655360 | tf_op jit(solution)/shard_map/all_to_all | solution.py:960
  26.2 0.0 collective-permute-done.3
  26.3 0.0 collective-permute-done.4.refs_5_.x_near
  26.3 0.0 collective-permute-done.5.refs_6_.x_far
  26.3 0.0 copy-start.1
  26.3 1.3 %copy-done.1 = f32[2560,128]{1,0:T(8,128)S(1)} copy-done((f32[2560,128]{1,0:T(8,128)S(1)}, f32[2560,128]{1,0:T(8,128)}, u32[]{:S(2)}) %copy-start.1) | copy-done | bytes 1310744
  27.6 0.0 copy-start.6
  27.6 9.2 %down.1 = (f32[640,128]{1,0:T(8,128)}, f32[73728,128]{1,0:T(8,128)}) custom-call(f32[2560,128]{1,0:T(8,128)S(1)} %copy-done.1, f32[184,128]{1,0:T(8,128)S(1)} %get-tuple-element.35.refs_1_.yr, f32[184,128]{1,0:T(8,128)S(1)} %get-tuple-element.34.refs_2_.yl, f32[208,128]{1,0:T(8,128)S(1)} %get-tuple-element.31.refs_3_.cr, ...), custom_call_target="tpu_custom_call" | custom-call | flops 10000000000 | bytes 3219456 | tf_op jit(solution)/shard_map/down/pallas_call | solution.py:919
  36.8 1.1 %all-to-all-done = f32[16,40,128]{2,1,0:T(8,128)S(1)} async-done(((f32[16,40,128]{2,1,0:T(8,128)}), f32[16,40,128]{2,1,0:T(8,128)S(1)}, u32[]{:S(2)}, u32[]{:S(2)}) %all-to-all-start) | async-done | bytes 327712 | tf_op jit(solution)/shard_map/all_to_all | solution.py:960
  37.9 5.9 %all-to-all-start.1 = ((f32[16,40,128]{2,1,0:T(8,128)}), f32[16,40,128]{2,1,0:T(8,128)S(1)}, u32[]{:S(2)}, u32[]{:S(2)}) async-start(f32[16,40,128]{2,1,0:T(8,128)} %bitcast.7), calls=%async_computation.1 | async-start | bytes 655360 | tf_op jit(solution)/shard_map/all_to_all | solution.py:981
  43.7 0.1 collective-permute-start.7
  43.8 0.0 copy-done.6
  43.8 2.2 %window_coeffs.1.refs_3_ = f32[2064,128]{1,0:T(8,128)S(1)} custom-call(f32[192,128]{1,0:T(8,128)S(1)} %copy-done.6, f32[1472,128]{1,0:T(8,128)S(1)} %collective-permute-done.4.refs_5_.x_near, f32[1472,128]{1,0:T(8,128)S(1)} %collective-permute-done.5.refs_6_.x_far, f32[184,128]{1,0:T(8,128)S(1)} %get-tuple-element.35.refs_1_.yr, ...), custom_call_target="tpu_custom_call" | custom-call | flops 4000000000 | bytes 2007040 | tf_op jit(solution)/shard_map/window_coeffs/pallas_call | solution.py:919
  46.0 0.0 copy-start.3
  46.0 1.0 %copy-done.3 = f32[2064,128]{1,0:T(8,128)} copy-done((f32[2064,128]{1,0:T(8,128)}, f32[2064,128]{1,0:T(8,128)S(1)}, u32[]{:S(2)}) %copy-start.3) | copy-done | bytes 1056792
  47.0 0.0 copy-start.2
  47.0 7.8 %all-to-all-done.1.refs_0_ = f32[16,40,128]{2,1,0:T(8,128)S(1)} async-done(((f32[16,40,128]{2,1,0:T(8,128)}), f32[16,40,128]{2,1,0:T(8,128)S(1)}, u32[]{:S(2)}, u32[]{:S(2)}) %all-to-all-start.1) | async-done | bytes 327712 | tf_op jit(solution)/shard_map/all_to_all | solution.py:981
  54.8 0.0 copy-start.4
  54.8 0.0 collective-permute-start.6
  54.8 0.0 collective-permute-done.7.other
  54.8 1.5 %global_coeffs.1.refs_2_ = f32[3840,128]{1,0:T(8,128)S(1)} custom-call(f32[4,160,128]{2,1,0:T(8,128)S(1)} %bitcast.11, f32[4,160,128]{2,1,0:T(8,128)S(1)} %collective-permute-done.7.other), custom_call_target="tpu_custom_call" | custom-call | flops 4000000000 | bytes 655360 | tf_op jit(solution)/shard_map/global_coeffs/pallas_call | solution.py:919
  56.3 0.1 collective-permute-done.6.refs_1_
  56.4 0.0 copy-done.2
  56.4 0.0 copy-done.4
  56.4 10.0 %up.1 = (f32[512,128]{1,0:T(8,128)}, f32[512,128]{1,0:T(8,128)}) custom-call(f32[16,40,128]{2,1,0:T(8,128)S(1)} %all-to-all-done.1.refs_0_, f32[16,40,128]{2,1,0:T(8,128)S(1)} %collective-permute-done.6.refs_1_, f32[3840,128]{1,0:T(8,128)S(1)} %global_coeffs.1.refs_2_, f32[2064,128]{1,0:T(8,128)S(1)} %copy-done.4, f32[2560,128]{1,0:T(8,128)S(1)} %copy-done.2, ...), custom_call_target="tpu_custom_call" | custom-call | flops 12000000000 | bytes 42737664 | tf_op jit(solution)/shard_map/up/pallas_call | solution.py:919
  (9 shorter events, 0.1 us)
Async XLA Ops:
  3.8 5.9 %collective-permute-start = (f32[184,128]{1,0:T(8,128)}, f32[184,128]{1,0:T(8,128)S(1)}, u32[]{:S(2)}, u32[]{:S(2)}) collective-permute-start(f32[184,128]{1,0:T(8,128)} %get-tuple-element.17), channel_id=1, source_target_pairs={{0,1},{1,0},{2,3},{3,2},{4,5},{5,4},{6,7},{7,6},{8,9},{9,8},{10,11... | collective-permute-start | bytes 282632 | tf_op jit(solution)/shard_map/ppermute | solution.py:945
  6.8 2.9 %collective-permute-start.1 = (f32[184,128]{1,0:T(8,128)}, f32[184,128]{1,0:T(8,128)S(1)}, u32[]{:S(2)}, u32[]{:S(2)}) collective-permute-start(f32[184,128]{1,0:T(8,128)} %get-tuple-element.18), channel_id=1, source_target_pairs={{1,2},{2,1},{5,6},{6,5},{9,10},{10,9},{13,14},{14,13},{17,18},{18,... | collective-permute-start | bytes 282632 | tf_op jit(solution)/shard_map/ppermute | solution.py:946
  7.5 18.8 %collective-permute-start.4 = (f32[1472,128]{1,0:T(8,128)}, f32[1472,128]{1,0:T(8,128)S(1)}, u32[]{:S(2)}, u32[]{:S(2)}) collective-permute-start(f32[1472,128]{1,0:T(8,128)} %get-tuple-element.21), channel_id=1, source_target_pairs={{0,4},{4,0},{8,12},{12,8},{16,20},{20,16},{24,28},{28,24},{1,5},{5... | collective-permute-start | bytes 2261000 | tf_op jit(solution)/shard_map/ppermute | solution.py:947
  7.6 18.7 %collective-permute-start.5 = (f32[1472,128]{1,0:T(8,128)}, f32[1472,128]{1,0:T(8,128)S(1)}, u32[]{:S(2)}, u32[]{:S(2)}) collective-permute-start(f32[1472,128]{1,0:T(8,128)} %get-tuple-element.22), channel_id=1, source_target_pairs={{4,8},{8,4},{12,16},{16,12},{20,24},{24,20},{5,9},{9,5},{13,17},{1... | collective-permute-start | bytes 2261000 | tf_op jit(solution)/shard_map/ppermute | solution.py:948
  9.9 5.4 %collective-permute-start.2 = (f32[208,128]{1,0:T(8,128)S(1)}, f32[208,128]{1,0:T(8,128)S(1)}, u32[]{:S(2)}, u32[]{:S(2)}) collective-permute-start(f32[208,128]{1,0:T(8,128)S(1)} %get-tuple-element.33), channel_id=1, source_target_pairs={{0,4},{4,0},{8,12},{12,8},{16,20},{20,16},{24,28},{28,24},{1,5},{5... | collective-permute-start | bytes 319496 | tf_op jit(solution)/shard_map/ppermute | solution.py:954
  11.4 14.8 %collective-permute-start.3 = (f32[208,128]{1,0:T(8,128)S(1)}, f32[208,128]{1,0:T(8,128)S(1)}, u32[]{:S(2)}, u32[]{:S(2)}) collective-permute-start(f32[208,128]{1,0:T(8,128)S(1)} %get-tuple-element.32), channel_id=1, source_target_pairs={{4,8},{8,4},{12,16},{16,12},{20,24},{24,20},{5,9},{9,5},{13,17},{1... | collective-permute-start | bytes 319496 | tf_op jit(solution)/shard_map/ppermute | solution.py:955
  12.1 1.3 %copy-start = (f32[2560,128]{1,0:T(8,128)S(1)}, f32[2560,128]{1,0:T(8,128)}, u32[]{:S(2)}) copy-start(f32[2560,128]{1,0:T(8,128)} %get-tuple-element.16.stack.refs_0_.refs_4_) | copy-start | bytes 3932164
  13.4 0.9 %copy-start.5 = (f32[192,128]{1,0:T(8,128)S(1)}, f32[192,128]{1,0:T(8,128)}, u32[]{:S(2)}) copy-start(f32[192,128]{1,0:T(8,128)} %get-tuple-element.19.share2) | copy-start | bytes 294916
  15.3 22.5 %all-to-all-start = ((f32[16,40,128]{2,1,0:T(8,128)}), f32[16,40,128]{2,1,0:T(8,128)S(1)}, u32[]{:S(2)}, u32[]{:S(2)}) async-start(f32[16,40,128]{2,1,0:T(8,128)} %bitcast.5), calls=%async_computation | async-start | bytes 655360 | tf_op jit(solution)/shard_map/all_to_all | solution.py:960
  26.3 1.3 %copy-start.1 = (f32[2560,128]{1,0:T(8,128)S(1)}, f32[2560,128]{1,0:T(8,128)}, u32[]{:S(2)}) copy-start(f32[2560,128]{1,0:T(8,128)} %get-tuple-element.16.stack.refs_0_.refs_4_) | copy-start | bytes 3932164
  27.6 16.2 %copy-start.6 = (f32[192,128]{1,0:T(8,128)S(1)}, f32[192,128]{1,0:T(8,128)}, u32[]{:S(2)}) copy-start(f32[192,128]{1,0:T(8,128)} %get-tuple-element.19.share2) | copy-start | bytes 294916
  37.9 16.9 %all-to-all-start.1 = ((f32[16,40,128]{2,1,0:T(8,128)}), f32[16,40,128]{2,1,0:T(8,128)S(1)}, u32[]{:S(2)}, u32[]{:S(2)}) async-start(f32[16,40,128]{2,1,0:T(8,128)} %bitcast.7), calls=%async_computation.1 | async-start | bytes 655360 | tf_op jit(solution)/shard_map/all_to_all | solution.py:981
  43.7 11.1 %collective-permute-start.7 = (f32[4,160,128]{2,1,0:T(8,128)S(1)}, f32[4,160,128]{2,1,0:T(8,128)S(1)}, u32[]{:S(2)}, u32[]{:S(2)}) collective-permute-start(f32[4,160,128]{2,1,0:T(8,128)S(1)} %bitcast.10), channel_id=1, source_target_pairs={{0,4},{4,0},{8,12},{12,8},{16,20},{20,16},{24,28},{28,24},{1,5},{5... | collective-permute-start | bytes 983048 | tf_op jit(solution)/shard_map/ppermute | solution.py:979
  46.0 1.0 %copy-start.3 = (f32[2064,128]{1,0:T(8,128)}, f32[2064,128]{1,0:T(8,128)S(1)}, u32[]{:S(2)}) copy-start(f32[2064,128]{1,0:T(8,128)S(1)} %window_coeffs.1.refs_3_) | copy-start | bytes 3170308
  47.0 9.4 %copy-start.2 = (f32[2560,128]{1,0:T(8,128)S(1)}, f32[2560,128]{1,0:T(8,128)}, u32[]{:S(2)}) copy-start(f32[2560,128]{1,0:T(8,128)} %get-tuple-element.16.stack.refs_0_.refs_4_) | copy-start | bytes 3932164
  54.8 1.6 %copy-start.4 = (f32[2064,128]{1,0:T(8,128)S(1)}, f32[2064,128]{1,0:T(8,128)}, u32[]{:S(2)}) copy-start(f32[2064,128]{1,0:T(8,128)} %copy-done.3) | copy-start | bytes 3170308
  54.8 1.6 %collective-permute-start.6 = (f32[16,40,128]{2,1,0:T(8,128)S(1)}, f32[16,40,128]{2,1,0:T(8,128)S(1)}, u32[]{:S(2)}, u32[]{:S(2)}) collective-permute-start(f32[16,40,128]{2,1,0:T(8,128)S(1)} %all-to-all-done.1.refs_0_), channel_id=1, source_target_pairs={{0,4},{4,0},{8,12},{12,8},{16,20},{20,16},{24,28},{28,24},{1,5},{5... | collective-permute-start | bytes 983048 | tf_op jit(solution)/shard_map/ppermute | solution.py:982

commit v10 on v9

--- a/solution.py
+++ b/solution.py
@@ -418,13 +418,13 @@
     return pltpu.roll(out, turn, 1)
 
 
-def share_kernel(devices, share2, stack, copies):
+def share_blocks(kinds):
     iy = lax.axis_index("gy")
     y, lane = iota((128, 128), 0), iota((128, 128), 1)
     x_in, y_in = y // 32, y % 32
     x_out, y_out = lane % 32 // 16, lane % 16
     pair_y, pair_x = y_in // 2 == y_out, x_in // 2 == x_out
-    a, b, c, d, kappa, cz = (share2[pl.ds(t * NZ, NZ), :] for t in range(6))
+    a, b, c, d, kappa, cz = kinds
     eighth = lambda mask: matrix(mask, 0.125)
     blocks = [
         mix(a, eighth(pair_y & (x_in == 2 * x_out))) + mix(b, eighth(pair_y & (x_in == 1) & (x_out == 1))),
@@ -434,10 +434,7 @@
         mix(kappa, matrix(pair_x & pair_y, 0.25)),
         mix(cz, matrix(pair_x & pair_y, 0.25)),
     ]
-    for t, cells in enumerate(blocks):
-        cells = fold_planes(cells, 16 * iy)
-        for n in range(devices):
-            copies[pl.ds(n * SHARE + 8 * t, 8), :] = cells
+    return [fold_planes(cells, 16 * iy) for cells in blocks]
 
 
 def fetch_all(sources, dests, sems, first=0):
@@ -447,7 +444,7 @@
     return copies
 
 
-def pack_kernel(f_in, kappa_in, cx_in, cy_in, cz_in, x_near, x_far, y_near, y_far, share2, stack, sems):
+def pack_kernel(devices, f_in, kappa_in, cx_in, cy_in, cz_in, x_near, x_far, y_near, y_far, share2, stack, copies, sems):
     even_x, even_y = lax.axis_index("gx") % 2 == 0, lax.axis_index("gy") % 2 == 0
     tiles = [stack.at[pl.ds(a * NZ * TX, NZ * TX), :] for a in range(5)]
     for copy in fetch_all((f_in, kappa_in, cx_in, cy_in, cz_in), tiles, sems):
@@ -480,6 +477,9 @@
     kinds = [merge(stack[:128], 1 / 128), merge(stack[128:256], 1 / 128)]
     kinds += [merge(sides[:, :128], 1 / 128), merge(sides[:, 128:], 1 / 128)]
     kinds += [merge(stack[256:384], 1 / 16), merge(stack[384:], 1 / 16)]
+    for t, cells in enumerate(share_blocks(kinds)):
+        for n in range(devices):
+            copies[pl.ds(n * SHARE + 8 * t, 8), :] = cells
     head = [jnp.zeros((8, 128), F32)] * 3
     tail = [jnp.zeros((8, 128), F32)] * 3
     slot = iota((8, 128), 1) % 32 // 4
@@ -774,7 +774,7 @@
             same = core == jx % 2
             return jnp.where(same, own[jx // 2 * gy + jy, at, :], other[jx // 2 * gy + jy, at, :])
         return jx[1][jx[0] // 2 * gy + jy, at, :]
-    f2, u2, kept2, wide, e_ref, e0_ref, kept0, u3, f3, r3, f4, u4 = take(12)
+    f2, u2, kept2, wide, e_ref, e0_ref, kept0, u3, f3, r3, f4, u4, pairs4 = take(13)
 
     rows, cols = 2 * gx, 16 * gy
     assemble3(lambda jx, jy: gathered(jx, jy, pl.ds(NZ, 8)), f3, gx, gy, rows)
@@ -794,29 +794,40 @@
     yy, jj = iota((128, 128), 0), iota((128, 128), 1)
     f4[...] = 0.25 * mix(fine.every_second(0, size, 0) + fine.every_second(0, size, 1), matrix(yy // 2 == jj))
     f4, u4 = Field(f4, rows), Field(u4, rows)
-    x_face4, y_face4, inv4, g4, c4 = stack_fields(whole, rows, 5, z_face=False, start=5 * NZ * 2 * rows)
-    line4 = StoredLine(inv4, g4, c4)
-    zero = jnp.zeros((rows, 128), F32)
+    first = iota((rows, 128), 1) < 64
+    fields = (f4, *stack_fields(whole, rows, 5, z_face=False, start=5 * NZ * 2 * rows))
+    pairs = [Field(pairs4, rows, 1, HALF, n * HALF * rows) for n in range(7)]
+    for field, pair in zip(fields, pairs):
+        for k in range(HALF):
+            pair[k] = jnp.where(first, field[k], shift(field[NZ - 1 - k], 64, 1))
+    fp, x_facep, y_facep, invp, gp, cp, up4 = pairs
+    middle = cp[HALF - 1]
+    scale = 1.0 / (1.0 - middle * shift(middle, 64, 1))
 
     def solve4(rhs, old):
-        kept, out = {}, {}
-        ends = sweep_in(rhs, line4, kept, zero, None)
-
-        def emit(k, value):
-            out[k] = OMEGA * value if old is None else (1.0 - OMEGA) * old[k] + OMEGA * value
-
-        sweep_out(ends, kept, line4, emit, None)
-        for k in range(NZ):
-            u4[k] = out[k]
-
-    solve4(lambda k: f4[k], None)
+        value = rhs(0) * invp[0]
+        kept = [value]
+        for k in range(1, HALF):
+            value = rhs(k) * invp[k] + gp[k] * value
+            kept.append(value)
+        value = (value + middle * shift(value, 64, 1)) * scale
+        for k in reversed(range(HALF)):
+            up4[k] = OMEGA * value if old is None else (1.0 - OMEGA) * old[k] + OMEGA * value
+            if k:
+                value = kept[k - 1] + cp[k - 1] * value
+
+    solve4(lambda k: fp[k], None)
 
     def relax(sweep, carry):
-        old = [u4[k] for k in range(NZ)]
-        solve4(lambda k: f4[k] + neighbours(old[k], x_face4[k], y_face4[k]), old)
+        old = [up4[k] for k in range(HALF)]
+        solve4(lambda k: fp[k] + neighbours(old[k], x_facep[k], y_facep[k]), old)
         return carry
 
     lax.fori_loop(0, COARSE_SWEEPS - 1, relax, 0)
+    for k in range(HALF):
+        both = up4[k]
+        u4[k] = jnp.where(first, both, 0.0)
+        u4[NZ - 1 - k] = jnp.where(first, shift(both, 64, 1), 0.0)
 
     cells = u4.ref[...].reshape(NZ, rows, 128)
     x = iota((1, rows, 128), 1)
@@ -909,7 +920,7 @@
 SAVED_ROWS = 72 * 1024
 MEBIBYTES = {"pack": 56}
 COSTS = {
-    "pack": 3 * 10**9, "share": 10**9, "down": 10**10,
+    "pack": 3 * 10**9, "down": 10**10,
     "window_coeffs": 4 * 10**9, "global_coeffs": 4 * 10**9, "up": 12 * 10**9,
 }
 
@@ -939,15 +950,19 @@
     near = lambda n: [(i, i ^ 1) for i in range(n)]
     far = lambda n: [(i, (i + 1 ^ 1) - 1) for i in range(1, n - 1)]
     even_x, even_y = lax.axis_index("gx") % 2 == 0, lax.axis_index("gy") % 2 == 0
-    x_near, x_far, y_near, y_far, share2, stack = call(
-        pack_kernel, "pack", [slab, slab, strip, strip, (6 * NZ, 128), (5 * NZ * TX, TY)], tiles, [dma(5)], [HBM] * 5
+    x_near, x_far, y_near, y_far, share2, stack, copies = call(
+        functools.partial(pack_kernel, devices // 2),
+        "pack",
+        [slab, slab, strip, strip, (6 * NZ, 128), (5 * NZ * TX, TY), (devices // 2 * SHARE, 128)],
+        tiles,
+        [dma(5)],
+        [HBM] * 5,
     )
     y_near = lax.ppermute(y_near, "gy", near(gy))
     y_far = lax.ppermute(y_far, "gy", far(gy))
     x_near = lax.ppermute(x_near, "gx", near(gx))
     x_far = lax.ppermute(x_far, "gx", far(gx))
     yr, yl = jnp.where(even_y, y_near, y_far), jnp.where(even_y, y_far, y_near)
-    copies = call(functools.partial(share_kernel, devices // 2), "share", [(devices // 2 * SHARE, 128)], [share2, stack])[0]
     half = STRIP // 2
     head = jnp.concatenate([yl[:half], yl[STRIP:], yr[:half], yr[STRIP:]])
     tail = jnp.concatenate([yl[half:], yr[half:]])
@@ -995,7 +1010,7 @@
         [(NZ * TX, TY)] * 2,
         [own_blocks, other_blocks, whole, k2, stack, saved],
         [vm(total0, 128), vm(total1, 128)] + level(TX, 3) + [vm(NZ * 2 * TX, 128), vm(*size), vm(*big), vm(*big)]
-        + level(rows3, 3) + level(rows4, 2) + [dma(2)],
+        + level(rows3, 3) + level(rows4, 2) + [vm(7 * HALF * rows4, 128), dma(2)],
         in_specs=[VMEM] * 5 + [ANY],
     )
     return field.reshape(right_side.shape), residual.reshape(right_side.shape)

time: 66.9 us -> 65 us (0.972)
  local copies, waits for them, and re-layouts: 4.53 us -> 2.33 us
    unnamed x14 -> x10, local copies, waits for them, and re-layouts: 4.5 us -> 2.3 us
    pallas_call x6 -> x5, Pallas kernels: 27.1 us -> 27 us  [call(): pl.pallas_call(kernel, name=name, out_shape=shapes, in_specs=in_specs or...]
  transfers between devices with their start and end apart: 10 -> 10, of which waited for: 4 -> 5; matrix products, arithmetic and copies ran while one was open for 0% -> 0% of each run, Pallas kernels for 21% -> 20%
where the time goes in v10:
time: 65 us; the launch traced here: 64.6 us
  Pallas kernels  27 us (42%)
  starting transfers between devices  23.8 us (37%)
  waiting for transfers between devices  10.6 us (16%)
  local copies, waits for them, and re-layouts  2.33 us (4%)
  between operations  0.85 us (1%)
    pallas_call x5, Pallas kernels, call(): pl.pallas_call(kernel, name=name, out_shape=shapes, in_specs=in_specs or...  27 us
    all_to_all x2, starting transfers between devices, body(): lax.all_to_all(blocks, ('gx', 'gy'), 0, 0, axis_index_groups=cores)  17.1 us
    all_to_all x2, waiting for transfers between devices, body(): lax.all_to_all(blocks, ('gx', 'gy'), 0, 0, axis_index_groups=cores)  8.76 us
    ppermute x1, starting transfers between devices, body(): y_near = lax.ppermute(y_near, 'gy', near(gy))  3 us
    unnamed x10, local copies, waits for them, and re-layouts  2.3 us
    ppermute x1, starting transfers between devices, body(): c_near = lax.ppermute(jnp.where(even_x, tail, head), 'gx', near(gx))  1.54 us
    ppermute x1, waiting for transfers between devices, body(): y_near = lax.ppermute(y_near, 'gy', near(gy))  1.44 us
  transfers between devices with their start and end apart: 10, of which 5 were waited for; matrix products, arithmetic and copies ran while one was open for 0% of the time, Pallas kernels for 20%

profile of v10, /device:TPU:0, one launch (start us, length us, event | category | flops | bytes accessed | tf_op | source)
XLA Modules:
  0.0 64.6 jit_solution(8451465046526898998)
XLA Ops:
  0.6 3.4 %pack.1 = (f32[1472,128]{1,0:T(8,128)}, f32[1472,128]{1,0:T(8,128)}, f32[184,128]{1,0:T(8,128)}, f32[184,128]{1,0:T(8,128)}, f32[192,128]{1,0:T(8,128)}, /*index=5*/f32[2560,128]{1,0:T(8,128)}, f32[640,128]{1,0:T(8,128)}) custom-call(f32[512,128]{1,0:T(8,128)} %bitcast.13, f32[512,128]{1,0:T(8,128)} %bitcast.14, f32[512,128]{1,0:T(8,128)} %bitcast.15, ...), custom_call_target="tpu_custom_call" | custom-call | flops 3000000000 | bytes 1310720 | tf_op jit(solution)/shard_map/pack/pallas_call | solution.py:930
  4.0 3.0 %collective-permute-start = (f32[184,128]{1,0:T(8,128)}, f32[184,128]{1,0:T(8,128)S(1)}, u32[]{:S(2)}, u32[]{:S(2)}) collective-permute-start(f32[184,128]{1,0:T(8,128)} %get-tuple-element.18), channel_id=1, source_target_pairs={{0,1},{1,0},{2,3},{3,2},{4,5},{5,4},{6,7},{7,6},{8,9},{9,8},{10,11... | collective-permute-start | bytes 282632 | tf_op jit(solution)/shard_map/ppermute | solution.py:961
  7.0 0.7 %collective-permute-start.1 = (f32[184,128]{1,0:T(8,128)}, f32[184,128]{1,0:T(8,128)S(1)}, u32[]{:S(2)}, u32[]{:S(2)}) collective-permute-start(f32[184,128]{1,0:T(8,128)} %get-tuple-element.19), channel_id=1, source_target_pairs={{1,2},{2,1},{5,6},{6,5},{9,10},{10,9},{13,14},{14,13},{17,18},{18,... | collective-permute-start | bytes 282632 | tf_op jit(solution)/shard_map/ppermute | solution.py:962
  7.7 0.1 collective-permute-start.4
  7.8 0.7 %collective-permute-start.5 = (f32[1472,128]{1,0:T(8,128)}, f32[1472,128]{1,0:T(8,128)S(1)}, u32[]{:S(2)}, u32[]{:S(2)}) collective-permute-start(f32[1472,128]{1,0:T(8,128)} %get-tuple-element.23), channel_id=1, source_target_pairs={{4,8},{8,4},{12,16},{16,12},{20,24},{24,20},{5,9},{9,5},{13,17},{1... | collective-permute-start | bytes 2261000 | tf_op jit(solution)/shard_map/ppermute | solution.py:964
  8.5 1.4 %collective-permute-done = f32[184,128]{1,0:T(8,128)S(1)} collective-permute-done((f32[184,128]{1,0:T(8,128)}, f32[184,128]{1,0:T(8,128)S(1)}, u32[]{:S(2)}, u32[]{:S(2)}) %collective-permute-start) | collective-permute-done | bytes 94240 | tf_op jit(solution)/shard_map/ppermute | solution.py:961
  9.9 0.0 collective-permute-done.1
  10.1 1.5 %collective-permute-start.2 = (f32[208,128]{1,0:T(8,128)S(1)}, f32[208,128]{1,0:T(8,128)S(1)}, u32[]{:S(2)}, u32[]{:S(2)}) collective-permute-start(f32[208,128]{1,0:T(8,128)S(1)} %get-tuple-element.35), channel_id=1, source_target_pairs={{0,4},{4,0},{8,12},{12,8},{16,20},{20,16},{24,28},{28,24},{1,5},{5... | collective-permute-start | bytes 319496 | tf_op jit(solution)/shard_map/ppermute | solution.py:969
  11.6 0.7 %collective-permute-start.3 = (f32[208,128]{1,0:T(8,128)S(1)}, f32[208,128]{1,0:T(8,128)S(1)}, u32[]{:S(2)}, u32[]{:S(2)}) collective-permute-start(f32[208,128]{1,0:T(8,128)S(1)} %get-tuple-element.34), channel_id=1, source_target_pairs={{4,8},{8,4},{12,16},{16,12},{20,24},{24,20},{5,9},{9,5},{13,17},{1... | collective-permute-start | bytes 319496 | tf_op jit(solution)/shard_map/ppermute | solution.py:970
  12.3 0.3 collective-permute-done.2
  12.6 10.6 %all-to-all-start = ((f32[16,40,128]{2,1,0:T(8,128)}), f32[16,40,128]{2,1,0:T(8,128)S(1)}, u32[]{:S(2)}, u32[]{:S(2)}) async-start(f32[16,40,128]{2,1,0:T(8,128)} %bitcast.12), calls=%async_computation | async-start | bytes 655360 | tf_op jit(solution)/shard_map/all_to_all | solution.py:975
  23.2 0.0 collective-permute-done.3
  23.3 0.0 collective-permute-done.4.refs_5_.x_near
  23.3 0.0 collective-permute-done.5.refs_6_.x_far
  23.3 0.0 copy-start
  23.3 1.3 %copy-done = f32[2560,128]{1,0:T(8,128)S(1)} copy-done((f32[2560,128]{1,0:T(8,128)S(1)}, f32[2560,128]{1,0:T(8,128)}, u32[]{:S(2)}) %copy-start) | copy-done | bytes 1310744
  24.6 0.0 copy-start.4
  24.6 9.2 %down.1 = (f32[640,128]{1,0:T(8,128)}, f32[73728,128]{1,0:T(8,128)}) custom-call(f32[2560,128]{1,0:T(8,128)S(1)} %copy-done, f32[184,128]{1,0:T(8,128)S(1)} %get-tuple-element.37.refs_1_.yr, f32[184,128]{1,0:T(8,128)S(1)} %get-tuple-element.36.refs_2_.yl, f32[208,128]{1,0:T(8,128)S(1)} %get-tuple-element.33.refs_3_.cr, ...), custom_call_target="tpu_custom_call" | custom-call | flops 10000000000 | bytes 3219456 | tf_op jit(solution)/shard_map/down/pallas_call | solution.py:930
  33.8 1.1 %all-to-all-done = f32[16,40,128]{2,1,0:T(8,128)S(1)} async-done(((f32[16,40,128]{2,1,0:T(8,128)}), f32[16,40,128]{2,1,0:T(8,128)S(1)}, u32[]{:S(2)}, u32[]{:S(2)}) %all-to-all-start) | async-done | bytes 327712 | tf_op jit(solution)/shard_map/all_to_all | solution.py:975
  34.8 6.4 %all-to-all-start.1 = ((f32[16,40,128]{2,1,0:T(8,128)}), f32[16,40,128]{2,1,0:T(8,128)S(1)}, u32[]{:S(2)}, u32[]{:S(2)}) async-start(f32[16,40,128]{2,1,0:T(8,128)} %bitcast.7), calls=%async_computation.1 | async-start | bytes 655360 | tf_op jit(solution)/shard_map/all_to_all | solution.py:996
  41.3 0.1 collective-permute-start.7
  41.4 0.0 copy-done.4
  41.4 2.2 %window_coeffs.1.refs_3_ = f32[2064,128]{1,0:T(8,128)S(1)} custom-call(f32[192,128]{1,0:T(8,128)S(1)} %copy-done.4, f32[1472,128]{1,0:T(8,128)S(1)} %collective-permute-done.4.refs_5_.x_near, f32[1472,128]{1,0:T(8,128)S(1)} %collective-permute-done.5.refs_6_.x_far, f32[184,128]{1,0:T(8,128)S(1)} %get-tuple-element.37.refs_1_.yr, ...), custom_call_target="tpu_custom_call" | custom-call | flops 4000000000 | bytes 2007040 | tf_op jit(solution)/shard_map/window_coeffs/pallas_call | solution.py:930
  43.6 0.0 copy-start.2
  43.6 1.0 %copy-done.2 = f32[2064,128]{1,0:T(8,128)} copy-done((f32[2064,128]{1,0:T(8,128)}, f32[2064,128]{1,0:T(8,128)S(1)}, u32[]{:S(2)}) %copy-start.2) | copy-done | bytes 1056792
  44.5 0.0 copy-start.1
  44.6 7.7 %all-to-all-done.1.refs_0_ = f32[16,40,128]{2,1,0:T(8,128)S(1)} async-done(((f32[16,40,128]{2,1,0:T(8,128)}), f32[16,40,128]{2,1,0:T(8,128)S(1)}, u32[]{:S(2)}, u32[]{:S(2)}) %all-to-all-start.1) | async-done | bytes 327712 | tf_op jit(solution)/shard_map/all_to_all | solution.py:996
  52.2 0.0 copy-start.3
  52.2 0.0 collective-permute-start.6
  52.2 0.0 collective-permute-done.7.other
  52.2 1.5 %global_coeffs.1.refs_2_ = f32[3840,128]{1,0:T(8,128)S(1)} custom-call(f32[4,160,128]{2,1,0:T(8,128)S(1)} %bitcast.11, f32[4,160,128]{2,1,0:T(8,128)S(1)} %collective-permute-done.7.other), custom_call_target="tpu_custom_call" | custom-call | flops 4000000000 | bytes 655360 | tf_op jit(solution)/shard_map/global_coeffs/pallas_call | solution.py:930
  53.8 0.1 collective-permute-done.6.refs_1_
  53.9 0.0 copy-done.1
  53.9 0.0 copy-done.3
  53.9 10.7 %up.1 = (f32[512,128]{1,0:T(8,128)}, f32[512,128]{1,0:T(8,128)}) custom-call(f32[16,40,128]{2,1,0:T(8,128)S(1)} %all-to-all-done.1.refs_0_, f32[16,40,128]{2,1,0:T(8,128)S(1)} %collective-permute-done.6.refs_1_, f32[3840,128]{1,0:T(8,128)S(1)} %global_coeffs.1.refs_2_, f32[2064,128]{1,0:T(8,128)S(1)} %copy-done.3, f32[2560,128]{1,0:T(8,128)S(1)} %copy-done.1, ...), custom_call_target="tpu_custom_call" | custom-call | flops 12000000000 | bytes 42737664 | tf_op jit(solution)/shard_map/up/pallas_call | solution.py:930
  (9 shorter events, 0.1 us)
Async XLA Ops:
  4.0 5.9 %collective-permute-start = (f32[184,128]{1,0:T(8,128)}, f32[184,128]{1,0:T(8,128)S(1)}, u32[]{:S(2)}, u32[]{:S(2)}) collective-permute-start(f32[184,128]{1,0:T(8,128)} %get-tuple-element.18), channel_id=1, source_target_pairs={{0,1},{1,0},{2,3},{3,2},{4,5},{5,4},{6,7},{7,6},{8,9},{9,8},{10,11... | collective-permute-start | bytes 282632 | tf_op jit(solution)/shard_map/ppermute | solution.py:961
  7.0 2.9 %collective-permute-start.1 = (f32[184,128]{1,0:T(8,128)}, f32[184,128]{1,0:T(8,128)S(1)}, u32[]{:S(2)}, u32[]{:S(2)}) collective-permute-start(f32[184,128]{1,0:T(8,128)} %get-tuple-element.19), channel_id=1, source_target_pairs={{1,2},{2,1},{5,6},{6,5},{9,10},{10,9},{13,14},{14,13},{17,18},{18,... | collective-permute-start | bytes 282632 | tf_op jit(solution)/shard_map/ppermute | solution.py:962
  7.7 15.6 %collective-permute-start.4 = (f32[1472,128]{1,0:T(8,128)}, f32[1472,128]{1,0:T(8,128)S(1)}, u32[]{:S(2)}, u32[]{:S(2)}) collective-permute-start(f32[1472,128]{1,0:T(8,128)} %get-tuple-element.22), channel_id=1, source_target_pairs={{0,4},{4,0},{8,12},{12,8},{16,20},{20,16},{24,28},{28,24},{1,5},{5... | collective-permute-start | bytes 2261000 | tf_op jit(solution)/shard_map/ppermute | solution.py:963
  7.8 15.5 %collective-permute-start.5 = (f32[1472,128]{1,0:T(8,128)}, f32[1472,128]{1,0:T(8,128)S(1)}, u32[]{:S(2)}, u32[]{:S(2)}) collective-permute-start(f32[1472,128]{1,0:T(8,128)} %get-tuple-element.23), channel_id=1, source_target_pairs={{4,8},{8,4},{12,16},{16,12},{20,24},{24,20},{5,9},{9,5},{13,17},{1... | collective-permute-start | bytes 2261000 | tf_op jit(solution)/shard_map/ppermute | solution.py:964
  10.1 2.5 %collective-permute-start.2 = (f32[208,128]{1,0:T(8,128)S(1)}, f32[208,128]{1,0:T(8,128)S(1)}, u32[]{:S(2)}, u32[]{:S(2)}) collective-permute-start(f32[208,128]{1,0:T(8,128)S(1)} %get-tuple-element.35), channel_id=1, source_target_pairs={{0,4},{4,0},{8,12},{12,8},{16,20},{20,16},{24,28},{28,24},{1,5},{5... | collective-permute-start | bytes 319496 | tf_op jit(solution)/shard_map/ppermute | solution.py:969
  11.6 11.6 %collective-permute-start.3 = (f32[208,128]{1,0:T(8,128)S(1)}, f32[208,128]{1,0:T(8,128)S(1)}, u32[]{:S(2)}, u32[]{:S(2)}) collective-permute-start(f32[208,128]{1,0:T(8,128)S(1)} %get-tuple-element.34), channel_id=1, source_target_pairs={{4,8},{8,4},{12,16},{16,12},{20,24},{24,20},{5,9},{9,5},{13,17},{1... | collective-permute-start | bytes 319496 | tf_op jit(solution)/shard_map/ppermute | solution.py:970
  12.6 22.3 %all-to-all-start = ((f32[16,40,128]{2,1,0:T(8,128)}), f32[16,40,128]{2,1,0:T(8,128)S(1)}, u32[]{:S(2)}, u32[]{:S(2)}) async-start(f32[16,40,128]{2,1,0:T(8,128)} %bitcast.12), calls=%async_computation | async-start | bytes 655360 | tf_op jit(solution)/shard_map/all_to_all | solution.py:975
  23.3 1.3 %copy-start = (f32[2560,128]{1,0:T(8,128)S(1)}, f32[2560,128]{1,0:T(8,128)}, u32[]{:S(2)}) copy-start(f32[2560,128]{1,0:T(8,128)} %get-tuple-element.17.refs_0_.refs_4_) | copy-start | bytes 3932164
  24.6 16.8 %copy-start.4 = (f32[192,128]{1,0:T(8,128)S(1)}, f32[192,128]{1,0:T(8,128)}, u32[]{:S(2)}) copy-start(f32[192,128]{1,0:T(8,128)} %get-tuple-element.28.share2) | copy-start | bytes 294916
  34.8 17.4 %all-to-all-start.1 = ((f32[16,40,128]{2,1,0:T(8,128)}), f32[16,40,128]{2,1,0:T(8,128)S(1)}, u32[]{:S(2)}, u32[]{:S(2)}) async-start(f32[16,40,128]{2,1,0:T(8,128)} %bitcast.7), calls=%async_computation.1 | async-start | bytes 655360 | tf_op jit(solution)/shard_map/all_to_all | solution.py:996
  41.3 11.0 %collective-permute-start.7 = (f32[4,160,128]{2,1,0:T(8,128)S(1)}, f32[4,160,128]{2,1,0:T(8,128)S(1)}, u32[]{:S(2)}, u32[]{:S(2)}) collective-permute-start(f32[4,160,128]{2,1,0:T(8,128)S(1)} %bitcast.10), channel_id=1, source_target_pairs={{0,4},{4,0},{8,12},{12,8},{16,20},{20,16},{24,28},{28,24},{1,5},{5... | collective-permute-start | bytes 983048 | tf_op jit(solution)/shard_map/ppermute | solution.py:994
  43.6 1.0 %copy-start.2 = (f32[2064,128]{1,0:T(8,128)}, f32[2064,128]{1,0:T(8,128)S(1)}, u32[]{:S(2)}) copy-start(f32[2064,128]{1,0:T(8,128)S(1)} %window_coeffs.1.refs_3_) | copy-start | bytes 3170308
  44.5 9.3 %copy-start.1 = (f32[2560,128]{1,0:T(8,128)S(1)}, f32[2560,128]{1,0:T(8,128)}, u32[]{:S(2)}) copy-start(f32[2560,128]{1,0:T(8,128)} %get-tuple-element.17.refs_0_.refs_4_) | copy-start | bytes 3932164
  52.2 1.6 %copy-start.3 = (f32[2064,128]{1,0:T(8,128)S(1)}, f32[2064,128]{1,0:T(8,128)}, u32[]{:S(2)}) copy-start(f32[2064,128]{1,0:T(8,128)} %copy-done.2) | copy-start | bytes 3170308
  52.2 1.6 %collective-permute-start.6 = (f32[16,40,128]{2,1,0:T(8,128)S(1)}, f32[16,40,128]{2,1,0:T(8,128)S(1)}, u32[]{:S(2)}, u32[]{:S(2)}) collective-permute-start(f32[16,40,128]{2,1,0:T(8,128)S(1)} %all-to-all-done.1.refs_0_), channel_id=1, source_target_pairs={{0,4},{4,0},{8,12},{12,8},{16,20},{20,16},{24,28},{28,24},{1,5},{5... | collective-permute-start | bytes 983048 | tf_op jit(solution)/shard_map/ppermute | solution.py:997

commit v11 on v9

--- a/solution.py
+++ b/solution.py
@@ -418,13 +418,13 @@
     return pltpu.roll(out, turn, 1)
 
 
-def share_kernel(devices, share2, stack, copies):
+def share_blocks(kinds):
     iy = lax.axis_index("gy")
     y, lane = iota((128, 128), 0), iota((128, 128), 1)
     x_in, y_in = y // 32, y % 32
     x_out, y_out = lane % 32 // 16, lane % 16
     pair_y, pair_x = y_in // 2 == y_out, x_in // 2 == x_out
-    a, b, c, d, kappa, cz = (share2[pl.ds(t * NZ, NZ), :] for t in range(6))
+    a, b, c, d, kappa, cz = kinds
     eighth = lambda mask: matrix(mask, 0.125)
     blocks = [
         mix(a, eighth(pair_y & (x_in == 2 * x_out))) + mix(b, eighth(pair_y & (x_in == 1) & (x_out == 1))),
@@ -434,10 +434,7 @@
         mix(kappa, matrix(pair_x & pair_y, 0.25)),
         mix(cz, matrix(pair_x & pair_y, 0.25)),
     ]
-    for t, cells in enumerate(blocks):
-        cells = fold_planes(cells, 16 * iy)
-        for n in range(devices):
-            copies[pl.ds(n * SHARE + 8 * t, 8), :] = cells
+    return [fold_planes(cells, 16 * iy) for cells in blocks]
 
 
 def fetch_all(sources, dests, sems, first=0):
@@ -447,7 +444,7 @@
     return copies
 
 
-def pack_kernel(f_in, kappa_in, cx_in, cy_in, cz_in, x_near, x_far, y_near, y_far, share2, stack, sems):
+def pack_kernel(devices, f_in, kappa_in, cx_in, cy_in, cz_in, x_near, x_far, y_near, y_far, share2, stack, copies, sems):
     even_x, even_y = lax.axis_index("gx") % 2 == 0, lax.axis_index("gy") % 2 == 0
     tiles = [stack.at[pl.ds(a * NZ * TX, NZ * TX), :] for a in range(5)]
     for copy in fetch_all((f_in, kappa_in, cx_in, cy_in, cz_in), tiles, sems):
@@ -480,6 +477,9 @@
     kinds = [merge(stack[:128], 1 / 128), merge(stack[128:256], 1 / 128)]
     kinds += [merge(sides[:, :128], 1 / 128), merge(sides[:, 128:], 1 / 128)]
     kinds += [merge(stack[256:384], 1 / 16), merge(stack[384:], 1 / 16)]
+    for t, cells in enumerate(share_blocks(kinds)):
+        for n in range(devices):
+            copies[pl.ds(n * SHARE + 8 * t, 8), :] = cells
     head = [jnp.zeros((8, 128), F32)] * 3
     tail = [jnp.zeros((8, 128), F32)] * 3
     slot = iota((8, 128), 1) % 32 // 4
@@ -687,9 +687,9 @@
         diag[z] = base_diag(jnp.where(mask0 > 0, kappa_k, 1.0), x_k, y_k)
         return cz_k
 
-    last = loop(NZ, prepare, jnp.zeros((rows, 256), F32), 2)
+    last = loop(NZ, prepare, jnp.zeros((rows, 256), F32), 4)
     z_face[NZ] = 0.5 * last
-    ends = factor(diag, z_face, tiles, inv, 4, f0, kept)
+    ends = factor(diag, z_face, tiles, inv, 8, f0, kept)
     copies = []
 
     def save(field):
@@ -701,7 +701,7 @@
 
     for field in (x_face, y_face, inv, f0):
         save(field)
-    smooth_down(f0, x_face, y_face, Line(inv, z_face), ends, kept, u, r, 2)
+    smooth_down(f0, x_face, y_face, Line(inv, z_face), ends, kept, u, r, 5)
     save(u)
     save(z_face)
 
@@ -823,7 +823,7 @@
     before = jnp.where(x > 0, shift(cells, 1, 1), 0.0)
     after = jnp.where(x < rows - 1, shift(cells, -1, 1), 0.0)
     spread_rows(cells, before, after, wide, size)
-    e_ref[...] = mix(wide[pl.ds(0, 2 * size), :], spread_matrix(iota((128, 128), 1), 0, cols), 3)
+    e_ref[...] = mix(wide[pl.ds(0, 2 * size), :], spread_matrix(iota((128, 128), 1), 0, cols))
     rows, cols = 2 * rows, 2 * cols
     smooth_up(f3, x_face3, y_face3, line3, u3, Field(e_ref, rows), r3, None, None)
 
@@ -855,7 +855,7 @@
     spread_rows(ring(cells, 4), ring(shift(cells, 1, 1), 4), ring(shift(cells, -1, 1), 4), wide, NZ * 8)
     lane = iota((128, 128), 1)
     fine_y = jnp.where(lane < 80, lane, lane - 128) + 32 * iy
-    e_ref[...] = mix(wide[pl.ds(0, NZ * TX), :], spread_matrix(fine_y, 0, cols), 3)
+    e_ref[...] = mix(wide[pl.ds(0, NZ * TX), :], spread_matrix(fine_y, 0, cols))
     mask2 = window_mask(TX, 128, 4, 32, 4, ix, iy, 4 * gx, 32 * gy)
     smooth_up(f2, x_face2, y_face2, line2, u2, Field(e_ref, TX), kept2, mask2, None)
 
@@ -863,7 +863,7 @@
     ring = lambda v: jnp.where(iota((1, 8, 128), 1) < 6, v[:, :8], v[:, 8:])
     spread_rows(ring(cells), ring(shift(cells, 1, 1)), ring(shift(cells, -1, 1)), wide, NZ * 8)
     fine_y = jnp.where(lane < 96, lane, lane - 128)
-    e_ref[...] = mix(wide[pl.ds(0, NZ * TX), :], spread_matrix(fine_y, 0, 0, circular=True), 3)
+    e_ref[...] = mix(wide[pl.ds(0, NZ * TX), :], spread_matrix(fine_y, 0, 0, circular=True))
     fetched[0].wait()
     x_face1, y_face1, inv1, f1, u1, z_face1 = stack_fields(held1, TX, 5)
     line1 = Line(inv1, z_face1)
@@ -876,13 +876,13 @@
     weights = spread_matrix(iota((128, 256), 1), 0, 0, circular=True)
     e0 = Field(e0_ref, rows, 2)
     for k in range(0, NZ, 8):
-        cells = mix(wide[pl.ds(k * rows, 8 * rows), :], weights, 3)
+        cells = mix(wide[pl.ds(k * rows, 8 * rows), :], weights)
         for t in range(2):
             e0_ref[pl.ds(e0.base(t, k), 8 * rows), :] = cells[:, 128 * t : 128 * (t + 1)]
     fetched[1].wait()
     x_face0, y_face0, inv0, f0, u0, z_face0 = stack_fields(held0, rows, 5, 2)
     mask0 = window_mask(rows, 256, TX, TY, HALO, ix, iy, TX * gx, TY * gy)
-    smooth_up(f0, x_face0, y_face0, Line(inv0, z_face0), u0, e0, Field(kept0, rows, 2), mask0, 2)
+    smooth_up(f0, x_face0, y_face0, Line(inv0, z_face0), u0, e0, Field(kept0, rows, 2), mask0, 4)
 
     kappa = Field(stack, TX, start=NZ * TX)
 
@@ -909,7 +909,7 @@
 SAVED_ROWS = 72 * 1024
 MEBIBYTES = {"pack": 56}
 COSTS = {
-    "pack": 3 * 10**9, "share": 10**9, "down": 10**10,
+    "pack": 3 * 10**9, "down": 10**10,
     "window_coeffs": 4 * 10**9, "global_coeffs": 4 * 10**9, "up": 12 * 10**9,
 }
 
@@ -939,15 +939,19 @@
     near = lambda n: [(i, i ^ 1) for i in range(n)]
     far = lambda n: [(i, (i + 1 ^ 1) - 1) for i in range(1, n - 1)]
     even_x, even_y = lax.axis_index("gx") % 2 == 0, lax.axis_index("gy") % 2 == 0
-    x_near, x_far, y_near, y_far, share2, stack = call(
-        pack_kernel, "pack", [slab, slab, strip, strip, (6 * NZ, 128), (5 * NZ * TX, TY)], tiles, [dma(5)], [HBM] * 5
+    x_near, x_far, y_near, y_far, share2, stack, copies = call(
+        functools.partial(pack_kernel, devices // 2),
+        "pack",
+        [slab, slab, strip, strip, (6 * NZ, 128), (5 * NZ * TX, TY), (devices // 2 * SHARE, 128)],
+        tiles,
+        [dma(5)],
+        [HBM] * 5,
     )
     y_near = lax.ppermute(y_near, "gy", near(gy))
     y_far = lax.ppermute(y_far, "gy", far(gy))
     x_near = lax.ppermute(x_near, "gx", near(gx))
     x_far = lax.ppermute(x_far, "gx", far(gx))
     yr, yl = jnp.where(even_y, y_near, y_far), jnp.where(even_y, y_far, y_near)
-    copies = call(functools.partial(share_kernel, devices // 2), "share", [(devices // 2 * SHARE, 128)], [share2, stack])[0]
     half = STRIP // 2
     head = jnp.concatenate([yl[:half], yl[STRIP:], yr[:half], yr[STRIP:]])
     tail = jnp.concatenate([yl[half:], yr[half:]])

time: 66.9 us -> 62.3 us (0.931)
  Pallas kernels: 27.1 us -> 24.3 us
  local copies, waits for them, and re-layouts: 4.53 us -> 2.33 us
  waiting for transfers between devices: 10.4 us -> 12.3 us
  starting transfers between devices: 23.5 us -> 22 us
    pallas_call x6 -> x5, Pallas kernels: 27.1 us -> 24.3 us  [call(): pl.pallas_call(kernel, name=name, out_shape=shapes, in_specs=in_specs or...]
    unnamed x14 -> x10, local copies, waits for them, and re-layouts: 4.5 us -> 2.3 us
    all_to_all x2, waiting for transfers between devices: 8.87 us -> 10.5 us  [body(): lax.all_to_all(blocks, ('gx', 'gy'), 0, 0, axis_index_groups=cores)]
    all_to_all x2, starting transfers between devices: 16.8 us -> 15.3 us  [body(): lax.all_to_all(blocks, ('gx', 'gy'), 0, 0, axis_index_groups=cores)]
  transfers between devices with their start and end apart: 10 -> 10, of which waited for: 4 -> 5; matrix products, arithmetic and copies ran while one was open for 0% -> 0% of each run, Pallas kernels for 21% -> 18%
where the time goes in v11:
time: 62.3 us; the launch traced here: 61.9 us
  Pallas kernels  24.3 us (39%)
  starting transfers between devices  22 us (35%)
  waiting for transfers between devices  12.3 us (20%)
  local copies, waits for them, and re-layouts  2.33 us (4%)
  between operations  0.85 us (1%)
    pallas_call x5, Pallas kernels, call(): pl.pallas_call(kernel, name=name, out_shape=shapes, in_specs=in_specs or...  24.3 us
    all_to_all x2, starting transfers between devices, body(): lax.all_to_all(blocks, ('gx', 'gy'), 0, 0, axis_index_groups=cores)  15.3 us
    all_to_all x2, waiting for transfers between devices, body(): lax.all_to_all(blocks, ('gx', 'gy'), 0, 0, axis_index_groups=cores)  10.5 us
    ppermute x1, starting transfers between devices, body(): y_near = lax.ppermute(y_near, 'gy', near(gy))  3 us
    unnamed x10, local copies, waits for them, and re-layouts  2.3 us
    ppermute x1, starting transfers between devices, body(): c_near = lax.ppermute(jnp.where(even_x, tail, head), 'gx', near(gx))  1.54 us
    ppermute x1, waiting for transfers between devices, body(): y_near = lax.ppermute(y_near, 'gy', near(gy))  1.44 us
  transfers between devices with their start and end apart: 10, of which 5 were waited for; matrix products, arithmetic and copies ran while one was open for 0% of the time, Pallas kernels for 18%

profile of v11, /device:TPU:0, one launch (start us, length us, event | category | flops | bytes accessed | tf_op | source)
XLA Modules:
  0.0 61.9 jit_solution(9513454703799990016)
XLA Ops:
  0.6 3.4 %pack.1 = (f32[1472,128]{1,0:T(8,128)}, f32[1472,128]{1,0:T(8,128)}, f32[184,128]{1,0:T(8,128)}, f32[184,128]{1,0:T(8,128)}, f32[192,128]{1,0:T(8,128)}, /*index=5*/f32[2560,128]{1,0:T(8,128)}, f32[640,128]{1,0:T(8,128)}) custom-call(f32[512,128]{1,0:T(8,128)} %bitcast.13, f32[512,128]{1,0:T(8,128)} %bitcast.14, f32[512,128]{1,0:T(8,128)} %bitcast.15, ...), custom_call_target="tpu_custom_call" | custom-call | flops 3000000000 | bytes 1310720 | tf_op jit(solution)/shard_map/pack/pallas_call | solution.py:919
  4.0 3.0 %collective-permute-start = (f32[184,128]{1,0:T(8,128)}, f32[184,128]{1,0:T(8,128)S(1)}, u32[]{:S(2)}, u32[]{:S(2)}) collective-permute-start(f32[184,128]{1,0:T(8,128)} %get-tuple-element.18), channel_id=1, source_target_pairs={{0,1},{1,0},{2,3},{3,2},{4,5},{5,4},{6,7},{7,6},{8,9},{9,8},{10,11... | collective-permute-start | bytes 282632 | tf_op jit(solution)/shard_map/ppermute | solution.py:950
  7.0 0.7 %collective-permute-start.1 = (f32[184,128]{1,0:T(8,128)}, f32[184,128]{1,0:T(8,128)S(1)}, u32[]{:S(2)}, u32[]{:S(2)}) collective-permute-start(f32[184,128]{1,0:T(8,128)} %get-tuple-element.19), channel_id=1, source_target_pairs={{1,2},{2,1},{5,6},{6,5},{9,10},{10,9},{13,14},{14,13},{17,18},{18,... | collective-permute-start | bytes 282632 | tf_op jit(solution)/shard_map/ppermute | solution.py:951
  7.7 0.1 collective-permute-start.4
  7.8 0.7 %collective-permute-start.5 = (f32[1472,128]{1,0:T(8,128)}, f32[1472,128]{1,0:T(8,128)S(1)}, u32[]{:S(2)}, u32[]{:S(2)}) collective-permute-start(f32[1472,128]{1,0:T(8,128)} %get-tuple-element.23), channel_id=1, source_target_pairs={{4,8},{8,4},{12,16},{16,12},{20,24},{24,20},{5,9},{9,5},{13,17},{1... | collective-permute-start | bytes 2261000 | tf_op jit(solution)/shard_map/ppermute | solution.py:953
  8.5 1.4 %collective-permute-done = f32[184,128]{1,0:T(8,128)S(1)} collective-permute-done((f32[184,128]{1,0:T(8,128)}, f32[184,128]{1,0:T(8,128)S(1)}, u32[]{:S(2)}, u32[]{:S(2)}) %collective-permute-start) | collective-permute-done | bytes 94240 | tf_op jit(solution)/shard_map/ppermute | solution.py:950
  9.9 0.0 collective-permute-done.1
  10.1 1.5 %collective-permute-start.2 = (f32[208,128]{1,0:T(8,128)S(1)}, f32[208,128]{1,0:T(8,128)S(1)}, u32[]{:S(2)}, u32[]{:S(2)}) collective-permute-start(f32[208,128]{1,0:T(8,128)S(1)} %get-tuple-element.35), channel_id=1, source_target_pairs={{0,4},{4,0},{8,12},{12,8},{16,20},{20,16},{24,28},{28,24},{1,5},{5... | collective-permute-start | bytes 319496 | tf_op jit(solution)/shard_map/ppermute | solution.py:958
  11.6 0.7 %collective-permute-start.3 = (f32[208,128]{1,0:T(8,128)S(1)}, f32[208,128]{1,0:T(8,128)S(1)}, u32[]{:S(2)}, u32[]{:S(2)}) collective-permute-start(f32[208,128]{1,0:T(8,128)S(1)} %get-tuple-element.34), channel_id=1, source_target_pairs={{4,8},{8,4},{12,16},{16,12},{20,24},{24,20},{5,9},{9,5},{13,17},{1... | collective-permute-start | bytes 319496 | tf_op jit(solution)/shard_map/ppermute | solution.py:959
  12.3 0.3 collective-permute-done.2
  12.6 10.6 %all-to-all-start = ((f32[16,40,128]{2,1,0:T(8,128)}), f32[16,40,128]{2,1,0:T(8,128)S(1)}, u32[]{:S(2)}, u32[]{:S(2)}) async-start(f32[16,40,128]{2,1,0:T(8,128)} %bitcast.12), calls=%async_computation | async-start | bytes 655360 | tf_op jit(solution)/shard_map/all_to_all | solution.py:964
  23.2 0.0 collective-permute-done.3
  23.3 0.0 collective-permute-done.4.refs_5_.x_near
  23.3 0.0 collective-permute-done.5.refs_6_.x_far
  23.3 0.0 copy-start
  23.3 1.3 %copy-done = f32[2560,128]{1,0:T(8,128)S(1)} copy-done((f32[2560,128]{1,0:T(8,128)S(1)}, f32[2560,128]{1,0:T(8,128)}, u32[]{:S(2)}) %copy-start) | copy-done | bytes 1310744
  24.6 0.0 copy-start.4
  24.6 7.4 %down.1 = (f32[640,128]{1,0:T(8,128)}, f32[73728,128]{1,0:T(8,128)}) custom-call(f32[2560,128]{1,0:T(8,128)S(1)} %copy-done, f32[184,128]{1,0:T(8,128)S(1)} %get-tuple-element.37.refs_1_.yr, f32[184,128]{1,0:T(8,128)S(1)} %get-tuple-element.36.refs_2_.yl, f32[208,128]{1,0:T(8,128)S(1)} %get-tuple-element.33.refs_3_.cr, ...), custom_call_target="tpu_custom_call" | custom-call | flops 10000000000 | bytes 3219456 | tf_op jit(solution)/shard_map/down/pallas_call | solution.py:919
  32.0 2.8 %all-to-all-done = f32[16,40,128]{2,1,0:T(8,128)S(1)} async-done(((f32[16,40,128]{2,1,0:T(8,128)}), f32[16,40,128]{2,1,0:T(8,128)S(1)}, u32[]{:S(2)}, u32[]{:S(2)}) %all-to-all-start) | async-done | bytes 327712 | tf_op jit(solution)/shard_map/all_to_all | solution.py:964
  34.8 4.7 %all-to-all-start.1 = ((f32[16,40,128]{2,1,0:T(8,128)}), f32[16,40,128]{2,1,0:T(8,128)S(1)}, u32[]{:S(2)}, u32[]{:S(2)}) async-start(f32[16,40,128]{2,1,0:T(8,128)} %bitcast.7), calls=%async_computation.1 | async-start | bytes 655360 | tf_op jit(solution)/shard_map/all_to_all | solution.py:985
  39.5 0.1 collective-permute-start.7
  39.6 0.0 copy-done.4
  39.6 2.2 %window_coeffs.1.refs_3_ = f32[2064,128]{1,0:T(8,128)S(1)} custom-call(f32[192,128]{1,0:T(8,128)S(1)} %copy-done.4, f32[1472,128]{1,0:T(8,128)S(1)} %collective-permute-done.4.refs_5_.x_near, f32[1472,128]{1,0:T(8,128)S(1)} %collective-permute-done.5.refs_6_.x_far, f32[184,128]{1,0:T(8,128)S(1)} %get-tuple-element.37.refs_1_.yr, ...), custom_call_target="tpu_custom_call" | custom-call | flops 4000000000 | bytes 2007040 | tf_op jit(solution)/shard_map/window_coeffs/pallas_call | solution.py:919
  41.8 0.0 copy-start.2
  41.8 1.0 %copy-done.2 = f32[2064,128]{1,0:T(8,128)} copy-done((f32[2064,128]{1,0:T(8,128)}, f32[2064,128]{1,0:T(8,128)S(1)}, u32[]{:S(2)}) %copy-start.2) | copy-done | bytes 1056792
  42.8 0.0 copy-start.1
  42.8 7.7 %all-to-all-done.1.refs_0_ = f32[16,40,128]{2,1,0:T(8,128)S(1)} async-done(((f32[16,40,128]{2,1,0:T(8,128)}), f32[16,40,128]{2,1,0:T(8,128)S(1)}, u32[]{:S(2)}, u32[]{:S(2)}) %all-to-all-start.1) | async-done | bytes 327712 | tf_op jit(solution)/shard_map/all_to_all | solution.py:985
  50.5 0.0 copy-start.3
  50.5 0.0 collective-permute-start.6
  50.5 0.0 collective-permute-done.7.other
  50.5 1.5 %global_coeffs.1.refs_2_ = f32[3840,128]{1,0:T(8,128)S(1)} custom-call(f32[4,160,128]{2,1,0:T(8,128)S(1)} %bitcast.11, f32[4,160,128]{2,1,0:T(8,128)S(1)} %collective-permute-done.7.other), custom_call_target="tpu_custom_call" | custom-call | flops 4000000000 | bytes 655360 | tf_op jit(solution)/shard_map/global_coeffs/pallas_call | solution.py:919
  52.0 0.1 collective-permute-done.6.refs_1_
  52.1 0.0 copy-done.1
  52.1 0.0 copy-done.3
  52.1 9.8 %up.1 = (f32[512,128]{1,0:T(8,128)}, f32[512,128]{1,0:T(8,128)}) custom-call(f32[16,40,128]{2,1,0:T(8,128)S(1)} %all-to-all-done.1.refs_0_, f32[16,40,128]{2,1,0:T(8,128)S(1)} %collective-permute-done.6.refs_1_, f32[3840,128]{1,0:T(8,128)S(1)} %global_coeffs.1.refs_2_, f32[2064,128]{1,0:T(8,128)S(1)} %copy-done.3, f32[2560,128]{1,0:T(8,128)S(1)} %copy-done.1, ...), custom_call_target="tpu_custom_call" | custom-call | flops 12000000000 | bytes 42737664 | tf_op jit(solution)/shard_map/up/pallas_call | solution.py:919
  (9 shorter events, 0.1 us)
Async XLA Ops:
  4.0 5.9 %collective-permute-start = (f32[184,128]{1,0:T(8,128)}, f32[184,128]{1,0:T(8,128)S(1)}, u32[]{:S(2)}, u32[]{:S(2)}) collective-permute-start(f32[184,128]{1,0:T(8,128)} %get-tuple-element.18), channel_id=1, source_target_pairs={{0,1},{1,0},{2,3},{3,2},{4,5},{5,4},{6,7},{7,6},{8,9},{9,8},{10,11... | collective-permute-start | bytes 282632 | tf_op jit(solution)/shard_map/ppermute | solution.py:950
  7.0 2.9 %collective-permute-start.1 = (f32[184,128]{1,0:T(8,128)}, f32[184,128]{1,0:T(8,128)S(1)}, u32[]{:S(2)}, u32[]{:S(2)}) collective-permute-start(f32[184,128]{1,0:T(8,128)} %get-tuple-element.19), channel_id=1, source_target_pairs={{1,2},{2,1},{5,6},{6,5},{9,10},{10,9},{13,14},{14,13},{17,18},{18,... | collective-permute-start | bytes 282632 | tf_op jit(solution)/shard_map/ppermute | solution.py:951
  7.7 15.6 %collective-permute-start.4 = (f32[1472,128]{1,0:T(8,128)}, f32[1472,128]{1,0:T(8,128)S(1)}, u32[]{:S(2)}, u32[]{:S(2)}) collective-permute-start(f32[1472,128]{1,0:T(8,128)} %get-tuple-element.22), channel_id=1, source_target_pairs={{0,4},{4,0},{8,12},{12,8},{16,20},{20,16},{24,28},{28,24},{1,5},{5... | collective-permute-start | bytes 2261000 | tf_op jit(solution)/shard_map/ppermute | solution.py:952
  7.8 15.5 %collective-permute-start.5 = (f32[1472,128]{1,0:T(8,128)}, f32[1472,128]{1,0:T(8,128)S(1)}, u32[]{:S(2)}, u32[]{:S(2)}) collective-permute-start(f32[1472,128]{1,0:T(8,128)} %get-tuple-element.23), channel_id=1, source_target_pairs={{4,8},{8,4},{12,16},{16,12},{20,24},{24,20},{5,9},{9,5},{13,17},{1... | collective-permute-start | bytes 2261000 | tf_op jit(solution)/shard_map/ppermute | solution.py:953
  10.1 2.5 %collective-permute-start.2 = (f32[208,128]{1,0:T(8,128)S(1)}, f32[208,128]{1,0:T(8,128)S(1)}, u32[]{:S(2)}, u32[]{:S(2)}) collective-permute-start(f32[208,128]{1,0:T(8,128)S(1)} %get-tuple-element.35), channel_id=1, source_target_pairs={{0,4},{4,0},{8,12},{12,8},{16,20},{20,16},{24,28},{28,24},{1,5},{5... | collective-permute-start | bytes 319496 | tf_op jit(solution)/shard_map/ppermute | solution.py:958
  11.6 11.6 %collective-permute-start.3 = (f32[208,128]{1,0:T(8,128)S(1)}, f32[208,128]{1,0:T(8,128)S(1)}, u32[]{:S(2)}, u32[]{:S(2)}) collective-permute-start(f32[208,128]{1,0:T(8,128)S(1)} %get-tuple-element.34), channel_id=1, source_target_pairs={{4,8},{8,4},{12,16},{16,12},{20,24},{24,20},{5,9},{9,5},{13,17},{1... | collective-permute-start | bytes 319496 | tf_op jit(solution)/shard_map/ppermute | solution.py:959
  12.6 22.3 %all-to-all-start = ((f32[16,40,128]{2,1,0:T(8,128)}), f32[16,40,128]{2,1,0:T(8,128)S(1)}, u32[]{:S(2)}, u32[]{:S(2)}) async-start(f32[16,40,128]{2,1,0:T(8,128)} %bitcast.12), calls=%async_computation | async-start | bytes 655360 | tf_op jit(solution)/shard_map/all_to_all | solution.py:964
  23.3 1.3 %copy-start = (f32[2560,128]{1,0:T(8,128)S(1)}, f32[2560,128]{1,0:T(8,128)}, u32[]{:S(2)}) copy-start(f32[2560,128]{1,0:T(8,128)} %get-tuple-element.17.refs_0_.refs_4_) | copy-start | bytes 3932164
  24.6 15.0 %copy-start.4 = (f32[192,128]{1,0:T(8,128)S(1)}, f32[192,128]{1,0:T(8,128)}, u32[]{:S(2)}) copy-start(f32[192,128]{1,0:T(8,128)} %get-tuple-element.28.share2) | copy-start | bytes 294916
  34.8 15.6 %all-to-all-start.1 = ((f32[16,40,128]{2,1,0:T(8,128)}), f32[16,40,128]{2,1,0:T(8,128)S(1)}, u32[]{:S(2)}, u32[]{:S(2)}) async-start(f32[16,40,128]{2,1,0:T(8,128)} %bitcast.7), calls=%async_computation.1 | async-start | bytes 655360 | tf_op jit(solution)/shard_map/all_to_all | solution.py:985
  39.5 11.0 %collective-permute-start.7 = (f32[4,160,128]{2,1,0:T(8,128)S(1)}, f32[4,160,128]{2,1,0:T(8,128)S(1)}, u32[]{:S(2)}, u32[]{:S(2)}) collective-permute-start(f32[4,160,128]{2,1,0:T(8,128)S(1)} %bitcast.10), channel_id=1, source_target_pairs={{0,4},{4,0},{8,12},{12,8},{16,20},{20,16},{24,28},{28,24},{1,5},{5... | collective-permute-start | bytes 983048 | tf_op jit(solution)/shard_map/ppermute | solution.py:983
  41.8 1.0 %copy-start.2 = (f32[2064,128]{1,0:T(8,128)}, f32[2064,128]{1,0:T(8,128)S(1)}, u32[]{:S(2)}) copy-start(f32[2064,128]{1,0:T(8,128)S(1)} %window_coeffs.1.refs_3_) | copy-start | bytes 3170308
  42.8 9.3 %copy-start.1 = (f32[2560,128]{1,0:T(8,128)S(1)}, f32[2560,128]{1,0:T(8,128)}, u32[]{:S(2)}) copy-start(f32[2560,128]{1,0:T(8,128)} %get-tuple-element.17.refs_0_.refs_4_) | copy-start | bytes 3932164
  50.5 1.6 %copy-start.3 = (f32[2064,128]{1,0:T(8,128)S(1)}, f32[2064,128]{1,0:T(8,128)}, u32[]{:S(2)}) copy-start(f32[2064,128]{1,0:T(8,128)} %copy-done.2) | copy-start | bytes 3170308
  50.5 1.6 %collective-permute-start.6 = (f32[16,40,128]{2,1,0:T(8,128)S(1)}, f32[16,40,128]{2,1,0:T(8,128)S(1)}, u32[]{:S(2)}, u32[]{:S(2)}) collective-permute-start(f32[16,40,128]{2,1,0:T(8,128)S(1)} %all-to-all-done.1.refs_0_), channel_id=1, source_target_pairs={{0,4},{4,0},{8,12},{12,8},{16,20},{20,16},{24,28},{28,24},{1,5},{5... | collective-permute-start | bytes 983048 | tf_op jit(solution)/shard_map/ppermute | solution.py:986

commit v12 on v11

--- a/solution.py
+++ b/solution.py
@@ -687,9 +687,9 @@
         diag[z] = base_diag(jnp.where(mask0 > 0, kappa_k, 1.0), x_k, y_k)
         return cz_k
 
-    last = loop(NZ, prepare, jnp.zeros((rows, 256), F32), 4)
+    last = loop(NZ, prepare, jnp.zeros((rows, 256), F32), 8)
     z_face[NZ] = 0.5 * last
-    ends = factor(diag, z_face, tiles, inv, 8, f0, kept)
+    ends = factor(diag, z_face, tiles, inv, None, f0, kept)
     copies = []
 
     def save(field):
@@ -701,7 +701,7 @@
 
     for field in (x_face, y_face, inv, f0):
         save(field)
-    smooth_down(f0, x_face, y_face, Line(inv, z_face), ends, kept, u, r, 5)
+    smooth_down(f0, x_face, y_face, Line(inv, z_face), ends, kept, u, r, None)
     save(u)
     save(z_face)
 
@@ -816,7 +816,7 @@
         solve4(lambda k: f4[k] + neighbours(old[k], x_face4[k], y_face4[k]), old)
         return carry
 
-    lax.fori_loop(0, COARSE_SWEEPS - 1, relax, 0)
+    lax.fori_loop(0, COARSE_SWEEPS - 1, relax, 0, unroll=5)
 
     cells = u4.ref[...].reshape(NZ, rows, 128)
     x = iota((1, rows, 128), 1)
@@ -882,7 +882,7 @@
     fetched[1].wait()
     x_face0, y_face0, inv0, f0, u0, z_face0 = stack_fields(held0, rows, 5, 2)
     mask0 = window_mask(rows, 256, TX, TY, HALO, ix, iy, TX * gx, TY * gy)
-    smooth_up(f0, x_face0, y_face0, Line(inv0, z_face0), u0, e0, Field(kept0, rows, 2), mask0, 4)
+    smooth_up(f0, x_face0, y_face0, Line(inv0, z_face0), u0, e0, Field(kept0, rows, 2), mask0, None)
 
     kappa = Field(stack, TX, start=NZ * TX)
 

time: 62.3 us -> 63.4 us (1.018)
  starting transfers between devices: 22 us -> 23.5 us
  waiting for transfers between devices: 12.3 us -> 10.8 us
  Pallas kernels: 24.3 us -> 25.2 us
    all_to_all x2, starting transfers between devices: 15.3 us -> 16.8 us  [body(): lax.all_to_all(blocks, ('gx', 'gy'), 0, 0, axis_index_groups=cores)]
    all_to_all x2, waiting for transfers between devices: 10.5 us -> 9 us  [body(): lax.all_to_all(blocks, ('gx', 'gy'), 0, 0, axis_index_groups=cores)]
    pallas_call x5, Pallas kernels: 24.3 us -> 25.2 us  [call(): pl.pallas_call(kernel, name=name, out_shape=shapes, in_specs=in_specs or...]
  transfers between devices with their start and end apart: 10 -> 10, of which waited for: 5 -> 5; matrix products, arithmetic and copies ran while one was open for 0% -> 0% of each run, Pallas kernels for 18% -> 20%
where the time goes in v12:
time: 63.4 us; the launch traced here: 63 us
  Pallas kernels  25.2 us (40%)
  starting transfers between devices  23.5 us (37%)
  waiting for transfers between devices  10.8 us (17%)
  local copies, waits for them, and re-layouts  2.33 us (4%)
  between operations  1.01 us (2%)
    pallas_call x5, Pallas kernels, call(): pl.pallas_call(kernel, name=name, out_shape=shapes, in_specs=in_specs or...  25.2 us
    all_to_all x2, starting transfers between devices, body(): lax.all_to_all(blocks, ('gx', 'gy'), 0, 0, axis_index_groups=cores)  16.8 us
    all_to_all x2, waiting for transfers between devices, body(): lax.all_to_all(blocks, ('gx', 'gy'), 0, 0, axis_index_groups=cores)  9 us
    ppermute x1, starting transfers between devices, body(): y_near = lax.ppermute(y_near, 'gy', near(gy))  3 us
    unnamed x10, local copies, waits for them, and re-layouts  2.3 us
    ppermute x1, starting transfers between devices, body(): c_near = lax.ppermute(jnp.where(even_x, tail, head), 'gx', near(gx))  1.54 us
    ppermute x1, waiting for transfers between devices, body(): y_near = lax.ppermute(y_near, 'gy', near(gy))  1.44 us
  transfers between devices with their start and end apart: 10, of which 5 were waited for; matrix products, arithmetic and copies ran while one was open for 0% of the time, Pallas kernels for 20%

profile of v12, /device:TPU:0, one launch (start us, length us, event | category | flops | bytes accessed | tf_op | source)
XLA Modules:
  0.0 63.0 jit_solution(5531516770035898451)
XLA Ops:
  0.6 3.4 %pack.1 = (f32[1472,128]{1,0:T(8,128)}, f32[1472,128]{1,0:T(8,128)}, f32[184,128]{1,0:T(8,128)}, f32[184,128]{1,0:T(8,128)}, f32[192,128]{1,0:T(8,128)}, /*index=5*/f32[2560,128]{1,0:T(8,128)}, f32[640,128]{1,0:T(8,128)}) custom-call(f32[512,128]{1,0:T(8,128)} %bitcast.13, f32[512,128]{1,0:T(8,128)} %bitcast.14, f32[512,128]{1,0:T(8,128)} %bitcast.15, ...), custom_call_target="tpu_custom_call" | custom-call | flops 3000000000 | bytes 1310720 | tf_op jit(solution)/shard_map/pack/pallas_call | solution.py:919
  4.0 3.0 %collective-permute-start = (f32[184,128]{1,0:T(8,128)}, f32[184,128]{1,0:T(8,128)S(1)}, u32[]{:S(2)}, u32[]{:S(2)}) collective-permute-start(f32[184,128]{1,0:T(8,128)} %get-tuple-element.18), channel_id=1, source_target_pairs={{0,1},{1,0},{2,3},{3,2},{4,5},{5,4},{6,7},{7,6},{8,9},{9,8},{10,11... | collective-permute-start | bytes 282632 | tf_op jit(solution)/shard_map/ppermute | solution.py:950
  7.0 0.7 %collective-permute-start.1 = (f32[184,128]{1,0:T(8,128)}, f32[184,128]{1,0:T(8,128)S(1)}, u32[]{:S(2)}, u32[]{:S(2)}) collective-permute-start(f32[184,128]{1,0:T(8,128)} %get-tuple-element.19), channel_id=1, source_target_pairs={{1,2},{2,1},{5,6},{6,5},{9,10},{10,9},{13,14},{14,13},{17,18},{18,... | collective-permute-start | bytes 282632 | tf_op jit(solution)/shard_map/ppermute | solution.py:951
  7.7 0.1 collective-permute-start.4
  7.8 0.7 %collective-permute-start.5 = (f32[1472,128]{1,0:T(8,128)}, f32[1472,128]{1,0:T(8,128)S(1)}, u32[]{:S(2)}, u32[]{:S(2)}) collective-permute-start(f32[1472,128]{1,0:T(8,128)} %get-tuple-element.23), channel_id=1, source_target_pairs={{4,8},{8,4},{12,16},{16,12},{20,24},{24,20},{5,9},{9,5},{13,17},{1... | collective-permute-start | bytes 2261000 | tf_op jit(solution)/shard_map/ppermute | solution.py:953
  8.5 1.4 %collective-permute-done = f32[184,128]{1,0:T(8,128)S(1)} collective-permute-done((f32[184,128]{1,0:T(8,128)}, f32[184,128]{1,0:T(8,128)S(1)}, u32[]{:S(2)}, u32[]{:S(2)}) %collective-permute-start) | collective-permute-done | bytes 94240 | tf_op jit(solution)/shard_map/ppermute | solution.py:950
  9.9 0.0 collective-permute-done.1
  10.1 1.5 %collective-permute-start.2 = (f32[208,128]{1,0:T(8,128)S(1)}, f32[208,128]{1,0:T(8,128)S(1)}, u32[]{:S(2)}, u32[]{:S(2)}) collective-permute-start(f32[208,128]{1,0:T(8,128)S(1)} %get-tuple-element.35), channel_id=1, source_target_pairs={{0,4},{4,0},{8,12},{12,8},{16,20},{20,16},{24,28},{28,24},{1,5},{5... | collective-permute-start | bytes 319496 | tf_op jit(solution)/shard_map/ppermute | solution.py:958
  11.6 0.7 %collective-permute-start.3 = (f32[208,128]{1,0:T(8,128)S(1)}, f32[208,128]{1,0:T(8,128)S(1)}, u32[]{:S(2)}, u32[]{:S(2)}) collective-permute-start(f32[208,128]{1,0:T(8,128)S(1)} %get-tuple-element.34), channel_id=1, source_target_pairs={{4,8},{8,4},{12,16},{16,12},{20,24},{24,20},{5,9},{9,5},{13,17},{1... | collective-permute-start | bytes 319496 | tf_op jit(solution)/shard_map/ppermute | solution.py:959
  12.3 0.3 collective-permute-done.2
  12.6 10.6 %all-to-all-start = ((f32[16,40,128]{2,1,0:T(8,128)}), f32[16,40,128]{2,1,0:T(8,128)S(1)}, u32[]{:S(2)}, u32[]{:S(2)}) async-start(f32[16,40,128]{2,1,0:T(8,128)} %bitcast.12), calls=%async_computation | async-start | bytes 655360 | tf_op jit(solution)/shard_map/all_to_all | solution.py:964
  23.2 0.0 collective-permute-done.3
  23.3 0.0 collective-permute-done.4.refs_5_.x_near
  23.3 0.0 collective-permute-done.5.refs_6_.x_far
  23.3 0.0 copy-start
  23.3 1.3 %copy-done = f32[2560,128]{1,0:T(8,128)S(1)} copy-done((f32[2560,128]{1,0:T(8,128)S(1)}, f32[2560,128]{1,0:T(8,128)}, u32[]{:S(2)}) %copy-start) | copy-done | bytes 1310744
  24.6 0.0 copy-start.4
  24.6 8.9 %down.1 = (f32[640,128]{1,0:T(8,128)}, f32[73728,128]{1,0:T(8,128)}) custom-call(f32[2560,128]{1,0:T(8,128)S(1)} %copy-done, f32[184,128]{1,0:T(8,128)S(1)} %get-tuple-element.37.refs_1_.yr, f32[184,128]{1,0:T(8,128)S(1)} %get-tuple-element.36.refs_2_.yl, f32[208,128]{1,0:T(8,128)S(1)} %get-tuple-element.33.refs_3_.cr, ...), custom_call_target="tpu_custom_call" | custom-call | flops 10000000000 | bytes 3219456 | tf_op jit(solution)/shard_map/down/pallas_call | solution.py:919
  33.5 1.3 %all-to-all-done = f32[16,40,128]{2,1,0:T(8,128)S(1)} async-done(((f32[16,40,128]{2,1,0:T(8,128)}), f32[16,40,128]{2,1,0:T(8,128)S(1)}, u32[]{:S(2)}, u32[]{:S(2)}) %all-to-all-start) | async-done | bytes 327712 | tf_op jit(solution)/shard_map/all_to_all | solution.py:964
  34.8 6.2 %all-to-all-start.1 = ((f32[16,40,128]{2,1,0:T(8,128)}), f32[16,40,128]{2,1,0:T(8,128)S(1)}, u32[]{:S(2)}, u32[]{:S(2)}) async-start(f32[16,40,128]{2,1,0:T(8,128)} %bitcast.7), calls=%async_computation.1 | async-start | bytes 655360 | tf_op jit(solution)/shard_map/all_to_all | solution.py:985
  41.0 0.1 collective-permute-start.7
  41.1 0.0 copy-done.4
  41.1 2.2 %window_coeffs.1.refs_3_ = f32[2064,128]{1,0:T(8,128)S(1)} custom-call(f32[192,128]{1,0:T(8,128)S(1)} %copy-done.4, f32[1472,128]{1,0:T(8,128)S(1)} %collective-permute-done.4.refs_5_.x_near, f32[1472,128]{1,0:T(8,128)S(1)} %collective-permute-done.5.refs_6_.x_far, f32[184,128]{1,0:T(8,128)S(1)} %get-tuple-element.37.refs_1_.yr, ...), custom_call_target="tpu_custom_call" | custom-call | flops 4000000000 | bytes 2007040 | tf_op jit(solution)/shard_map/window_coeffs/pallas_call | solution.py:919
  43.3 0.0 copy-start.2
  43.3 1.0 %copy-done.2 = f32[2064,128]{1,0:T(8,128)} copy-done((f32[2064,128]{1,0:T(8,128)}, f32[2064,128]{1,0:T(8,128)S(1)}, u32[]{:S(2)}) %copy-start.2) | copy-done | bytes 1056792
  44.3 0.0 copy-start.1
  44.3 7.7 %all-to-all-done.1.refs_0_ = f32[16,40,128]{2,1,0:T(8,128)S(1)} async-done(((f32[16,40,128]{2,1,0:T(8,128)}), f32[16,40,128]{2,1,0:T(8,128)S(1)}, u32[]{:S(2)}, u32[]{:S(2)}) %all-to-all-start.1) | async-done | bytes 327712 | tf_op jit(solution)/shard_map/all_to_all | solution.py:985
  52.0 0.0 copy-start.3
  52.0 0.0 collective-permute-start.6
  52.0 0.0 collective-permute-done.7.other
  52.0 1.5 %global_coeffs.1.refs_2_ = f32[3840,128]{1,0:T(8,128)S(1)} custom-call(f32[4,160,128]{2,1,0:T(8,128)S(1)} %bitcast.11, f32[4,160,128]{2,1,0:T(8,128)S(1)} %collective-permute-done.7.other), custom_call_target="tpu_custom_call" | custom-call | flops 4000000000 | bytes 655360 | tf_op jit(solution)/shard_map/global_coeffs/pallas_call | solution.py:919
  53.5 0.1 collective-permute-done.6.refs_1_
  53.6 0.0 copy-done.1
  53.6 0.0 copy-done.3
  53.6 9.2 %up.1 = (f32[512,128]{1,0:T(8,128)}, f32[512,128]{1,0:T(8,128)}) custom-call(f32[16,40,128]{2,1,0:T(8,128)S(1)} %all-to-all-done.1.refs_0_, f32[16,40,128]{2,1,0:T(8,128)S(1)} %collective-permute-done.6.refs_1_, f32[3840,128]{1,0:T(8,128)S(1)} %global_coeffs.1.refs_2_, f32[2064,128]{1,0:T(8,128)S(1)} %copy-done.3, f32[2560,128]{1,0:T(8,128)S(1)} %copy-done.1, ...), custom_call_target="tpu_custom_call" | custom-call | flops 12000000000 | bytes 42737664 | tf_op jit(solution)/shard_map/up/pallas_call | solution.py:919
  (9 shorter events, 0.1 us)
Async XLA Ops:
  4.0 5.9 %collective-permute-start = (f32[184,128]{1,0:T(8,128)}, f32[184,128]{1,0:T(8,128)S(1)}, u32[]{:S(2)}, u32[]{:S(2)}) collective-permute-start(f32[184,128]{1,0:T(8,128)} %get-tuple-element.18), channel_id=1, source_target_pairs={{0,1},{1,0},{2,3},{3,2},{4,5},{5,4},{6,7},{7,6},{8,9},{9,8},{10,11... | collective-permute-start | bytes 282632 | tf_op jit(solution)/shard_map/ppermute | solution.py:950
  7.0 2.9 %collective-permute-start.1 = (f32[184,128]{1,0:T(8,128)}, f32[184,128]{1,0:T(8,128)S(1)}, u32[]{:S(2)}, u32[]{:S(2)}) collective-permute-start(f32[184,128]{1,0:T(8,128)} %get-tuple-element.19), channel_id=1, source_target_pairs={{1,2},{2,1},{5,6},{6,5},{9,10},{10,9},{13,14},{14,13},{17,18},{18,... | collective-permute-start | bytes 282632 | tf_op jit(solution)/shard_map/ppermute | solution.py:951
  7.7 15.6 %collective-permute-start.4 = (f32[1472,128]{1,0:T(8,128)}, f32[1472,128]{1,0:T(8,128)S(1)}, u32[]{:S(2)}, u32[]{:S(2)}) collective-permute-start(f32[1472,128]{1,0:T(8,128)} %get-tuple-element.22), channel_id=1, source_target_pairs={{0,4},{4,0},{8,12},{12,8},{16,20},{20,16},{24,28},{28,24},{1,5},{5... | collective-permute-start | bytes 2261000 | tf_op jit(solution)/shard_map/ppermute | solution.py:952
  7.8 15.5 %collective-permute-start.5 = (f32[1472,128]{1,0:T(8,128)}, f32[1472,128]{1,0:T(8,128)S(1)}, u32[]{:S(2)}, u32[]{:S(2)}) collective-permute-start(f32[1472,128]{1,0:T(8,128)} %get-tuple-element.23), channel_id=1, source_target_pairs={{4,8},{8,4},{12,16},{16,12},{20,24},{24,20},{5,9},{9,5},{13,17},{1... | collective-permute-start | bytes 2261000 | tf_op jit(solution)/shard_map/ppermute | solution.py:953
  10.1 2.5 %collective-permute-start.2 = (f32[208,128]{1,0:T(8,128)S(1)}, f32[208,128]{1,0:T(8,128)S(1)}, u32[]{:S(2)}, u32[]{:S(2)}) collective-permute-start(f32[208,128]{1,0:T(8,128)S(1)} %get-tuple-element.35), channel_id=1, source_target_pairs={{0,4},{4,0},{8,12},{12,8},{16,20},{20,16},{24,28},{28,24},{1,5},{5... | collective-permute-start | bytes 319496 | tf_op jit(solution)/shard_map/ppermute | solution.py:958
  11.6 11.6 %collective-permute-start.3 = (f32[208,128]{1,0:T(8,128)S(1)}, f32[208,128]{1,0:T(8,128)S(1)}, u32[]{:S(2)}, u32[]{:S(2)}) collective-permute-start(f32[208,128]{1,0:T(8,128)S(1)} %get-tuple-element.34), channel_id=1, source_target_pairs={{4,8},{8,4},{12,16},{16,12},{20,24},{24,20},{5,9},{9,5},{13,17},{1... | collective-permute-start | bytes 319496 | tf_op jit(solution)/shard_map/ppermute | solution.py:959
  12.6 22.3 %all-to-all-start = ((f32[16,40,128]{2,1,0:T(8,128)}), f32[16,40,128]{2,1,0:T(8,128)S(1)}, u32[]{:S(2)}, u32[]{:S(2)}) async-start(f32[16,40,128]{2,1,0:T(8,128)} %bitcast.12), calls=%async_computation | async-start | bytes 655360 | tf_op jit(solution)/shard_map/all_to_all | solution.py:964
  23.3 1.3 %copy-start = (f32[2560,128]{1,0:T(8,128)S(1)}, f32[2560,128]{1,0:T(8,128)}, u32[]{:S(2)}) copy-start(f32[2560,128]{1,0:T(8,128)} %get-tuple-element.17.refs_0_.refs_4_) | copy-start | bytes 3932164
  24.6 16.5 %copy-start.4 = (f32[192,128]{1,0:T(8,128)S(1)}, f32[192,128]{1,0:T(8,128)}, u32[]{:S(2)}) copy-start(f32[192,128]{1,0:T(8,128)} %get-tuple-element.28.share2) | copy-start | bytes 294916
  34.8 17.1 %all-to-all-start.1 = ((f32[16,40,128]{2,1,0:T(8,128)}), f32[16,40,128]{2,1,0:T(8,128)S(1)}, u32[]{:S(2)}, u32[]{:S(2)}) async-start(f32[16,40,128]{2,1,0:T(8,128)} %bitcast.7), calls=%async_computation.1 | async-start | bytes 655360 | tf_op jit(solution)/shard_map/all_to_all | solution.py:985
  41.0 11.0 %collective-permute-start.7 = (f32[4,160,128]{2,1,0:T(8,128)S(1)}, f32[4,160,128]{2,1,0:T(8,128)S(1)}, u32[]{:S(2)}, u32[]{:S(2)}) collective-permute-start(f32[4,160,128]{2,1,0:T(8,128)S(1)} %bitcast.10), channel_id=1, source_target_pairs={{0,4},{4,0},{8,12},{12,8},{16,20},{20,16},{24,28},{28,24},{1,5},{5... | collective-permute-start | bytes 983048 | tf_op jit(solution)/shard_map/ppermute | solution.py:983
  43.3 1.0 %copy-start.2 = (f32[2064,128]{1,0:T(8,128)}, f32[2064,128]{1,0:T(8,128)S(1)}, u32[]{:S(2)}) copy-start(f32[2064,128]{1,0:T(8,128)S(1)} %window_coeffs.1.refs_3_) | copy-start | bytes 3170308
  44.3 9.3 %copy-start.1 = (f32[2560,128]{1,0:T(8,128)S(1)}, f32[2560,128]{1,0:T(8,128)}, u32[]{:S(2)}) copy-start(f32[2560,128]{1,0:T(8,128)} %get-tuple-element.17.refs_0_.refs_4_) | copy-start | bytes 3932164
  52.0 1.6 %copy-start.3 = (f32[2064,128]{1,0:T(8,128)S(1)}, f32[2064,128]{1,0:T(8,128)}, u32[]{:S(2)}) copy-start(f32[2064,128]{1,0:T(8,128)} %copy-done.2) | copy-start | bytes 3170308
  52.0 1.6 %collective-permute-start.6 = (f32[16,40,128]{2,1,0:T(8,128)S(1)}, f32[16,40,128]{2,1,0:T(8,128)S(1)}, u32[]{:S(2)}, u32[]{:S(2)}) collective-permute-start(f32[16,40,128]{2,1,0:T(8,128)S(1)} %all-to-all-done.1.refs_0_), channel_id=1, source_target_pairs={{0,4},{4,0},{8,12},{12,8},{16,20},{20,16},{24,28},{28,24},{1,5},{5... | collective-permute-start | bytes 983048 | tf_op jit(solution)/shard_map/ppermute | solution.py:986

commit v13 on v11

--- a/solution.py
+++ b/solution.py
@@ -816,7 +816,7 @@
         solve4(lambda k: f4[k] + neighbours(old[k], x_face4[k], y_face4[k]), old)
         return carry
 
-    lax.fori_loop(0, COARSE_SWEEPS - 1, relax, 0)
+    lax.fori_loop(0, COARSE_SWEEPS - 1, relax, 0, unroll=5)
 
     cells = u4.ref[...].reshape(NZ, rows, 128)
     x = iota((1, rows, 128), 1)
@@ -882,7 +882,7 @@
     fetched[1].wait()
     x_face0, y_face0, inv0, f0, u0, z_face0 = stack_fields(held0, rows, 5, 2)
     mask0 = window_mask(rows, 256, TX, TY, HALO, ix, iy, TX * gx, TY * gy)
-    smooth_up(f0, x_face0, y_face0, Line(inv0, z_face0), u0, e0, Field(kept0, rows, 2), mask0, 4)
+    smooth_up(f0, x_face0, y_face0, Line(inv0, z_face0), u0, e0, Field(kept0, rows, 2), mask0, None)
 
     kappa = Field(stack, TX, start=NZ * TX)
 

time: 62.3 us -> 61.7 us (level)
  no operation moved by 1% of the time
where the time goes in v13:
time: 61.7 us; the launch traced here: 61.3 us
  Pallas kernels  23.7 us (38%)
  starting transfers between devices  22 us (36%)
  waiting for transfers between devices  12.3 us (20%)
  local copies, waits for them, and re-layouts  2.33 us (4%)
  between operations  0.85 us (1%)
    pallas_call x5, Pallas kernels, call(): pl.pallas_call(kernel, name=name, out_shape=shapes, in_specs=in_specs or...  23.7 us
    all_to_all x2, starting transfers between devices, body(): lax.all_to_all(blocks, ('gx', 'gy'), 0, 0, axis_index_groups=cores)  15.3 us
    all_to_all x2, waiting for transfers between devices, body(): lax.all_to_all(blocks, ('gx', 'gy'), 0, 0, axis_index_groups=cores)  10.5 us
    ppermute x1, starting transfers between devices, body(): y_near = lax.ppermute(y_near, 'gy', near(gy))  3 us
    unnamed x10, local copies, waits for them, and re-layouts  2.3 us
    ppermute x1, starting transfers between devices, body(): c_near = lax.ppermute(jnp.where(even_x, tail, head), 'gx', near(gx))  1.54 us
    ppermute x1, waiting for transfers between devices, body(): y_near = lax.ppermute(y_near, 'gy', near(gy))  1.44 us
  transfers between devices with their start and end apart: 10, of which 5 were waited for; matrix products, arithmetic and copies ran while one was open for 0% of the time, Pallas kernels for 18%

profile of v13, /device:TPU:0, one launch (start us, length us, event | category | flops | bytes accessed | tf_op | source)
XLA Modules:
  0.0 61.3 jit_solution(2699779335885330561)
XLA Ops:
  0.6 3.4 %pack.1 = (f32[1472,128]{1,0:T(8,128)}, f32[1472,128]{1,0:T(8,128)}, f32[184,128]{1,0:T(8,128)}, f32[184,128]{1,0:T(8,128)}, f32[192,128]{1,0:T(8,128)}, /*index=5*/f32[2560,128]{1,0:T(8,128)}, f32[640,128]{1,0:T(8,128)}) custom-call(f32[512,128]{1,0:T(8,128)} %bitcast.13, f32[512,128]{1,0:T(8,128)} %bitcast.14, f32[512,128]{1,0:T(8,128)} %bitcast.15, ...), custom_call_target="tpu_custom_call" | custom-call | flops 3000000000 | bytes 1310720 | tf_op jit(solution)/shard_map/pack/pallas_call | solution.py:919
  4.0 3.0 %collective-permute-start = (f32[184,128]{1,0:T(8,128)}, f32[184,128]{1,0:T(8,128)S(1)}, u32[]{:S(2)}, u32[]{:S(2)}) collective-permute-start(f32[184,128]{1,0:T(8,128)} %get-tuple-element.18), channel_id=1, source_target_pairs={{0,1},{1,0},{2,3},{3,2},{4,5},{5,4},{6,7},{7,6},{8,9},{9,8},{10,11... | collective-permute-start | bytes 282632 | tf_op jit(solution)/shard_map/ppermute | solution.py:950
  7.0 0.7 %collective-permute-start.1 = (f32[184,128]{1,0:T(8,128)}, f32[184,128]{1,0:T(8,128)S(1)}, u32[]{:S(2)}, u32[]{:S(2)}) collective-permute-start(f32[184,128]{1,0:T(8,128)} %get-tuple-element.19), channel_id=1, source_target_pairs={{1,2},{2,1},{5,6},{6,5},{9,10},{10,9},{13,14},{14,13},{17,18},{18,... | collective-permute-start | bytes 282632 | tf_op jit(solution)/shard_map/ppermute | solution.py:951
  7.7 0.1 collective-permute-start.4
  7.8 0.7 %collective-permute-start.5 = (f32[1472,128]{1,0:T(8,128)}, f32[1472,128]{1,0:T(8,128)S(1)}, u32[]{:S(2)}, u32[]{:S(2)}) collective-permute-start(f32[1472,128]{1,0:T(8,128)} %get-tuple-element.23), channel_id=1, source_target_pairs={{4,8},{8,4},{12,16},{16,12},{20,24},{24,20},{5,9},{9,5},{13,17},{1... | collective-permute-start | bytes 2261000 | tf_op jit(solution)/shard_map/ppermute | solution.py:953
  8.5 1.4 %collective-permute-done = f32[184,128]{1,0:T(8,128)S(1)} collective-permute-done((f32[184,128]{1,0:T(8,128)}, f32[184,128]{1,0:T(8,128)S(1)}, u32[]{:S(2)}, u32[]{:S(2)}) %collective-permute-start) | collective-permute-done | bytes 94240 | tf_op jit(solution)/shard_map/ppermute | solution.py:950
  9.9 0.0 collective-permute-done.1
  10.1 1.5 %collective-permute-start.2 = (f32[208,128]{1,0:T(8,128)S(1)}, f32[208,128]{1,0:T(8,128)S(1)}, u32[]{:S(2)}, u32[]{:S(2)}) collective-permute-start(f32[208,128]{1,0:T(8,128)S(1)} %get-tuple-element.35), channel_id=1, source_target_pairs={{0,4},{4,0},{8,12},{12,8},{16,20},{20,16},{24,28},{28,24},{1,5},{5... | collective-permute-start | bytes 319496 | tf_op jit(solution)/shard_map/ppermute | solution.py:958
  11.6 0.7 %collective-permute-start.3 = (f32[208,128]{1,0:T(8,128)S(1)}, f32[208,128]{1,0:T(8,128)S(1)}, u32[]{:S(2)}, u32[]{:S(2)}) collective-permute-start(f32[208,128]{1,0:T(8,128)S(1)} %get-tuple-element.34), channel_id=1, source_target_pairs={{4,8},{8,4},{12,16},{16,12},{20,24},{24,20},{5,9},{9,5},{13,17},{1... | collective-permute-start | bytes 319496 | tf_op jit(solution)/shard_map/ppermute | solution.py:959
  12.3 0.3 collective-permute-done.2
  12.6 10.6 %all-to-all-start = ((f32[16,40,128]{2,1,0:T(8,128)}), f32[16,40,128]{2,1,0:T(8,128)S(1)}, u32[]{:S(2)}, u32[]{:S(2)}) async-start(f32[16,40,128]{2,1,0:T(8,128)} %bitcast.12), calls=%async_computation | async-start | bytes 655360 | tf_op jit(solution)/shard_map/all_to_all | solution.py:964
  23.2 0.0 collective-permute-done.3
  23.3 0.0 collective-permute-done.4.refs_5_.x_near
  23.3 0.0 collective-permute-done.5.refs_6_.x_far
  23.3 0.0 copy-start
  23.3 1.3 %copy-done = f32[2560,128]{1,0:T(8,128)S(1)} copy-done((f32[2560,128]{1,0:T(8,128)S(1)}, f32[2560,128]{1,0:T(8,128)}, u32[]{:S(2)}) %copy-start) | copy-done | bytes 1310744
  24.6 0.0 copy-start.4
  24.6 7.4 %down.1 = (f32[640,128]{1,0:T(8,128)}, f32[73728,128]{1,0:T(8,128)}) custom-call(f32[2560,128]{1,0:T(8,128)S(1)} %copy-done, f32[184,128]{1,0:T(8,128)S(1)} %get-tuple-element.37.refs_1_.yr, f32[184,128]{1,0:T(8,128)S(1)} %get-tuple-element.36.refs_2_.yl, f32[208,128]{1,0:T(8,128)S(1)} %get-tuple-element.33.refs_3_.cr, ...), custom_call_target="tpu_custom_call" | custom-call | flops 10000000000 | bytes 3219456 | tf_op jit(solution)/shard_map/down/pallas_call | solution.py:919
  32.0 2.8 %all-to-all-done = f32[16,40,128]{2,1,0:T(8,128)S(1)} async-done(((f32[16,40,128]{2,1,0:T(8,128)}), f32[16,40,128]{2,1,0:T(8,128)S(1)}, u32[]{:S(2)}, u32[]{:S(2)}) %all-to-all-start) | async-done | bytes 327712 | tf_op jit(solution)/shard_map/all_to_all | solution.py:964
  34.8 4.7 %all-to-all-start.1 = ((f32[16,40,128]{2,1,0:T(8,128)}), f32[16,40,128]{2,1,0:T(8,128)S(1)}, u32[]{:S(2)}, u32[]{:S(2)}) async-start(f32[16,40,128]{2,1,0:T(8,128)} %bitcast.7), calls=%async_computation.1 | async-start | bytes 655360 | tf_op jit(solution)/shard_map/all_to_all | solution.py:985
  39.5 0.1 collective-permute-start.7
  39.6 0.0 copy-done.4
  39.6 2.2 %window_coeffs.1.refs_3_ = f32[2064,128]{1,0:T(8,128)S(1)} custom-call(f32[192,128]{1,0:T(8,128)S(1)} %copy-done.4, f32[1472,128]{1,0:T(8,128)S(1)} %collective-permute-done.4.refs_5_.x_near, f32[1472,128]{1,0:T(8,128)S(1)} %collective-permute-done.5.refs_6_.x_far, f32[184,128]{1,0:T(8,128)S(1)} %get-tuple-element.37.refs_1_.yr, ...), custom_call_target="tpu_custom_call" | custom-call | flops 4000000000 | bytes 2007040 | tf_op jit(solution)/shard_map/window_coeffs/pallas_call | solution.py:919
  41.8 0.0 copy-start.2
  41.8 1.0 %copy-done.2 = f32[2064,128]{1,0:T(8,128)} copy-done((f32[2064,128]{1,0:T(8,128)}, f32[2064,128]{1,0:T(8,128)S(1)}, u32[]{:S(2)}) %copy-start.2) | copy-done | bytes 1056792
  42.8 0.0 copy-start.1
  42.8 7.7 %all-to-all-done.1.refs_0_ = f32[16,40,128]{2,1,0:T(8,128)S(1)} async-done(((f32[16,40,128]{2,1,0:T(8,128)}), f32[16,40,128]{2,1,0:T(8,128)S(1)}, u32[]{:S(2)}, u32[]{:S(2)}) %all-to-all-start.1) | async-done | bytes 327712 | tf_op jit(solution)/shard_map/all_to_all | solution.py:985
  50.5 0.0 copy-start.3
  50.5 0.0 collective-permute-start.6
  50.5 0.0 collective-permute-done.7.other
  50.5 1.5 %global_coeffs.1.refs_2_ = f32[3840,128]{1,0:T(8,128)S(1)} custom-call(f32[4,160,128]{2,1,0:T(8,128)S(1)} %bitcast.11, f32[4,160,128]{2,1,0:T(8,128)S(1)} %collective-permute-done.7.other), custom_call_target="tpu_custom_call" | custom-call | flops 4000000000 | bytes 655360 | tf_op jit(solution)/shard_map/global_coeffs/pallas_call | solution.py:919
  52.0 0.1 collective-permute-done.6.refs_1_
  52.1 0.0 copy-done.1
  52.1 0.0 copy-done.3
  52.1 9.2 %up.1 = (f32[512,128]{1,0:T(8,128)}, f32[512,128]{1,0:T(8,128)}) custom-call(f32[16,40,128]{2,1,0:T(8,128)S(1)} %all-to-all-done.1.refs_0_, f32[16,40,128]{2,1,0:T(8,128)S(1)} %collective-permute-done.6.refs_1_, f32[3840,128]{1,0:T(8,128)S(1)} %global_coeffs.1.refs_2_, f32[2064,128]{1,0:T(8,128)S(1)} %copy-done.3, f32[2560,128]{1,0:T(8,128)S(1)} %copy-done.1, ...), custom_call_target="tpu_custom_call" | custom-call | flops 12000000000 | bytes 42737664 | tf_op jit(solution)/shard_map/up/pallas_call | solution.py:919
  (9 shorter events, 0.1 us)
Async XLA Ops:
  4.0 5.9 %collective-permute-start = (f32[184,128]{1,0:T(8,128)}, f32[184,128]{1,0:T(8,128)S(1)}, u32[]{:S(2)}, u32[]{:S(2)}) collective-permute-start(f32[184,128]{1,0:T(8,128)} %get-tuple-element.18), channel_id=1, source_target_pairs={{0,1},{1,0},{2,3},{3,2},{4,5},{5,4},{6,7},{7,6},{8,9},{9,8},{10,11... | collective-permute-start | bytes 282632 | tf_op jit(solution)/shard_map/ppermute | solution.py:950
  7.0 2.9 %collective-permute-start.1 = (f32[184,128]{1,0:T(8,128)}, f32[184,128]{1,0:T(8,128)S(1)}, u32[]{:S(2)}, u32[]{:S(2)}) collective-permute-start(f32[184,128]{1,0:T(8,128)} %get-tuple-element.19), channel_id=1, source_target_pairs={{1,2},{2,1},{5,6},{6,5},{9,10},{10,9},{13,14},{14,13},{17,18},{18,... | collective-permute-start | bytes 282632 | tf_op jit(solution)/shard_map/ppermute | solution.py:951
  7.7 15.6 %collective-permute-start.4 = (f32[1472,128]{1,0:T(8,128)}, f32[1472,128]{1,0:T(8,128)S(1)}, u32[]{:S(2)}, u32[]{:S(2)}) collective-permute-start(f32[1472,128]{1,0:T(8,128)} %get-tuple-element.22), channel_id=1, source_target_pairs={{0,4},{4,0},{8,12},{12,8},{16,20},{20,16},{24,28},{28,24},{1,5},{5... | collective-permute-start | bytes 2261000 | tf_op jit(solution)/shard_map/ppermute | solution.py:952
  7.8 15.5 %collective-permute-start.5 = (f32[1472,128]{1,0:T(8,128)}, f32[1472,128]{1,0:T(8,128)S(1)}, u32[]{:S(2)}, u32[]{:S(2)}) collective-permute-start(f32[1472,128]{1,0:T(8,128)} %get-tuple-element.23), channel_id=1, source_target_pairs={{4,8},{8,4},{12,16},{16,12},{20,24},{24,20},{5,9},{9,5},{13,17},{1... | collective-permute-start | bytes 2261000 | tf_op jit(solution)/shard_map/ppermute | solution.py:953
  10.1 2.5 %collective-permute-start.2 = (f32[208,128]{1,0:T(8,128)S(1)}, f32[208,128]{1,0:T(8,128)S(1)}, u32[]{:S(2)}, u32[]{:S(2)}) collective-permute-start(f32[208,128]{1,0:T(8,128)S(1)} %get-tuple-element.35), channel_id=1, source_target_pairs={{0,4},{4,0},{8,12},{12,8},{16,20},{20,16},{24,28},{28,24},{1,5},{5... | collective-permute-start | bytes 319496 | tf_op jit(solution)/shard_map/ppermute | solution.py:958
  11.6 11.6 %collective-permute-start.3 = (f32[208,128]{1,0:T(8,128)S(1)}, f32[208,128]{1,0:T(8,128)S(1)}, u32[]{:S(2)}, u32[]{:S(2)}) collective-permute-start(f32[208,128]{1,0:T(8,128)S(1)} %get-tuple-element.34), channel_id=1, source_target_pairs={{4,8},{8,4},{12,16},{16,12},{20,24},{24,20},{5,9},{9,5},{13,17},{1... | collective-permute-start | bytes 319496 | tf_op jit(solution)/shard_map/ppermute | solution.py:959
  12.6 22.3 %all-to-all-start = ((f32[16,40,128]{2,1,0:T(8,128)}), f32[16,40,128]{2,1,0:T(8,128)S(1)}, u32[]{:S(2)}, u32[]{:S(2)}) async-start(f32[16,40,128]{2,1,0:T(8,128)} %bitcast.12), calls=%async_computation | async-start | bytes 655360 | tf_op jit(solution)/shard_map/all_to_all | solution.py:964
  23.3 1.3 %copy-start = (f32[2560,128]{1,0:T(8,128)S(1)}, f32[2560,128]{1,0:T(8,128)}, u32[]{:S(2)}) copy-start(f32[2560,128]{1,0:T(8,128)} %get-tuple-element.17.refs_0_.refs_4_) | copy-start | bytes 3932164
  24.6 15.0 %copy-start.4 = (f32[192,128]{1,0:T(8,128)S(1)}, f32[192,128]{1,0:T(8,128)}, u32[]{:S(2)}) copy-start(f32[192,128]{1,0:T(8,128)} %get-tuple-element.28.share2) | copy-start | bytes 294916
  34.8 15.6 %all-to-all-start.1 = ((f32[16,40,128]{2,1,0:T(8,128)}), f32[16,40,128]{2,1,0:T(8,128)S(1)}, u32[]{:S(2)}, u32[]{:S(2)}) async-start(f32[16,40,128]{2,1,0:T(8,128)} %bitcast.7), calls=%async_computation.1 | async-start | bytes 655360 | tf_op jit(solution)/shard_map/all_to_all | solution.py:985
  39.5 11.0 %collective-permute-start.7 = (f32[4,160,128]{2,1,0:T(8,128)S(1)}, f32[4,160,128]{2,1,0:T(8,128)S(1)}, u32[]{:S(2)}, u32[]{:S(2)}) collective-permute-start(f32[4,160,128]{2,1,0:T(8,128)S(1)} %bitcast.10), channel_id=1, source_target_pairs={{0,4},{4,0},{8,12},{12,8},{16,20},{20,16},{24,28},{28,24},{1,5},{5... | collective-permute-start | bytes 983048 | tf_op jit(solution)/shard_map/ppermute | solution.py:983
  41.8 1.0 %copy-start.2 = (f32[2064,128]{1,0:T(8,128)}, f32[2064,128]{1,0:T(8,128)S(1)}, u32[]{:S(2)}) copy-start(f32[2064,128]{1,0:T(8,128)S(1)} %window_coeffs.1.refs_3_) | copy-start | bytes 3170308
  42.8 9.3 %copy-start.1 = (f32[2560,128]{1,0:T(8,128)S(1)}, f32[2560,128]{1,0:T(8,128)}, u32[]{:S(2)}) copy-start(f32[2560,128]{1,0:T(8,128)} %get-tuple-element.17.refs_0_.refs_4_) | copy-start | bytes 3932164
  50.5 1.6 %copy-start.3 = (f32[2064,128]{1,0:T(8,128)S(1)}, f32[2064,128]{1,0:T(8,128)}, u32[]{:S(2)}) copy-start(f32[2064,128]{1,0:T(8,128)} %copy-done.2) | copy-start | bytes 3170308
  50.5 1.6 %collective-permute-start.6 = (f32[16,40,128]{2,1,0:T(8,128)S(1)}, f32[16,40,128]{2,1,0:T(8,128)S(1)}, u32[]{:S(2)}, u32[]{:S(2)}) collective-permute-start(f32[16,40,128]{2,1,0:T(8,128)S(1)} %all-to-all-done.1.refs_0_), channel_id=1, source_target_pairs={{0,4},{4,0},{8,12},{12,8},{16,20},{20,16},{24,28},{28,24},{1,5},{5... | collective-permute-start | bytes 983048 | tf_op jit(solution)/shard_map/ppermute | solution.py:986
